TPU v7x, 32 devices: a whole 2x2x4 slice. The times are simulated.
32 devices in a mesh: pert: 4 (over y, x), doc: 8 (over z, core).
Axes of the slice: x: 2, y: 2, z: 4, core: 2. Of those that a mesh axis runs over, the one named last changes fastest.
Arguments:
- counts: int32 [4, 64, 16384], P('pert', 'doc'), may hold values from 1 to 11
- tile_mask: int32 [4, 64, 128], P('pert', 'doc'), may hold values 0 or 1
- member_topics: float32 [4, 64, 64], P('pert', 'doc'), may hold values from 0.05 to 0.5
- start_dict: float32 [4, 16384, 64], P('pert', 'doc'), may hold values from 0.05 to 0.5
- align_perm: int32 [4, 64], P('pert'), may hold values from 0 to 63, each once within a row
- base_counts: int32 [128, 16384], P(('pert', 'doc')), may hold values from 1 to 11
- base_topics: float32 [128, 64], P(('pert', 'doc')), may hold values from 0.05 to 0.5
Outputs:
- median_dict: float32 [8, 4, 512, 64], P('doc', 'pert')
- refit_topics: float32 [128, 64], P(('pert', 'doc'))
Inputs may be any that keep to these rules, and one draw needn't show every extreme that they name: `align_perm`: each row is a permutation of 0 to 63.
All inputs are finite; a program needn't handle non-finite values. No bound on the sum of `tile_mask` on one device may be relied on, other than what follows from the above.
Results may differ from a plain program's by a relative error of at most 0.0003.
Values sent between devices are 32-bit elements; how exact they have to be, the bound alone decides.
No kernel may reach another device: no remote copies, remote signals or barrier semaphores. Data moves between devices by JAX's collectives and lax.ppermute only.
A program may use at most 64 MiB of HBM per device.

v0:
```python
import functools

import jax
import jax.numpy as jnp
from jax import lax
from jax.experimental import pallas as pl
from jax.experimental.pallas import tpu as pltpu
from jax.sharding import PartitionSpec as P

UPDATES = 3
REFITS = 2

EXACT = lax.Precision.HIGHEST
ROUGH = lax.Precision.HIGH
VMEM_BYTES = 14 * 1024 * 1024
SPREAD_BYTES = 60 * 1024 * 1024


def dot(left, right, dims, precision=ROUGH):
    return lax.dot_general(left, right, (dims, ((), ())), precision=precision)


def middle(pieces):
    pieces = list(pieces)
    count = len(pieces)
    for turn in range(count):
        for low in range(turn % 2, count - 1, 2):
            pieces[low], pieces[low + 1] = (
                jnp.minimum(pieces[low], pieces[low + 1]),
                jnp.maximum(pieces[low], pieces[low + 1]),
            )
    return 0.5 * (pieces[count // 2 - 1] + pieces[count // 2])


def call(kernel, outs, *args, flops=0, moved=0):
    return pl.pallas_call(
        kernel,
        out_shape=outs,
        compiler_params=pltpu.CompilerParams(vmem_limit_bytes=VMEM_BYTES),
        cost_estimate=pl.CostEstimate(flops=flops, bytes_accessed=moved, transcendentals=0),
    )(*args)


def shape(*dims, dtype=jnp.float32):
    return jax.ShapeDtypeStruct(dims, dtype)


def high_low(x):
    high = x.astype(jnp.bfloat16).astype(jnp.float32)
    return high, x - high


def matmul(left, right):
    return jnp.dot(
        left.astype(jnp.bfloat16), right.astype(jnp.bfloat16), preferred_element_type=jnp.float32
    )


def spread_kernel(chips, cores, own_words, counts_hbm, mask_hbm, topics_hbm, base_hbm, base_topics_hbm, *refs):
    out_refs, (counts_ref, mask_ref, topics_ref, base_ref, base_topics_ref, sems) = (
        refs[:-6],
        refs[-6:],
    )
    copies = [
        pltpu.make_async_copy(src, dst, sems.at[at])
        for at, (src, dst) in enumerate(
            [
                (mask_hbm, mask_ref),
                (counts_hbm, counts_ref),
                (topics_hbm, topics_ref),
                (base_hbm, base_ref),
                (base_topics_hbm, base_topics_ref),
            ]
        )
    ]
    for copy in copies:
        copy.start()
    docs, words = counts_ref.shape
    base_docs = base_ref.shape[0]
    tiles = mask_ref.shape[1]
    width = words // tiles
    own_tiles = own_words // width
    at_doc = lax.axis_index("doc")
    at_chip, at_core = at_doc // cores, at_doc % cores
    tile_ids = lax.broadcasted_iota(jnp.int32, (docs, tiles), 1)
    doc_ids = at_doc * docs + lax.broadcasted_iota(jnp.int32, (docs, tiles), 0)
    forced = (tile_ids == doc_ids % tiles).astype(jnp.int32)
    copies[0].wait()
    occupied = jnp.maximum(mask_ref[...], forced).astype(jnp.float32)
    for copy in copies[1:]:
        copy.wait()
    for step in range(chips):
        base_out, base_row = (out_refs[step], docs) if step < 2 else (out_refs[chips + step - 2], 0)
        base_rows = slice(base_row, base_row + base_docs)
        for half in range(cores):
            block = (at_chip ^ step) * cores + (at_core ^ ((step + half) % cores))
            first = pl.multiple_of(block * own_words, 128)
            near = pltpu.roll(occupied, lax.rem(tiles - block * own_tiles, tiles), 1)
            for tile in range(own_tiles):
                at = slice(half * own_words + tile * width, half * own_words + (tile + 1) * width)
                picked = counts_ref[:, pl.ds(first + tile * width, width)].astype(jnp.float32)
                out_refs[step][:docs, at] = picked * near[:, tile : tile + 1]
            at = slice(half * own_words, (half + 1) * own_words)
            base_out[base_rows, at] = base_ref[:, pl.ds(first, own_words)].astype(jnp.float32)
        out_refs[step][:docs, cores * own_words :] = topics_ref[...]
        base_out[base_rows, cores * own_words :] = base_topics_ref[...]


def moved_columns(x, onehot):
    rows = x.shape[0]
    high, rest = high_low(x)
    mid, low = high_low(rest)
    moved = matmul(jnp.concatenate([high, mid, low], axis=0), onehot)
    return moved[:rows] + moved[rows : 2 * rows] + moved[2 * rows :]


def dictionary_kernel(half_count, perm_ref, *refs):
    topics, words = refs[0].shape
    wide_ref, tall_ref, total_ref, aligned_ref, onehot_ref = refs[half_count:]
    onehot = (
        lax.broadcasted_iota(jnp.int32, (topics, topics), 0) == perm_ref[...]
    ).astype(jnp.float32)
    onehot_ref[...] = onehot
    total = jnp.zeros((1, topics), jnp.float32)
    for half in range(half_count):
        at = slice(half * words, (half + 1) * words)
        full = refs[half][...]
        high, rest = high_low(full)
        mid, low = high_low(rest)
        wide_ref[:topics, at] = high.astype(jnp.bfloat16)
        wide_ref[topics:, at] = rest.astype(jnp.bfloat16)
        if half == 0:
            turned = onehot.T
            aligned_ref[...] = matmul(
                jnp.concatenate([turned] * 3, axis=1), jnp.concatenate([high, mid, low], axis=0)
            )
        tall = full.T
        total += jnp.sum(tall, axis=0, keepdims=True)
        tall_ref[at, :] = jnp.concatenate(high_low(tall), axis=1).astype(jnp.bfloat16)
    total_ref[...] = jnp.broadcast_to(total, total_ref.shape)


def recon_of(topics, wide):
    rows = topics.shape[0]
    high, low = high_low(topics)
    left = jnp.concatenate(
        [jnp.concatenate([high, high], axis=1), jnp.concatenate([low, low], axis=1)], axis=0
    )
    both = matmul(left, wide)
    return both[:rows] + both[rows:]


def product_of(quotient, tall):
    rows, topics = quotient.shape[0], tall.shape[1] // 2
    both = matmul(jnp.concatenate(high_low(quotient), axis=0), tall)
    both = both[:rows] + both[rows:]
    return both[:, :topics] + both[:, topics:]


def sum_blocks(rows, own, got):
    chips = len(got) + 1
    total = own[: chips * rows]
    for step in range(1, chips):
        total = total + jnp.concatenate(
            [got[step - 1][(c ^ step) * rows : ((c ^ step) + 1) * rows] for c in range(chips)], axis=0
        )
    return total


def first_kernel(chips, wide_ref, tall_ref, *refs):
    payload, (topics_ref, part_ref) = refs[:chips], refs[chips:]
    docs = topics_ref.shape[0] // chips
    span = wide_ref.shape[1]
    topics = jnp.concatenate([ref[:docs, span:] for ref in payload], axis=0)
    topics_ref[...] = topics
    weighted = jnp.concatenate([ref[:docs, :span] for ref in payload], axis=0)
    part_ref[...] = product_of(weighted / recon_of(topics, wide_ref[...]), tall_ref[...])


def update_kernel(chips, wide_ref, tall_ref, before_ref, total_ref, *refs):
    payload, parts, (topics_ref, part_ref) = refs[:chips], refs[chips : 2 * chips], refs[2 * chips :]
    docs = topics_ref.shape[0] // chips
    span = wide_ref.shape[1]
    total = sum_blocks(docs, parts[0][...], [ref[...] for ref in parts[1:]])
    topics = before_ref[...] * total / total_ref[:1]
    topics_ref[...] = topics
    weighted = jnp.concatenate([ref[:docs, :span] for ref in payload], axis=0)
    part_ref[...] = product_of(weighted / recon_of(topics, wide_ref[...]), tall_ref[...])


def numerator_of(topics, quotient):
    high, low = high_low(topics.T)
    quotient_high, quotient_low = high_low(quotient)
    return matmul(
        jnp.concatenate([high, low, high], axis=1),
        jnp.concatenate([quotient_high, quotient_high, quotient_low], axis=0),
    )


def last_kernel(chips, cores, wide_ref, onehot_ref, before_ref, total_ref, *refs):
    payload, parts, (topics_ref, out_ref) = refs[:chips], refs[chips : 2 * chips], refs[2 * chips :]
    docs = topics_ref.shape[0] // chips
    words = wide_ref.shape[1] // cores
    at = slice((cores - 1) * words, cores * words)
    total = sum_blocks(docs, parts[0][...], [ref[...] for ref in parts[1:]])
    topics = before_ref[...] * total / total_ref[:1]
    weighted = jnp.concatenate([ref[:docs, at] for ref in payload], axis=0)
    aligned = moved_columns(topics, onehot_ref[...])
    topics_ref[...] = jnp.concatenate([topics, aligned], axis=1)
    out_ref[:, :words] = numerator_of(aligned, weighted / recon_of(topics, wide_ref[:, at]))
    load = jnp.sum(aligned.T, axis=1, keepdims=True)
    out_ref[:, words:] = jnp.broadcast_to(load, (load.shape[0], out_ref.shape[1] - words))


def own_kernel(chips, wide_ref, topics_ref, *refs):
    payload, out_ref = refs[:chips], refs[chips]
    words = out_ref.shape[1]
    topic_count = out_ref.shape[0]
    topics, aligned = topics_ref[:, :topic_count], topics_ref[:, topic_count:]
    docs = topics.shape[0] // chips
    weighted = jnp.concatenate([ref[:docs, :words] for ref in payload], axis=0)
    out_ref[...] = numerator_of(aligned, weighted / recon_of(topics, wide_ref[:, :words]))


def aligned_kernel(own_ref, sent_ref, got_ref, dict_ref, out_ref):
    words = out_ref.shape[1]
    load = sent_ref[:, words : words + 1] + got_ref[:, words : words + 1]
    out_ref[...] = dict_ref[...] * (own_ref[...] + got_ref[:, :words]) / load


def base_rows_of(refs, base_docs, at):
    return jnp.concatenate([ref[ref.shape[0] - base_docs :, at] for ref in refs], axis=0)


def refit_kernel(chips, half, base_docs, median_ref, *refs):
    payload, before = refs[:chips], refs[chips:-4]
    wide_ref, tall_ref, part_ref, total_ref = refs[-4:]
    topics, words = median_ref.shape
    span = payload[0].shape[1] - topics
    high, low = high_low(median_ref[...])
    wide = jnp.concatenate([high, low], axis=0).astype(jnp.bfloat16)
    wide_ref[...] = wide
    tall_full = median_ref[...].T
    total = jnp.sum(tall_full, axis=0, keepdims=True)
    tall = jnp.concatenate(high_low(tall_full), axis=1).astype(jnp.bfloat16)
    tall_ref[...] = tall
    weighted = base_rows_of(payload, base_docs, slice(half * words, (half + 1) * words))
    refit = base_rows_of(payload, base_docs, slice(span, span + topics))
    part = product_of(weighted / recon_of(refit, wide), tall)
    if before:
        part = part + before[0][...]
        total = total + before[1][:1]
    part_ref[: part.shape[0]] = part
    if part_ref.shape[0] > part.shape[0]:
        part_ref[part.shape[0] :] = jnp.broadcast_to(total, (8, topics))
    total_ref[...] = jnp.broadcast_to(total, total_ref.shape)


def refit_again_kernel(chips, cores, base_docs, *refs):
    payload, parts, halves, (topics_ref, part_ref, total_ref) = (
        refs[:chips],
        refs[chips : 2 * chips],
        refs[2 * chips : -3],
        refs[-3:],
    )
    rows, topics = topics_ref.shape
    span = payload[0].shape[1] - topics
    words = span // cores
    total = sum_blocks(base_docs, parts[0][...], [ref[...] for ref in parts[1:]])
    median_total = parts[0][rows : rows + 1]
    for ref in parts[1:]:
        median_total = median_total + ref[rows : rows + 1]
    refit = base_rows_of(payload, base_docs, slice(span, span + topics)) * total / median_total
    topics_ref[...] = refit
    total_ref[...] = jnp.broadcast_to(median_total, total_ref.shape)
    part = jnp.zeros((rows, topics), jnp.float32)
    for half in range(cores):
        weighted = base_rows_of(payload, base_docs, slice(half * words, (half + 1) * words))
        wide_ref, tall_ref = halves[2 * half], halves[2 * half + 1]
        part = part + product_of(weighted / recon_of(refit, wide_ref[...]), tall_ref[...])
    part_ref[...] = part


def per_device(counts, tile_mask, member_topics, start_dict, align_perm, base_counts, base_topics):
    doc_size = lax.axis_size("doc")
    members = lax.axis_size("pert")
    cores = 2 - doc_size % 2
    chips = doc_size // cores
    at_pert = lax.axis_index("pert")
    at_doc = lax.axis_index("doc")
    at_chip, at_core = at_doc // cores, at_doc % cores
    docs = counts.shape[1]
    base_docs = base_counts.shape[0]
    topic_count = member_topics.shape[2]
    owned = start_dict.shape[1]
    span = cores * owned
    rows = chips * docs
    sub = owned // members

    def over_chips(array, step):
        return lax.ppermute(
            array,
            "doc",
            [
                (c * cores + k, (c ^ step) * cores + (k + step) % cores)
                for c in range(chips)
                for k in range(cores)
            ],
        )

    def over_cores(array):
        return lax.ppermute(array, "doc", [(d, d ^ 1) for d in range(doc_size)])

    def over_pert(array, step):
        return lax.ppermute(array, "pert", [(m, m ^ step) for m in range(members)])

    paired = min(chips, 2)
    sent = pl.pallas_call(
        functools.partial(spread_kernel, chips, cores, owned),
        out_shape=[
            shape(docs + (base_docs if step < paired else 0), span + topic_count)
            for step in range(chips)
        ]
        + [shape(base_docs, span + topic_count) for _ in range(paired, chips)],
        in_specs=[pl.BlockSpec(memory_space=pltpu.HBM)] * 5,
        scratch_shapes=[
            pltpu.VMEM(counts.shape[1:], jnp.int32),
            pltpu.VMEM(tile_mask.shape[1:], jnp.int32),
            pltpu.VMEM(member_topics.shape[1:], jnp.float32),
            pltpu.VMEM(base_counts.shape, jnp.int32),
            pltpu.VMEM(base_topics.shape, jnp.float32),
            pltpu.SemaphoreType.DMA((5,)),
        ],
        compiler_params=pltpu.CompilerParams(vmem_limit_bytes=SPREAD_BYTES),
        cost_estimate=pl.CostEstimate(flops=0, bytes_accessed=12 * counts.size, transcendentals=0),
    )(counts[0], tile_mask[0], member_topics[0], base_counts, base_topics)
    sent, base_sent = sent[:chips], sent[chips:]
    got = [over_chips(sent[step], step) for step in range(1, chips)]
    payload = [sent[0]] + got
    dict_own = start_dict[0].T
    halves = [dict_own] + [over_cores(dict_own)] * (cores - 1)
    sent, halves = lax.optimization_barrier((sent, halves))
    wide, tall, col_part, dict_own, onehot = call(
        functools.partial(dictionary_kernel, cores),
        [
            shape(2 * topic_count, span, dtype=jnp.bfloat16),
            shape(span, 2 * topic_count, dtype=jnp.bfloat16),
            shape(8, topic_count),
            shape(topic_count, owned),
            shape(topic_count, topic_count),
        ],
        align_perm,
        *halves,
        moved=4 * 4 * span * topic_count,
    )

    update_flops = 2 * 2 * 4 * rows * topic_count * span
    topics, part = call(
        functools.partial(first_kernel, chips),
        [shape(rows, topic_count), shape(rows, topic_count)],
        wide,
        tall,
        *payload,
        flops=update_flops,
        moved=4 * span * (rows + 2 * topic_count),
    )
    part = jnp.concatenate([part, col_part], axis=0)
    parts = [part] + [over_chips(part, step) for step in range(1, chips)]
    col_total = sum(p[rows:] for p in parts)
    for update in range(1, UPDATES):
        topics, part = call(
            functools.partial(update_kernel, chips),
            [shape(rows, topic_count), shape(rows, topic_count)],
            wide,
            tall,
            topics,
            col_total,
            *payload,
            *parts,
            flops=update_flops,
            moved=4 * span * (rows + 2 * topic_count),
        )
        parts = [part] + [over_chips(part, step) for step in range(1, chips)]

    topics, numerator = call(
        functools.partial(last_kernel, chips, cores),
        [shape(rows, 2 * topic_count), shape(topic_count, owned + 128)],
        wide,
        onehot,
        topics,
        col_total,
        *payload,
        *parts,
        flops=update_flops // 2,
        moved=2 * span * (rows + 2 * topic_count),
    )
    if cores > 1:
        got_half = over_cores(numerator)
        own_half = call(
            functools.partial(own_kernel, chips),
            shape(topic_count, owned),
            wide,
            topics,
            *payload,
            flops=update_flops // 2,
            moved=2 * span * (rows + 2 * topic_count),
        )
    else:
        got_half = jnp.zeros_like(numerator)
        own_half = numerator[:, :owned]
    aligned = call(
        aligned_kernel,
        shape(topic_count, owned),
        own_half,
        numerator,
        got_half,
        dict_own,
        moved=16 * topic_count * owned,
    )

    def words_of(array, member):
        return lax.dynamic_slice_in_dim(array, member * sub, sub, 1)

    aligned, base_sent = lax.optimization_barrier((aligned, base_sent))
    base_got = [over_chips(base_sent[step - paired], step) for step in range(paired, chips)]
    pieces = [words_of(aligned, at_pert)] + [
        over_pert(words_of(aligned, at_pert ^ step), step) for step in range(1, members)
    ]
    late = len(base_got) // 2
    pieces[1], base_got[late:] = lax.optimization_barrier((pieces[1], base_got[late:]))
    median = middle(pieces)
    gathered = [over_pert(median, step) for step in range(1, members)]
    gathered[0], base_got[:late] = lax.optimization_barrier((gathered[0], base_got[:late]))
    median_own = jnp.zeros((topic_count, owned), jnp.float32)
    for step, piece in enumerate([median] + gathered):
        median_own = lax.dynamic_update_slice_in_dim(median_own, piece, (at_pert ^ step) * sub, 1)
    base_all = list(payload[:paired]) + list(base_got)

    median_halves = [median_own] + [over_cores(median_own)] * (cores - 1)
    base_rows = chips * base_docs
    refit_flops = 2 * 2 * 4 * base_rows * topic_count * owned
    forms, before = [], []
    for half in range(cores):
        last = half == cores - 1
        wide, tall, part, total = call(
            functools.partial(refit_kernel, chips, half, base_docs),
            [
                shape(2 * topic_count, owned, dtype=jnp.bfloat16),
                shape(owned, 2 * topic_count, dtype=jnp.bfloat16),
                shape(base_rows + (8 if last else 0), topic_count),
                shape(8, topic_count),
            ],
            median_halves[half],
            *base_all,
            *before,
            flops=refit_flops,
            moved=16 * owned * topic_count,
        )
        forms += [wide, tall]
        before = [part, total]
    parts = [part] + [over_chips(part, step) for step in range(1, chips)]
    refit, part, median_total = call(
        functools.partial(refit_again_kernel, chips, cores, base_docs),
        [shape(base_rows, topic_count), shape(base_rows, topic_count), shape(8, topic_count)],
        *base_all,
        *parts,
        *forms,
        flops=2 * refit_flops,
        moved=16 * owned * topic_count,
    )
    total = part[:base_docs]
    for step in range(1, chips):
        total = total + over_chips(part[step * base_docs : (step + 1) * base_docs], step)
    refit = refit[:base_docs] * total / median_total[:1]
    return (median.T[None, None], refit)


def solution(mesh):
    return jax.shard_map(
        per_device,
        mesh=mesh,
        in_specs=(
            P("pert", "doc", None),
            P("pert", "doc", None),
            P("pert", "doc", None),
            P("pert", "doc", None),
            P("pert", None),
            P(("pert", "doc"), None),
            P(("pert", "doc"), None),
        ),
        out_specs=(P("doc", "pert", None, None), P(("pert", "doc"), None)),
        check_vma=False,
    )
```

profile of v0, /device:TPU:0, one launch (start us, length us, event | category | flops | bytes accessed | tf_op | source)
XLA Modules:
  0.0 86.1 jit_solution(14827459996628600242)
XLA Ops:
  0.6 0.5 collective-permute-start
  1.2 2.5 %shard_map.86 = (f32[12,4160]{1,0:T(8,128)}, f32[12,4160]{1,0:T(8,128)}, f32[8,4160]{1,0:T(8,128)}, f32[8,4160]{1,0:T(8,128)}, f32[4,4160]{1,0:T(4,128)}, /*index=5*/f32[4,4160]{1,0:T(4,128)}) custom-call(s32[8,16384]{1,0:T(8,128)} %bitcast.13, s32[8,128]{1,0:T(8,128)} %bitcast.15, f32[8,64]{1,0:T(8,128)} %bitcast.16, s32[4,16384]{1,0:T(4,128)} %base_hbm.1, ...), custom_call_target="tpu_custom_call" | custom-call | bytes 1572864 | tf_op jit(solution)/shard_map/pallas_call | solution.py:318
  3.7 2.8 %collective-permute-start.1 = (f32[12,4160]{1,0:T(8,128)}, f32[12,4160]{1,0:T(8,128)S(1)}, u32[]{:S(2)}, u32[]{:S(2)}) collective-permute-start(f32[12,4160]{1,0:T(8,128)} %get-tuple-element.41), channel_id=1, source_target_pairs={{0,3},{1,2},{2,1},{3,0},{4,7},{5,6},{6,5},{7,4},{8,11},{9,10},{10,... | collective-permute-start | bytes 599048 | tf_op jit(solution)/shard_map/ppermute | solution.py:301
  6.4 2.6 %collective-permute-start.2 = (f32[8,4160]{1,0:T(8,128)}, f32[8,4160]{1,0:T(8,128)S(1)}, u32[]{:S(2)}, u32[]{:S(2)}) collective-permute-start(f32[8,4160]{1,0:T(8,128)} %get-tuple-element.42), channel_id=1, source_target_pairs={{0,4},{1,5},{2,6},{3,7},{4,0},{5,1},{6,2},{7,3},{8,12},{9,13},{10,... | collective-permute-start | bytes 399368 | tf_op jit(solution)/shard_map/ppermute | solution.py:301
  9.0 0.0 collective-permute-start.3
  9.0 0.0 collective-permute-done.refs_1_
  9.0 0.6 copy-done.2
  9.7 1.1 %shard_map.87 = (bf16[128,4096]{1,0:T(8,128)(2,1)S(1)}, bf16[4096,128]{1,0:T(8,128)(2,1)S(1)}, f32[8,64]{1,0:T(8,128)S(1)}, f32[64,2048]{1,0:T(8,128)S(1)}, f32[64,64]{1,0:T(8,128)S(1)}) custom-call(s32[1,64]{1,0:T(1,128)S(1)} %copy-done.2, f32[64,2048]{1,0:T(8,128)S(1)} %bitcast.12, f32[64,2048]{1,0:T(8,128)S(1)} %collective-permute-done.refs_1_), custom_call_target="tpu_custom_call" | custom-call | bytes 4194304 | tf_op jit(solution)/shard_map/pallas_call | solution.py:36
  10.7 5.7 %collective-permute-done.2.refs_2_ = f32[8,4160]{1,0:T(8,128)S(1)} collective-permute-done((f32[8,4160]{1,0:T(8,128)}, f32[8,4160]{1,0:T(8,128)S(1)}, u32[]{:S(2)}, u32[]{:S(2)}) %collective-permute-start.2) | collective-permute-done | bytes 133152 | tf_op jit(solution)/shard_map/ppermute | solution.py:301
  16.5 4.6 %collective-permute-done.3.refs_3_ = f32[8,4160]{1,0:T(8,128)S(1)} collective-permute-done((f32[8,4160]{1,0:T(8,128)}, f32[8,4160]{1,0:T(8,128)S(1)}, u32[]{:S(2)}, u32[]{:S(2)}) %collective-permute-start.3) | collective-permute-done | bytes 133152 | tf_op jit(solution)/shard_map/ppermute | solution.py:301
  21.1 0.0 collective-permute-done.1.refs_1_
  21.1 0.6 shard_map.88
  21.7 0.7 collective-permute-start.4
  22.5 1.4 %collective-permute-start.5 = (f32[40,64]{1,0:T(8,128)S(1)}, f32[40,64]{1,0:T(8,128)S(1)}, u32[]{:S(2)}, u32[]{:S(2)}) collective-permute-start(f32[40,64]{1,0:T(8,128)S(1)} %constant_dynamic-update-slice_fusion.refs_4_), channel_id=1, source_target_pairs={{0,4},{1,5},{2,6},{3,7},{4,0},{5,1},{6,2},{7,3},{8,12},{9,13},{10,... | collective-permute-start | bytes 30728 | tf_op jit(solution)/shard_map/ppermute | solution.py:301
  23.8 1.8 %collective-permute-start.6 = (f32[40,64]{1,0:T(8,128)S(1)}, f32[40,64]{1,0:T(8,128)S(1)}, u32[]{:S(2)}, u32[]{:S(2)}) collective-permute-start(f32[40,64]{1,0:T(8,128)S(1)} %constant_dynamic-update-slice_fusion.refs_4_), channel_id=1, source_target_pairs={{0,7},{1,6},{2,5},{3,4},{4,3},{5,2},{6,1},{7,0},{8,15},{9,14},{10,... | collective-permute-start | bytes 30728 | tf_op jit(solution)/shard_map/ppermute | solution.py:301
  25.6 1.7 %collective-permute-done.5.refs_6_ = f32[40,64]{1,0:T(8,128)S(1)} collective-permute-done((f32[40,64]{1,0:T(8,128)S(1)}, f32[40,64]{1,0:T(8,128)S(1)}, u32[]{:S(2)}, u32[]{:S(2)}) %collective-permute-start.5) | collective-permute-done | bytes 10272 | tf_op jit(solution)/shard_map/ppermute | solution.py:301
  27.3 1.7 %collective-permute-done.6.refs_7_ = f32[40,64]{1,0:T(8,128)S(1)} collective-permute-done((f32[40,64]{1,0:T(8,128)S(1)}, f32[40,64]{1,0:T(8,128)S(1)}, u32[]{:S(2)}, u32[]{:S(2)}) %collective-permute-start.6) | collective-permute-done | bytes 10272 | tf_op jit(solution)/shard_map/ppermute | solution.py:301
  29.1 0.6 shard_map.89
  29.6 0.0 collective-permute-start.7
  29.7 2.6 %collective-permute-start.8 = (f32[32,64]{1,0:T(8,128)S(1)}, f32[32,64]{1,0:T(8,128)S(1)}, u32[]{:S(2)}, u32[]{:S(2)}) collective-permute-start(f32[32,64]{1,0:T(8,128)S(1)} %get-tuple-element.53.refs_4_), channel_id=1, source_target_pairs={{0,4},{1,5},{2,6},{3,7},{4,0},{5,1},{6,2},{7,3},{8,12},{9,13},{10,... | collective-permute-start | bytes 24584 | tf_op jit(solution)/shard_map/ppermute | solution.py:301
  32.3 1.2 %collective-permute-start.9 = (f32[32,64]{1,0:T(8,128)S(1)}, f32[32,64]{1,0:T(8,128)S(1)}, u32[]{:S(2)}, u32[]{:S(2)}) collective-permute-start(f32[32,64]{1,0:T(8,128)S(1)} %get-tuple-element.53.refs_4_), channel_id=1, source_target_pairs={{0,7},{1,6},{2,5},{3,4},{4,3},{5,2},{6,1},{7,0},{8,15},{9,14},{10,... | collective-permute-start | bytes 24584 | tf_op jit(solution)/shard_map/ppermute | solution.py:301
  33.5 0.9 %collective-permute-done.8.refs_6_ = f32[32,64]{1,0:T(8,128)S(1)} collective-permute-done((f32[32,64]{1,0:T(8,128)S(1)}, f32[32,64]{1,0:T(8,128)S(1)}, u32[]{:S(2)}, u32[]{:S(2)}) %collective-permute-start.8) | collective-permute-done | bytes 8224 | tf_op jit(solution)/shard_map/ppermute | solution.py:301
  34.4 2.9 %collective-permute-done.9.refs_7_ = f32[32,64]{1,0:T(8,128)S(1)} collective-permute-done((f32[32,64]{1,0:T(8,128)S(1)}, f32[32,64]{1,0:T(8,128)S(1)}, u32[]{:S(2)}, u32[]{:S(2)}) %collective-permute-start.9) | collective-permute-done | bytes 8224 | tf_op jit(solution)/shard_map/ppermute | solution.py:301
  37.2 0.6 shard_map.90
  37.8 0.0 collective-permute-start.10
  37.8 1.8 %collective-permute-start.11 = (f32[32,64]{1,0:T(8,128)S(1)}, f32[32,64]{1,0:T(8,128)S(1)}, u32[]{:S(2)}, u32[]{:S(2)}) collective-permute-start(f32[32,64]{1,0:T(8,128)S(1)} %get-tuple-element.55.refs_4_), channel_id=1, source_target_pairs={{0,4},{1,5},{2,6},{3,7},{4,0},{5,1},{6,2},{7,3},{8,12},{9,13},{10,... | collective-permute-start | bytes 24584 | tf_op jit(solution)/shard_map/ppermute | solution.py:301
  39.7 2.0 %collective-permute-start.12 = (f32[32,64]{1,0:T(8,128)S(1)}, f32[32,64]{1,0:T(8,128)S(1)}, u32[]{:S(2)}, u32[]{:S(2)}) collective-permute-start(f32[32,64]{1,0:T(8,128)S(1)} %get-tuple-element.55.refs_4_), channel_id=1, source_target_pairs={{0,7},{1,6},{2,5},{3,4},{4,3},{5,2},{6,1},{7,0},{8,15},{9,14},{10,... | collective-permute-start | bytes 24584 | tf_op jit(solution)/shard_map/ppermute | solution.py:301
  41.7 1.0 %collective-permute-done.11.refs_6_ = f32[32,64]{1,0:T(8,128)S(1)} collective-permute-done((f32[32,64]{1,0:T(8,128)S(1)}, f32[32,64]{1,0:T(8,128)S(1)}, u32[]{:S(2)}, u32[]{:S(2)}) %collective-permute-start.11) | collective-permute-done | bytes 8224 | tf_op jit(solution)/shard_map/ppermute | solution.py:301
  42.7 1.9 %collective-permute-done.12.refs_7_ = f32[32,64]{1,0:T(8,128)S(1)} collective-permute-done((f32[32,64]{1,0:T(8,128)S(1)}, f32[32,64]{1,0:T(8,128)S(1)}, u32[]{:S(2)}, u32[]{:S(2)}) %collective-permute-start.12) | collective-permute-done | bytes 8224 | tf_op jit(solution)/shard_map/ppermute | solution.py:301
  44.6 0.5 shard_map.91
  45.1 0.2 collective-permute-start.13
  45.3 0.4 shard_map.92.own_ref
  45.8 1.4 %collective-permute-done.13.got_ref = f32[64,2176]{1,0:T(8,128)S(1)} collective-permute-done((f32[64,2176]{1,0:T(8,128)S(1)}, f32[64,2176]{1,0:T(8,128)S(1)}, u32[]{:S(2)}, u32[]{:S(2)}) %collective-permute-start.13) | collective-permute-done | bytes 557088 | tf_op jit(solution)/shard_map/ppermute | solution.py:312
  47.1 0.1 shard_map.93
  47.3 0.0 copy-start.5
  47.3 1.5 %collective-permute-start.14 = (f32[64,512]{1,0:T(8,128)S(1)}, f32[64,512]{1,0:T(8,128)S(1)}, u32[]{:S(2)}, u32[]{:S(2)}) collective-permute-start(f32[64,512]{1,0:T(8,128)S(1)} %get-tuple-element.80), channel_id=1, source_target_pairs={{0,8},{8,0},{16,24},{24,16},{1,9},{9,1},{17,25},{25,17},{2,10},{10... | collective-permute-start | bytes 393224 | tf_op jit(solution)/shard_map/ppermute | solution.py:315
  48.9 1.5 %collective-permute-start.16 = (f32[64,512]{1,0:T(8,128)S(1)}, f32[64,512]{1,0:T(8,128)S(1)}, u32[]{:S(2)}, u32[]{:S(2)}) collective-permute-start(f32[64,512]{1,0:T(8,128)S(1)} %get-tuple-element.82), channel_id=1, source_target_pairs={{0,16},{8,24},{16,0},{24,8},{1,17},{9,25},{17,1},{25,9},{2,18},{10... | collective-permute-start | bytes 393224 | tf_op jit(solution)/shard_map/ppermute | solution.py:315
  50.4 0.5 collective-permute-start.17
  50.9 1.2 %collective-permute-start.15 = (f32[4,4160]{1,0:T(4,128)S(1)}, f32[4,4160]{1,0:T(4,128)S(1)}, u32[]{:S(2)}, u32[]{:S(2)}) collective-permute-start(f32[4,4160]{1,0:T(4,128)S(1)} %copy-done.5), channel_id=1, source_target_pairs={{0,7},{1,6},{2,5},{3,4},{4,3},{5,2},{6,1},{7,0},{8,15},{9,14},{10,... | collective-permute-start | bytes 199688 | tf_op jit(solution)/shard_map/ppermute | solution.py:301
  52.1 4.5 %collective-permute-done.15.refs_3_ = f32[4,4160]{1,0:T(4,128)S(1)} collective-permute-done((f32[4,4160]{1,0:T(4,128)S(1)}, f32[4,4160]{1,0:T(4,128)S(1)}, u32[]{:S(2)}, u32[]{:S(2)}) %collective-permute-start.15) | collective-permute-done | bytes 66592 | tf_op jit(solution)/shard_map/ppermute | solution.py:301
  56.6 0.3 collective-permute-done.16
  57.0 0.1 constant_dynamic-update-slice_fusion.5
  57.1 0.0 copy-start.3
  57.1 1.3 %collective-permute-start.18 = (f32[64,512]{1,0:T(8,128)S(1)}, f32[64,512]{1,0:T(8,128)S(1)}, u32[]{:S(2)}, u32[]{:S(2)}) collective-permute-start(f32[64,512]{1,0:T(8,128)S(1)} %get-tuple-element.79), channel_id=1, source_target_pairs={{0,8},{8,0},{16,24},{24,16},{1,9},{9,1},{17,25},{25,17},{2,10},{10... | collective-permute-start | bytes 393224 | tf_op jit(solution)/shard_map/ppermute | solution.py:315
  58.4 1.4 %collective-permute-start.20 = (f32[64,512]{1,0:T(8,128)S(1)}, f32[64,512]{1,0:T(8,128)S(1)}, u32[]{:S(2)}, u32[]{:S(2)}) collective-permute-start(f32[64,512]{1,0:T(8,128)S(1)} %get-tuple-element.79), channel_id=1, source_target_pairs={{0,16},{8,24},{16,0},{24,8},{1,17},{9,25},{17,1},{25,9},{2,18},{10... | collective-permute-start | bytes 393224 | tf_op jit(solution)/shard_map/ppermute | solution.py:315
  59.8 0.8 collective-permute-start.21
  60.7 3.1 %collective-permute-done.19.refs_2_ = f32[4,4160]{1,0:T(4,128)S(1)} collective-permute-done((f32[4,4160]{1,0:T(4,128)S(1)}, f32[4,4160]{1,0:T(4,128)S(1)}, u32[]{:S(2)}, u32[]{:S(2)}) %collective-permute-start.19) | collective-permute-done | bytes 66592 | tf_op jit(solution)/shard_map/ppermute | solution.py:301
  63.8 2.4 %collective-permute-done.20 = f32[64,512]{1,0:T(8,128)S(1)} collective-permute-done((f32[64,512]{1,0:T(8,128)S(1)}, f32[64,512]{1,0:T(8,128)S(1)}, u32[]{:S(2)}, u32[]{:S(2)}) %collective-permute-start.20) | collective-permute-done | bytes 131104 | tf_op jit(solution)/shard_map/ppermute | solution.py:315
  66.2 0.1 collective-permute-start.22
  66.3 0.8 shard_map.94
  67.1 1.1 %collective-permute-done.22.median_ref = f32[64,2048]{1,0:T(8,128)S(1)} collective-permute-done((f32[64,2048]{1,0:T(8,128)S(1)}, f32[64,2048]{1,0:T(8,128)S(1)}, u32[]{:S(2)}, u32[]{:S(2)}) %collective-permute-start.22) | collective-permute-done | bytes 524320 | tf_op jit(solution)/shard_map/ppermute | solution.py:312
  68.2 1.2 %shard_map.95 = (bf16[128,2048]{1,0:T(8,128)(2,1)S(1)}, bf16[2048,128]{1,0:T(8,128)(2,1)S(1)}, f32[24,64]{1,0:T(8,128)S(1)}, f32[8,64]{1,0:T(8,128)}) custom-call(f32[64,2048]{1,0:T(8,128)S(1)} %collective-permute-done.22.median_ref, f32[12,4160]{1,0:T(8,128)S(1)} %copy-done, f32[12,4160]{1,0:T(8,128)S(1)} %collective-permute-done.1.refs_1_, ...), custom_call_target="tpu_custom_call" | custom-call | flops 33554432 | bytes 2097152 | tf_op jit(solution)/shard_map/pallas_call | solution.py:36
  69.4 2.6 %collective-permute-start.23 = (f32[24,64]{1,0:T(8,128)S(1)}, f32[24,64]{1,0:T(8,128)S(1)}, u32[]{:S(2)}, u32[]{:S(2)}) collective-permute-start(f32[24,64]{1,0:T(8,128)S(1)} %get-tuple-element.70.refs_4_), channel_id=1, source_target_pairs={{0,3},{1,2},{2,1},{3,0},{4,7},{5,6},{6,5},{7,4},{8,11},{9,10},{10,... | collective-permute-start | bytes 18440 | tf_op jit(solution)/shard_map/ppermute | solution.py:301
  72.1 0.3 collective-permute-start.24
  72.3 1.8 %collective-permute-start.25 = (f32[24,64]{1,0:T(8,128)S(1)}, f32[24,64]{1,0:T(8,128)S(1)}, u32[]{:S(2)}, u32[]{:S(2)}) collective-permute-start(f32[24,64]{1,0:T(8,128)S(1)} %get-tuple-element.70.refs_4_), channel_id=1, source_target_pairs={{0,7},{1,6},{2,5},{3,4},{4,3},{5,2},{6,1},{7,0},{8,15},{9,14},{10,... | collective-permute-start | bytes 18440 | tf_op jit(solution)/shard_map/ppermute | solution.py:301
  74.1 2.6 %collective-permute-done.24.refs_6_ = f32[24,64]{1,0:T(8,128)S(1)} collective-permute-done((f32[24,64]{1,0:T(8,128)S(1)}, f32[24,64]{1,0:T(8,128)S(1)}, u32[]{:S(2)}, u32[]{:S(2)}) %collective-permute-start.24) | collective-permute-done | bytes 6176 | tf_op jit(solution)/shard_map/ppermute | solution.py:301
  76.8 0.5 collective-permute-done.25.refs_7_
  77.3 0.7 shard_map.96
  78.0 0.0 collective-permute-start.26
  78.0 2.7 %collective-permute-start.27 = (f32[4,64]{1,0:T(4,128)S(1)}, f32[4,64]{1,0:T(4,128)S(1)}, u32[]{:S(2)}, u32[]{:S(2)}) collective-permute-start(f32[4,64]{1,0:T(4,128)S(1)} %get-tuple-element.85), channel_id=1, source_target_pairs={{0,4},{1,5},{2,6},{3,7},{4,0},{5,1},{6,2},{7,3},{8,12},{9,13},{10,... | collective-permute-start | bytes 3080 | tf_op jit(solution)/shard_map/ppermute | solution.py:301
  80.7 1.1 %collective-permute-start.28 = (f32[4,64]{1,0:T(4,128)S(1)}, f32[4,64]{1,0:T(4,128)S(1)}, u32[]{:S(2)}, u32[]{:S(2)}) collective-permute-start(f32[4,64]{1,0:T(4,128)S(1)} %get-tuple-element.84), channel_id=1, source_target_pairs={{0,7},{1,6},{2,5},{3,4},{4,3},{5,2},{6,1},{7,0},{8,15},{9,14},{10,... | collective-permute-start | bytes 3080 | tf_op jit(solution)/shard_map/ppermute | solution.py:301
  81.8 0.7 collective-permute-done.27
  82.5 3.0 %collective-permute-done.28 = f32[4,64]{1,0:T(4,128)S(1)} collective-permute-done((f32[4,64]{1,0:T(4,128)S(1)}, f32[4,64]{1,0:T(4,128)S(1)}, u32[]{:S(2)}, u32[]{:S(2)}) %collective-permute-start.28) | collective-permute-done | bytes 1056 | tf_op jit(solution)/shard_map/ppermute | solution.py:301
  85.5 0.6 multiply_divide_fusion
  (29 shorter events, 0.2 us)
Async XLA Ops:
  0.6 8.4 %copy-start.1 = (f32[1,2048,64]{1,2,0:T(8,128)S(1)}, f32[1,2048,64]{1,2,0:T(8,128)}, u32[]{:S(2)}) copy-start(f32[1,2048,64]{1,2,0:T(8,128)} %param.10) | copy-start | bytes 1572868
  0.6 8.4 %collective-permute-start = (f32[64,2048]{1,0:T(8,128)}, f32[64,2048]{1,0:T(8,128)S(1)}, u32[]{:S(2)}, u32[]{:S(2)}) collective-permute-start(f32[64,2048]{1,0:T(8,128)} %bitcast.11), channel_id=1, source_target_pairs={{0,1},{1,0},{2,3},{3,2},{4,5},{5,4},{6,7},{7,6},{8,9},{9,8},{10,11... | collective-permute-start | bytes 1572872 | tf_op jit(solution)/shard_map/ppermute | solution.py:312
  3.7 17.5 %collective-permute-start.1 = (f32[12,4160]{1,0:T(8,128)}, f32[12,4160]{1,0:T(8,128)S(1)}, u32[]{:S(2)}, u32[]{:S(2)}) collective-permute-start(f32[12,4160]{1,0:T(8,128)} %get-tuple-element.41), channel_id=1, source_target_pairs={{0,3},{1,2},{2,1},{3,0},{4,7},{5,6},{6,5},{7,4},{8,11},{9,10},{10,... | collective-permute-start | bytes 599048 | tf_op jit(solution)/shard_map/ppermute | solution.py:301
  6.4 10.1 %collective-permute-start.2 = (f32[8,4160]{1,0:T(8,128)}, f32[8,4160]{1,0:T(8,128)S(1)}, u32[]{:S(2)}, u32[]{:S(2)}) collective-permute-start(f32[8,4160]{1,0:T(8,128)} %get-tuple-element.42), channel_id=1, source_target_pairs={{0,4},{1,5},{2,6},{3,7},{4,0},{5,1},{6,2},{7,3},{8,12},{9,13},{10,... | collective-permute-start | bytes 399368 | tf_op jit(solution)/shard_map/ppermute | solution.py:301
  9.0 0.7 copy-start.2
  9.0 12.1 %collective-permute-start.3 = (f32[8,4160]{1,0:T(8,128)}, f32[8,4160]{1,0:T(8,128)S(1)}, u32[]{:S(2)}, u32[]{:S(2)}) collective-permute-start(f32[8,4160]{1,0:T(8,128)} %get-tuple-element.43), channel_id=1, source_target_pairs={{0,7},{1,6},{2,5},{3,4},{4,3},{5,2},{6,1},{7,0},{8,15},{9,14},{10,... | collective-permute-start | bytes 399368 | tf_op jit(solution)/shard_map/ppermute | solution.py:301
  9.7 11.5 %copy-start = (f32[12,4160]{1,0:T(8,128)S(1)}, f32[12,4160]{1,0:T(8,128)}, u32[]{:S(2)}) copy-start(f32[12,4160]{1,0:T(8,128)} %get-tuple-element.40.refs_0_) | copy-start | bytes 599044
  21.7 3.9 %collective-permute-start.4 = (f32[40,64]{1,0:T(8,128)S(1)}, f32[40,64]{1,0:T(8,128)S(1)}, u32[]{:S(2)}, u32[]{:S(2)}) collective-permute-start(f32[40,64]{1,0:T(8,128)S(1)} %constant_dynamic-update-slice_fusion.refs_4_), channel_id=1, source_target_pairs={{0,3},{1,2},{2,1},{3,0},{4,7},{5,6},{6,5},{7,4},{8,11},{9,10},{10,... | collective-permute-start | bytes 30728 | tf_op jit(solution)/shard_map/ppermute | solution.py:301
  22.5 4.9 %collective-permute-start.5 = (f32[40,64]{1,0:T(8,128)S(1)}, f32[40,64]{1,0:T(8,128)S(1)}, u32[]{:S(2)}, u32[]{:S(2)}) collective-permute-start(f32[40,64]{1,0:T(8,128)S(1)} %constant_dynamic-update-slice_fusion.refs_4_), channel_id=1, source_target_pairs={{0,4},{1,5},{2,6},{3,7},{4,0},{5,1},{6,2},{7,3},{8,12},{9,13},{10,... | collective-permute-start | bytes 30728 | tf_op jit(solution)/shard_map/ppermute | solution.py:301
  23.8 5.2 %collective-permute-start.6 = (f32[40,64]{1,0:T(8,128)S(1)}, f32[40,64]{1,0:T(8,128)S(1)}, u32[]{:S(2)}, u32[]{:S(2)}) collective-permute-start(f32[40,64]{1,0:T(8,128)S(1)} %constant_dynamic-update-slice_fusion.refs_4_), channel_id=1, source_target_pairs={{0,7},{1,6},{2,5},{3,4},{4,3},{5,2},{6,1},{7,0},{8,15},{9,14},{10,... | collective-permute-start | bytes 30728 | tf_op jit(solution)/shard_map/ppermute | solution.py:301
  29.6 3.8 %collective-permute-start.7 = (f32[32,64]{1,0:T(8,128)S(1)}, f32[32,64]{1,0:T(8,128)S(1)}, u32[]{:S(2)}, u32[]{:S(2)}) collective-permute-start(f32[32,64]{1,0:T(8,128)S(1)} %get-tuple-element.53.refs_4_), channel_id=1, source_target_pairs={{0,3},{1,2},{2,1},{3,0},{4,7},{5,6},{6,5},{7,4},{8,11},{9,10},{10,... | collective-permute-start | bytes 24584 | tf_op jit(solution)/shard_map/ppermute | solution.py:301
  29.7 4.7 %collective-permute-start.8 = (f32[32,64]{1,0:T(8,128)S(1)}, f32[32,64]{1,0:T(8,128)S(1)}, u32[]{:S(2)}, u32[]{:S(2)}) collective-permute-start(f32[32,64]{1,0:T(8,128)S(1)} %get-tuple-element.53.refs_4_), channel_id=1, source_target_pairs={{0,4},{1,5},{2,6},{3,7},{4,0},{5,1},{6,2},{7,3},{8,12},{9,13},{10,... | collective-permute-start | bytes 24584 | tf_op jit(solution)/shard_map/ppermute | solution.py:301
  32.3 5.0 %collective-permute-start.9 = (f32[32,64]{1,0:T(8,128)S(1)}, f32[32,64]{1,0:T(8,128)S(1)}, u32[]{:S(2)}, u32[]{:S(2)}) collective-permute-start(f32[32,64]{1,0:T(8,128)S(1)} %get-tuple-element.53.refs_4_), channel_id=1, source_target_pairs={{0,7},{1,6},{2,5},{3,4},{4,3},{5,2},{6,1},{7,0},{8,15},{9,14},{10,... | collective-permute-start | bytes 24584 | tf_op jit(solution)/shard_map/ppermute | solution.py:301
  37.8 3.8 %collective-permute-start.10 = (f32[32,64]{1,0:T(8,128)S(1)}, f32[32,64]{1,0:T(8,128)S(1)}, u32[]{:S(2)}, u32[]{:S(2)}) collective-permute-start(f32[32,64]{1,0:T(8,128)S(1)} %get-tuple-element.55.refs_4_), channel_id=1, source_target_pairs={{0,3},{1,2},{2,1},{3,0},{4,7},{5,6},{6,5},{7,4},{8,11},{9,10},{10,... | collective-permute-start | bytes 24584 | tf_op jit(solution)/shard_map/ppermute | solution.py:301
  37.8 4.8 %collective-permute-start.11 = (f32[32,64]{1,0:T(8,128)S(1)}, f32[32,64]{1,0:T(8,128)S(1)}, u32[]{:S(2)}, u32[]{:S(2)}) collective-permute-start(f32[32,64]{1,0:T(8,128)S(1)} %get-tuple-element.55.refs_4_), channel_id=1, source_target_pairs={{0,4},{1,5},{2,6},{3,7},{4,0},{5,1},{6,2},{7,3},{8,12},{9,13},{10,... | collective-permute-start | bytes 24584 | tf_op jit(solution)/shard_map/ppermute | solution.py:301
  39.7 5.0 %collective-permute-start.12 = (f32[32,64]{1,0:T(8,128)S(1)}, f32[32,64]{1,0:T(8,128)S(1)}, u32[]{:S(2)}, u32[]{:S(2)}) collective-permute-start(f32[32,64]{1,0:T(8,128)S(1)} %get-tuple-element.55.refs_4_), channel_id=1, source_target_pairs={{0,7},{1,6},{2,5},{3,4},{4,3},{5,2},{6,1},{7,0},{8,15},{9,14},{10,... | collective-permute-start | bytes 24584 | tf_op jit(solution)/shard_map/ppermute | solution.py:301
  45.1 2.0 %collective-permute-start.13 = (f32[64,2176]{1,0:T(8,128)S(1)}, f32[64,2176]{1,0:T(8,128)S(1)}, u32[]{:S(2)}, u32[]{:S(2)}) collective-permute-start(f32[64,2176]{1,0:T(8,128)S(1)} %get-tuple-element.57.sent_ref), channel_id=1, source_target_pairs={{0,1},{1,0},{2,3},{3,2},{4,5},{5,4},{6,7},{7,6},{8,9},{9,8},{10,11... | collective-permute-start | bytes 1671176 | tf_op jit(solution)/shard_map/ppermute | solution.py:312
  47.3 3.6 %copy-start.5 = (f32[4,4160]{1,0:T(4,128)S(1)}, f32[4,4160]{1,0:T(4,128)}, u32[]{:S(2)}) copy-start(f32[4,4160]{1,0:T(4,128)} %get-tuple-element.62) | copy-start | bytes 199684
  47.3 9.3 %collective-permute-start.14 = (f32[64,512]{1,0:T(8,128)S(1)}, f32[64,512]{1,0:T(8,128)S(1)}, u32[]{:S(2)}, u32[]{:S(2)}) collective-permute-start(f32[64,512]{1,0:T(8,128)S(1)} %get-tuple-element.80), channel_id=1, source_target_pairs={{0,8},{8,0},{16,24},{24,16},{1,9},{9,1},{17,25},{25,17},{2,10},{10... | collective-permute-start | bytes 393224 | tf_op jit(solution)/shard_map/ppermute | solution.py:315
  48.9 8.1 %collective-permute-start.16 = (f32[64,512]{1,0:T(8,128)S(1)}, f32[64,512]{1,0:T(8,128)S(1)}, u32[]{:S(2)}, u32[]{:S(2)}) collective-permute-start(f32[64,512]{1,0:T(8,128)S(1)} %get-tuple-element.82), channel_id=1, source_target_pairs={{0,16},{8,24},{16,0},{24,8},{1,17},{9,25},{17,1},{25,9},{2,18},{10... | collective-permute-start | bytes 393224 | tf_op jit(solution)/shard_map/ppermute | solution.py:315
  50.4 6.6 %collective-permute-start.17 = (f32[64,512]{1,0:T(8,128)S(1)}, f32[64,512]{1,0:T(8,128)S(1)}, u32[]{:S(2)}, u32[]{:S(2)}) collective-permute-start(f32[64,512]{1,0:T(8,128)S(1)} %get-tuple-element.81), channel_id=1, source_target_pairs={{0,24},{8,16},{16,8},{24,0},{1,25},{9,17},{17,9},{25,1},{2,26},{10... | collective-permute-start | bytes 393224 | tf_op jit(solution)/shard_map/ppermute | solution.py:315
  50.9 5.7 %collective-permute-start.15 = (f32[4,4160]{1,0:T(4,128)S(1)}, f32[4,4160]{1,0:T(4,128)S(1)}, u32[]{:S(2)}, u32[]{:S(2)}) collective-permute-start(f32[4,4160]{1,0:T(4,128)S(1)} %copy-done.5), channel_id=1, source_target_pairs={{0,7},{1,6},{2,5},{3,4},{4,3},{5,2},{6,1},{7,0},{8,15},{9,14},{10,... | collective-permute-start | bytes 199688 | tf_op jit(solution)/shard_map/ppermute | solution.py:301
  57.0 1.4 %copy-start.4 = (f32[4,4160]{1,0:T(4,128)S(1)}, f32[4,4160]{1,0:T(4,128)}, u32[]{:S(2)}) copy-start(f32[4,4160]{1,0:T(4,128)} %get-tuple-element.64) | copy-start | bytes 199684
  57.1 6.7 %copy-start.3 = (f32[64,512]{1,0:T(8,128)}, f32[64,512]{1,0:T(8,128)S(1)}, u32[]{:S(2)}) copy-start(f32[64,512]{1,0:T(8,128)S(1)} %get-tuple-element.79) | copy-start | bytes 393220
  57.1 6.7 %collective-permute-start.18 = (f32[64,512]{1,0:T(8,128)S(1)}, f32[64,512]{1,0:T(8,128)S(1)}, u32[]{:S(2)}, u32[]{:S(2)}) collective-permute-start(f32[64,512]{1,0:T(8,128)S(1)} %get-tuple-element.79), channel_id=1, source_target_pairs={{0,8},{8,0},{16,24},{24,16},{1,9},{9,1},{17,25},{25,17},{2,10},{10... | collective-permute-start | bytes 393224 | tf_op jit(solution)/shard_map/ppermute | solution.py:315
  58.4 5.4 %collective-permute-start.19 = (f32[4,4160]{1,0:T(4,128)S(1)}, f32[4,4160]{1,0:T(4,128)S(1)}, u32[]{:S(2)}, u32[]{:S(2)}) collective-permute-start(f32[4,4160]{1,0:T(4,128)S(1)} %copy-done.4), channel_id=1, source_target_pairs={{0,4},{1,5},{2,6},{3,7},{4,0},{5,1},{6,2},{7,3},{8,12},{9,13},{10,... | collective-permute-start | bytes 199688 | tf_op jit(solution)/shard_map/ppermute | solution.py:301
  58.4 7.8 %collective-permute-start.20 = (f32[64,512]{1,0:T(8,128)S(1)}, f32[64,512]{1,0:T(8,128)S(1)}, u32[]{:S(2)}, u32[]{:S(2)}) collective-permute-start(f32[64,512]{1,0:T(8,128)S(1)} %get-tuple-element.79), channel_id=1, source_target_pairs={{0,16},{8,24},{16,0},{24,8},{1,17},{9,25},{17,1},{25,9},{2,18},{10... | collective-permute-start | bytes 393224 | tf_op jit(solution)/shard_map/ppermute | solution.py:315
  59.8 6.4 %collective-permute-start.21 = (f32[64,512]{1,0:T(8,128)S(1)}, f32[64,512]{1,0:T(8,128)S(1)}, u32[]{:S(2)}, u32[]{:S(2)}) collective-permute-start(f32[64,512]{1,0:T(8,128)S(1)} %get-tuple-element.79), channel_id=1, source_target_pairs={{0,24},{8,16},{16,8},{24,0},{1,25},{9,17},{17,9},{25,1},{2,26},{10... | collective-permute-start | bytes 393224 | tf_op jit(solution)/shard_map/ppermute | solution.py:315
  66.2 2.0 %collective-permute-start.22 = (f32[64,2048]{1,0:T(8,128)S(1)}, f32[64,2048]{1,0:T(8,128)S(1)}, u32[]{:S(2)}, u32[]{:S(2)}) collective-permute-start(f32[64,2048]{1,0:T(8,128)S(1)} %constant_dynamic-update-slice_fusion.2.median_ref), channel_id=1, source_target_pairs={{0,1},{1,0},{2,3},{3,2},{4,5},{5,4},{6,7},{7,6},{8,9},{9,8},{10,11... | collective-permute-start | bytes 1572872 | tf_op jit(solution)/shard_map/ppermute | solution.py:312
  69.4 4.7 %collective-permute-start.23 = (f32[24,64]{1,0:T(8,128)S(1)}, f32[24,64]{1,0:T(8,128)S(1)}, u32[]{:S(2)}, u32[]{:S(2)}) collective-permute-start(f32[24,64]{1,0:T(8,128)S(1)} %get-tuple-element.70.refs_4_), channel_id=1, source_target_pairs={{0,3},{1,2},{2,1},{3,0},{4,7},{5,6},{6,5},{7,4},{8,11},{9,10},{10,... | collective-permute-start | bytes 18440 | tf_op jit(solution)/shard_map/ppermute | solution.py:301
  72.1 4.7 %collective-permute-start.24 = (f32[24,64]{1,0:T(8,128)S(1)}, f32[24,64]{1,0:T(8,128)S(1)}, u32[]{:S(2)}, u32[]{:S(2)}) collective-permute-start(f32[24,64]{1,0:T(8,128)S(1)} %get-tuple-element.70.refs_4_), channel_id=1, source_target_pairs={{0,4},{1,5},{2,6},{3,7},{4,0},{5,1},{6,2},{7,3},{8,12},{9,13},{10,... | collective-permute-start | bytes 18440 | tf_op jit(solution)/shard_map/ppermute | solution.py:301
  72.3 4.9 %collective-permute-start.25 = (f32[24,64]{1,0:T(8,128)S(1)}, f32[24,64]{1,0:T(8,128)S(1)}, u32[]{:S(2)}, u32[]{:S(2)}) collective-permute-start(f32[24,64]{1,0:T(8,128)S(1)} %get-tuple-element.70.refs_4_), channel_id=1, source_target_pairs={{0,7},{1,6},{2,5},{3,4},{4,3},{5,2},{6,1},{7,0},{8,15},{9,14},{10,... | collective-permute-start | bytes 18440 | tf_op jit(solution)/shard_map/ppermute | solution.py:301
  78.0 3.9 %collective-permute-start.26 = (f32[4,64]{1,0:T(4,128)S(1)}, f32[4,64]{1,0:T(4,128)S(1)}, u32[]{:S(2)}, u32[]{:S(2)}) collective-permute-start(f32[4,64]{1,0:T(4,128)S(1)} %get-tuple-element.83), channel_id=1, source_target_pairs={{0,3},{1,2},{2,1},{3,0},{4,7},{5,6},{6,5},{7,4},{8,11},{9,10},{10,... | collective-permute-start | bytes 3080 | tf_op jit(solution)/shard_map/ppermute | solution.py:301
  78.0 4.5 %collective-permute-start.27 = (f32[4,64]{1,0:T(4,128)S(1)}, f32[4,64]{1,0:T(4,128)S(1)}, u32[]{:S(2)}, u32[]{:S(2)}) collective-permute-start(f32[4,64]{1,0:T(4,128)S(1)} %get-tuple-element.85), channel_id=1, source_target_pairs={{0,4},{1,5},{2,6},{3,7},{4,0},{5,1},{6,2},{7,3},{8,12},{9,13},{10,... | collective-permute-start | bytes 3080 | tf_op jit(solution)/shard_map/ppermute | solution.py:301
  80.7 4.8 %collective-permute-start.28 = (f32[4,64]{1,0:T(4,128)S(1)}, f32[4,64]{1,0:T(4,128)S(1)}, u32[]{:S(2)}, u32[]{:S(2)}) collective-permute-start(f32[4,64]{1,0:T(4,128)S(1)} %get-tuple-element.84), channel_id=1, source_target_pairs={{0,7},{1,6},{2,5},{3,4},{4,3},{5,2},{6,1},{7,0},{8,15},{9,14},{10,... | collective-permute-start | bytes 3080 | tf_op jit(solution)/shard_map/ppermute | solution.py:301
where the time goes:
time: 86.2 us; the launch traced here: 86.1 us
  waiting for transfers between devices  40.2 us (47%)
  starting transfers between devices  34.6 us (40%)
  Pallas kernels  9.06 us (11%)
    ppermute x20, waiting for transfers between devices, over_chips(): lax.ppermute(array, 'doc', [(c * cores + k, (c ^ step) * cores + (k + ste...  34.9 us
    ppermute x20, starting transfers between devices, over_chips(): lax.ppermute(array, 'doc', [(c * cores + k, (c ^ step) * cores + (k + ste...  26.7 us
    ppermute x6, starting transfers between devices, over_pert(): return lax.ppermute(array, 'pert', [(m, m ^ step) for m in range(members)])  7.11 us
    pallas_call x10, Pallas kernels, call(): pl.pallas_call(kernel, out_shape=outs, compiler_params=pltpu.CompilerPara...  6.57 us
    ppermute x6, waiting for transfers between devices, over_pert(): return lax.ppermute(array, 'pert', [(m, m ^ step) for m in range(members)])  2.71 us
    ppermute x3, waiting for transfers between devices, over_cores(): return lax.ppermute(array, 'doc', [(d, d ^ 1) for d in range(doc_size)])  2.51 us
    pallas_call x1, Pallas kernels, per_device(): pl.pallas_call(functools.partial(spread_kernel, chips, cores, owned), out...  2.49 us
  transfers between devices with their start and end apart: 29, of which 18 were waited for; matrix products, arithmetic and copies ran while one was open for 0% of the time, Pallas kernels for 6%

commit v1 on v0

v1 whole, which is shorter than its diff:
```python
import functools

import jax
import jax.numpy as jnp
from jax import lax
from jax.experimental import pallas as pl
from jax.experimental.pallas import tpu as pltpu
from jax.sharding import PartitionSpec as P

UPDATES = 3
REFITS = 2

EXACT = lax.Precision.HIGHEST
ROUGH = lax.Precision.HIGH
VMEM_BYTES = 14 * 1024 * 1024
SPREAD_BYTES = 60 * 1024 * 1024


def dot(left, right, dims, precision=ROUGH):
    return lax.dot_general(left, right, (dims, ((), ())), precision=precision)


def middle(pieces):
    pieces = list(pieces)
    count = len(pieces)
    for turn in range(count):
        for low in range(turn % 2, count - 1, 2):
            pieces[low], pieces[low + 1] = (
                jnp.minimum(pieces[low], pieces[low + 1]),
                jnp.maximum(pieces[low], pieces[low + 1]),
            )
    return 0.5 * (pieces[count // 2 - 1] + pieces[count // 2])


def call(kernel, outs, *args, flops=0, moved=0, unread=0):
    read = len(args) - unread
    return pl.pallas_call(
        kernel,
        out_shape=outs,
        in_specs=[pl.BlockSpec(memory_space=pltpu.VMEM)] * read
        + [pl.BlockSpec(memory_space=pl.ANY)] * unread,
        compiler_params=pltpu.CompilerParams(vmem_limit_bytes=VMEM_BYTES),
        cost_estimate=pl.CostEstimate(flops=flops, bytes_accessed=moved, transcendentals=0),
    )(*args)


def shape(*dims, dtype=jnp.float32):
    return jax.ShapeDtypeStruct(dims, dtype)


def high_low(x):
    high = x.astype(jnp.bfloat16).astype(jnp.float32)
    return high, x - high


def matmul(left, right):
    return jnp.dot(
        left.astype(jnp.bfloat16), right.astype(jnp.bfloat16), preferred_element_type=jnp.float32
    )


def blocks_of(chips, cores, step):
    at_doc = lax.axis_index("doc")
    at_chip, at_core = at_doc // cores, at_doc % cores
    return [(at_chip ^ step) * cores + (at_core ^ ((step + half) % cores)) for half in range(cores)]


def spread_kernel(chips, cores, own_words, mask_hbm, topics_hbm, counts_hbm, *refs):
    out_hbms, (mask_ref, topics_ref, counts_ref, out_ref, small_sems, in_sems, out_sems) = (
        refs[:chips],
        refs[chips:],
    )
    small = [
        pltpu.make_async_copy(mask_hbm, mask_ref, small_sems.at[0]),
        pltpu.make_async_copy(topics_hbm, topics_ref, small_sems.at[1]),
    ]
    for copy in small:
        copy.start()
    steps = list(range(chips - 1, -1, -1))
    arriving = {}
    for step in steps:
        for half, block in enumerate(blocks_of(chips, cores, step)):
            at = slice(half * own_words, (half + 1) * own_words)
            arriving[step, half] = pltpu.make_async_copy(
                counts_hbm.at[:, pl.ds(pl.multiple_of(block * own_words, 128), own_words)],
                counts_ref.at[step, :, at],
                in_sems.at[step, half],
            )
            arriving[step, half].start()
    docs, tiles = mask_ref.shape
    width = chips * cores * own_words // tiles
    own_tiles = own_words // width
    tile_ids = lax.broadcasted_iota(jnp.int32, (docs, tiles), 1)
    doc_ids = lax.axis_index("doc") * docs + lax.broadcasted_iota(jnp.int32, (docs, tiles), 0)
    forced = (tile_ids == doc_ids % tiles).astype(jnp.int32)
    for copy in small:
        copy.wait()
    occupied = jnp.maximum(mask_ref[...], forced).astype(jnp.float32)
    leaving = []
    for step in steps:
        for half, block in enumerate(blocks_of(chips, cores, step)):
            near = pltpu.roll(occupied, lax.rem(tiles - block * own_tiles, tiles), 1)
            arriving[step, half].wait()
            for tile in range(own_tiles):
                at = slice(half * own_words + tile * width, half * own_words + (tile + 1) * width)
                picked = counts_ref[step, :, at].astype(jnp.float32)
                out_ref[step, :, at] = picked * near[:, tile : tile + 1]
        out_ref[step, :, cores * own_words :] = topics_ref[...]
        leaving.append(pltpu.make_async_copy(out_ref.at[step], out_hbms[step], out_sems.at[step]))
        leaving[-1].start()
    for copy in leaving:
        copy.wait()


def base_kernel(chips, cores, counts_ref, topics_ref, *out_refs):
    span = out_refs[0].shape[1] - topics_ref.shape[1]
    own_words = span // cores
    for step in range(chips):
        for half, block in enumerate(blocks_of(chips, cores, step)):
            at = slice(half * own_words, (half + 1) * own_words)
            first = pl.multiple_of(block * own_words, 128)
            out_refs[step][:, at] = counts_ref[:, pl.ds(first, own_words)].astype(jnp.float32)
        out_refs[step][:, span:] = topics_ref[...]


def moved_columns(x, onehot):
    rows = x.shape[0]
    high, rest = high_low(x)
    mid, low = high_low(rest)
    moved = matmul(jnp.concatenate([high, mid, low], axis=0), onehot)
    return moved[:rows] + moved[rows : 2 * rows] + moved[2 * rows :]


def dictionary_kernel(half_count, perm_ref, *refs):
    topics, words = refs[0].shape
    wide_ref, tall_ref, total_ref, aligned_ref, onehot_ref = refs[half_count:]
    onehot = (
        lax.broadcasted_iota(jnp.int32, (topics, topics), 0) == perm_ref[...]
    ).astype(jnp.float32)
    onehot_ref[...] = onehot
    total = jnp.zeros((1, topics), jnp.float32)
    for half in range(half_count):
        at = slice(half * words, (half + 1) * words)
        full = refs[half][...]
        high, rest = high_low(full)
        mid, low = high_low(rest)
        wide_ref[:topics, at] = high.astype(jnp.bfloat16)
        wide_ref[topics:, at] = rest.astype(jnp.bfloat16)
        if half == 0:
            turned = onehot.T
            aligned_ref[...] = matmul(
                jnp.concatenate([turned] * 3, axis=1), jnp.concatenate([high, mid, low], axis=0)
            )
        tall = full.T
        total += jnp.sum(tall, axis=0, keepdims=True)
        tall_ref[at, :] = jnp.concatenate(high_low(tall), axis=1).astype(jnp.bfloat16)
    total_ref[...] = jnp.broadcast_to(total, total_ref.shape)


def recon_of(topics, wide):
    rows = topics.shape[0]
    high, low = high_low(topics)
    left = jnp.concatenate(
        [jnp.concatenate([high, high], axis=1), jnp.concatenate([low, low], axis=1)], axis=0
    )
    both = matmul(left, wide)
    return both[:rows] + both[rows:]


def product_of(quotient, tall):
    rows, topics = quotient.shape[0], tall.shape[1] // 2
    both = matmul(jnp.concatenate(high_low(quotient), axis=0), tall)
    both = both[:rows] + both[rows:]
    return both[:, :topics] + both[:, topics:]


def sum_blocks(rows, own, got):
    got = got[::-1]
    chips = len(got) + 1
    total = own[: chips * rows]
    for step in range(1, chips):
        total = total + jnp.concatenate(
            [got[step - 1][(c ^ step) * rows : ((c ^ step) + 1) * rows] for c in range(chips)], axis=0
        )
    return total


def first_kernel(chips, wide_ref, tall_ref, *refs):
    payload, (topics_ref, part_ref) = refs[:chips][::-1], refs[-2:]
    docs = topics_ref.shape[0] // chips
    span = wide_ref.shape[1]
    topics = jnp.concatenate([ref[:, span:] for ref in payload], axis=0)
    topics_ref[...] = topics
    weighted = jnp.concatenate([ref[:, :span] for ref in payload], axis=0)
    part_ref[...] = product_of(weighted / recon_of(topics, wide_ref[...]), tall_ref[...])


def update_kernel(chips, wide_ref, tall_ref, before_ref, *refs):
    docs = before_ref.shape[0] // chips
    first = refs[-1].shape[0] == 8
    if first:
        payload, parts, (topics_ref, part_ref, total_ref) = refs[:chips][::-1], refs[chips:-3], refs[-3:]
        got = [ref[...] for ref in parts]
        total_ref[...] = sum(part[chips * docs :] for part in got)
    else:
        total_ref, payload, parts = refs[0], refs[1 : chips + 1][::-1], refs[chips + 1 : -2]
        topics_ref, part_ref = refs[-2:]
        got = [ref[...] for ref in parts]
    span = wide_ref.shape[1]
    topics = before_ref[...] * sum_blocks(docs, got[0], got[1:]) / total_ref[:1]
    topics_ref[...] = topics
    weighted = jnp.concatenate([ref[:, :span] for ref in payload], axis=0)
    part_ref[...] = product_of(weighted / recon_of(topics, wide_ref[...]), tall_ref[...])


def numerator_of(topics, quotient):
    high, low = high_low(topics.T)
    quotient_high, quotient_low = high_low(quotient)
    return matmul(
        jnp.concatenate([high, low, high], axis=1),
        jnp.concatenate([quotient_high, quotient_high, quotient_low], axis=0),
    )


def last_kernel(chips, cores, wide_ref, onehot_ref, before_ref, total_ref, *refs):
    payload, parts, (topics_ref, out_ref) = refs[:chips][::-1], refs[chips : 2 * chips], refs[2 * chips :]
    docs = topics_ref.shape[0] // chips
    words = wide_ref.shape[1] // cores
    at = slice((cores - 1) * words, cores * words)
    total = sum_blocks(docs, parts[0][...], [ref[...] for ref in parts[1:]])
    topics = before_ref[...] * total / total_ref[:1]
    weighted = jnp.concatenate([ref[:, at] for ref in payload], axis=0)
    aligned = moved_columns(topics, onehot_ref[...])
    topics_ref[...] = jnp.concatenate([topics, aligned], axis=1)
    out_ref[:, :words] = numerator_of(aligned, weighted / recon_of(topics, wide_ref[:, at]))
    load = jnp.sum(aligned.T, axis=1, keepdims=True)
    out_ref[:, words:] = jnp.broadcast_to(load, (load.shape[0], out_ref.shape[1] - words))


def own_kernel(chips, wide_ref, topics_ref, *refs):
    payload, out_ref = refs[:chips][::-1], refs[chips]
    words = out_ref.shape[1]
    topic_count = out_ref.shape[0]
    topics, aligned = topics_ref[:, :topic_count], topics_ref[:, topic_count:]
    docs = topics.shape[0] // chips
    weighted = jnp.concatenate([ref[:, :words] for ref in payload], axis=0)
    out_ref[...] = numerator_of(aligned, weighted / recon_of(topics, wide_ref[:, :words]))


def aligned_kernel(own_ref, sent_ref, got_ref, dict_ref, out_ref):
    words = out_ref.shape[1]
    load = sent_ref[:, words : words + 1] + got_ref[:, words : words + 1]
    out_ref[...] = dict_ref[...] * (own_ref[...] + got_ref[:, :words]) / load


def base_rows_of(refs, at):
    return jnp.concatenate([ref[:, at] for ref in refs], axis=0)


def refit_kernel(chips, half, median_ref, *refs):
    payload, refs = refs[:chips], refs[chips:]
    if half == 0:
        before, (sub_ref, wide_ref, tall_ref, part_ref, sub_out_ref) = [], refs
        sub_out_ref[...] = sub_ref[...]
    else:
        *before, wide_ref, tall_ref, part_ref = refs
    topics, words = median_ref.shape
    span = payload[0].shape[1] - topics
    high, low = high_low(median_ref[...])
    wide = jnp.concatenate([high, low], axis=0).astype(jnp.bfloat16)
    wide_ref[...] = wide
    tall_full = median_ref[...].T
    total = jnp.broadcast_to(jnp.sum(tall_full, axis=0, keepdims=True), (8, topics))
    tall = jnp.concatenate(high_low(tall_full), axis=1).astype(jnp.bfloat16)
    tall_ref[...] = tall
    weighted = base_rows_of(payload, slice(half * words, (half + 1) * words))
    refit = base_rows_of(payload, slice(span, span + topics))
    part = product_of(weighted / recon_of(refit, wide), tall)
    rows = part.shape[0]
    if before:
        part = part + before[0][:rows]
        total = total + before[0][rows:]
    part_ref[:rows] = part
    part_ref[rows:] = total


def refit_again_kernel(chips, cores, base_docs, *refs):
    payload, parts, halves = refs[:chips], refs[chips : 2 * chips], refs[2 * chips : 2 * (chips + cores)]
    scale_ref, *part_refs = refs[2 * (chips + cores) :]
    topics = scale_ref.shape[1]
    rows = chips * base_docs
    span = payload[0].shape[1] - topics
    words = span // cores
    got = [ref[...] for ref in parts]
    median_total = sum(part[rows : rows + 1] for part in got)
    total = sum_blocks(base_docs, got[0], got[1:])
    refit = base_rows_of(payload, slice(span, span + topics)) * total / median_total
    scale_ref[...] = refit[:base_docs] / median_total
    part = jnp.zeros((rows, topics), jnp.float32)
    for half in range(cores):
        weighted = base_rows_of(payload, slice(half * words, (half + 1) * words))
        wide_ref, tall_ref = halves[2 * half], halves[2 * half + 1]
        part = part + product_of(weighted / recon_of(refit, wide_ref[...]), tall_ref[...])
    for step in range(chips):
        part_refs[step][...] = part[step * base_docs : (step + 1) * base_docs]


def finish_kernel(scale_ref, *refs):
    parts, out_ref = refs[:-1], refs[-1]
    out_ref[...] = scale_ref[...] * sum(ref[...] for ref in parts)


def median_kernel(members, *refs):
    refs[-1][...] = middle([ref[...] for ref in refs[:members]])


def assemble_kernel(members, *refs):
    out_ref = refs[-1]
    sub = refs[0].shape[1]
    for me in range(members):

        @pl.when(lax.axis_index("pert") == me)
        def _():
            for at in range(members):
                step = (members - at) % members
                owner = me ^ step
                out_ref[:, owner * sub : (owner + 1) * sub] = refs[at][...]


def per_device(counts, tile_mask, member_topics, start_dict, align_perm, base_counts, base_topics):
    doc_size = lax.axis_size("doc")
    members = lax.axis_size("pert")
    cores = 2 - doc_size % 2
    chips = doc_size // cores
    at_pert = lax.axis_index("pert")
    at_doc = lax.axis_index("doc")
    at_chip, at_core = at_doc // cores, at_doc % cores
    docs = counts.shape[1]
    base_docs = base_counts.shape[0]
    topic_count = member_topics.shape[2]
    owned = start_dict.shape[1]
    span = cores * owned
    rows = chips * docs
    sub = owned // members

    def over_chips(array, step):
        return lax.ppermute(
            array,
            "doc",
            [
                (c * cores + k, (c ^ step) * cores + (k + step) % cores)
                for c in range(chips)
                for k in range(cores)
            ],
        )

    def over_cores(array):
        return lax.ppermute(array, "doc", [(d, d ^ 1) for d in range(doc_size)])

    def over_pert(array, step):
        return lax.ppermute(array, "pert", [(m, m ^ step) for m in range(members)])

    sent = pl.pallas_call(
        functools.partial(spread_kernel, chips, cores, owned),
        out_shape=[shape(docs, span + topic_count)] * chips,
        in_specs=[pl.BlockSpec(memory_space=pl.ANY)] * 3,
        out_specs=[pl.BlockSpec(memory_space=pl.ANY)] * chips,
        scratch_shapes=[
            pltpu.VMEM(tile_mask.shape[1:], jnp.int32),
            pltpu.VMEM(member_topics.shape[1:], jnp.float32),
            pltpu.VMEM((chips, docs, span), jnp.int32),
            pltpu.VMEM((chips, docs, span + topic_count), jnp.float32),
            pltpu.SemaphoreType.DMA((2,)),
            pltpu.SemaphoreType.DMA((chips, cores)),
            pltpu.SemaphoreType.DMA((chips,)),
        ],
        compiler_params=pltpu.CompilerParams(vmem_limit_bytes=SPREAD_BYTES),
        cost_estimate=pl.CostEstimate(flops=0, bytes_accessed=12 * counts.size, transcendentals=0),
    )(tile_mask[0], member_topics[0], counts[0])
    base_sent = call(
        functools.partial(base_kernel, chips, cores),
        [shape(base_docs, span + topic_count)] * chips,
        base_counts,
        base_topics,
        moved=8 * base_counts.size,
    )
    got = [over_chips(sent[step], step) for step in range(chips - 1, 0, -1)][::-1]
    payload = [sent[0]] + got
    near = [over_chips(base_sent[step], step) for step in range(1, min(chips, 2))]
    dict_own = start_dict[0].T
    halves = [dict_own] + [over_cores(dict_own)] * (cores - 1)
    wide, tall, col_part, dict_own, onehot = call(
        functools.partial(dictionary_kernel, cores),
        [
            shape(2 * topic_count, span, dtype=jnp.bfloat16),
            shape(span, 2 * topic_count, dtype=jnp.bfloat16),
            shape(8, topic_count),
            shape(topic_count, owned),
            shape(topic_count, topic_count),
        ],
        align_perm,
        *halves,
        moved=4 * 4 * span * topic_count,
    )

    update_flops = 2 * 2 * 4 * rows * topic_count * span
    topics, part = call(
        functools.partial(first_kernel, chips),
        [shape(rows, topic_count), shape(rows, topic_count)],
        wide,
        tall,
        *payload[::-1],
        *near,
        unread=len(near),
        flops=update_flops,
        moved=4 * span * (rows + 2 * topic_count),
    )
    part = jnp.concatenate([part, col_part], axis=0)
    parts = [part] + [over_chips(part, step) for step in range(chips - 1, 0, -1)]
    totals = []
    for update in range(1, UPDATES):
        topics, part, *new_totals = call(
            functools.partial(update_kernel, chips),
            [shape(rows, topic_count), shape(rows, topic_count)]
            + ([] if totals else [shape(8, topic_count)]),
            wide,
            tall,
            topics,
            *totals,
            *payload[::-1],
            *parts,
            flops=update_flops,
            moved=4 * span * (rows + 2 * topic_count),
        )
        totals = totals or new_totals
        parts = [part] + [over_chips(part, step) for step in range(chips - 1, 0, -1)]
    (col_total,) = totals

    topics, numerator = call(
        functools.partial(last_kernel, chips, cores),
        [shape(rows, 2 * topic_count), shape(topic_count, owned + 128)],
        wide,
        onehot,
        topics,
        col_total,
        *payload[::-1],
        *parts,
        flops=update_flops // 2,
        moved=2 * span * (rows + 2 * topic_count),
    )
    if cores > 1:
        got_half = over_cores(numerator)
        own_half = call(
            functools.partial(own_kernel, chips),
            shape(topic_count, owned),
            wide,
            topics,
            *payload[::-1],
            flops=update_flops // 2,
            moved=2 * span * (rows + 2 * topic_count),
        )
    else:
        got_half = jnp.zeros_like(numerator)
        own_half = numerator[:, :owned]
    aligned = call(
        aligned_kernel,
        shape(topic_count, owned),
        own_half,
        numerator,
        got_half,
        dict_own,
        moved=16 * topic_count * owned,
    )

    def words_of(array, member):
        return lax.dynamic_slice_in_dim(array, member * sub, sub, 1)

    aligned, base_sent = lax.optimization_barrier((aligned, base_sent))
    base_got = [over_chips(base_sent[step], step) for step in range(2, chips)]
    late = len(base_got) // 2
    median = call(
        functools.partial(median_kernel, members),
        shape(topic_count, sub),
        words_of(aligned, at_pert),
        *[over_pert(words_of(aligned, at_pert ^ step), step) for step in range(members - 1, 0, -1)],
        *base_got[late:],
        unread=len(base_got) - late,
    )
    median_own = call(
        functools.partial(assemble_kernel, members),
        shape(topic_count, owned),
        median,
        *[over_pert(median, step) for step in range(members - 1, 0, -1)],
        *base_got[:late],
        unread=late,
    )
    base_all = [base_sent[0]] + near + base_got

    median_halves = [median_own] + [over_cores(median_own)] * (cores - 1)
    base_rows = chips * base_docs
    refit_flops = 2 * 2 * 4 * base_rows * topic_count * owned
    forms, before = [], [median]
    for half in range(cores):
        wide, tall, part, *own_median = call(
            functools.partial(refit_kernel, chips, half),
            [
                shape(2 * topic_count, owned, dtype=jnp.bfloat16),
                shape(owned, 2 * topic_count, dtype=jnp.bfloat16),
                shape(base_rows + 8, topic_count),
            ]
            + ([] if half else [shape(topic_count, sub)]),
            median_halves[half],
            *base_all,
            *before,
            flops=refit_flops,
            moved=16 * owned * topic_count,
        )
        forms += [wide, tall]
        before = [part]
        median = own_median[0] if own_median else median
    scale, *parts = call(
        functools.partial(refit_again_kernel, chips, cores, base_docs),
        [shape(base_docs, topic_count)] * (chips + 1),
        *base_all,
        part,
        *[over_chips(part, step) for step in range(chips - 1, 0, -1)],
        *forms,
        flops=2 * refit_flops,
        moved=16 * owned * topic_count,
    )
    refit = call(
        finish_kernel,
        shape(base_docs, topic_count),
        scale,
        parts[0],
        *[over_chips(parts[step], step) for step in range(chips - 1, 0, -1)],
    )
    return (median.T[None, None], refit)


def solution(mesh):
    return jax.shard_map(
        per_device,
        mesh=mesh,
        in_specs=(
            P("pert", "doc", None),
            P("pert", "doc", None),
            P("pert", "doc", None),
            P("pert", "doc", None),
            P("pert", None),
            P(("pert", "doc"), None),
            P(("pert", "doc"), None),
        ),
        out_specs=(P("doc", "pert", None, None), P(("pert", "doc"), None)),
        check_vma=False,
    )
```

time: 86.2 us -> 79.5 us (0.922)
  waiting for transfers between devices: 40.2 us -> 31.7 us
  starting transfers between devices: 34.6 us -> 35.8 us
  Pallas kernels: 9.06 us -> 10.1 us
    ppermute x20 -> x21, waiting for transfers between devices: 34.9 us -> 29.7 us  [over_chips(): lax.ppermute(array, 'doc', [(c * cores + k, (c ^ step) * cores + (k + ste...]
    ppermute x6, waiting for transfers between devices: 2.71 us -> 0.03 us  [over_pert(): return lax.ppermute(array, 'pert', [(m, m ^ step) for m in range(members)])]
    ppermute x20 -> x21, starting transfers between devices: 26.7 us -> 28 us  [over_chips(): lax.ppermute(array, 'doc', [(c * cores + k, (c ^ step) * cores + (k + ste...]
    pallas_call x10 -> x14, Pallas kernels: 6.57 us -> 7.54 us  [call(): pl.pallas_call(kernel, out_shape=outs, in_specs=[pl.BlockSpec(memory_spac...]
  transfers between devices with their start and end apart: 29 -> 30, of which waited for: 18 -> 17; matrix products, arithmetic and copies ran while one was open for 0% -> 0% of each run, Pallas kernels for 6% -> 7%
where the time goes in v1:
time: 79.5 us; the launch traced here: 79.3 us
  starting transfers between devices  35.8 us (45%)
  waiting for transfers between devices  31.7 us (40%)
  Pallas kernels  10.1 us (13%)
  local copies, waits for them, and re-layouts  1.03 us (1%)
  between operations  0.8 us (1%)
    ppermute x21, waiting for transfers between devices, over_chips(): lax.ppermute(array, 'doc', [(c * cores + k, (c ^ step) * cores + (k + ste...  29.7 us
    ppermute x21, starting transfers between devices, over_chips(): lax.ppermute(array, 'doc', [(c * cores + k, (c ^ step) * cores + (k + ste...  28 us
    pallas_call x14, Pallas kernels, call(): pl.pallas_call(kernel, out_shape=outs, in_specs=[pl.BlockSpec(memory_spac...  7.54 us
    ppermute x6, starting transfers between devices, over_pert(): return lax.ppermute(array, 'pert', [(m, m ^ step) for m in range(members)])  7.11 us
    pallas_call x1, Pallas kernels, per_device(): pl.pallas_call(functools.partial(spread_kernel, chips, cores, owned), out...  2.52 us
    ppermute x3, waiting for transfers between devices, over_cores(): return lax.ppermute(array, 'doc', [(d, d ^ 1) for d in range(doc_size)])  1.97 us
  transfers between devices with their start and end apart: 30, of which 17 were waited for; matrix products, arithmetic and copies ran while one was open for 0% of the time, Pallas kernels for 7%

profile of v1, /device:TPU:0, one launch (start us, length us, event | category | flops | bytes accessed | tf_op | source)
XLA Modules:
  0.0 79.3 jit_solution(6322466293931459685)
XLA Ops:
  0.6 0.5 collective-permute-start
  1.2 2.5 %shard_map.87 = (f32[8,4160]{1,0:T(8,128)}, f32[8,4160]{1,0:T(8,128)}, f32[8,4160]{1,0:T(8,128)}, f32[8,4160]{1,0:T(8,128)}) custom-call(s32[8,128]{1,0:T(8,128)} %bitcast.12, f32[8,64]{1,0:T(8,128)} %bitcast.13, s32[8,16384]{1,0:T(8,128)} %bitcast.11), custom_call_target="tpu_custom_call" | custom-call | bytes 1572864 | tf_op jit(solution)/shard_map/pallas_call | solution.py:363
  3.7 0.0 copy-start.3
  3.7 4.8 %collective-permute-start.1 = (f32[8,4160]{1,0:T(8,128)}, f32[8,4160]{1,0:T(8,128)S(1)}, u32[]{:S(2)}, u32[]{:S(2)}) collective-permute-start(f32[8,4160]{1,0:T(8,128)} %get-tuple-element.43), channel_id=1, source_target_pairs={{0,7},{1,6},{2,5},{3,4},{4,3},{5,2},{6,1},{7,0},{8,15},{9,14},{10,... | collective-permute-start | bytes 399368 | tf_op jit(solution)/shard_map/ppermute | solution.py:347
  8.5 0.4 collective-permute-start.3
  8.9 0.9 %copy-done.2 = s32[4,16384]{1,0:T(4,128)S(1)} copy-done((s32[4,16384]{1,0:T(4,128)S(1)}, s32[4,16384]{1,0:T(4,128)}, u32[]{:S(2)}) %copy-start.2) | copy-done | bytes 262168
  9.8 0.0 copy-start.4
  9.9 1.5 %collective-permute-start.4 = (f32[4,4160]{1,0:T(4,128)S(1)}, f32[4,4160]{1,0:T(4,128)S(1)}, u32[]{:S(2)}, u32[]{:S(2)}) collective-permute-start(f32[4,4160]{1,0:T(4,128)S(1)} %get-tuple-element.47), channel_id=1, source_target_pairs={{0,3},{1,2},{2,1},{3,0},{4,7},{5,6},{6,5},{7,4},{8,11},{9,10},{10,... | collective-permute-start | bytes 199688 | tf_op jit(solution)/shard_map/ppermute | solution.py:347
  11.3 0.0 collective-permute-done.refs_1_
  11.3 1.1 %shard_map.86 = (bf16[128,4096]{1,0:T(8,128)(2,1)S(1)}, bf16[4096,128]{1,0:T(8,128)(2,1)S(1)}, f32[8,64]{1,0:T(8,128)S(1)}, f32[64,2048]{1,0:T(8,128)S(1)}, f32[64,64]{1,0:T(8,128)S(1)}) custom-call(s32[1,64]{1,0:T(1,128)S(1)} %copy-done.4, f32[64,2048]{1,0:T(8,128)S(1)} %bitcast.10, f32[64,2048]{1,0:T(8,128)S(1)} %collective-permute-done.refs_1_), custom_call_target="tpu_custom_call" | custom-call | bytes 4194304 | tf_op jit(solution)/shard_map/pallas_call | solution.py:37
  12.4 7.0 %collective-permute-done.4.refs_4_.refs_1_ = f32[4,4160]{1,0:T(4,128)S(1)} collective-permute-done((f32[4,4160]{1,0:T(4,128)S(1)}, f32[4,4160]{1,0:T(4,128)S(1)}, u32[]{:S(2)}, u32[]{:S(2)}) %collective-permute-start.4) | collective-permute-done | bytes 66592 | tf_op jit(solution)/shard_map/ppermute | solution.py:347
  19.4 1.2 %collective-permute-done.2.refs_1_.refs_2_ = f32[8,4160]{1,0:T(8,128)S(1)} collective-permute-done((f32[8,4160]{1,0:T(8,128)}, f32[8,4160]{1,0:T(8,128)S(1)}, u32[]{:S(2)}, u32[]{:S(2)}) %collective-permute-start.2) | collective-permute-done | bytes 133152 | tf_op jit(solution)/shard_map/ppermute | solution.py:347
  20.6 0.6 shard_map.89
  21.2 2.8 %collective-permute-start.5 = (f32[40,64]{1,0:T(8,128)S(1)}, f32[40,64]{1,0:T(8,128)S(1)}, u32[]{:S(2)}, u32[]{:S(2)}) collective-permute-start(f32[40,64]{1,0:T(8,128)S(1)} %constant_dynamic-update-slice_fusion.refs_4_), channel_id=1, source_target_pairs={{0,7},{1,6},{2,5},{3,4},{4,3},{5,2},{6,1},{7,0},{8,15},{9,14},{10,... | collective-permute-start | bytes 30728 | tf_op jit(solution)/shard_map/ppermute | solution.py:347
  24.0 1.1 %collective-permute-start.7 = (f32[40,64]{1,0:T(8,128)S(1)}, f32[40,64]{1,0:T(8,128)S(1)}, u32[]{:S(2)}, u32[]{:S(2)}) collective-permute-start(f32[40,64]{1,0:T(8,128)S(1)} %constant_dynamic-update-slice_fusion.refs_4_), channel_id=1, source_target_pairs={{0,3},{1,2},{2,1},{3,0},{4,7},{5,6},{6,5},{7,4},{8,11},{9,10},{10,... | collective-permute-start | bytes 30728 | tf_op jit(solution)/shard_map/ppermute | solution.py:347
  25.1 1.2 %collective-permute-done.5.refs_5_ = f32[40,64]{1,0:T(8,128)S(1)} collective-permute-done((f32[40,64]{1,0:T(8,128)S(1)}, f32[40,64]{1,0:T(8,128)S(1)}, u32[]{:S(2)}, u32[]{:S(2)}) %collective-permute-start.5) | collective-permute-done | bytes 10272 | tf_op jit(solution)/shard_map/ppermute | solution.py:347
  26.3 2.4 %collective-permute-done.6.refs_6_ = f32[40,64]{1,0:T(8,128)S(1)} collective-permute-done((f32[40,64]{1,0:T(8,128)S(1)}, f32[40,64]{1,0:T(8,128)S(1)}, u32[]{:S(2)}, u32[]{:S(2)}) %collective-permute-start.6) | collective-permute-done | bytes 10272 | tf_op jit(solution)/shard_map/ppermute | solution.py:347
  28.7 0.6 shard_map.90
  29.3 1.0 %collective-permute-start.8 = (f32[32,64]{1,0:T(8,128)S(1)}, f32[32,64]{1,0:T(8,128)S(1)}, u32[]{:S(2)}, u32[]{:S(2)}) collective-permute-start(f32[32,64]{1,0:T(8,128)S(1)} %get-tuple-element.53.refs_5_), channel_id=1, source_target_pairs={{0,7},{1,6},{2,5},{3,4},{4,3},{5,2},{6,1},{7,0},{8,15},{9,14},{10,... | collective-permute-start | bytes 24584 | tf_op jit(solution)/shard_map/ppermute | solution.py:347
  30.2 0.6 collective-permute-start.9
  30.8 2.3 %collective-permute-start.10 = (f32[32,64]{1,0:T(8,128)S(1)}, f32[32,64]{1,0:T(8,128)S(1)}, u32[]{:S(2)}, u32[]{:S(2)}) collective-permute-start(f32[32,64]{1,0:T(8,128)S(1)} %get-tuple-element.53.refs_5_), channel_id=1, source_target_pairs={{0,3},{1,2},{2,1},{3,0},{4,7},{5,6},{6,5},{7,4},{8,11},{9,10},{10,... | collective-permute-start | bytes 24584 | tf_op jit(solution)/shard_map/ppermute | solution.py:347
  33.1 1.1 %collective-permute-done.8.refs_6_ = f32[32,64]{1,0:T(8,128)S(1)} collective-permute-done((f32[32,64]{1,0:T(8,128)S(1)}, f32[32,64]{1,0:T(8,128)S(1)}, u32[]{:S(2)}, u32[]{:S(2)}) %collective-permute-start.8) | collective-permute-done | bytes 8224 | tf_op jit(solution)/shard_map/ppermute | solution.py:347
  34.3 0.6 collective-permute-done.9.refs_7_
  34.9 0.1 collective-permute-done.10.refs_8_
  35.0 0.6 shard_map.91
  35.5 1.7 %collective-permute-start.11 = (f32[32,64]{1,0:T(8,128)S(1)}, f32[32,64]{1,0:T(8,128)S(1)}, u32[]{:S(2)}, u32[]{:S(2)}) collective-permute-start(f32[32,64]{1,0:T(8,128)S(1)} %get-tuple-element.55.refs_4_), channel_id=1, source_target_pairs={{0,7},{1,6},{2,5},{3,4},{4,3},{5,2},{6,1},{7,0},{8,15},{9,14},{10,... | collective-permute-start | bytes 24584 | tf_op jit(solution)/shard_map/ppermute | solution.py:347
  37.3 1.0 %collective-permute-start.12 = (f32[32,64]{1,0:T(8,128)S(1)}, f32[32,64]{1,0:T(8,128)S(1)}, u32[]{:S(2)}, u32[]{:S(2)}) collective-permute-start(f32[32,64]{1,0:T(8,128)S(1)} %get-tuple-element.55.refs_4_), channel_id=1, source_target_pairs={{0,4},{1,5},{2,6},{3,7},{4,0},{5,1},{6,2},{7,3},{8,12},{9,13},{10,... | collective-permute-start | bytes 24584 | tf_op jit(solution)/shard_map/ppermute | solution.py:347
  38.3 1.1 %collective-permute-start.13 = (f32[32,64]{1,0:T(8,128)S(1)}, f32[32,64]{1,0:T(8,128)S(1)}, u32[]{:S(2)}, u32[]{:S(2)}) collective-permute-start(f32[32,64]{1,0:T(8,128)S(1)} %get-tuple-element.55.refs_4_), channel_id=1, source_target_pairs={{0,3},{1,2},{2,1},{3,0},{4,7},{5,6},{6,5},{7,4},{8,11},{9,10},{10,... | collective-permute-start | bytes 24584 | tf_op jit(solution)/shard_map/ppermute | solution.py:347
  39.4 1.1 %collective-permute-done.11.refs_5_ = f32[32,64]{1,0:T(8,128)S(1)} collective-permute-done((f32[32,64]{1,0:T(8,128)S(1)}, f32[32,64]{1,0:T(8,128)S(1)}, u32[]{:S(2)}, u32[]{:S(2)}) %collective-permute-start.11) | collective-permute-done | bytes 8224 | tf_op jit(solution)/shard_map/ppermute | solution.py:347
  40.5 1.4 %collective-permute-done.12.refs_6_ = f32[32,64]{1,0:T(8,128)S(1)} collective-permute-done((f32[32,64]{1,0:T(8,128)S(1)}, f32[32,64]{1,0:T(8,128)S(1)}, u32[]{:S(2)}, u32[]{:S(2)}) %collective-permute-start.12) | collective-permute-done | bytes 8224 | tf_op jit(solution)/shard_map/ppermute | solution.py:347
  41.9 0.5 shard_map.92
  42.4 0.1 collective-permute-start.14
  42.5 0.5 shard_map.93.own_ref
  43.0 1.5 %collective-permute-done.14.got_ref = f32[64,2176]{1,0:T(8,128)S(1)} collective-permute-done((f32[64,2176]{1,0:T(8,128)S(1)}, f32[64,2176]{1,0:T(8,128)S(1)}, u32[]{:S(2)}, u32[]{:S(2)}) %collective-permute-start.14) | collective-permute-done | bytes 557088 | tf_op jit(solution)/shard_map/ppermute | solution.py:358
  44.5 0.1 shard_map.94
  44.7 2.5 %collective-permute-start.15 = (f32[64,512]{1,0:T(8,128)S(1)}, f32[64,512]{1,0:T(8,128)S(1)}, u32[]{:S(2)}, u32[]{:S(2)}) collective-permute-start(f32[64,512]{1,0:T(8,128)S(1)} %get-tuple-element.80), channel_id=1, source_target_pairs={{0,24},{8,16},{16,8},{24,0},{1,25},{9,17},{17,9},{25,1},{2,26},{10... | collective-permute-start | bytes 393224 | tf_op jit(solution)/shard_map/ppermute | solution.py:361
  47.2 0.5 collective-permute-start.16
  47.7 0.5 collective-permute-start.17
  48.2 0.7 collective-permute-start.18
  48.9 5.1 %collective-permute-done.18.refs_4_.refs_3_ = f32[4,4160]{1,0:T(4,128)S(1)} collective-permute-done((f32[4,4160]{1,0:T(4,128)S(1)}, f32[4,4160]{1,0:T(4,128)S(1)}, u32[]{:S(2)}, u32[]{:S(2)}) %collective-permute-start.18) | collective-permute-done | bytes 66592 | tf_op jit(solution)/shard_map/ppermute | solution.py:347
  54.0 0.0 collective-permute-done.17.refs_3_
  54.1 0.1 shard_map.95.refs_0_.refs_4_
  54.1 2.5 %collective-permute-start.19 = (f32[64,512]{1,0:T(8,128)S(1)}, f32[64,512]{1,0:T(8,128)S(1)}, u32[]{:S(2)}, u32[]{:S(2)}) collective-permute-start(f32[64,512]{1,0:T(8,128)S(1)} %shard_map.95.refs_0_.refs_4_), channel_id=1, source_target_pairs={{0,24},{8,16},{16,8},{24,0},{1,25},{9,17},{17,9},{25,1},{2,26},{10... | collective-permute-start | bytes 393224 | tf_op jit(solution)/shard_map/ppermute | solution.py:361
  56.6 0.5 collective-permute-start.20
  57.2 0.5 collective-permute-start.21
  57.7 1.5 %collective-permute-start.22 = (f32[4,4160]{1,0:T(4,128)S(1)}, f32[4,4160]{1,0:T(4,128)S(1)}, u32[]{:S(2)}, u32[]{:S(2)}) collective-permute-start(f32[4,4160]{1,0:T(4,128)S(1)} %get-tuple-element.64), channel_id=1, source_target_pairs={{0,4},{1,5},{2,6},{3,7},{4,0},{5,1},{6,2},{7,3},{8,12},{9,13},{10,... | collective-permute-start | bytes 199688 | tf_op jit(solution)/shard_map/ppermute | solution.py:347
  59.1 4.4 %collective-permute-done.22.refs_4_.refs_2_ = f32[4,4160]{1,0:T(4,128)S(1)} collective-permute-done((f32[4,4160]{1,0:T(4,128)S(1)}, f32[4,4160]{1,0:T(4,128)S(1)}, u32[]{:S(2)}, u32[]{:S(2)}) %collective-permute-start.22) | collective-permute-done | bytes 66592 | tf_op jit(solution)/shard_map/ppermute | solution.py:347
  63.6 0.1 shard_map.96.median_ref
  63.7 0.1 collective-permute-start.23
  63.7 1.4 %shard_map.97 = (bf16[128,2048]{1,0:T(8,128)(2,1)S(1)}, bf16[2048,128]{1,0:T(8,128)(2,1)S(1)}, f32[24,64]{1,0:T(8,128)S(1)}, f32[64,512]{1,0:T(8,128)}) custom-call(f32[64,2048]{1,0:T(8,128)S(1)} %shard_map.96.median_ref, f32[4,4160]{1,0:T(4,128)S(1)} %get-tuple-element.65.refs_0_, f32[4,4160]{1,0:T(4,128)S(1)} %collective-permute-done.4.refs_4_.refs_1_, ...), custom_call_target="tpu_custom_call" | custom-call | flops 33554432 | bytes 2097152 | tf_op jit(solution)/shard_map/pallas_call | solution.py:37
  65.1 0.5 collective-permute-done.23.median_ref
  65.6 0.8 shard_map.98
  66.4 1.5 %collective-permute-start.24 = (f32[24,64]{1,0:T(8,128)S(1)}, f32[24,64]{1,0:T(8,128)S(1)}, u32[]{:S(2)}, u32[]{:S(2)}) collective-permute-start(f32[24,64]{1,0:T(8,128)S(1)} %get-tuple-element.68.refs_4_), channel_id=1, source_target_pairs={{0,7},{1,6},{2,5},{3,4},{4,3},{5,2},{6,1},{7,0},{8,15},{9,14},{10,... | collective-permute-start | bytes 18440 | tf_op jit(solution)/shard_map/ppermute | solution.py:347
  68.0 0.2 collective-permute-start.25
  68.2 2.1 %collective-permute-start.26 = (f32[24,64]{1,0:T(8,128)S(1)}, f32[24,64]{1,0:T(8,128)S(1)}, u32[]{:S(2)}, u32[]{:S(2)}) collective-permute-start(f32[24,64]{1,0:T(8,128)S(1)} %get-tuple-element.68.refs_4_), channel_id=1, source_target_pairs={{0,3},{1,2},{2,1},{3,0},{4,7},{5,6},{6,5},{7,4},{8,11},{9,10},{10,... | collective-permute-start | bytes 18440 | tf_op jit(solution)/shard_map/ppermute | solution.py:347
  70.3 1.1 %collective-permute-done.24.refs_5_ = f32[24,64]{1,0:T(8,128)S(1)} collective-permute-done((f32[24,64]{1,0:T(8,128)S(1)}, f32[24,64]{1,0:T(8,128)S(1)}, u32[]{:S(2)}, u32[]{:S(2)}) %collective-permute-start.24) | collective-permute-done | bytes 6176 | tf_op jit(solution)/shard_map/ppermute | solution.py:347
  71.4 1.2 %collective-permute-done.25.refs_6_ = f32[24,64]{1,0:T(8,128)S(1)} collective-permute-done((f32[24,64]{1,0:T(8,128)S(1)}, f32[24,64]{1,0:T(8,128)S(1)}, u32[]{:S(2)}, u32[]{:S(2)}) %collective-permute-start.25) | collective-permute-done | bytes 6176 | tf_op jit(solution)/shard_map/ppermute | solution.py:347
  72.6 0.7 shard_map.99
  73.3 1.0 %collective-permute-start.27 = (f32[4,64]{1,0:T(4,128)S(1)}, f32[4,64]{1,0:T(4,128)S(1)}, u32[]{:S(2)}, u32[]{:S(2)}) collective-permute-start(f32[4,64]{1,0:T(4,128)S(1)} %get-tuple-element.75), channel_id=1, source_target_pairs={{0,7},{1,6},{2,5},{3,4},{4,3},{5,2},{6,1},{7,0},{8,15},{9,14},{10,... | collective-permute-start | bytes 3080 | tf_op jit(solution)/shard_map/ppermute | solution.py:347
  74.3 1.3 %collective-permute-start.28 = (f32[4,64]{1,0:T(4,128)S(1)}, f32[4,64]{1,0:T(4,128)S(1)}, u32[]{:S(2)}, u32[]{:S(2)}) collective-permute-start(f32[4,64]{1,0:T(4,128)S(1)} %get-tuple-element.76), channel_id=1, source_target_pairs={{0,4},{1,5},{2,6},{3,7},{4,0},{5,1},{6,2},{7,3},{8,12},{9,13},{10,... | collective-permute-start | bytes 3080 | tf_op jit(solution)/shard_map/ppermute | solution.py:347
  75.6 1.5 %collective-permute-start.29 = (f32[4,64]{1,0:T(4,128)S(1)}, f32[4,64]{1,0:T(4,128)S(1)}, u32[]{:S(2)}, u32[]{:S(2)}) collective-permute-start(f32[4,64]{1,0:T(4,128)S(1)} %get-tuple-element.77), channel_id=1, source_target_pairs={{0,3},{1,2},{2,1},{3,0},{4,7},{5,6},{6,5},{7,4},{8,11},{9,10},{10,... | collective-permute-start | bytes 3080 | tf_op jit(solution)/shard_map/ppermute | solution.py:347
  77.1 1.0 %collective-permute-done.27.refs_1_ = f32[4,64]{1,0:T(4,128)S(1)} collective-permute-done((f32[4,64]{1,0:T(4,128)S(1)}, f32[4,64]{1,0:T(4,128)S(1)}, u32[]{:S(2)}, u32[]{:S(2)}) %collective-permute-start.27) | collective-permute-done | bytes 1056 | tf_op jit(solution)/shard_map/ppermute | solution.py:347
  78.1 0.7 collective-permute-done.28.refs_2_
  78.8 0.6 shard_map.100
  (24 shorter events, 0.1 us)
Async XLA Ops:
  0.6 10.7 %copy-start.1 = (f32[1,2048,64]{1,2,0:T(8,128)S(1)}, f32[1,2048,64]{1,2,0:T(8,128)}, u32[]{:S(2)}) copy-start(f32[1,2048,64]{1,2,0:T(8,128)} %param.10) | copy-start | bytes 1572868
  0.6 10.7 %collective-permute-start = (f32[64,2048]{1,0:T(8,128)}, f32[64,2048]{1,0:T(8,128)S(1)}, u32[]{:S(2)}, u32[]{:S(2)}) collective-permute-start(f32[64,2048]{1,0:T(8,128)} %bitcast.9), channel_id=1, source_target_pairs={{0,1},{1,0},{2,3},{3,2},{4,5},{5,4},{6,7},{7,6},{8,9},{9,8},{10,11... | collective-permute-start | bytes 1572872 | tf_op jit(solution)/shard_map/ppermute | solution.py:358
  3.7 5.2 %copy-start.3 = (f32[4,64]{1,0:T(4,128)S(1)}, f32[4,64]{1,0:T(4,128)}, u32[]{:S(2)}) copy-start(f32[4,64]{1,0:T(4,128)} %topics_ref.1) | copy-start | bytes 3076
  3.7 15.7 %collective-permute-start.1 = (f32[8,4160]{1,0:T(8,128)}, f32[8,4160]{1,0:T(8,128)S(1)}, u32[]{:S(2)}, u32[]{:S(2)}) collective-permute-start(f32[8,4160]{1,0:T(8,128)} %get-tuple-element.43), channel_id=1, source_target_pairs={{0,7},{1,6},{2,5},{3,4},{4,3},{5,2},{6,1},{7,0},{8,15},{9,14},{10,... | collective-permute-start | bytes 399368 | tf_op jit(solution)/shard_map/ppermute | solution.py:347
  8.5 12.1 %collective-permute-start.2 = (f32[8,4160]{1,0:T(8,128)}, f32[8,4160]{1,0:T(8,128)S(1)}, u32[]{:S(2)}, u32[]{:S(2)}) collective-permute-start(f32[8,4160]{1,0:T(8,128)} %get-tuple-element.44), channel_id=1, source_target_pairs={{0,4},{1,5},{2,6},{3,7},{4,0},{5,1},{6,2},{7,3},{8,12},{9,13},{10,... | collective-permute-start | bytes 399368 | tf_op jit(solution)/shard_map/ppermute | solution.py:347
  8.5 12.1 %collective-permute-start.3 = (f32[8,4160]{1,0:T(8,128)}, f32[8,4160]{1,0:T(8,128)S(1)}, u32[]{:S(2)}, u32[]{:S(2)}) collective-permute-start(f32[8,4160]{1,0:T(8,128)} %get-tuple-element.45), channel_id=1, source_target_pairs={{0,3},{1,2},{2,1},{3,0},{4,7},{5,6},{6,5},{7,4},{8,11},{9,10},{10,... | collective-permute-start | bytes 399368 | tf_op jit(solution)/shard_map/ppermute | solution.py:347
  8.9 1.0 %copy-start.2 = (s32[4,16384]{1,0:T(4,128)S(1)}, s32[4,16384]{1,0:T(4,128)}, u32[]{:S(2)}) copy-start(s32[4,16384]{1,0:T(4,128)} %counts_ref.1) | copy-start | bytes 786436
  9.8 1.5 %copy-start.4 = (s32[1,64]{1,0:T(1,128)S(1)}, s32[1,64]{1,0:T(1,128)}, u32[]{:S(2)}) copy-start(s32[1,64]{1,0:T(1,128)} %perm_ref.1) | copy-start | bytes 772
  9.8 10.8 %copy-start = (f32[8,4160]{1,0:T(8,128)S(1)}, f32[8,4160]{1,0:T(8,128)}, u32[]{:S(2)}) copy-start(f32[8,4160]{1,0:T(8,128)} %get-tuple-element.46.refs_3_.refs_4_) | copy-start | bytes 399364
  9.9 9.5 %collective-permute-start.4 = (f32[4,4160]{1,0:T(4,128)S(1)}, f32[4,4160]{1,0:T(4,128)S(1)}, u32[]{:S(2)}, u32[]{:S(2)}) collective-permute-start(f32[4,4160]{1,0:T(4,128)S(1)} %get-tuple-element.47), channel_id=1, source_target_pairs={{0,3},{1,2},{2,1},{3,0},{4,7},{5,6},{6,5},{7,4},{8,11},{9,10},{10,... | collective-permute-start | bytes 199688 | tf_op jit(solution)/shard_map/ppermute | solution.py:347
  21.2 5.1 %collective-permute-start.5 = (f32[40,64]{1,0:T(8,128)S(1)}, f32[40,64]{1,0:T(8,128)S(1)}, u32[]{:S(2)}, u32[]{:S(2)}) collective-permute-start(f32[40,64]{1,0:T(8,128)S(1)} %constant_dynamic-update-slice_fusion.refs_4_), channel_id=1, source_target_pairs={{0,7},{1,6},{2,5},{3,4},{4,3},{5,2},{6,1},{7,0},{8,15},{9,14},{10,... | collective-permute-start | bytes 30728 | tf_op jit(solution)/shard_map/ppermute | solution.py:347
  24.0 4.7 %collective-permute-start.6 = (f32[40,64]{1,0:T(8,128)S(1)}, f32[40,64]{1,0:T(8,128)S(1)}, u32[]{:S(2)}, u32[]{:S(2)}) collective-permute-start(f32[40,64]{1,0:T(8,128)S(1)} %constant_dynamic-update-slice_fusion.refs_4_), channel_id=1, source_target_pairs={{0,4},{1,5},{2,6},{3,7},{4,0},{5,1},{6,2},{7,3},{8,12},{9,13},{10,... | collective-permute-start | bytes 30728 | tf_op jit(solution)/shard_map/ppermute | solution.py:347
  24.0 4.7 %collective-permute-start.7 = (f32[40,64]{1,0:T(8,128)S(1)}, f32[40,64]{1,0:T(8,128)S(1)}, u32[]{:S(2)}, u32[]{:S(2)}) collective-permute-start(f32[40,64]{1,0:T(8,128)S(1)} %constant_dynamic-update-slice_fusion.refs_4_), channel_id=1, source_target_pairs={{0,3},{1,2},{2,1},{3,0},{4,7},{5,6},{6,5},{7,4},{8,11},{9,10},{10,... | collective-permute-start | bytes 30728 | tf_op jit(solution)/shard_map/ppermute | solution.py:347
  29.3 5.0 %collective-permute-start.8 = (f32[32,64]{1,0:T(8,128)S(1)}, f32[32,64]{1,0:T(8,128)S(1)}, u32[]{:S(2)}, u32[]{:S(2)}) collective-permute-start(f32[32,64]{1,0:T(8,128)S(1)} %get-tuple-element.53.refs_5_), channel_id=1, source_target_pairs={{0,7},{1,6},{2,5},{3,4},{4,3},{5,2},{6,1},{7,0},{8,15},{9,14},{10,... | collective-permute-start | bytes 24584 | tf_op jit(solution)/shard_map/ppermute | solution.py:347
  30.2 4.7 %collective-permute-start.9 = (f32[32,64]{1,0:T(8,128)S(1)}, f32[32,64]{1,0:T(8,128)S(1)}, u32[]{:S(2)}, u32[]{:S(2)}) collective-permute-start(f32[32,64]{1,0:T(8,128)S(1)} %get-tuple-element.53.refs_5_), channel_id=1, source_target_pairs={{0,4},{1,5},{2,6},{3,7},{4,0},{5,1},{6,2},{7,3},{8,12},{9,13},{10,... | collective-permute-start | bytes 24584 | tf_op jit(solution)/shard_map/ppermute | solution.py:347
  30.8 4.1 %collective-permute-start.10 = (f32[32,64]{1,0:T(8,128)S(1)}, f32[32,64]{1,0:T(8,128)S(1)}, u32[]{:S(2)}, u32[]{:S(2)}) collective-permute-start(f32[32,64]{1,0:T(8,128)S(1)} %get-tuple-element.53.refs_5_), channel_id=1, source_target_pairs={{0,3},{1,2},{2,1},{3,0},{4,7},{5,6},{6,5},{7,4},{8,11},{9,10},{10,... | collective-permute-start | bytes 24584 | tf_op jit(solution)/shard_map/ppermute | solution.py:347
  35.5 5.0 %collective-permute-start.11 = (f32[32,64]{1,0:T(8,128)S(1)}, f32[32,64]{1,0:T(8,128)S(1)}, u32[]{:S(2)}, u32[]{:S(2)}) collective-permute-start(f32[32,64]{1,0:T(8,128)S(1)} %get-tuple-element.55.refs_4_), channel_id=1, source_target_pairs={{0,7},{1,6},{2,5},{3,4},{4,3},{5,2},{6,1},{7,0},{8,15},{9,14},{10,... | collective-permute-start | bytes 24584 | tf_op jit(solution)/shard_map/ppermute | solution.py:347
  37.3 4.6 %collective-permute-start.12 = (f32[32,64]{1,0:T(8,128)S(1)}, f32[32,64]{1,0:T(8,128)S(1)}, u32[]{:S(2)}, u32[]{:S(2)}) collective-permute-start(f32[32,64]{1,0:T(8,128)S(1)} %get-tuple-element.55.refs_4_), channel_id=1, source_target_pairs={{0,4},{1,5},{2,6},{3,7},{4,0},{5,1},{6,2},{7,3},{8,12},{9,13},{10,... | collective-permute-start | bytes 24584 | tf_op jit(solution)/shard_map/ppermute | solution.py:347
  38.3 3.6 %collective-permute-start.13 = (f32[32,64]{1,0:T(8,128)S(1)}, f32[32,64]{1,0:T(8,128)S(1)}, u32[]{:S(2)}, u32[]{:S(2)}) collective-permute-start(f32[32,64]{1,0:T(8,128)S(1)} %get-tuple-element.55.refs_4_), channel_id=1, source_target_pairs={{0,3},{1,2},{2,1},{3,0},{4,7},{5,6},{6,5},{7,4},{8,11},{9,10},{10,... | collective-permute-start | bytes 24584 | tf_op jit(solution)/shard_map/ppermute | solution.py:347
  42.4 2.0 %collective-permute-start.14 = (f32[64,2176]{1,0:T(8,128)S(1)}, f32[64,2176]{1,0:T(8,128)S(1)}, u32[]{:S(2)}, u32[]{:S(2)}) collective-permute-start(f32[64,2176]{1,0:T(8,128)S(1)} %get-tuple-element.57.sent_ref), channel_id=1, source_target_pairs={{0,1},{1,0},{2,3},{3,2},{4,5},{5,4},{6,7},{7,6},{8,9},{9,8},{10,11... | collective-permute-start | bytes 1671176 | tf_op jit(solution)/shard_map/ppermute | solution.py:358
  44.7 9.4 %collective-permute-start.15 = (f32[64,512]{1,0:T(8,128)S(1)}, f32[64,512]{1,0:T(8,128)S(1)}, u32[]{:S(2)}, u32[]{:S(2)}) collective-permute-start(f32[64,512]{1,0:T(8,128)S(1)} %get-tuple-element.80), channel_id=1, source_target_pairs={{0,24},{8,16},{16,8},{24,0},{1,25},{9,17},{17,9},{25,1},{2,26},{10... | collective-permute-start | bytes 393224 | tf_op jit(solution)/shard_map/ppermute | solution.py:361
  47.2 6.9 %collective-permute-start.16 = (f32[64,512]{1,0:T(8,128)S(1)}, f32[64,512]{1,0:T(8,128)S(1)}, u32[]{:S(2)}, u32[]{:S(2)}) collective-permute-start(f32[64,512]{1,0:T(8,128)S(1)} %get-tuple-element.79), channel_id=1, source_target_pairs={{0,16},{8,24},{16,0},{24,8},{1,17},{9,25},{17,1},{25,9},{2,18},{10... | collective-permute-start | bytes 393224 | tf_op jit(solution)/shard_map/ppermute | solution.py:361
  47.7 6.4 %collective-permute-start.17 = (f32[64,512]{1,0:T(8,128)S(1)}, f32[64,512]{1,0:T(8,128)S(1)}, u32[]{:S(2)}, u32[]{:S(2)}) collective-permute-start(f32[64,512]{1,0:T(8,128)S(1)} %get-tuple-element.78), channel_id=1, source_target_pairs={{0,8},{8,0},{16,24},{24,16},{1,9},{9,1},{17,25},{25,17},{2,10},{10... | collective-permute-start | bytes 393224 | tf_op jit(solution)/shard_map/ppermute | solution.py:361
  48.2 5.8 %collective-permute-start.18 = (f32[4,4160]{1,0:T(4,128)S(1)}, f32[4,4160]{1,0:T(4,128)S(1)}, u32[]{:S(2)}, u32[]{:S(2)}) collective-permute-start(f32[4,4160]{1,0:T(4,128)S(1)} %get-tuple-element.63), channel_id=1, source_target_pairs={{0,7},{1,6},{2,5},{3,4},{4,3},{5,2},{6,1},{7,0},{8,15},{9,14},{10,... | collective-permute-start | bytes 199688 | tf_op jit(solution)/shard_map/ppermute | solution.py:347
  54.1 9.5 %collective-permute-start.19 = (f32[64,512]{1,0:T(8,128)S(1)}, f32[64,512]{1,0:T(8,128)S(1)}, u32[]{:S(2)}, u32[]{:S(2)}) collective-permute-start(f32[64,512]{1,0:T(8,128)S(1)} %shard_map.95.refs_0_.refs_4_), channel_id=1, source_target_pairs={{0,24},{8,16},{16,8},{24,0},{1,25},{9,17},{17,9},{25,1},{2,26},{10... | collective-permute-start | bytes 393224 | tf_op jit(solution)/shard_map/ppermute | solution.py:361
  56.6 7.0 %collective-permute-start.20 = (f32[64,512]{1,0:T(8,128)S(1)}, f32[64,512]{1,0:T(8,128)S(1)}, u32[]{:S(2)}, u32[]{:S(2)}) collective-permute-start(f32[64,512]{1,0:T(8,128)S(1)} %shard_map.95.refs_0_.refs_4_), channel_id=1, source_target_pairs={{0,16},{8,24},{16,0},{24,8},{1,17},{9,25},{17,1},{25,9},{2,18},{10... | collective-permute-start | bytes 393224 | tf_op jit(solution)/shard_map/ppermute | solution.py:361
  57.2 6.4 %collective-permute-start.21 = (f32[64,512]{1,0:T(8,128)S(1)}, f32[64,512]{1,0:T(8,128)S(1)}, u32[]{:S(2)}, u32[]{:S(2)}) collective-permute-start(f32[64,512]{1,0:T(8,128)S(1)} %shard_map.95.refs_0_.refs_4_), channel_id=1, source_target_pairs={{0,8},{8,0},{16,24},{24,16},{1,9},{9,1},{17,25},{25,17},{2,10},{10... | collective-permute-start | bytes 393224 | tf_op jit(solution)/shard_map/ppermute | solution.py:361
  57.7 5.9 %collective-permute-start.22 = (f32[4,4160]{1,0:T(4,128)S(1)}, f32[4,4160]{1,0:T(4,128)S(1)}, u32[]{:S(2)}, u32[]{:S(2)}) collective-permute-start(f32[4,4160]{1,0:T(4,128)S(1)} %get-tuple-element.64), channel_id=1, source_target_pairs={{0,4},{1,5},{2,6},{3,7},{4,0},{5,1},{6,2},{7,3},{8,12},{9,13},{10,... | collective-permute-start | bytes 199688 | tf_op jit(solution)/shard_map/ppermute | solution.py:347
  63.7 2.0 %collective-permute-start.23 = (f32[64,2048]{1,0:T(8,128)S(1)}, f32[64,2048]{1,0:T(8,128)S(1)}, u32[]{:S(2)}, u32[]{:S(2)}) collective-permute-start(f32[64,2048]{1,0:T(8,128)S(1)} %shard_map.96.median_ref), channel_id=1, source_target_pairs={{0,1},{1,0},{2,3},{3,2},{4,5},{5,4},{6,7},{7,6},{8,9},{9,8},{10,11... | collective-permute-start | bytes 1572872 | tf_op jit(solution)/shard_map/ppermute | solution.py:358
  66.4 4.9 %collective-permute-start.24 = (f32[24,64]{1,0:T(8,128)S(1)}, f32[24,64]{1,0:T(8,128)S(1)}, u32[]{:S(2)}, u32[]{:S(2)}) collective-permute-start(f32[24,64]{1,0:T(8,128)S(1)} %get-tuple-element.68.refs_4_), channel_id=1, source_target_pairs={{0,7},{1,6},{2,5},{3,4},{4,3},{5,2},{6,1},{7,0},{8,15},{9,14},{10,... | collective-permute-start | bytes 18440 | tf_op jit(solution)/shard_map/ppermute | solution.py:347
  68.0 4.6 %collective-permute-start.25 = (f32[24,64]{1,0:T(8,128)S(1)}, f32[24,64]{1,0:T(8,128)S(1)}, u32[]{:S(2)}, u32[]{:S(2)}) collective-permute-start(f32[24,64]{1,0:T(8,128)S(1)} %get-tuple-element.68.refs_4_), channel_id=1, source_target_pairs={{0,4},{1,5},{2,6},{3,7},{4,0},{5,1},{6,2},{7,3},{8,12},{9,13},{10,... | collective-permute-start | bytes 18440 | tf_op jit(solution)/shard_map/ppermute | solution.py:347
  68.2 4.4 %collective-permute-start.26 = (f32[24,64]{1,0:T(8,128)S(1)}, f32[24,64]{1,0:T(8,128)S(1)}, u32[]{:S(2)}, u32[]{:S(2)}) collective-permute-start(f32[24,64]{1,0:T(8,128)S(1)} %get-tuple-element.68.refs_4_), channel_id=1, source_target_pairs={{0,3},{1,2},{2,1},{3,0},{4,7},{5,6},{6,5},{7,4},{8,11},{9,10},{10,... | collective-permute-start | bytes 18440 | tf_op jit(solution)/shard_map/ppermute | solution.py:347
  73.3 4.8 %collective-permute-start.27 = (f32[4,64]{1,0:T(4,128)S(1)}, f32[4,64]{1,0:T(4,128)S(1)}, u32[]{:S(2)}, u32[]{:S(2)}) collective-permute-start(f32[4,64]{1,0:T(4,128)S(1)} %get-tuple-element.75), channel_id=1, source_target_pairs={{0,7},{1,6},{2,5},{3,4},{4,3},{5,2},{6,1},{7,0},{8,15},{9,14},{10,... | collective-permute-start | bytes 3080 | tf_op jit(solution)/shard_map/ppermute | solution.py:347
  74.3 4.5 %collective-permute-start.28 = (f32[4,64]{1,0:T(4,128)S(1)}, f32[4,64]{1,0:T(4,128)S(1)}, u32[]{:S(2)}, u32[]{:S(2)}) collective-permute-start(f32[4,64]{1,0:T(4,128)S(1)} %get-tuple-element.76), channel_id=1, source_target_pairs={{0,4},{1,5},{2,6},{3,7},{4,0},{5,1},{6,2},{7,3},{8,12},{9,13},{10,... | collective-permute-start | bytes 3080 | tf_op jit(solution)/shard_map/ppermute | solution.py:347
  75.6 3.2 %collective-permute-start.29 = (f32[4,64]{1,0:T(4,128)S(1)}, f32[4,64]{1,0:T(4,128)S(1)}, u32[]{:S(2)}, u32[]{:S(2)}) collective-permute-start(f32[4,64]{1,0:T(4,128)S(1)} %get-tuple-element.77), channel_id=1, source_target_pairs={{0,3},{1,2},{2,1},{3,0},{4,7},{5,6},{6,5},{7,4},{8,11},{9,10},{10,... | collective-permute-start | bytes 3080 | tf_op jit(solution)/shard_map/ppermute | solution.py:347

commit v2 on v1

v2 whole, which is shorter than its diff:
```python
import functools

import jax
import jax.numpy as jnp
from jax import lax
from jax.experimental import pallas as pl
from jax.experimental.pallas import tpu as pltpu
from jax.sharding import PartitionSpec as P

UPDATES = 3
REFITS = 2

EXACT = lax.Precision.HIGHEST
ROUGH = lax.Precision.HIGH
VMEM_BYTES = 14 * 1024 * 1024
SPREAD_BYTES = 60 * 1024 * 1024


def dot(left, right, dims, precision=ROUGH):
    return lax.dot_general(left, right, (dims, ((), ())), precision=precision)


def middle(pieces):
    pieces = list(pieces)
    count = len(pieces)
    for turn in range(count):
        for low in range(turn % 2, count - 1, 2):
            pieces[low], pieces[low + 1] = (
                jnp.minimum(pieces[low], pieces[low + 1]),
                jnp.maximum(pieces[low], pieces[low + 1]),
            )
    return 0.5 * (pieces[count // 2 - 1] + pieces[count // 2])


def call(kernel, outs, *args, flops=0, moved=0, unread=0, scratch=()):
    read = len(args) - unread
    return pl.pallas_call(
        kernel,
        out_shape=outs,
        in_specs=[pl.BlockSpec(memory_space=pltpu.VMEM)] * read
        + [pl.BlockSpec(memory_space=pl.ANY)] * unread,
        scratch_shapes=scratch,
        compiler_params=pltpu.CompilerParams(vmem_limit_bytes=VMEM_BYTES),
        cost_estimate=pl.CostEstimate(flops=flops, bytes_accessed=moved, transcendentals=0),
    )(*args)


def shape(*dims, dtype=jnp.float32):
    return jax.ShapeDtypeStruct(dims, dtype)


def high_low(x):
    high = x.astype(jnp.bfloat16).astype(jnp.float32)
    return high, x - high


def matmul(left, right):
    return jnp.dot(
        left.astype(jnp.bfloat16), right.astype(jnp.bfloat16), preferred_element_type=jnp.float32
    )


def blocks_of(chips, cores, step):
    at_doc = lax.axis_index("doc")
    at_chip, at_core = at_doc // cores, at_doc % cores
    return [(at_chip ^ step) * cores + (at_core ^ ((step + half) % cores)) for half in range(cores)]


def spread_kernel(chips, cores, own_words, mask_hbm, topics_hbm, counts_hbm, *refs):
    out_refs, (mask_ref, topics_ref, counts_ref, small_sems, in_sems) = (
        refs[:chips],
        refs[chips:],
    )
    small = [
        pltpu.make_async_copy(mask_hbm, mask_ref, small_sems.at[0]),
        pltpu.make_async_copy(topics_hbm, topics_ref, small_sems.at[1]),
    ]
    for copy in small:
        copy.start()
    steps = list(range(chips - 1, -1, -1))
    arriving = {}
    for step in steps:
        for half, block in enumerate(blocks_of(chips, cores, step)):
            at = slice(half * own_words, (half + 1) * own_words)
            arriving[step, half] = pltpu.make_async_copy(
                counts_hbm.at[:, pl.ds(pl.multiple_of(block * own_words, 128), own_words)],
                counts_ref.at[step, :, at],
                in_sems.at[step, half],
            )
            arriving[step, half].start()
    docs, tiles = mask_ref.shape
    width = chips * cores * own_words // tiles
    own_tiles = own_words // width
    tile_ids = lax.broadcasted_iota(jnp.int32, (docs, tiles), 1)
    doc_ids = lax.axis_index("doc") * docs + lax.broadcasted_iota(jnp.int32, (docs, tiles), 0)
    forced = (tile_ids == doc_ids % tiles).astype(jnp.int32)
    for copy in small:
        copy.wait()
    occupied = jnp.maximum(mask_ref[...], forced).astype(jnp.float32)
    for step in steps:
        for half, block in enumerate(blocks_of(chips, cores, step)):
            near = pltpu.roll(occupied, lax.rem(tiles - block * own_tiles, tiles), 1)
            arriving[step, half].wait()
            for tile in range(own_tiles):
                at = slice(half * own_words + tile * width, half * own_words + (tile + 1) * width)
                picked = counts_ref[step, :, at].astype(jnp.float32)
                out_refs[step][:, at] = picked * near[:, tile : tile + 1]
        out_refs[step][:, cores * own_words :] = jnp.concatenate([topics_ref[...]] * 2, axis=1)


def base_kernel(chips, cores, counts_ref, topics_ref, *out_refs):
    span = out_refs[0].shape[1] - 2 * topics_ref.shape[1]
    own_words = span // cores
    for step in range(chips):
        for half, block in enumerate(blocks_of(chips, cores, step)):
            at = slice(half * own_words, (half + 1) * own_words)
            first = pl.multiple_of(block * own_words, 128)
            out_refs[step][:, at] = counts_ref[:, pl.ds(first, own_words)].astype(jnp.float32)
        out_refs[step][:, span:] = jnp.concatenate([topics_ref[...]] * 2, axis=1)


def moved_columns(x, onehot):
    rows = x.shape[0]
    high, rest = high_low(x)
    mid, low = high_low(rest)
    moved = matmul(jnp.concatenate([high, mid, low], axis=0), onehot)
    return moved[:rows] + moved[rows : 2 * rows] + moved[2 * rows :]


def dictionary_kernel(half_count, perm_ref, *refs):
    topics, words = refs[0].shape
    wide_ref, tall_ref, total_ref, aligned_ref, onehot_ref = refs[half_count:]
    onehot = (
        lax.broadcasted_iota(jnp.int32, (topics, topics), 0) == perm_ref[...]
    ).astype(jnp.float32)
    onehot_ref[...] = onehot
    total = jnp.zeros((1, topics), jnp.float32)
    for half in range(half_count):
        at = slice(half * words, (half + 1) * words)
        full = refs[half][...]
        high, rest = high_low(full)
        mid, low = high_low(rest)
        wide_ref[:topics, at] = high.astype(jnp.bfloat16)
        wide_ref[topics:, at] = rest.astype(jnp.bfloat16)
        if half == 0:
            turned = onehot.T
            aligned_ref[...] = matmul(
                jnp.concatenate([turned] * 3, axis=1), jnp.concatenate([high, mid, low], axis=0)
            )
        tall = full.T
        total += jnp.sum(tall, axis=0, keepdims=True)
        tall_ref[at, :] = jnp.concatenate(high_low(tall), axis=1).astype(jnp.bfloat16)
    total_ref[...] = jnp.concatenate([jnp.broadcast_to(total, (8, topics))] * 2, axis=1)


def recon_of(doubled, wide):
    rows = doubled.shape[0]
    both = matmul(jnp.concatenate(high_low(doubled), axis=0), wide)
    return both[:rows] + both[rows:]


def product_of(quotient, tall):
    rows = quotient.shape[0]
    both = matmul(jnp.concatenate(high_low(quotient), axis=0), tall)
    both = both[:rows] + both[rows:]
    return both + turned(both)


def turned(x):
    return pltpu.roll(x, x.shape[1] // 2, 1)


def left_half(x):
    return lax.broadcasted_iota(jnp.int32, x.shape, 1) < x.shape[1] // 2


def pack(doubled):
    half = doubled.shape[0] // 2
    lower, upper = doubled[:half], doubled[half:]
    return jnp.where(left_half(lower), lower, upper)


def sum_packed(chips, parts):
    parts = [parts[0], *parts[:0:-1]]
    side = max(chips // 2, 1)
    rows = parts[0].shape[0] // side

    def moved(x, step):
        if step == 0:
            return x
        return jnp.concatenate([x[(c ^ step) * rows : ((c ^ step) + 1) * rows] for c in range(side)], axis=0)

    sums = []
    for first in range(0, chips, side):
        sums.append(sum(moved(parts[step], step - first) for step in range(first, first + side)))
    packed, other = sums[0] + turned(sums[1]), turned(sums[0]) + sums[1]
    left = left_half(packed)
    return jnp.concatenate([jnp.where(left, packed, other), jnp.where(left, other, packed)], axis=0)


def write_parts(refs, part):
    rows = part.shape[0]
    for ref in refs:
        ref[:rows] = part
        if ref.shape[0] > rows:
            ref[rows:] = jnp.zeros((ref.shape[0] - rows, part.shape[1]), part.dtype)


def first_kernel(chips, cores, wide_ref, tall_ref, col_part_ref, *refs):
    payload, (topics_ref, part_ref, *half_refs) = refs[:chips][::-1], refs[-2 - cores :]
    span = wide_ref.shape[1]
    topics = jnp.concatenate([ref[:, span:] for ref in payload], axis=0)
    topics_ref[...] = topics
    weighted = jnp.concatenate([ref[:, :span] for ref in payload], axis=0)
    part = pack(product_of(weighted / recon_of(topics, wide_ref[...]), tall_ref[...]))
    part_ref[: part.shape[0]] = part
    part_ref[part.shape[0] :] = col_part_ref[...]
    words = span // cores
    for half, ref in enumerate(half_refs):
        ref[...] = weighted[:, half * words : (half + 1) * words]


def update_kernel(chips, wide_ref, tall_ref, before_ref, *refs):
    packed = before_ref.shape[0] // 2
    if refs[-1].shape[0] == 8:
        payload, parts = refs[:chips][::-1], refs[chips : 2 * chips]
        topics_ref, *part_refs, total_ref = refs[2 * chips :]
        total_ref[...] = sum(ref[packed:] for ref in parts)
    else:
        total_ref, payload, parts = refs[0], refs[1 : chips + 1][::-1], refs[chips + 1 : 2 * chips + 1]
        topics_ref, *part_refs = refs[2 * chips + 1 :]
    span = wide_ref.shape[1]
    total = sum_packed(chips, [ref[:packed] for ref in parts])
    topics = before_ref[...] / total_ref[:1] * total
    topics_ref[...] = topics
    weighted = jnp.concatenate([ref[:, :span] for ref in payload], axis=0)
    write_parts(part_refs, pack(product_of(weighted / recon_of(topics, wide_ref[...]), tall_ref[...])))


def numerator_of(topics, quotient):
    high, low = high_low(topics.T)
    quotient_high, quotient_low = high_low(quotient)
    return matmul(
        jnp.concatenate([high, low, high], axis=1),
        jnp.concatenate([quotient_high, quotient_high, quotient_low], axis=0),
    )


def topics_kernel(chips, before_ref, total_ref, *refs):
    parts, topics_ref = refs[:chips], refs[-1]
    total = sum_packed(chips, [ref[: before_ref.shape[0] // 2] for ref in parts])
    topics_ref[...] = before_ref[...] / total_ref[:1] * total


def numerator_kernel(wide_ref, onehot_ref, topics_ref, weighted_ref, *refs):
    before, out_ref = refs[:-1], refs[-1]
    topic_count, words = onehot_ref.shape[0], weighted_ref.shape[1]
    quotient = weighted_ref[...] / recon_of(topics_ref[...], wide_ref[:, :words])
    aligned = moved_columns(topics_ref[:, :topic_count], onehot_ref[...])
    numerator = numerator_of(aligned, quotient)
    load = jnp.sum(aligned.T, axis=1, keepdims=True)
    if out_ref.shape[1] > words:
        out_ref[:, :words] = numerator
        out_ref[:, words:] = jnp.broadcast_to(load, (topic_count, out_ref.shape[1] - words))
    else:
        dict_ref, *other = before
        for ref in other:
            numerator = numerator + ref[:, :words]
            load = load + ref[:, words : words + 1]
        out_ref[...] = dict_ref[...] * numerator / load


def base_rows_of(refs, at):
    return jnp.concatenate([ref[:, at] for ref in refs], axis=0)


def refit_kernel(members, chips, half, *refs):
    pieces, payload = refs[:members], refs[members : members + chips]
    *before, wide_ref, tall_ref, part_ref, median_ref = refs[members + chips :]
    sub = pieces[0].shape[1]
    for me in range(members):

        @pl.when(lax.axis_index("pert") == me)
        def _():
            for at in range(members):
                owner = me ^ ((members - at) % members)
                median_ref[:, owner * sub : (owner + 1) * sub] = pieces[at][...]

    words = median_ref.shape[1]
    span = payload[0].shape[1] - part_ref.shape[1]
    wide = jnp.concatenate(high_low(median_ref[...]), axis=0).astype(jnp.bfloat16)
    wide_ref[...] = wide
    tall = jnp.concatenate(high_low(median_ref[...].T), axis=1)
    total = jnp.sum(tall, axis=0, keepdims=True)
    total = jnp.broadcast_to(total + turned(total), (8, total.shape[1]))
    tall = tall.astype(jnp.bfloat16)
    tall_ref[...] = tall
    weighted = base_rows_of(payload, slice(half * words, (half + 1) * words))
    refit = base_rows_of(payload, slice(span, None))
    part = pack(product_of(weighted / recon_of(refit, wide), tall))
    both = jnp.concatenate([part, total], axis=0)
    part_ref[...] = both + before[0][...] if before else both


def refit_again_kernel(chips, cores, base_docs, *refs):
    payload, parts, halves = refs[:chips], refs[chips : 2 * chips], refs[2 * chips : 2 * (chips + cores)]
    scale_ref, *part_refs = refs[2 * (chips + cores) :]
    packed = chips * base_docs // 2
    span = payload[0].shape[1] - scale_ref.shape[1]
    words = span // cores
    median_total = sum(ref[packed : packed + 1] for ref in parts)
    total = sum_packed(chips, [ref[:packed] for ref in parts])
    refit = base_rows_of(payload, slice(span, None)) / median_total * total
    scale_ref[...] = refit[:base_docs] / median_total
    part = None
    for half in range(cores):
        weighted = base_rows_of(payload, slice(half * words, (half + 1) * words))
        wide_ref, tall_ref = halves[2 * half], halves[2 * half + 1]
        new = product_of(weighted / recon_of(refit, wide_ref[...]), tall_ref[...])
        part = new if part is None else part + new
    for step in range(chips):
        part_refs[step][...] = part[step * base_docs : (step + 1) * base_docs]


def finish_kernel(scale_ref, *refs):
    parts, out_ref = refs[:-1], refs[-1]
    out_ref[...] = (scale_ref[...] * sum(ref[...] for ref in parts))[:, : out_ref.shape[1]]


def median_kernel(members, *refs):
    refs[-1][...] = middle([ref[...] for ref in refs[:members]])


def per_device(counts, tile_mask, member_topics, start_dict, align_perm, base_counts, base_topics):
    doc_size = lax.axis_size("doc")
    members = lax.axis_size("pert")
    cores = 2 - doc_size % 2
    chips = doc_size // cores
    at_pert = lax.axis_index("pert")
    at_doc = lax.axis_index("doc")
    at_chip, at_core = at_doc // cores, at_doc % cores
    docs = counts.shape[1]
    base_docs = base_counts.shape[0]
    topic_count = member_topics.shape[2]
    owned = start_dict.shape[1]
    span = cores * owned
    rows = chips * docs
    sub = owned // members

    def over_chips(array, step):
        return lax.ppermute(
            array,
            "doc",
            [
                (c * cores + k, (c ^ step) * cores + (k + step) % cores)
                for c in range(chips)
                for k in range(cores)
            ],
        )

    def over_cores(array):
        return lax.ppermute(array, "doc", [(d, d ^ 1) for d in range(doc_size)])

    def over_pert(array, step):
        return lax.ppermute(array, "pert", [(m, m ^ step) for m in range(members)])

    sent = pl.pallas_call(
        functools.partial(spread_kernel, chips, cores, owned),
        out_shape=[pltpu.VMEM((docs, span + 2 * topic_count), jnp.float32)] * chips,
        in_specs=[pl.BlockSpec(memory_space=pltpu.HBM)] * 3,
        out_specs=[pl.BlockSpec(memory_space=pltpu.VMEM)] * chips,
        scratch_shapes=[
            pltpu.VMEM(tile_mask.shape[1:], jnp.int32),
            pltpu.VMEM(member_topics.shape[1:], jnp.float32),
            pltpu.VMEM((chips, docs, span), jnp.int32),
            pltpu.SemaphoreType.DMA((2,)),
            pltpu.SemaphoreType.DMA((chips, cores)),
        ],
        compiler_params=pltpu.CompilerParams(vmem_limit_bytes=VMEM_BYTES),
        cost_estimate=pl.CostEstimate(flops=0, bytes_accessed=12 * counts.size, transcendentals=0),
    )(*[pltpu.with_memory_space_constraint(x, pltpu.HBM) for x in (tile_mask[0], member_topics[0], counts[0])])
    base_sent = call(
        functools.partial(base_kernel, chips, cores),
        [shape(base_docs, span + 2 * topic_count)] * chips,
        base_counts,
        base_topics,
        moved=8 * base_counts.size,
    )
    got = [over_chips(sent[step], step) for step in range(chips - 1, 0, -1)][::-1]
    payload = [sent[0]] + got
    near = [over_chips(base_sent[step], step) for step in range(1, min(chips, 2))]
    dict_own = start_dict[0].T
    halves = [dict_own] + [over_cores(dict_own)] * (cores - 1)
    wide, tall, col_part, dict_own, onehot = call(
        functools.partial(dictionary_kernel, cores),
        [
            shape(2 * topic_count, span, dtype=jnp.bfloat16),
            shape(span, 2 * topic_count, dtype=jnp.bfloat16),
            shape(8, 2 * topic_count),
            shape(topic_count, owned),
            shape(topic_count, topic_count),
        ],
        align_perm,
        *halves,
        moved=4 * 4 * span * topic_count,
    )

    update_flops = 2 * 2 * 4 * rows * topic_count * span
    topics, part, *weighted = call(
        functools.partial(first_kernel, chips, cores),
        [shape(rows, 2 * topic_count), shape(rows // 2 + 8, 2 * topic_count)]
        + [shape(rows, owned)] * cores,
        wide,
        tall,
        col_part,
        *payload[::-1],
        *near,
        unread=len(near),
        flops=update_flops,
        moved=4 * span * (rows + 2 * topic_count),
    )
    parts = [part] + [over_chips(part, step) for step in range(chips - 1, 0, -1)]
    crossed = [over_cores(weighted[1])] if cores > 1 else []
    totals = []
    for update in range(1, UPDATES):
        topics, *outs = call(
            functools.partial(update_kernel, chips),
            [shape(rows, 2 * topic_count)]
            + [shape(rows // 2 + 8 * (step - 1), 2 * topic_count) for step in range(1, chips)]
            + ([] if totals else [shape(8, 2 * topic_count)]),
            wide,
            tall,
            topics,
            *totals,
            *payload[::-1],
            *parts,
            flops=update_flops,
            moved=4 * span * (rows + 2 * topic_count),
        )
        totals = totals or outs[chips - 1 :]
        parts = [outs[0]] + [over_chips(outs[step - 1], step) for step in range(chips - 1, 0, -1)]
    (col_total,) = totals

    topics = call(
        functools.partial(topics_kernel, chips),
        shape(rows, 2 * topic_count),
        topics,
        col_total,
        *parts,
        *crossed,
        unread=len(crossed),
    )
    other = []
    if cores > 1:
        other_topics = over_cores(topics)
        other = [
            call(
                numerator_kernel,
                shape(topic_count, owned + 128),
                wide,
                onehot,
                topics,
                weighted[0],
                flops=update_flops // 2,
                moved=2 * span * (rows + 2 * topic_count),
            )
        ]
        topics, weighted = other_topics, crossed
    aligned = call(
        numerator_kernel,
        shape(topic_count, owned),
        wide,
        onehot,
        topics,
        weighted[0],
        dict_own,
        *other,
        flops=update_flops // 2,
        moved=2 * span * (rows + 2 * topic_count),
    )

    def words_of(array, member):
        return lax.dynamic_slice_in_dim(array, member * sub, sub, 1)

    aligned, base_sent = lax.optimization_barrier((aligned, base_sent))
    base_got = [over_chips(base_sent[step], step) for step in range(2, chips)]
    late = len(base_got) // 2
    base_got = base_got[::-1]
    median = call(
        functools.partial(median_kernel, members),
        pltpu.VMEM((topic_count, sub), jnp.float32),
        words_of(aligned, at_pert),
        *[over_pert(words_of(aligned, at_pert ^ step), step) for step in range(members - 1, 0, -1)],
        *base_got[late:],
        unread=len(base_got) - late,
    )
    pieces = [median] + [over_pert(median, step) for step in range(members - 1, 0, -1)]
    pieces[1], *base_got[:late] = lax.optimization_barrier((pieces[1], *base_got[:late]))
    median_halves = [pieces] + [[over_cores(piece) for piece in pieces]] * (cores - 1)
    base_all = [base_sent[0]] + near + base_got[::-1]

    base_rows = chips * base_docs
    refit_flops = 2 * 2 * 4 * base_rows * topic_count * owned
    forms, before = [], []
    for half in range(cores):
        wide, tall, part = call(
            functools.partial(refit_kernel, members, chips, half),
            [
                shape(2 * topic_count, owned, dtype=jnp.bfloat16),
                shape(owned, 2 * topic_count, dtype=jnp.bfloat16),
                shape(base_rows // 2 + 8, 2 * topic_count),
            ],
            *median_halves[half],
            *base_all,
            *before,
            flops=refit_flops,
            moved=16 * owned * topic_count,
            scratch=[pltpu.VMEM((topic_count, owned), jnp.float32)],
        )
        forms += [wide, tall]
        before = [part]
    scale, *parts = call(
        functools.partial(refit_again_kernel, chips, cores, base_docs),
        [shape(base_docs, 2 * topic_count)] * (chips + 1),
        *base_all,
        part,
        *[over_chips(part, step) for step in range(chips - 1, 0, -1)],
        *forms,
        flops=2 * refit_flops,
        moved=16 * owned * topic_count,
    )
    refit = call(
        finish_kernel,
        shape(base_docs, topic_count),
        scale,
        parts[0],
        *[over_chips(parts[step], step) for step in range(chips - 1, 0, -1)],
    )
    return (median.T[None, None], refit)


def solution(mesh):
    return jax.shard_map(
        per_device,
        mesh=mesh,
        in_specs=(
            P("pert", "doc", None),
            P("pert", "doc", None),
            P("pert", "doc", None),
            P("pert", "doc", None),
            P("pert", None),
            P(("pert", "doc"), None),
            P(("pert", "doc"), None),
        ),
        out_specs=(P("doc", "pert", None, None), P(("pert", "doc"), None)),
        check_vma=False,
    )
```

time: 79.5 us -> 77.1 us (0.970)
  waiting for transfers between devices: 31.7 us -> 28.5 us
  starting transfers between devices: 35.8 us -> 37 us
  Pallas kernels: 10.1 us -> 9.04 us
    ppermute x21, waiting for transfers between devices: 29.7 us -> 27.5 us  [over_chips(): lax.ppermute(array, 'doc', [(c * cores + k, (c ^ step) * cores + (k + ste...]
    ppermute x3 -> x7, starting transfers between devices: 0.66 us -> 2.54 us  [over_cores(): return lax.ppermute(array, 'doc', [(d, d ^ 1) for d in range(doc_size)])]
    ppermute x3 -> x7, waiting for transfers between devices: 1.97 us -> 0.97 us  [over_cores(): return lax.ppermute(array, 'doc', [(d, d ^ 1) for d in range(doc_size)])]
    unnamed x11 -> x9, local copies, waits for them, and re-layouts: 0.98 us -> 1.62 us
    pallas_call x14 -> x13, Pallas kernels: 7.54 us -> 7.19 us  [call(): pl.pallas_call(kernel, out_shape=outs, in_specs=[pl.BlockSpec(memory_spac...]
  transfers between devices with their start and end apart: 30 -> 34, of which waited for: 17 -> 17; matrix products, arithmetic and copies ran while one was open for 0% -> 1% of each run, Pallas kernels for 7% -> 7%
where the time goes in v2:
time: 77.1 us; the launch traced here: 77 us
  starting transfers between devices  37 us (48%)
  waiting for transfers between devices  28.5 us (37%)
  Pallas kernels  9.04 us (12%)
  local copies, waits for them, and re-layouts  1.67 us (2%)
  between operations  0.78 us (1%)
    ppermute x21, waiting for transfers between devices, over_chips(): lax.ppermute(array, 'doc', [(c * cores + k, (c ^ step) * cores + (k + ste...  27.5 us
    ppermute x21, starting transfers between devices, over_chips(): lax.ppermute(array, 'doc', [(c * cores + k, (c ^ step) * cores + (k + ste...  27.4 us
    pallas_call x13, Pallas kernels, call(): pl.pallas_call(kernel, out_shape=outs, in_specs=[pl.BlockSpec(memory_spac...  7.19 us
    ppermute x6, starting transfers between devices, over_pert(): return lax.ppermute(array, 'pert', [(m, m ^ step) for m in range(members)])  7.11 us
    ppermute x7, starting transfers between devices, over_cores(): return lax.ppermute(array, 'doc', [(d, d ^ 1) for d in range(doc_size)])  2.54 us
    pallas_call x1, Pallas kernels, per_device(): pl.pallas_call(functools.partial(spread_kernel, chips, cores, owned), out...  1.85 us
    unnamed x9, local copies, waits for them, and re-layouts  1.62 us
  transfers between devices with their start and end apart: 34, of which 17 were waited for; matrix products, arithmetic and copies ran while one was open for 1% of the time, Pallas kernels for 7%

profile of v2, /device:TPU:0, one launch (start us, length us, event | category | flops | bytes accessed | tf_op | source)
XLA Modules:
  0.0 77.0 jit_solution(11994485000500370032)
XLA Ops:
  0.6 0.5 collective-permute-start
  1.2 1.8 %shard_map.87 = (f32[8,4224]{1,0:T(8,128)S(1)}, f32[8,4224]{1,0:T(8,128)S(1)}, f32[8,4224]{1,0:T(8,128)S(1)}, f32[8,4224]{1,0:T(8,128)S(1)}) custom-call(s32[8,128]{1,0:T(8,128)} %bitcast.13, f32[8,64]{1,0:T(8,128)} %bitcast.14, s32[8,16384]{1,0:T(8,128)} %bitcast.12), custom_call_target="tpu_custom_call" | custom-call | bytes 1572864 | tf_op jit(solution)/shard_map/pallas_call | solution.py:367
  3.0 4.8 %collective-permute-start.1 = (f32[8,4224]{1,0:T(8,128)S(1)}, f32[8,4224]{1,0:T(8,128)S(1)}, u32[]{:S(2)}, u32[]{:S(2)}) collective-permute-start(f32[8,4224]{1,0:T(8,128)S(1)} %get-tuple-element.49), channel_id=1, source_target_pairs={{0,7},{1,6},{2,5},{3,4},{4,3},{5,2},{6,1},{7,0},{8,15},{9,14},{10,... | collective-permute-start | bytes 405512 | tf_op jit(solution)/shard_map/ppermute | solution.py:351
  7.8 0.4 collective-permute-start.3
  8.2 0.9 %copy-done.1 = s32[4,16384]{1,0:T(4,128)S(1)} copy-done((s32[4,16384]{1,0:T(4,128)S(1)}, s32[4,16384]{1,0:T(4,128)}, u32[]{:S(2)}) %copy-start.1) | copy-done | bytes 262168
  9.1 0.1 shard_map.88
  9.2 1.4 %collective-permute-start.4 = (f32[4,4224]{1,0:T(4,128)S(1)}, f32[4,4224]{1,0:T(4,128)S(1)}, u32[]{:S(2)}, u32[]{:S(2)}) collective-permute-start(f32[4,4224]{1,0:T(4,128)S(1)} %get-tuple-element.53), channel_id=1, source_target_pairs={{0,3},{1,2},{2,1},{3,0},{4,7},{5,6},{6,5},{7,4},{8,11},{9,10},{10,... | collective-permute-start | bytes 202760 | tf_op jit(solution)/shard_map/ppermute | solution.py:351
  10.6 1.1 %shard_map.86 = (bf16[128,4096]{1,0:T(8,128)(2,1)S(1)}, bf16[4096,128]{1,0:T(8,128)(2,1)S(1)}, f32[8,128]{1,0:T(8,128)S(1)}, f32[64,2048]{1,0:T(8,128)S(1)}, f32[64,64]{1,0:T(8,128)S(1)}) custom-call(s32[1,64]{1,0:T(1,128)S(1)} %copy-done.3, f32[64,2048]{1,0:T(8,128)S(1)} %bitcast.11, f32[64,2048]{1,0:T(8,128)S(1)} %collective-permute-done.refs_1_), custom_call_target="tpu_custom_call" | custom-call | bytes 4194304 | tf_op jit(solution)/shard_map/pallas_call | solution.py:37
  11.7 6.7 %collective-permute-done.4.refs_4_.refs_5_.refs_1_ = f32[4,4224]{1,0:T(4,128)S(1)} collective-permute-done((f32[4,4224]{1,0:T(4,128)S(1)}, f32[4,4224]{1,0:T(4,128)S(1)}, u32[]{:S(2)}, u32[]{:S(2)}) %collective-permute-start.4) | collective-permute-done | bytes 67616 | tf_op jit(solution)/shard_map/ppermute | solution.py:351
  18.5 1.2 %collective-permute-done.2.refs_1_.refs_2_ = f32[8,4224]{1,0:T(8,128)S(1)} collective-permute-done((f32[8,4224]{1,0:T(8,128)S(1)}, f32[8,4224]{1,0:T(8,128)S(1)}, u32[]{:S(2)}, u32[]{:S(2)}) %collective-permute-start.2) | collective-permute-done | bytes 135200 | tf_op jit(solution)/shard_map/ppermute | solution.py:351
  19.8 0.5 shard_map.89
  20.3 0.0 collective-permute-start.14
  20.3 3.1 %collective-permute-start.5 = (f32[24,128]{1,0:T(8,128)S(1)}, f32[24,128]{1,0:T(8,128)S(1)}, u32[]{:S(2)}, u32[]{:S(2)}) collective-permute-start(f32[24,128]{1,0:T(8,128)S(1)} %get-tuple-element.55.refs_4_), channel_id=1, source_target_pairs={{0,7},{1,6},{2,5},{3,4},{4,3},{5,2},{6,1},{7,0},{8,15},{9,14},{10,... | collective-permute-start | bytes 36872 | tf_op jit(solution)/shard_map/ppermute | solution.py:351
  23.4 0.8 %collective-permute-start.7 = (f32[24,128]{1,0:T(8,128)S(1)}, f32[24,128]{1,0:T(8,128)S(1)}, u32[]{:S(2)}, u32[]{:S(2)}) collective-permute-start(f32[24,128]{1,0:T(8,128)S(1)} %get-tuple-element.55.refs_4_), channel_id=1, source_target_pairs={{0,3},{1,2},{2,1},{3,0},{4,7},{5,6},{6,5},{7,4},{8,11},{9,10},{10,... | collective-permute-start | bytes 36872 | tf_op jit(solution)/shard_map/ppermute | solution.py:351
  24.2 1.1 %collective-permute-done.5.refs_5_ = f32[24,128]{1,0:T(8,128)S(1)} collective-permute-done((f32[24,128]{1,0:T(8,128)S(1)}, f32[24,128]{1,0:T(8,128)S(1)}, u32[]{:S(2)}, u32[]{:S(2)}) %collective-permute-start.5) | collective-permute-done | bytes 12320 | tf_op jit(solution)/shard_map/ppermute | solution.py:351
  25.3 2.7 %collective-permute-done.6.refs_6_ = f32[24,128]{1,0:T(8,128)S(1)} collective-permute-done((f32[24,128]{1,0:T(8,128)S(1)}, f32[24,128]{1,0:T(8,128)S(1)}, u32[]{:S(2)}, u32[]{:S(2)}) %collective-permute-start.6) | collective-permute-done | bytes 12320 | tf_op jit(solution)/shard_map/ppermute | solution.py:351
  28.0 0.6 shard_map.90
  28.5 0.9 %collective-permute-start.8 = (f32[32,128]{1,0:T(8,128)S(1)}, f32[32,128]{1,0:T(8,128)S(1)}, u32[]{:S(2)}, u32[]{:S(2)}) collective-permute-start(f32[32,128]{1,0:T(8,128)S(1)} %get-tuple-element.59), channel_id=1, source_target_pairs={{0,7},{1,6},{2,5},{3,4},{4,3},{5,2},{6,1},{7,0},{8,15},{9,14},{10,... | collective-permute-start | bytes 49160 | tf_op jit(solution)/shard_map/ppermute | solution.py:351
  29.4 0.7 collective-permute-start.9
  30.2 2.2 %collective-permute-start.10 = (f32[16,128]{1,0:T(8,128)S(1)}, f32[16,128]{1,0:T(8,128)S(1)}, u32[]{:S(2)}, u32[]{:S(2)}) collective-permute-start(f32[16,128]{1,0:T(8,128)S(1)} %get-tuple-element.58.refs_5_), channel_id=1, source_target_pairs={{0,3},{1,2},{2,1},{3,0},{4,7},{5,6},{6,5},{7,4},{8,11},{9,10},{10,... | collective-permute-start | bytes 24584 | tf_op jit(solution)/shard_map/ppermute | solution.py:351
  32.4 1.4 %collective-permute-done.10.refs_8_ = f32[16,128]{1,0:T(8,128)S(1)} collective-permute-done((f32[16,128]{1,0:T(8,128)S(1)}, f32[16,128]{1,0:T(8,128)S(1)}, u32[]{:S(2)}, u32[]{:S(2)}) %collective-permute-start.10) | collective-permute-done | bytes 8224 | tf_op jit(solution)/shard_map/ppermute | solution.py:351
  33.7 0.3 collective-permute-done.9.refs_7_
  34.0 0.6 shard_map.91
  34.6 1.6 %collective-permute-start.11 = (f32[32,128]{1,0:T(8,128)S(1)}, f32[32,128]{1,0:T(8,128)S(1)}, u32[]{:S(2)}, u32[]{:S(2)}) collective-permute-start(f32[32,128]{1,0:T(8,128)S(1)} %get-tuple-element.63), channel_id=1, source_target_pairs={{0,7},{1,6},{2,5},{3,4},{4,3},{5,2},{6,1},{7,0},{8,15},{9,14},{10,... | collective-permute-start | bytes 49160 | tf_op jit(solution)/shard_map/ppermute | solution.py:351
  36.2 1.3 %collective-permute-start.12 = (f32[24,128]{1,0:T(8,128)S(1)}, f32[24,128]{1,0:T(8,128)S(1)}, u32[]{:S(2)}, u32[]{:S(2)}) collective-permute-start(f32[24,128]{1,0:T(8,128)S(1)} %get-tuple-element.64), channel_id=1, source_target_pairs={{0,4},{1,5},{2,6},{3,7},{4,0},{5,1},{6,2},{7,3},{8,12},{9,13},{10,... | collective-permute-start | bytes 36872 | tf_op jit(solution)/shard_map/ppermute | solution.py:351
  37.5 1.0 %collective-permute-start.13 = (f32[16,128]{1,0:T(8,128)S(1)}, f32[16,128]{1,0:T(8,128)S(1)}, u32[]{:S(2)}, u32[]{:S(2)}) collective-permute-start(f32[16,128]{1,0:T(8,128)S(1)} %get-tuple-element.62.refs_0_), channel_id=1, source_target_pairs={{0,3},{1,2},{2,1},{3,0},{4,7},{5,6},{6,5},{7,4},{8,11},{9,10},{10,... | collective-permute-start | bytes 24584 | tf_op jit(solution)/shard_map/ppermute | solution.py:351
  38.5 2.1 %collective-permute-done.13.refs_3_ = f32[16,128]{1,0:T(8,128)S(1)} collective-permute-done((f32[16,128]{1,0:T(8,128)S(1)}, f32[16,128]{1,0:T(8,128)S(1)}, u32[]{:S(2)}, u32[]{:S(2)}) %collective-permute-start.13) | collective-permute-done | bytes 8224 | tf_op jit(solution)/shard_map/ppermute | solution.py:351
  40.6 0.2 collective-permute-done.12.refs_2_
  40.8 0.1 shard_map.92.topics_ref
  40.9 0.0 collective-permute-start.15
  40.9 0.6 shard_map.93.refs_1_
  41.5 0.6 collective-permute-done.15.topics_ref
  42.1 0.6 shard_map.94
  42.7 2.6 %collective-permute-start.16 = (f32[64,512]{1,0:T(8,128)S(1)}, f32[64,512]{1,0:T(8,128)S(1)}, u32[]{:S(2)}, u32[]{:S(2)}) collective-permute-start(f32[64,512]{1,0:T(8,128)S(1)} %get-tuple-element.90), channel_id=1, source_target_pairs={{0,24},{8,16},{16,8},{24,0},{1,25},{9,17},{17,9},{25,1},{2,26},{10... | collective-permute-start | bytes 393224 | tf_op jit(solution)/shard_map/ppermute | solution.py:365
  45.3 0.5 collective-permute-start.17
  45.8 0.5 collective-permute-start.18
  46.3 1.4 %collective-permute-start.19 = (f32[4,4224]{1,0:T(4,128)S(1)}, f32[4,4224]{1,0:T(4,128)S(1)}, u32[]{:S(2)}, u32[]{:S(2)}) collective-permute-start(f32[4,4224]{1,0:T(4,128)S(1)} %get-tuple-element.72), channel_id=1, source_target_pairs={{0,4},{1,5},{2,6},{3,7},{4,0},{5,1},{6,2},{7,3},{8,12},{9,13},{10,... | collective-permute-start | bytes 202760 | tf_op jit(solution)/shard_map/ppermute | solution.py:351
  47.7 4.5 %collective-permute-done.19.refs_4_.refs_6_.refs_2_ = f32[4,4224]{1,0:T(4,128)S(1)} collective-permute-done((f32[4,4224]{1,0:T(4,128)S(1)}, f32[4,4224]{1,0:T(4,128)S(1)}, u32[]{:S(2)}, u32[]{:S(2)}) %collective-permute-start.19) | collective-permute-done | bytes 67616 | tf_op jit(solution)/shard_map/ppermute | solution.py:351
  52.2 0.1 shard_map.95.refs_0_
  52.3 2.6 %collective-permute-start.20 = (f32[64,512]{1,0:T(8,128)S(1)}, f32[64,512]{1,0:T(8,128)S(1)}, u32[]{:S(2)}, u32[]{:S(2)}) collective-permute-start(f32[64,512]{1,0:T(8,128)S(1)} %shard_map.95.refs_0_), channel_id=1, source_target_pairs={{0,24},{8,16},{16,8},{24,0},{1,25},{9,17},{17,9},{25,1},{2,26},{10... | collective-permute-start | bytes 393224 | tf_op jit(solution)/shard_map/ppermute | solution.py:365
  54.9 0.5 collective-permute-start.24
  55.4 0.5 collective-permute-start.26
  55.8 0.1 collective-permute-start.21
  56.0 1.4 %collective-permute-start.22 = (f32[64,512]{1,0:T(8,128)S(1)}, f32[64,512]{1,0:T(8,128)S(1)}, u32[]{:S(2)}, u32[]{:S(2)}) collective-permute-start(f32[64,512]{1,0:T(8,128)S(1)} %shard_map.95.refs_0_), channel_id=1, source_target_pairs={{0,1},{1,0},{2,3},{3,2},{4,5},{5,4},{6,7},{7,6},{8,9},{9,8},{10,11... | collective-permute-start | bytes 393224 | tf_op jit(solution)/shard_map/ppermute | solution.py:362
  57.4 4.0 %collective-permute-done.21.refs_7_.refs_3_ = f32[4,4224]{1,0:T(4,128)S(1)} collective-permute-done((f32[4,4224]{1,0:T(4,128)S(1)}, f32[4,4224]{1,0:T(4,128)S(1)}, u32[]{:S(2)}, u32[]{:S(2)}) %collective-permute-start.21) | collective-permute-done | bytes 67616 | tf_op jit(solution)/shard_map/ppermute | solution.py:351
  61.4 0.5 collective-permute-start.25
  61.9 0.1 collective-permute-start.27
  62.0 0.9 %shard_map.96 = (bf16[128,2048]{1,0:T(8,128)(2,1)S(1)}, bf16[2048,128]{1,0:T(8,128)(2,1)S(1)}, f32[16,128]{1,0:T(8,128)S(1)}) custom-call(f32[64,512]{1,0:T(8,128)S(1)} %shard_map.95.refs_0_, f32[64,512]{1,0:T(8,128)S(1)} %collective-permute-done.20.refs_1_, f32[64,512]{1,0:T(8,128)S(1)} %collective-permute-done.24.refs_2_, ...), custom_call_target="tpu_custom_call" | custom-call | flops 33554432 | bytes 2097152 | tf_op jit(solution)/shard_map/pallas_call | solution.py:37
  62.9 0.1 collective-permute-done.25.refs_2_
  63.0 0.3 collective-permute-done.27.refs_3_
  63.3 0.9 %shard_map.97 = (bf16[128,2048]{1,0:T(8,128)(2,1)S(1)}, bf16[2048,128]{1,0:T(8,128)(2,1)S(1)}, f32[16,128]{1,0:T(8,128)S(1)}) custom-call(f32[64,512]{1,0:T(8,128)S(1)} %collective-permute-done.22.refs_0_, f32[64,512]{1,0:T(8,128)S(1)} %collective-permute-done.23.refs_1_, f32[64,512]{1,0:T(8,128)S(1)} %collective-permute-done.25.refs_2_, ...), custom_call_target="tpu_custom_call" | custom-call | flops 33554432 | bytes 2097152 | tf_op jit(solution)/shard_map/pallas_call | solution.py:37
  64.2 1.3 %collective-permute-start.28 = (f32[16,128]{1,0:T(8,128)S(1)}, f32[16,128]{1,0:T(8,128)S(1)}, u32[]{:S(2)}, u32[]{:S(2)}) collective-permute-start(f32[16,128]{1,0:T(8,128)S(1)} %get-tuple-element.78.refs_4_), channel_id=1, source_target_pairs={{0,7},{1,6},{2,5},{3,4},{4,3},{5,2},{6,1},{7,0},{8,15},{9,14},{10,... | collective-permute-start | bytes 24584 | tf_op jit(solution)/shard_map/ppermute | solution.py:351
  65.4 0.8 %collective-permute-start.29 = (f32[16,128]{1,0:T(8,128)S(1)}, f32[16,128]{1,0:T(8,128)S(1)}, u32[]{:S(2)}, u32[]{:S(2)}) collective-permute-start(f32[16,128]{1,0:T(8,128)S(1)} %get-tuple-element.78.refs_4_), channel_id=1, source_target_pairs={{0,4},{1,5},{2,6},{3,7},{4,0},{5,1},{6,2},{7,3},{8,12},{9,13},{10,... | collective-permute-start | bytes 24584 | tf_op jit(solution)/shard_map/ppermute | solution.py:351
  66.2 1.8 %collective-permute-start.30 = (f32[16,128]{1,0:T(8,128)S(1)}, f32[16,128]{1,0:T(8,128)S(1)}, u32[]{:S(2)}, u32[]{:S(2)}) collective-permute-start(f32[16,128]{1,0:T(8,128)S(1)} %get-tuple-element.78.refs_4_), channel_id=1, source_target_pairs={{0,3},{1,2},{2,1},{3,0},{4,7},{5,6},{6,5},{7,4},{8,11},{9,10},{10,... | collective-permute-start | bytes 24584 | tf_op jit(solution)/shard_map/ppermute | solution.py:351
  68.0 1.0 %collective-permute-done.28.refs_5_ = f32[16,128]{1,0:T(8,128)S(1)} collective-permute-done((f32[16,128]{1,0:T(8,128)S(1)}, f32[16,128]{1,0:T(8,128)S(1)}, u32[]{:S(2)}, u32[]{:S(2)}) %collective-permute-start.28) | collective-permute-done | bytes 8224 | tf_op jit(solution)/shard_map/ppermute | solution.py:351
  69.0 0.9 %collective-permute-done.29.refs_6_ = f32[16,128]{1,0:T(8,128)S(1)} collective-permute-done((f32[16,128]{1,0:T(8,128)S(1)}, f32[16,128]{1,0:T(8,128)S(1)}, u32[]{:S(2)}, u32[]{:S(2)}) %collective-permute-start.29) | collective-permute-done | bytes 8224 | tf_op jit(solution)/shard_map/ppermute | solution.py:351
  70.0 0.7 shard_map.98
  70.7 1.2 %collective-permute-start.31 = (f32[4,128]{1,0:T(4,128)S(1)}, f32[4,128]{1,0:T(4,128)S(1)}, u32[]{:S(2)}, u32[]{:S(2)}) collective-permute-start(f32[4,128]{1,0:T(4,128)S(1)} %get-tuple-element.85), channel_id=1, source_target_pairs={{0,7},{1,6},{2,5},{3,4},{4,3},{5,2},{6,1},{7,0},{8,15},{9,14},{10,... | collective-permute-start | bytes 6152 | tf_op jit(solution)/shard_map/ppermute | solution.py:351
  71.9 1.4 %collective-permute-start.32 = (f32[4,128]{1,0:T(4,128)S(1)}, f32[4,128]{1,0:T(4,128)S(1)}, u32[]{:S(2)}, u32[]{:S(2)}) collective-permute-start(f32[4,128]{1,0:T(4,128)S(1)} %get-tuple-element.86), channel_id=1, source_target_pairs={{0,4},{1,5},{2,6},{3,7},{4,0},{5,1},{6,2},{7,3},{8,12},{9,13},{10,... | collective-permute-start | bytes 6152 | tf_op jit(solution)/shard_map/ppermute | solution.py:351
  73.3 1.2 %collective-permute-start.33 = (f32[4,128]{1,0:T(4,128)S(1)}, f32[4,128]{1,0:T(4,128)S(1)}, u32[]{:S(2)}, u32[]{:S(2)}) collective-permute-start(f32[4,128]{1,0:T(4,128)S(1)} %get-tuple-element.87), channel_id=1, source_target_pairs={{0,3},{1,2},{2,1},{3,0},{4,7},{5,6},{6,5},{7,4},{8,11},{9,10},{10,... | collective-permute-start | bytes 6152 | tf_op jit(solution)/shard_map/ppermute | solution.py:351
  74.5 0.7 copy.9
  75.2 0.3 collective-permute-done.31.refs_1_
  75.5 0.9 %collective-permute-done.32.refs_2_ = f32[4,128]{1,0:T(4,128)S(1)} collective-permute-done((f32[4,128]{1,0:T(4,128)S(1)}, f32[4,128]{1,0:T(4,128)S(1)}, u32[]{:S(2)}, u32[]{:S(2)}) %collective-permute-start.32) | collective-permute-done | bytes 2080 | tf_op jit(solution)/shard_map/ppermute | solution.py:351
  76.4 0.6 shard_map.99
  (28 shorter events, 0.1 us)
Async XLA Ops:
  0.6 10.0 %copy-start = (f32[1,2048,64]{1,2,0:T(8,128)S(1)}, f32[1,2048,64]{1,2,0:T(8,128)}, u32[]{:S(2)}) copy-start(f32[1,2048,64]{1,2,0:T(8,128)} %param.10) | copy-start | bytes 1572868
  0.6 10.0 %collective-permute-start = (f32[64,2048]{1,0:T(8,128)}, f32[64,2048]{1,0:T(8,128)S(1)}, u32[]{:S(2)}, u32[]{:S(2)}) collective-permute-start(f32[64,2048]{1,0:T(8,128)} %bitcast.10), channel_id=1, source_target_pairs={{0,1},{1,0},{2,3},{3,2},{4,5},{5,4},{6,7},{7,6},{8,9},{9,8},{10,11... | collective-permute-start | bytes 1572872 | tf_op jit(solution)/shard_map/ppermute | solution.py:362
  3.0 5.2 %copy-start.2 = (f32[4,64]{1,0:T(4,128)S(1)}, f32[4,64]{1,0:T(4,128)}, u32[]{:S(2)}) copy-start(f32[4,64]{1,0:T(4,128)} %topics_ref.1) | copy-start | bytes 3076
  3.0 15.5 %collective-permute-start.1 = (f32[8,4224]{1,0:T(8,128)S(1)}, f32[8,4224]{1,0:T(8,128)S(1)}, u32[]{:S(2)}, u32[]{:S(2)}) collective-permute-start(f32[8,4224]{1,0:T(8,128)S(1)} %get-tuple-element.49), channel_id=1, source_target_pairs={{0,7},{1,6},{2,5},{3,4},{4,3},{5,2},{6,1},{7,0},{8,15},{9,14},{10,... | collective-permute-start | bytes 405512 | tf_op jit(solution)/shard_map/ppermute | solution.py:351
  7.8 11.9 %collective-permute-start.2 = (f32[8,4224]{1,0:T(8,128)S(1)}, f32[8,4224]{1,0:T(8,128)S(1)}, u32[]{:S(2)}, u32[]{:S(2)}) collective-permute-start(f32[8,4224]{1,0:T(8,128)S(1)} %get-tuple-element.50), channel_id=1, source_target_pairs={{0,4},{1,5},{2,6},{3,7},{4,0},{5,1},{6,2},{7,3},{8,12},{9,13},{10,... | collective-permute-start | bytes 405512 | tf_op jit(solution)/shard_map/ppermute | solution.py:351
  7.8 11.9 %collective-permute-start.3 = (f32[8,4224]{1,0:T(8,128)S(1)}, f32[8,4224]{1,0:T(8,128)S(1)}, u32[]{:S(2)}, u32[]{:S(2)}) collective-permute-start(f32[8,4224]{1,0:T(8,128)S(1)} %get-tuple-element.51), channel_id=1, source_target_pairs={{0,3},{1,2},{2,1},{3,0},{4,7},{5,6},{6,5},{7,4},{8,11},{9,10},{10,... | collective-permute-start | bytes 405512 | tf_op jit(solution)/shard_map/ppermute | solution.py:351
  8.2 1.0 %copy-start.1 = (s32[4,16384]{1,0:T(4,128)S(1)}, s32[4,16384]{1,0:T(4,128)}, u32[]{:S(2)}) copy-start(s32[4,16384]{1,0:T(4,128)} %counts_ref.1) | copy-start | bytes 786436
  9.2 1.4 %copy-start.3 = (s32[1,64]{1,0:T(1,128)S(1)}, s32[1,64]{1,0:T(1,128)}, u32[]{:S(2)}) copy-start(s32[1,64]{1,0:T(1,128)} %perm_ref.1) | copy-start | bytes 772
  9.2 9.3 %collective-permute-start.4 = (f32[4,4224]{1,0:T(4,128)S(1)}, f32[4,4224]{1,0:T(4,128)S(1)}, u32[]{:S(2)}, u32[]{:S(2)}) collective-permute-start(f32[4,4224]{1,0:T(4,128)S(1)} %get-tuple-element.53), channel_id=1, source_target_pairs={{0,3},{1,2},{2,1},{3,0},{4,7},{5,6},{6,5},{7,4},{8,11},{9,10},{10,... | collective-permute-start | bytes 202760 | tf_op jit(solution)/shard_map/ppermute | solution.py:351
  20.3 20.5 %collective-permute-start.14 = (f32[32,2048]{1,0:T(8,128)S(1)}, f32[32,2048]{1,0:T(8,128)S(1)}, u32[]{:S(2)}, u32[]{:S(2)}) collective-permute-start(f32[32,2048]{1,0:T(8,128)S(1)} %get-tuple-element.65), channel_id=1, source_target_pairs={{0,1},{1,0},{2,3},{3,2},{4,5},{5,4},{6,7},{7,6},{8,9},{9,8},{10,11... | collective-permute-start | bytes 786440 | tf_op jit(solution)/shard_map/ppermute | solution.py:362
  20.3 5.0 %collective-permute-start.5 = (f32[24,128]{1,0:T(8,128)S(1)}, f32[24,128]{1,0:T(8,128)S(1)}, u32[]{:S(2)}, u32[]{:S(2)}) collective-permute-start(f32[24,128]{1,0:T(8,128)S(1)} %get-tuple-element.55.refs_4_), channel_id=1, source_target_pairs={{0,7},{1,6},{2,5},{3,4},{4,3},{5,2},{6,1},{7,0},{8,15},{9,14},{10,... | collective-permute-start | bytes 36872 | tf_op jit(solution)/shard_map/ppermute | solution.py:351
  23.4 4.6 %collective-permute-start.6 = (f32[24,128]{1,0:T(8,128)S(1)}, f32[24,128]{1,0:T(8,128)S(1)}, u32[]{:S(2)}, u32[]{:S(2)}) collective-permute-start(f32[24,128]{1,0:T(8,128)S(1)} %get-tuple-element.55.refs_4_), channel_id=1, source_target_pairs={{0,4},{1,5},{2,6},{3,7},{4,0},{5,1},{6,2},{7,3},{8,12},{9,13},{10,... | collective-permute-start | bytes 36872 | tf_op jit(solution)/shard_map/ppermute | solution.py:351
  23.4 4.6 %collective-permute-start.7 = (f32[24,128]{1,0:T(8,128)S(1)}, f32[24,128]{1,0:T(8,128)S(1)}, u32[]{:S(2)}, u32[]{:S(2)}) collective-permute-start(f32[24,128]{1,0:T(8,128)S(1)} %get-tuple-element.55.refs_4_), channel_id=1, source_target_pairs={{0,3},{1,2},{2,1},{3,0},{4,7},{5,6},{6,5},{7,4},{8,11},{9,10},{10,... | collective-permute-start | bytes 36872 | tf_op jit(solution)/shard_map/ppermute | solution.py:351
  28.5 5.5 %collective-permute-start.8 = (f32[32,128]{1,0:T(8,128)S(1)}, f32[32,128]{1,0:T(8,128)S(1)}, u32[]{:S(2)}, u32[]{:S(2)}) collective-permute-start(f32[32,128]{1,0:T(8,128)S(1)} %get-tuple-element.59), channel_id=1, source_target_pairs={{0,7},{1,6},{2,5},{3,4},{4,3},{5,2},{6,1},{7,0},{8,15},{9,14},{10,... | collective-permute-start | bytes 49160 | tf_op jit(solution)/shard_map/ppermute | solution.py:351
  29.4 4.6 %collective-permute-start.9 = (f32[24,128]{1,0:T(8,128)S(1)}, f32[24,128]{1,0:T(8,128)S(1)}, u32[]{:S(2)}, u32[]{:S(2)}) collective-permute-start(f32[24,128]{1,0:T(8,128)S(1)} %get-tuple-element.60), channel_id=1, source_target_pairs={{0,4},{1,5},{2,6},{3,7},{4,0},{5,1},{6,2},{7,3},{8,12},{9,13},{10,... | collective-permute-start | bytes 36872 | tf_op jit(solution)/shard_map/ppermute | solution.py:351
  30.2 3.6 %collective-permute-start.10 = (f32[16,128]{1,0:T(8,128)S(1)}, f32[16,128]{1,0:T(8,128)S(1)}, u32[]{:S(2)}, u32[]{:S(2)}) collective-permute-start(f32[16,128]{1,0:T(8,128)S(1)} %get-tuple-element.58.refs_5_), channel_id=1, source_target_pairs={{0,3},{1,2},{2,1},{3,0},{4,7},{5,6},{6,5},{7,4},{8,11},{9,10},{10,... | collective-permute-start | bytes 24584 | tf_op jit(solution)/shard_map/ppermute | solution.py:351
  34.6 6.2 %collective-permute-start.11 = (f32[32,128]{1,0:T(8,128)S(1)}, f32[32,128]{1,0:T(8,128)S(1)}, u32[]{:S(2)}, u32[]{:S(2)}) collective-permute-start(f32[32,128]{1,0:T(8,128)S(1)} %get-tuple-element.63), channel_id=1, source_target_pairs={{0,7},{1,6},{2,5},{3,4},{4,3},{5,2},{6,1},{7,0},{8,15},{9,14},{10,... | collective-permute-start | bytes 49160 | tf_op jit(solution)/shard_map/ppermute | solution.py:351
  36.2 4.6 %collective-permute-start.12 = (f32[24,128]{1,0:T(8,128)S(1)}, f32[24,128]{1,0:T(8,128)S(1)}, u32[]{:S(2)}, u32[]{:S(2)}) collective-permute-start(f32[24,128]{1,0:T(8,128)S(1)} %get-tuple-element.64), channel_id=1, source_target_pairs={{0,4},{1,5},{2,6},{3,7},{4,0},{5,1},{6,2},{7,3},{8,12},{9,13},{10,... | collective-permute-start | bytes 36872 | tf_op jit(solution)/shard_map/ppermute | solution.py:351
  37.5 3.1 %collective-permute-start.13 = (f32[16,128]{1,0:T(8,128)S(1)}, f32[16,128]{1,0:T(8,128)S(1)}, u32[]{:S(2)}, u32[]{:S(2)}) collective-permute-start(f32[16,128]{1,0:T(8,128)S(1)} %get-tuple-element.62.refs_0_), channel_id=1, source_target_pairs={{0,3},{1,2},{2,1},{3,0},{4,7},{5,6},{6,5},{7,4},{8,11},{9,10},{10,... | collective-permute-start | bytes 24584 | tf_op jit(solution)/shard_map/ppermute | solution.py:351
  40.9 1.2 %collective-permute-start.15 = (f32[32,128]{1,0:T(8,128)S(1)}, f32[32,128]{1,0:T(8,128)S(1)}, u32[]{:S(2)}, u32[]{:S(2)}) collective-permute-start(f32[32,128]{1,0:T(8,128)S(1)} %shard_map.92.topics_ref), channel_id=1, source_target_pairs={{0,1},{1,0},{2,3},{3,2},{4,5},{5,4},{6,7},{7,6},{8,9},{9,8},{10,11... | collective-permute-start | bytes 49160 | tf_op jit(solution)/shard_map/ppermute | solution.py:362
  42.7 9.5 %collective-permute-start.16 = (f32[64,512]{1,0:T(8,128)S(1)}, f32[64,512]{1,0:T(8,128)S(1)}, u32[]{:S(2)}, u32[]{:S(2)}) collective-permute-start(f32[64,512]{1,0:T(8,128)S(1)} %get-tuple-element.90), channel_id=1, source_target_pairs={{0,24},{8,16},{16,8},{24,0},{1,25},{9,17},{17,9},{25,1},{2,26},{10... | collective-permute-start | bytes 393224 | tf_op jit(solution)/shard_map/ppermute | solution.py:365
  45.3 6.9 %collective-permute-start.17 = (f32[64,512]{1,0:T(8,128)S(1)}, f32[64,512]{1,0:T(8,128)S(1)}, u32[]{:S(2)}, u32[]{:S(2)}) collective-permute-start(f32[64,512]{1,0:T(8,128)S(1)} %get-tuple-element.89), channel_id=1, source_target_pairs={{0,16},{8,24},{16,0},{24,8},{1,17},{9,25},{17,1},{25,9},{2,18},{10... | collective-permute-start | bytes 393224 | tf_op jit(solution)/shard_map/ppermute | solution.py:365
  45.8 6.4 %collective-permute-start.18 = (f32[64,512]{1,0:T(8,128)S(1)}, f32[64,512]{1,0:T(8,128)S(1)}, u32[]{:S(2)}, u32[]{:S(2)}) collective-permute-start(f32[64,512]{1,0:T(8,128)S(1)} %get-tuple-element.88), channel_id=1, source_target_pairs={{0,8},{8,0},{16,24},{24,16},{1,9},{9,1},{17,25},{25,17},{2,10},{10... | collective-permute-start | bytes 393224 | tf_op jit(solution)/shard_map/ppermute | solution.py:365
  46.3 5.9 %collective-permute-start.19 = (f32[4,4224]{1,0:T(4,128)S(1)}, f32[4,4224]{1,0:T(4,128)S(1)}, u32[]{:S(2)}, u32[]{:S(2)}) collective-permute-start(f32[4,4224]{1,0:T(4,128)S(1)} %get-tuple-element.72), channel_id=1, source_target_pairs={{0,4},{1,5},{2,6},{3,7},{4,0},{5,1},{6,2},{7,3},{8,12},{9,13},{10,... | collective-permute-start | bytes 202760 | tf_op jit(solution)/shard_map/ppermute | solution.py:351
  52.3 9.1 %collective-permute-start.20 = (f32[64,512]{1,0:T(8,128)S(1)}, f32[64,512]{1,0:T(8,128)S(1)}, u32[]{:S(2)}, u32[]{:S(2)}) collective-permute-start(f32[64,512]{1,0:T(8,128)S(1)} %shard_map.95.refs_0_), channel_id=1, source_target_pairs={{0,24},{8,16},{16,8},{24,0},{1,25},{9,17},{17,9},{25,1},{2,26},{10... | collective-permute-start | bytes 393224 | tf_op jit(solution)/shard_map/ppermute | solution.py:365
  54.9 6.6 %collective-permute-start.24 = (f32[64,512]{1,0:T(8,128)S(1)}, f32[64,512]{1,0:T(8,128)S(1)}, u32[]{:S(2)}, u32[]{:S(2)}) collective-permute-start(f32[64,512]{1,0:T(8,128)S(1)} %shard_map.95.refs_0_), channel_id=1, source_target_pairs={{0,16},{8,24},{16,0},{24,8},{1,17},{9,25},{17,1},{25,9},{2,18},{10... | collective-permute-start | bytes 393224 | tf_op jit(solution)/shard_map/ppermute | solution.py:365
  55.4 6.6 %collective-permute-start.26 = (f32[64,512]{1,0:T(8,128)S(1)}, f32[64,512]{1,0:T(8,128)S(1)}, u32[]{:S(2)}, u32[]{:S(2)}) collective-permute-start(f32[64,512]{1,0:T(8,128)S(1)} %shard_map.95.refs_0_), channel_id=1, source_target_pairs={{0,8},{8,0},{16,24},{24,16},{1,9},{9,1},{17,25},{25,17},{2,10},{10... | collective-permute-start | bytes 393224 | tf_op jit(solution)/shard_map/ppermute | solution.py:365
  55.8 5.6 %collective-permute-start.21 = (f32[4,4224]{1,0:T(4,128)S(1)}, f32[4,4224]{1,0:T(4,128)S(1)}, u32[]{:S(2)}, u32[]{:S(2)}) collective-permute-start(f32[4,4224]{1,0:T(4,128)S(1)} %get-tuple-element.74), channel_id=1, source_target_pairs={{0,7},{1,6},{2,5},{3,4},{4,3},{5,2},{6,1},{7,0},{8,15},{9,14},{10,... | collective-permute-start | bytes 202760 | tf_op jit(solution)/shard_map/ppermute | solution.py:351
  56.0 6.9 %collective-permute-start.22 = (f32[64,512]{1,0:T(8,128)S(1)}, f32[64,512]{1,0:T(8,128)S(1)}, u32[]{:S(2)}, u32[]{:S(2)}) collective-permute-start(f32[64,512]{1,0:T(8,128)S(1)} %shard_map.95.refs_0_), channel_id=1, source_target_pairs={{0,1},{1,0},{2,3},{3,2},{4,5},{5,4},{6,7},{7,6},{8,9},{9,8},{10,11... | collective-permute-start | bytes 393224 | tf_op jit(solution)/shard_map/ppermute | solution.py:362
  61.4 1.5 %collective-permute-start.23 = (f32[64,512]{1,0:T(8,128)S(1)}, f32[64,512]{1,0:T(8,128)S(1)}, u32[]{:S(2)}, u32[]{:S(2)}) collective-permute-start(f32[64,512]{1,0:T(8,128)S(1)} %collective-permute-done.20.refs_1_), channel_id=1, source_target_pairs={{0,1},{1,0},{2,3},{3,2},{4,5},{5,4},{6,7},{7,6},{8,9},{9,8},{10,11... | collective-permute-start | bytes 393224 | tf_op jit(solution)/shard_map/ppermute | solution.py:362
  61.4 1.5 %collective-permute-start.25 = (f32[64,512]{1,0:T(8,128)S(1)}, f32[64,512]{1,0:T(8,128)S(1)}, u32[]{:S(2)}, u32[]{:S(2)}) collective-permute-start(f32[64,512]{1,0:T(8,128)S(1)} %collective-permute-done.24.refs_2_), channel_id=1, source_target_pairs={{0,1},{1,0},{2,3},{3,2},{4,5},{5,4},{6,7},{7,6},{8,9},{9,8},{10,11... | collective-permute-start | bytes 393224 | tf_op jit(solution)/shard_map/ppermute | solution.py:362
  61.9 1.3 %collective-permute-start.27 = (f32[64,512]{1,0:T(8,128)S(1)}, f32[64,512]{1,0:T(8,128)S(1)}, u32[]{:S(2)}, u32[]{:S(2)}) collective-permute-start(f32[64,512]{1,0:T(8,128)S(1)} %collective-permute-done.26.refs_3_), channel_id=1, source_target_pairs={{0,1},{1,0},{2,3},{3,2},{4,5},{5,4},{6,7},{7,6},{8,9},{9,8},{10,11... | collective-permute-start | bytes 393224 | tf_op jit(solution)/shard_map/ppermute | solution.py:362
  64.2 4.9 %collective-permute-start.28 = (f32[16,128]{1,0:T(8,128)S(1)}, f32[16,128]{1,0:T(8,128)S(1)}, u32[]{:S(2)}, u32[]{:S(2)}) collective-permute-start(f32[16,128]{1,0:T(8,128)S(1)} %get-tuple-element.78.refs_4_), channel_id=1, source_target_pairs={{0,7},{1,6},{2,5},{3,4},{4,3},{5,2},{6,1},{7,0},{8,15},{9,14},{10,... | collective-permute-start | bytes 24584 | tf_op jit(solution)/shard_map/ppermute | solution.py:351
  65.4 4.6 %collective-permute-start.29 = (f32[16,128]{1,0:T(8,128)S(1)}, f32[16,128]{1,0:T(8,128)S(1)}, u32[]{:S(2)}, u32[]{:S(2)}) collective-permute-start(f32[16,128]{1,0:T(8,128)S(1)} %get-tuple-element.78.refs_4_), channel_id=1, source_target_pairs={{0,4},{1,5},{2,6},{3,7},{4,0},{5,1},{6,2},{7,3},{8,12},{9,13},{10,... | collective-permute-start | bytes 24584 | tf_op jit(solution)/shard_map/ppermute | solution.py:351
  66.2 3.8 %collective-permute-start.30 = (f32[16,128]{1,0:T(8,128)S(1)}, f32[16,128]{1,0:T(8,128)S(1)}, u32[]{:S(2)}, u32[]{:S(2)}) collective-permute-start(f32[16,128]{1,0:T(8,128)S(1)} %get-tuple-element.78.refs_4_), channel_id=1, source_target_pairs={{0,3},{1,2},{2,1},{3,0},{4,7},{5,6},{6,5},{7,4},{8,11},{9,10},{10,... | collective-permute-start | bytes 24584 | tf_op jit(solution)/shard_map/ppermute | solution.py:351
  70.7 4.8 %collective-permute-start.31 = (f32[4,128]{1,0:T(4,128)S(1)}, f32[4,128]{1,0:T(4,128)S(1)}, u32[]{:S(2)}, u32[]{:S(2)}) collective-permute-start(f32[4,128]{1,0:T(4,128)S(1)} %get-tuple-element.85), channel_id=1, source_target_pairs={{0,7},{1,6},{2,5},{3,4},{4,3},{5,2},{6,1},{7,0},{8,15},{9,14},{10,... | collective-permute-start | bytes 6152 | tf_op jit(solution)/shard_map/ppermute | solution.py:351
  71.9 4.5 %collective-permute-start.32 = (f32[4,128]{1,0:T(4,128)S(1)}, f32[4,128]{1,0:T(4,128)S(1)}, u32[]{:S(2)}, u32[]{:S(2)}) collective-permute-start(f32[4,128]{1,0:T(4,128)S(1)} %get-tuple-element.86), channel_id=1, source_target_pairs={{0,4},{1,5},{2,6},{3,7},{4,0},{5,1},{6,2},{7,3},{8,12},{9,13},{10,... | collective-permute-start | bytes 6152 | tf_op jit(solution)/shard_map/ppermute | solution.py:351
  73.3 3.1 %collective-permute-start.33 = (f32[4,128]{1,0:T(4,128)S(1)}, f32[4,128]{1,0:T(4,128)S(1)}, u32[]{:S(2)}, u32[]{:S(2)}) collective-permute-start(f32[4,128]{1,0:T(4,128)S(1)} %get-tuple-element.87), channel_id=1, source_target_pairs={{0,3},{1,2},{2,1},{3,0},{4,7},{5,6},{6,5},{7,4},{8,11},{9,10},{10,... | collective-permute-start | bytes 6152 | tf_op jit(solution)/shard_map/ppermute | solution.py:351

commit v3 on v2

--- a/solution.py
+++ b/solution.py
@@ -66,14 +66,15 @@
     return [(at_chip ^ step) * cores + (at_core ^ ((step + half) % cores)) for half in range(cores)]
 
 
-def spread_kernel(chips, cores, own_words, mask_hbm, topics_hbm, counts_hbm, *refs):
-    out_refs, (mask_ref, topics_ref, counts_ref, small_sems, in_sems) = (
+def spread_kernel(chips, cores, own_words, mask_hbm, topics_hbm, perm_hbm, counts_hbm, *refs):
+    out_refs, (mask_ref, topics_ref, perm_ref, counts_ref, small_sems, in_sems) = (
         refs[:chips],
         refs[chips:],
     )
     small = [
         pltpu.make_async_copy(mask_hbm, mask_ref, small_sems.at[0]),
         pltpu.make_async_copy(topics_hbm, topics_ref, small_sems.at[1]),
+        pltpu.make_async_copy(perm_hbm, perm_ref, small_sems.at[2]),
     ]
     for copy in small:
         copy.start()
@@ -97,6 +98,11 @@
     for copy in small:
         copy.wait()
     occupied = jnp.maximum(mask_ref[...], forced).astype(jnp.float32)
+    topic_count = topics_ref.shape[1]
+    onehot = lax.broadcasted_iota(jnp.int32, (topic_count, 2 * topic_count), 0) == jnp.concatenate(
+        [perm_ref[...]] * 2, axis=1
+    )
+    topics = moved_columns(topics_ref[...], onehot.astype(jnp.float32))
     for step in steps:
         for half, block in enumerate(blocks_of(chips, cores, step)):
             near = pltpu.roll(occupied, lax.rem(tiles - block * own_tiles, tiles), 1)
@@ -105,7 +111,7 @@
                 at = slice(half * own_words + tile * width, half * own_words + (tile + 1) * width)
                 picked = counts_ref[step, :, at].astype(jnp.float32)
                 out_refs[step][:, at] = picked * near[:, tile : tile + 1]
-        out_refs[step][:, cores * own_words :] = jnp.concatenate([topics_ref[...]] * 2, axis=1)
+        out_refs[step][:, cores * own_words :] = topics
 
 
 def base_kernel(chips, cores, counts_ref, topics_ref, *out_refs):
@@ -129,28 +135,26 @@
 
 def dictionary_kernel(half_count, perm_ref, *refs):
     topics, words = refs[0].shape
-    wide_ref, tall_ref, total_ref, aligned_ref, onehot_ref = refs[half_count:]
-    onehot = (
-        lax.broadcasted_iota(jnp.int32, (topics, topics), 0) == perm_ref[...]
-    ).astype(jnp.float32)
-    onehot_ref[...] = onehot
-    total = jnp.zeros((1, topics), jnp.float32)
+    wide_ref, tall_ref, total_ref, own_ref = refs[half_count:]
+    turned_onehot = (
+        (lax.broadcasted_iota(jnp.int32, (topics, topics), 0) == perm_ref[...]).astype(jnp.float32).T
+    )
+    total = jnp.zeros((1, 2 * topics), jnp.float32)
     for half in range(half_count):
         at = slice(half * words, (half + 1) * words)
-        full = refs[half][...]
-        high, rest = high_low(full)
+        high, rest = high_low(refs[half][...])
         mid, low = high_low(rest)
-        wide_ref[:topics, at] = high.astype(jnp.bfloat16)
-        wide_ref[topics:, at] = rest.astype(jnp.bfloat16)
+        aligned = matmul(
+            jnp.concatenate([turned_onehot] * 3, axis=1), jnp.concatenate([high, mid, low], axis=0)
+        )
         if half == 0:
-            turned = onehot.T
-            aligned_ref[...] = matmul(
-                jnp.concatenate([turned] * 3, axis=1), jnp.concatenate([high, mid, low], axis=0)
-            )
-        tall = full.T
+            own_ref[...] = aligned
+        wide = jnp.concatenate(high_low(aligned), axis=0)
+        wide_ref[:, at] = wide.astype(jnp.bfloat16)
+        tall = wide.T
         total += jnp.sum(tall, axis=0, keepdims=True)
-        tall_ref[at, :] = jnp.concatenate(high_low(tall), axis=1).astype(jnp.bfloat16)
-    total_ref[...] = jnp.concatenate([jnp.broadcast_to(total, (8, topics))] * 2, axis=1)
+        tall_ref[at, :] = tall.astype(jnp.bfloat16)
+    total_ref[...] = jnp.broadcast_to(total + turned(total), total_ref.shape)
 
 
 def recon_of(doubled, wide):
@@ -159,10 +163,12 @@
     return both[:rows] + both[rows:]
 
 
-def product_of(quotient, tall):
+def product_of(quotient, tall, ones=0):
     rows = quotient.shape[0]
-    both = matmul(jnp.concatenate(high_low(quotient), axis=0), tall)
-    both = both[:rows] + both[rows:]
+    left = [*high_low(quotient)] + [jnp.ones((ones, quotient.shape[1]), jnp.float32)] * (ones > 0)
+    both = matmul(jnp.concatenate(left, axis=0), tall)
+    both = [both[:rows] + both[rows : 2 * rows], both[2 * rows :]]
+    both = jnp.concatenate(both, axis=0) if ones else both[0]
     return both + turned(both)
 
 
@@ -206,8 +212,9 @@
             ref[rows:] = jnp.zeros((ref.shape[0] - rows, part.shape[1]), part.dtype)
 
 
-def first_kernel(chips, cores, wide_ref, tall_ref, col_part_ref, *refs):
-    payload, (topics_ref, part_ref, *half_refs) = refs[:chips][::-1], refs[-2 - cores :]
+def first_kernel(chips, cores, order, wide_ref, tall_ref, col_part_ref, *refs):
+    payload = [refs[order.index(step)] for step in range(chips)]
+    topics_ref, part_ref, *half_refs = refs[-2 - cores :]
     span = wide_ref.shape[1]
     topics = jnp.concatenate([ref[:, span:] for ref in payload], axis=0)
     topics_ref[...] = topics
@@ -238,7 +245,7 @@
 
 
 def numerator_of(topics, quotient):
-    high, low = high_low(topics.T)
+    high, low = high_low(topics.T[: topics.shape[1] // 2])
     quotient_high, quotient_low = high_low(quotient)
     return matmul(
         jnp.concatenate([high, low, high], axis=1),
@@ -252,22 +259,21 @@
     topics_ref[...] = before_ref[...] / total_ref[:1] * total
 
 
-def numerator_kernel(wide_ref, onehot_ref, topics_ref, weighted_ref, *refs):
+def numerator_kernel(wide_ref, topics_ref, weighted_ref, *refs):
     before, out_ref = refs[:-1], refs[-1]
-    topic_count, words = onehot_ref.shape[0], weighted_ref.shape[1]
-    quotient = weighted_ref[...] / recon_of(topics_ref[...], wide_ref[:, :words])
-    aligned = moved_columns(topics_ref[:, :topic_count], onehot_ref[...])
-    numerator = numerator_of(aligned, quotient)
-    load = jnp.sum(aligned.T, axis=1, keepdims=True)
+    words = weighted_ref.shape[1]
+    topics = topics_ref[...]
+    load = jnp.sum(topics.T[: topics.shape[1] // 2], axis=1, keepdims=True)
+    numerator = numerator_of(topics, weighted_ref[...] / recon_of(topics, wide_ref[:, :words]))
     if out_ref.shape[1] > words:
         out_ref[:, :words] = numerator
-        out_ref[:, words:] = jnp.broadcast_to(load, (topic_count, out_ref.shape[1] - words))
+        out_ref[:, words:] = jnp.broadcast_to(load, (load.shape[0], out_ref.shape[1] - words))
     else:
         dict_ref, *other = before
         for ref in other:
             numerator = numerator + ref[:, :words]
             load = load + ref[:, words : words + 1]
-        out_ref[...] = dict_ref[...] * numerator / load
+        out_ref[...] = dict_ref[...] / load * numerator
 
 
 def base_rows_of(refs, at):
@@ -288,17 +294,15 @@
 
     words = median_ref.shape[1]
     span = payload[0].shape[1] - part_ref.shape[1]
-    wide = jnp.concatenate(high_low(median_ref[...]), axis=0).astype(jnp.bfloat16)
+    wide = jnp.concatenate(high_low(median_ref[...]), axis=0)
+    tall = wide.T.astype(jnp.bfloat16)
+    wide = wide.astype(jnp.bfloat16)
     wide_ref[...] = wide
-    tall = jnp.concatenate(high_low(median_ref[...].T), axis=1)
-    total = jnp.sum(tall, axis=0, keepdims=True)
-    total = jnp.broadcast_to(total + turned(total), (8, total.shape[1]))
-    tall = tall.astype(jnp.bfloat16)
     tall_ref[...] = tall
     weighted = base_rows_of(payload, slice(half * words, (half + 1) * words))
     refit = base_rows_of(payload, slice(span, None))
-    part = pack(product_of(weighted / recon_of(refit, wide), tall))
-    both = jnp.concatenate([part, total], axis=0)
+    both = product_of(weighted / recon_of(refit, wide), tall, ones=8)
+    both = jnp.concatenate([pack(both[:-8]), both[-8:]], axis=0)
     part_ref[...] = both + before[0][...] if before else both
 
 
@@ -367,18 +371,19 @@
     sent = pl.pallas_call(
         functools.partial(spread_kernel, chips, cores, owned),
         out_shape=[pltpu.VMEM((docs, span + 2 * topic_count), jnp.float32)] * chips,
-        in_specs=[pl.BlockSpec(memory_space=pltpu.HBM)] * 3,
+        in_specs=[pl.BlockSpec(memory_space=pltpu.HBM)] * 4,
         out_specs=[pl.BlockSpec(memory_space=pltpu.VMEM)] * chips,
         scratch_shapes=[
             pltpu.VMEM(tile_mask.shape[1:], jnp.int32),
             pltpu.VMEM(member_topics.shape[1:], jnp.float32),
+            pltpu.VMEM(align_perm.shape, jnp.int32),
             pltpu.VMEM((chips, docs, span), jnp.int32),
-            pltpu.SemaphoreType.DMA((2,)),
+            pltpu.SemaphoreType.DMA((3,)),
             pltpu.SemaphoreType.DMA((chips, cores)),
         ],
         compiler_params=pltpu.CompilerParams(vmem_limit_bytes=VMEM_BYTES),
         cost_estimate=pl.CostEstimate(flops=0, bytes_accessed=12 * counts.size, transcendentals=0),
-    )(*[pltpu.with_memory_space_constraint(x, pltpu.HBM) for x in (tile_mask[0], member_topics[0], counts[0])])
+    )(*[pltpu.with_memory_space_constraint(x, pltpu.HBM) for x in (tile_mask[0], member_topics[0], align_perm, counts[0])])
     base_sent = call(
         functools.partial(base_kernel, chips, cores),
         [shape(base_docs, span + 2 * topic_count)] * chips,
@@ -391,14 +396,13 @@
     near = [over_chips(base_sent[step], step) for step in range(1, min(chips, 2))]
     dict_own = start_dict[0].T
     halves = [dict_own] + [over_cores(dict_own)] * (cores - 1)
-    wide, tall, col_part, dict_own, onehot = call(
+    wide, tall, col_part, dict_own = call(
         functools.partial(dictionary_kernel, cores),
         [
             shape(2 * topic_count, span, dtype=jnp.bfloat16),
             shape(span, 2 * topic_count, dtype=jnp.bfloat16),
             shape(8, 2 * topic_count),
             shape(topic_count, owned),
-            shape(topic_count, topic_count),
         ],
         align_perm,
         *halves,
@@ -406,14 +410,15 @@
     )
 
     update_flops = 2 * 2 * 4 * rows * topic_count * span
+    count_order = [chips // 2] + [s for s in range(1, chips) if s != chips // 2] + [0]
     topics, part, *weighted = call(
-        functools.partial(first_kernel, chips, cores),
+        functools.partial(first_kernel, chips, cores, count_order),
         [shape(rows, 2 * topic_count), shape(rows // 2 + 8, 2 * topic_count)]
         + [shape(rows, owned)] * cores,
         wide,
         tall,
         col_part,
-        *payload[::-1],
+        *[payload[step] for step in count_order],
         *near,
         unread=len(near),
         flops=update_flops,
@@ -458,7 +463,6 @@
                 numerator_kernel,
                 shape(topic_count, owned + 128),
                 wide,
-                onehot,
                 topics,
                 weighted[0],
                 flops=update_flops // 2,
@@ -470,7 +474,6 @@
         numerator_kernel,
         shape(topic_count, owned),
         wide,
-        onehot,
         topics,
         weighted[0],
         dict_own,

time: 77.1 us -> 76.3 us (0.990)
  Pallas kernels: 9.04 us -> 8.06 us
    pallas_call x13, Pallas kernels: 7.19 us -> 6.1 us  [call(): pl.pallas_call(kernel, out_shape=outs, in_specs=[pl.BlockSpec(memory_spac...]
where the time goes in v3:
time: 76.3 us; the launch traced here: 76.1 us
  starting transfers between devices  36.7 us (48%)
  waiting for transfers between devices  29 us (38%)
  Pallas kernels  8.06 us (11%)
  local copies, waits for them, and re-layouts  1.67 us (2%)
    ppermute x21, waiting for transfers between devices, over_chips(): lax.ppermute(array, 'doc', [(c * cores + k, (c ^ step) * cores + (k + ste...  27.4 us
    ppermute x21, starting transfers between devices, over_chips(): lax.ppermute(array, 'doc', [(c * cores + k, (c ^ step) * cores + (k + ste...  26.9 us
    ppermute x6, starting transfers between devices, over_pert(): return lax.ppermute(array, 'pert', [(m, m ^ step) for m in range(members)])  7.11 us
    pallas_call x13, Pallas kernels, call(): pl.pallas_call(kernel, out_shape=outs, in_specs=[pl.BlockSpec(memory_spac...  6.1 us
    ppermute x7, starting transfers between devices, over_cores(): return lax.ppermute(array, 'doc', [(d, d ^ 1) for d in range(doc_size)])  2.7 us
    pallas_call x1, Pallas kernels, per_device(): pl.pallas_call(functools.partial(spread_kernel, chips, cores, owned), out...  1.95 us
    unnamed x9, local copies, waits for them, and re-layouts  1.62 us
  transfers between devices with their start and end apart: 34, of which 17 were waited for; matrix products, arithmetic and copies ran while one was open for 1% of the time, Pallas kernels for 7%

profile of v3, /device:TPU:0, one launch (start us, length us, event | category | flops | bytes accessed | tf_op | source)
XLA Modules:
  0.0 76.1 jit_solution(7889187566827526082)
XLA Ops:
  0.6 0.5 collective-permute-start
  1.2 2.0 %shard_map.87 = (f32[8,4224]{1,0:T(8,128)S(1)}, f32[8,4224]{1,0:T(8,128)S(1)}, f32[8,4224]{1,0:T(8,128)S(1)}, f32[8,4224]{1,0:T(8,128)S(1)}) custom-call(s32[8,128]{1,0:T(8,128)} %bitcast.13, f32[8,64]{1,0:T(8,128)} %bitcast.14, s32[1,64]{1,0:T(1,128)} %perm_hbm.1, s32[8,16384]{1,0:T(8,128)} %bitcast.12), custom_call_target="tpu_custom_call" | custom-call | bytes 1572864 | tf_op jit(solution)/shard_map/pallas_call | solution.py:371
  3.1 3.7 %collective-permute-start.1 = (f32[8,4224]{1,0:T(8,128)S(1)}, f32[8,4224]{1,0:T(8,128)S(1)}, u32[]{:S(2)}, u32[]{:S(2)}) collective-permute-start(f32[8,4224]{1,0:T(8,128)S(1)} %get-tuple-element.47), channel_id=1, source_target_pairs={{0,4},{1,5},{2,6},{3,7},{4,0},{5,1},{6,2},{7,3},{8,12},{9,13},{10,... | collective-permute-start | bytes 405512 | tf_op jit(solution)/shard_map/ppermute | solution.py:355
  6.8 1.3 %collective-permute-start.2 = (f32[8,4224]{1,0:T(8,128)S(1)}, f32[8,4224]{1,0:T(8,128)S(1)}, u32[]{:S(2)}, u32[]{:S(2)}) collective-permute-start(f32[8,4224]{1,0:T(8,128)S(1)} %get-tuple-element.48), channel_id=1, source_target_pairs={{0,3},{1,2},{2,1},{3,0},{4,7},{5,6},{6,5},{7,4},{8,11},{9,10},{10,... | collective-permute-start | bytes 405512 | tf_op jit(solution)/shard_map/ppermute | solution.py:355
  8.2 0.9 %copy-done.1 = s32[4,16384]{1,0:T(4,128)S(1)} copy-done((s32[4,16384]{1,0:T(4,128)S(1)}, s32[4,16384]{1,0:T(4,128)}, u32[]{:S(2)}) %copy-start.1) | copy-done | bytes 262168
  9.2 0.1 shard_map.88
  9.2 0.7 collective-permute-start.4
  9.9 1.1 %shard_map.86 = (bf16[128,4096]{1,0:T(8,128)(2,1)S(1)}, bf16[4096,128]{1,0:T(8,128)(2,1)S(1)}, f32[8,128]{1,0:T(8,128)S(1)}, f32[64,2048]{1,0:T(8,128)S(1)}) custom-call(s32[1,64]{1,0:T(1,128)S(1)} %copy-done.3, f32[64,2048]{1,0:T(8,128)S(1)} %bitcast.11, f32[64,2048]{1,0:T(8,128)S(1)} %collective-permute-done.refs_1_), custom_call_target="tpu_custom_call" | custom-call | bytes 4194304 | tf_op jit(solution)/shard_map/pallas_call | solution.py:37
  11.0 7.5 %collective-permute-done.4.refs_4_.refs_5_.refs_1_ = f32[4,4224]{1,0:T(4,128)S(1)} collective-permute-done((f32[4,4224]{1,0:T(4,128)S(1)}, f32[4,4224]{1,0:T(4,128)S(1)}, u32[]{:S(2)}, u32[]{:S(2)}) %collective-permute-start.4) | collective-permute-done | bytes 67616 | tf_op jit(solution)/shard_map/ppermute | solution.py:355
  18.6 0.5 shard_map.89
  19.1 0.1 collective-permute-start.14
  19.2 3.2 %collective-permute-start.5 = (f32[24,128]{1,0:T(8,128)S(1)}, f32[24,128]{1,0:T(8,128)S(1)}, u32[]{:S(2)}, u32[]{:S(2)}) collective-permute-start(f32[24,128]{1,0:T(8,128)S(1)} %get-tuple-element.53.refs_4_), channel_id=1, source_target_pairs={{0,7},{1,6},{2,5},{3,4},{4,3},{5,2},{6,1},{7,0},{8,15},{9,14},{10,... | collective-permute-start | bytes 36872 | tf_op jit(solution)/shard_map/ppermute | solution.py:355
  22.4 0.6 collective-permute-start.6
  23.1 0.3 collective-permute-start.7
  23.3 0.8 %collective-permute-done.5.refs_5_ = f32[24,128]{1,0:T(8,128)S(1)} collective-permute-done((f32[24,128]{1,0:T(8,128)S(1)}, f32[24,128]{1,0:T(8,128)S(1)}, u32[]{:S(2)}, u32[]{:S(2)}) %collective-permute-start.5) | collective-permute-done | bytes 12320 | tf_op jit(solution)/shard_map/ppermute | solution.py:355
  24.1 2.9 %collective-permute-done.6.refs_6_ = f32[24,128]{1,0:T(8,128)S(1)} collective-permute-done((f32[24,128]{1,0:T(8,128)S(1)}, f32[24,128]{1,0:T(8,128)S(1)}, u32[]{:S(2)}, u32[]{:S(2)}) %collective-permute-start.6) | collective-permute-done | bytes 12320 | tf_op jit(solution)/shard_map/ppermute | solution.py:355
  27.0 0.6 shard_map.90
  27.6 1.8 %collective-permute-start.8 = (f32[32,128]{1,0:T(8,128)S(1)}, f32[32,128]{1,0:T(8,128)S(1)}, u32[]{:S(2)}, u32[]{:S(2)}) collective-permute-start(f32[32,128]{1,0:T(8,128)S(1)} %get-tuple-element.57), channel_id=1, source_target_pairs={{0,7},{1,6},{2,5},{3,4},{4,3},{5,2},{6,1},{7,0},{8,15},{9,14},{10,... | collective-permute-start | bytes 49160 | tf_op jit(solution)/shard_map/ppermute | solution.py:355
  29.4 2.0 %collective-permute-start.10 = (f32[16,128]{1,0:T(8,128)S(1)}, f32[16,128]{1,0:T(8,128)S(1)}, u32[]{:S(2)}, u32[]{:S(2)}) collective-permute-start(f32[16,128]{1,0:T(8,128)S(1)} %get-tuple-element.56.refs_5_), channel_id=1, source_target_pairs={{0,3},{1,2},{2,1},{3,0},{4,7},{5,6},{6,5},{7,4},{8,11},{9,10},{10,... | collective-permute-start | bytes 24584 | tf_op jit(solution)/shard_map/ppermute | solution.py:355
  31.5 1.4 %collective-permute-done.10.refs_8_ = f32[16,128]{1,0:T(8,128)S(1)} collective-permute-done((f32[16,128]{1,0:T(8,128)S(1)}, f32[16,128]{1,0:T(8,128)S(1)}, u32[]{:S(2)}, u32[]{:S(2)}) %collective-permute-start.10) | collective-permute-done | bytes 8224 | tf_op jit(solution)/shard_map/ppermute | solution.py:355
  32.8 1.2 %collective-permute-done.9.refs_7_ = f32[24,128]{1,0:T(8,128)S(1)} collective-permute-done((f32[24,128]{1,0:T(8,128)S(1)}, f32[24,128]{1,0:T(8,128)S(1)}, u32[]{:S(2)}, u32[]{:S(2)}) %collective-permute-start.9) | collective-permute-done | bytes 12320 | tf_op jit(solution)/shard_map/ppermute | solution.py:355
  34.0 0.6 shard_map.91
  34.6 1.1 %collective-permute-start.11 = (f32[32,128]{1,0:T(8,128)S(1)}, f32[32,128]{1,0:T(8,128)S(1)}, u32[]{:S(2)}, u32[]{:S(2)}) collective-permute-start(f32[32,128]{1,0:T(8,128)S(1)} %get-tuple-element.61), channel_id=1, source_target_pairs={{0,7},{1,6},{2,5},{3,4},{4,3},{5,2},{6,1},{7,0},{8,15},{9,14},{10,... | collective-permute-start | bytes 49160 | tf_op jit(solution)/shard_map/ppermute | solution.py:355
  35.7 0.9 %collective-permute-start.12 = (f32[24,128]{1,0:T(8,128)S(1)}, f32[24,128]{1,0:T(8,128)S(1)}, u32[]{:S(2)}, u32[]{:S(2)}) collective-permute-start(f32[24,128]{1,0:T(8,128)S(1)} %get-tuple-element.62), channel_id=1, source_target_pairs={{0,4},{1,5},{2,6},{3,7},{4,0},{5,1},{6,2},{7,3},{8,12},{9,13},{10,... | collective-permute-start | bytes 36872 | tf_op jit(solution)/shard_map/ppermute | solution.py:355
  36.6 1.9 %collective-permute-start.13 = (f32[16,128]{1,0:T(8,128)S(1)}, f32[16,128]{1,0:T(8,128)S(1)}, u32[]{:S(2)}, u32[]{:S(2)}) collective-permute-start(f32[16,128]{1,0:T(8,128)S(1)} %get-tuple-element.60.refs_0_), channel_id=1, source_target_pairs={{0,3},{1,2},{2,1},{3,0},{4,7},{5,6},{6,5},{7,4},{8,11},{9,10},{10,... | collective-permute-start | bytes 24584 | tf_op jit(solution)/shard_map/ppermute | solution.py:355
  38.5 1.4 %collective-permute-done.13.refs_3_ = f32[16,128]{1,0:T(8,128)S(1)} collective-permute-done((f32[16,128]{1,0:T(8,128)S(1)}, f32[16,128]{1,0:T(8,128)S(1)}, u32[]{:S(2)}, u32[]{:S(2)}) %collective-permute-start.13) | collective-permute-done | bytes 8224 | tf_op jit(solution)/shard_map/ppermute | solution.py:355
  39.9 0.6 collective-permute-done.12.refs_2_
  40.5 0.1 shard_map.92.topics_ref
  40.6 0.0 collective-permute-start.15
  40.6 0.4 shard_map.93.refs_1_
  41.0 0.8 collective-permute-done.15.topics_ref
  41.7 0.4 shard_map.94
  42.2 2.6 %collective-permute-start.16 = (f32[64,512]{1,0:T(8,128)S(1)}, f32[64,512]{1,0:T(8,128)S(1)}, u32[]{:S(2)}, u32[]{:S(2)}) collective-permute-start(f32[64,512]{1,0:T(8,128)S(1)} %get-tuple-element.88), channel_id=1, source_target_pairs={{0,24},{8,16},{16,8},{24,0},{1,25},{9,17},{17,9},{25,1},{2,26},{10... | collective-permute-start | bytes 393224 | tf_op jit(solution)/shard_map/ppermute | solution.py:369
  44.8 0.5 collective-permute-start.17
  45.3 0.5 collective-permute-start.18
  45.8 1.3 %collective-permute-start.19 = (f32[4,4224]{1,0:T(4,128)S(1)}, f32[4,4224]{1,0:T(4,128)S(1)}, u32[]{:S(2)}, u32[]{:S(2)}) collective-permute-start(f32[4,4224]{1,0:T(4,128)S(1)} %get-tuple-element.70), channel_id=1, source_target_pairs={{0,4},{1,5},{2,6},{3,7},{4,0},{5,1},{6,2},{7,3},{8,12},{9,13},{10,... | collective-permute-start | bytes 202760 | tf_op jit(solution)/shard_map/ppermute | solution.py:355
  47.0 4.6 %collective-permute-done.19.refs_4_.refs_6_.refs_2_ = f32[4,4224]{1,0:T(4,128)S(1)} collective-permute-done((f32[4,4224]{1,0:T(4,128)S(1)}, f32[4,4224]{1,0:T(4,128)S(1)}, u32[]{:S(2)}, u32[]{:S(2)}) %collective-permute-start.19) | collective-permute-done | bytes 67616 | tf_op jit(solution)/shard_map/ppermute | solution.py:355
  51.7 0.1 shard_map.95.refs_0_
  51.7 2.6 %collective-permute-start.20 = (f32[64,512]{1,0:T(8,128)S(1)}, f32[64,512]{1,0:T(8,128)S(1)}, u32[]{:S(2)}, u32[]{:S(2)}) collective-permute-start(f32[64,512]{1,0:T(8,128)S(1)} %shard_map.95.refs_0_), channel_id=1, source_target_pairs={{0,24},{8,16},{16,8},{24,0},{1,25},{9,17},{17,9},{25,1},{2,26},{10... | collective-permute-start | bytes 393224 | tf_op jit(solution)/shard_map/ppermute | solution.py:369
  54.3 0.5 collective-permute-start.24
  54.8 0.5 collective-permute-start.26
  55.3 0.4 collective-permute-start.21
  55.7 1.5 %collective-permute-start.22 = (f32[64,512]{1,0:T(8,128)S(1)}, f32[64,512]{1,0:T(8,128)S(1)}, u32[]{:S(2)}, u32[]{:S(2)}) collective-permute-start(f32[64,512]{1,0:T(8,128)S(1)} %shard_map.95.refs_0_), channel_id=1, source_target_pairs={{0,1},{1,0},{2,3},{3,2},{4,5},{5,4},{6,7},{7,6},{8,9},{9,8},{10,11... | collective-permute-start | bytes 393224 | tf_op jit(solution)/shard_map/ppermute | solution.py:366
  57.2 3.7 %collective-permute-done.21.refs_7_.refs_3_ = f32[4,4224]{1,0:T(4,128)S(1)} collective-permute-done((f32[4,4224]{1,0:T(4,128)S(1)}, f32[4,4224]{1,0:T(4,128)S(1)}, u32[]{:S(2)}, u32[]{:S(2)}) %collective-permute-start.21) | collective-permute-done | bytes 67616 | tf_op jit(solution)/shard_map/ppermute | solution.py:355
  60.9 0.5 collective-permute-start.25
  61.4 0.1 collective-permute-start.27
  61.5 0.5 shard_map.96
  62.0 0.2 collective-permute-done.23.refs_1_
  62.2 0.2 collective-permute-done.25.refs_2_
  62.4 0.3 collective-permute-done.27.refs_3_
  62.7 0.5 shard_map.97
  63.3 1.5 %collective-permute-start.28 = (f32[16,128]{1,0:T(8,128)S(1)}, f32[16,128]{1,0:T(8,128)S(1)}, u32[]{:S(2)}, u32[]{:S(2)}) collective-permute-start(f32[16,128]{1,0:T(8,128)S(1)} %get-tuple-element.76.refs_4_), channel_id=1, source_target_pairs={{0,7},{1,6},{2,5},{3,4},{4,3},{5,2},{6,1},{7,0},{8,15},{9,14},{10,... | collective-permute-start | bytes 24584 | tf_op jit(solution)/shard_map/ppermute | solution.py:355
  64.8 0.8 %collective-permute-start.29 = (f32[16,128]{1,0:T(8,128)S(1)}, f32[16,128]{1,0:T(8,128)S(1)}, u32[]{:S(2)}, u32[]{:S(2)}) collective-permute-start(f32[16,128]{1,0:T(8,128)S(1)} %get-tuple-element.76.refs_4_), channel_id=1, source_target_pairs={{0,4},{1,5},{2,6},{3,7},{4,0},{5,1},{6,2},{7,3},{8,12},{9,13},{10,... | collective-permute-start | bytes 24584 | tf_op jit(solution)/shard_map/ppermute | solution.py:355
  65.6 1.5 %collective-permute-start.30 = (f32[16,128]{1,0:T(8,128)S(1)}, f32[16,128]{1,0:T(8,128)S(1)}, u32[]{:S(2)}, u32[]{:S(2)}) collective-permute-start(f32[16,128]{1,0:T(8,128)S(1)} %get-tuple-element.76.refs_4_), channel_id=1, source_target_pairs={{0,3},{1,2},{2,1},{3,0},{4,7},{5,6},{6,5},{7,4},{8,11},{9,10},{10,... | collective-permute-start | bytes 24584 | tf_op jit(solution)/shard_map/ppermute | solution.py:355
  67.1 1.0 %collective-permute-done.28.refs_5_ = f32[16,128]{1,0:T(8,128)S(1)} collective-permute-done((f32[16,128]{1,0:T(8,128)S(1)}, f32[16,128]{1,0:T(8,128)S(1)}, u32[]{:S(2)}, u32[]{:S(2)}) %collective-permute-start.28) | collective-permute-done | bytes 8224 | tf_op jit(solution)/shard_map/ppermute | solution.py:355
  68.1 1.2 %collective-permute-done.29.refs_6_ = f32[16,128]{1,0:T(8,128)S(1)} collective-permute-done((f32[16,128]{1,0:T(8,128)S(1)}, f32[16,128]{1,0:T(8,128)S(1)}, u32[]{:S(2)}, u32[]{:S(2)}) %collective-permute-start.29) | collective-permute-done | bytes 8224 | tf_op jit(solution)/shard_map/ppermute | solution.py:355
  69.4 0.7 shard_map.98
  70.0 1.0 %collective-permute-start.31 = (f32[4,128]{1,0:T(4,128)S(1)}, f32[4,128]{1,0:T(4,128)S(1)}, u32[]{:S(2)}, u32[]{:S(2)}) collective-permute-start(f32[4,128]{1,0:T(4,128)S(1)} %get-tuple-element.83), channel_id=1, source_target_pairs={{0,7},{1,6},{2,5},{3,4},{4,3},{5,2},{6,1},{7,0},{8,15},{9,14},{10,... | collective-permute-start | bytes 6152 | tf_op jit(solution)/shard_map/ppermute | solution.py:355
  71.0 1.4 %collective-permute-start.32 = (f32[4,128]{1,0:T(4,128)S(1)}, f32[4,128]{1,0:T(4,128)S(1)}, u32[]{:S(2)}, u32[]{:S(2)}) collective-permute-start(f32[4,128]{1,0:T(4,128)S(1)} %get-tuple-element.84), channel_id=1, source_target_pairs={{0,4},{1,5},{2,6},{3,7},{4,0},{5,1},{6,2},{7,3},{8,12},{9,13},{10,... | collective-permute-start | bytes 6152 | tf_op jit(solution)/shard_map/ppermute | solution.py:355
  72.4 1.4 %collective-permute-start.33 = (f32[4,128]{1,0:T(4,128)S(1)}, f32[4,128]{1,0:T(4,128)S(1)}, u32[]{:S(2)}, u32[]{:S(2)}) collective-permute-start(f32[4,128]{1,0:T(4,128)S(1)} %get-tuple-element.85), channel_id=1, source_target_pairs={{0,3},{1,2},{2,1},{3,0},{4,7},{5,6},{6,5},{7,4},{8,11},{9,10},{10,... | collective-permute-start | bytes 6152 | tf_op jit(solution)/shard_map/ppermute | solution.py:355
  73.9 0.7 copy.9
  74.5 0.3 collective-permute-done.31.refs_1_
  74.9 0.7 collective-permute-done.32.refs_2_
  75.5 0.6 shard_map.99
  (28 shorter events, 0.1 us)
Async XLA Ops:
  0.6 9.3 %copy-start = (f32[1,2048,64]{1,2,0:T(8,128)S(1)}, f32[1,2048,64]{1,2,0:T(8,128)}, u32[]{:S(2)}) copy-start(f32[1,2048,64]{1,2,0:T(8,128)} %param.10) | copy-start | bytes 1572868
  0.6 9.3 %collective-permute-start = (f32[64,2048]{1,0:T(8,128)}, f32[64,2048]{1,0:T(8,128)S(1)}, u32[]{:S(2)}, u32[]{:S(2)}) collective-permute-start(f32[64,2048]{1,0:T(8,128)} %bitcast.10), channel_id=1, source_target_pairs={{0,1},{1,0},{2,3},{3,2},{4,5},{5,4},{6,7},{7,6},{8,9},{9,8},{10,11... | collective-permute-start | bytes 1572872 | tf_op jit(solution)/shard_map/ppermute | solution.py:366
  3.1 5.1 %copy-start.2 = (f32[4,64]{1,0:T(4,128)S(1)}, f32[4,64]{1,0:T(4,128)}, u32[]{:S(2)}) copy-start(f32[4,64]{1,0:T(4,128)} %topics_ref.1) | copy-start | bytes 3076
  3.1 15.4 %collective-permute-start.1 = (f32[8,4224]{1,0:T(8,128)S(1)}, f32[8,4224]{1,0:T(8,128)S(1)}, u32[]{:S(2)}, u32[]{:S(2)}) collective-permute-start(f32[8,4224]{1,0:T(8,128)S(1)} %get-tuple-element.47), channel_id=1, source_target_pairs={{0,4},{1,5},{2,6},{3,7},{4,0},{5,1},{6,2},{7,3},{8,12},{9,13},{10,... | collective-permute-start | bytes 405512 | tf_op jit(solution)/shard_map/ppermute | solution.py:355
  6.8 11.7 %collective-permute-start.2 = (f32[8,4224]{1,0:T(8,128)S(1)}, f32[8,4224]{1,0:T(8,128)S(1)}, u32[]{:S(2)}, u32[]{:S(2)}) collective-permute-start(f32[8,4224]{1,0:T(8,128)S(1)} %get-tuple-element.48), channel_id=1, source_target_pairs={{0,3},{1,2},{2,1},{3,0},{4,7},{5,6},{6,5},{7,4},{8,11},{9,10},{10,... | collective-permute-start | bytes 405512 | tf_op jit(solution)/shard_map/ppermute | solution.py:355
  8.2 10.4 %collective-permute-start.3 = (f32[8,4224]{1,0:T(8,128)S(1)}, f32[8,4224]{1,0:T(8,128)S(1)}, u32[]{:S(2)}, u32[]{:S(2)}) collective-permute-start(f32[8,4224]{1,0:T(8,128)S(1)} %get-tuple-element.49), channel_id=1, source_target_pairs={{0,7},{1,6},{2,5},{3,4},{4,3},{5,2},{6,1},{7,0},{8,15},{9,14},{10,... | collective-permute-start | bytes 405512 | tf_op jit(solution)/shard_map/ppermute | solution.py:355
  8.2 1.0 %copy-start.1 = (s32[4,16384]{1,0:T(4,128)S(1)}, s32[4,16384]{1,0:T(4,128)}, u32[]{:S(2)}) copy-start(s32[4,16384]{1,0:T(4,128)} %counts_ref.1) | copy-start | bytes 786436
  9.2 0.7 copy-start.3
  9.2 9.3 %collective-permute-start.4 = (f32[4,4224]{1,0:T(4,128)S(1)}, f32[4,4224]{1,0:T(4,128)S(1)}, u32[]{:S(2)}, u32[]{:S(2)}) collective-permute-start(f32[4,4224]{1,0:T(4,128)S(1)} %get-tuple-element.51), channel_id=1, source_target_pairs={{0,3},{1,2},{2,1},{3,0},{4,7},{5,6},{6,5},{7,4},{8,11},{9,10},{10,... | collective-permute-start | bytes 202760 | tf_op jit(solution)/shard_map/ppermute | solution.py:355
  19.1 21.4 %collective-permute-start.14 = (f32[32,2048]{1,0:T(8,128)S(1)}, f32[32,2048]{1,0:T(8,128)S(1)}, u32[]{:S(2)}, u32[]{:S(2)}) collective-permute-start(f32[32,2048]{1,0:T(8,128)S(1)} %get-tuple-element.63), channel_id=1, source_target_pairs={{0,1},{1,0},{2,3},{3,2},{4,5},{5,4},{6,7},{7,6},{8,9},{9,8},{10,11... | collective-permute-start | bytes 786440 | tf_op jit(solution)/shard_map/ppermute | solution.py:366
  19.2 4.9 %collective-permute-start.5 = (f32[24,128]{1,0:T(8,128)S(1)}, f32[24,128]{1,0:T(8,128)S(1)}, u32[]{:S(2)}, u32[]{:S(2)}) collective-permute-start(f32[24,128]{1,0:T(8,128)S(1)} %get-tuple-element.53.refs_4_), channel_id=1, source_target_pairs={{0,7},{1,6},{2,5},{3,4},{4,3},{5,2},{6,1},{7,0},{8,15},{9,14},{10,... | collective-permute-start | bytes 36872 | tf_op jit(solution)/shard_map/ppermute | solution.py:355
  22.4 4.6 %collective-permute-start.6 = (f32[24,128]{1,0:T(8,128)S(1)}, f32[24,128]{1,0:T(8,128)S(1)}, u32[]{:S(2)}, u32[]{:S(2)}) collective-permute-start(f32[24,128]{1,0:T(8,128)S(1)} %get-tuple-element.53.refs_4_), channel_id=1, source_target_pairs={{0,4},{1,5},{2,6},{3,7},{4,0},{5,1},{6,2},{7,3},{8,12},{9,13},{10,... | collective-permute-start | bytes 36872 | tf_op jit(solution)/shard_map/ppermute | solution.py:355
  23.1 4.0 %collective-permute-start.7 = (f32[24,128]{1,0:T(8,128)S(1)}, f32[24,128]{1,0:T(8,128)S(1)}, u32[]{:S(2)}, u32[]{:S(2)}) collective-permute-start(f32[24,128]{1,0:T(8,128)S(1)} %get-tuple-element.53.refs_4_), channel_id=1, source_target_pairs={{0,3},{1,2},{2,1},{3,0},{4,7},{5,6},{6,5},{7,4},{8,11},{9,10},{10,... | collective-permute-start | bytes 36872 | tf_op jit(solution)/shard_map/ppermute | solution.py:355
  27.6 6.4 %collective-permute-start.8 = (f32[32,128]{1,0:T(8,128)S(1)}, f32[32,128]{1,0:T(8,128)S(1)}, u32[]{:S(2)}, u32[]{:S(2)}) collective-permute-start(f32[32,128]{1,0:T(8,128)S(1)} %get-tuple-element.57), channel_id=1, source_target_pairs={{0,7},{1,6},{2,5},{3,4},{4,3},{5,2},{6,1},{7,0},{8,15},{9,14},{10,... | collective-permute-start | bytes 49160 | tf_op jit(solution)/shard_map/ppermute | solution.py:355
  29.4 4.6 %collective-permute-start.9 = (f32[24,128]{1,0:T(8,128)S(1)}, f32[24,128]{1,0:T(8,128)S(1)}, u32[]{:S(2)}, u32[]{:S(2)}) collective-permute-start(f32[24,128]{1,0:T(8,128)S(1)} %get-tuple-element.58), channel_id=1, source_target_pairs={{0,4},{1,5},{2,6},{3,7},{4,0},{5,1},{6,2},{7,3},{8,12},{9,13},{10,... | collective-permute-start | bytes 36872 | tf_op jit(solution)/shard_map/ppermute | solution.py:355
  29.4 3.4 %collective-permute-start.10 = (f32[16,128]{1,0:T(8,128)S(1)}, f32[16,128]{1,0:T(8,128)S(1)}, u32[]{:S(2)}, u32[]{:S(2)}) collective-permute-start(f32[16,128]{1,0:T(8,128)S(1)} %get-tuple-element.56.refs_5_), channel_id=1, source_target_pairs={{0,3},{1,2},{2,1},{3,0},{4,7},{5,6},{6,5},{7,4},{8,11},{9,10},{10,... | collective-permute-start | bytes 24584 | tf_op jit(solution)/shard_map/ppermute | solution.py:355
  34.6 5.9 %collective-permute-start.11 = (f32[32,128]{1,0:T(8,128)S(1)}, f32[32,128]{1,0:T(8,128)S(1)}, u32[]{:S(2)}, u32[]{:S(2)}) collective-permute-start(f32[32,128]{1,0:T(8,128)S(1)} %get-tuple-element.61), channel_id=1, source_target_pairs={{0,7},{1,6},{2,5},{3,4},{4,3},{5,2},{6,1},{7,0},{8,15},{9,14},{10,... | collective-permute-start | bytes 49160 | tf_op jit(solution)/shard_map/ppermute | solution.py:355
  35.7 4.8 %collective-permute-start.12 = (f32[24,128]{1,0:T(8,128)S(1)}, f32[24,128]{1,0:T(8,128)S(1)}, u32[]{:S(2)}, u32[]{:S(2)}) collective-permute-start(f32[24,128]{1,0:T(8,128)S(1)} %get-tuple-element.62), channel_id=1, source_target_pairs={{0,4},{1,5},{2,6},{3,7},{4,0},{5,1},{6,2},{7,3},{8,12},{9,13},{10,... | collective-permute-start | bytes 36872 | tf_op jit(solution)/shard_map/ppermute | solution.py:355
  36.6 3.3 %collective-permute-start.13 = (f32[16,128]{1,0:T(8,128)S(1)}, f32[16,128]{1,0:T(8,128)S(1)}, u32[]{:S(2)}, u32[]{:S(2)}) collective-permute-start(f32[16,128]{1,0:T(8,128)S(1)} %get-tuple-element.60.refs_0_), channel_id=1, source_target_pairs={{0,3},{1,2},{2,1},{3,0},{4,7},{5,6},{6,5},{7,4},{8,11},{9,10},{10,... | collective-permute-start | bytes 24584 | tf_op jit(solution)/shard_map/ppermute | solution.py:355
  40.6 1.2 %collective-permute-start.15 = (f32[32,128]{1,0:T(8,128)S(1)}, f32[32,128]{1,0:T(8,128)S(1)}, u32[]{:S(2)}, u32[]{:S(2)}) collective-permute-start(f32[32,128]{1,0:T(8,128)S(1)} %shard_map.92.topics_ref), channel_id=1, source_target_pairs={{0,1},{1,0},{2,3},{3,2},{4,5},{5,4},{6,7},{7,6},{8,9},{9,8},{10,11... | collective-permute-start | bytes 49160 | tf_op jit(solution)/shard_map/ppermute | solution.py:366
  42.2 9.5 %collective-permute-start.16 = (f32[64,512]{1,0:T(8,128)S(1)}, f32[64,512]{1,0:T(8,128)S(1)}, u32[]{:S(2)}, u32[]{:S(2)}) collective-permute-start(f32[64,512]{1,0:T(8,128)S(1)} %get-tuple-element.88), channel_id=1, source_target_pairs={{0,24},{8,16},{16,8},{24,0},{1,25},{9,17},{17,9},{25,1},{2,26},{10... | collective-permute-start | bytes 393224 | tf_op jit(solution)/shard_map/ppermute | solution.py:369
  44.8 6.9 %collective-permute-start.17 = (f32[64,512]{1,0:T(8,128)S(1)}, f32[64,512]{1,0:T(8,128)S(1)}, u32[]{:S(2)}, u32[]{:S(2)}) collective-permute-start(f32[64,512]{1,0:T(8,128)S(1)} %get-tuple-element.87), channel_id=1, source_target_pairs={{0,16},{8,24},{16,0},{24,8},{1,17},{9,25},{17,1},{25,9},{2,18},{10... | collective-permute-start | bytes 393224 | tf_op jit(solution)/shard_map/ppermute | solution.py:369
  45.3 6.4 %collective-permute-start.18 = (f32[64,512]{1,0:T(8,128)S(1)}, f32[64,512]{1,0:T(8,128)S(1)}, u32[]{:S(2)}, u32[]{:S(2)}) collective-permute-start(f32[64,512]{1,0:T(8,128)S(1)} %get-tuple-element.86), channel_id=1, source_target_pairs={{0,8},{8,0},{16,24},{24,16},{1,9},{9,1},{17,25},{25,17},{2,10},{10... | collective-permute-start | bytes 393224 | tf_op jit(solution)/shard_map/ppermute | solution.py:369
  45.8 5.9 %collective-permute-start.19 = (f32[4,4224]{1,0:T(4,128)S(1)}, f32[4,4224]{1,0:T(4,128)S(1)}, u32[]{:S(2)}, u32[]{:S(2)}) collective-permute-start(f32[4,4224]{1,0:T(4,128)S(1)} %get-tuple-element.70), channel_id=1, source_target_pairs={{0,4},{1,5},{2,6},{3,7},{4,0},{5,1},{6,2},{7,3},{8,12},{9,13},{10,... | collective-permute-start | bytes 202760 | tf_op jit(solution)/shard_map/ppermute | solution.py:355
  51.7 9.1 %collective-permute-start.20 = (f32[64,512]{1,0:T(8,128)S(1)}, f32[64,512]{1,0:T(8,128)S(1)}, u32[]{:S(2)}, u32[]{:S(2)}) collective-permute-start(f32[64,512]{1,0:T(8,128)S(1)} %shard_map.95.refs_0_), channel_id=1, source_target_pairs={{0,24},{8,16},{16,8},{24,0},{1,25},{9,17},{17,9},{25,1},{2,26},{10... | collective-permute-start | bytes 393224 | tf_op jit(solution)/shard_map/ppermute | solution.py:369
  54.3 6.6 %collective-permute-start.24 = (f32[64,512]{1,0:T(8,128)S(1)}, f32[64,512]{1,0:T(8,128)S(1)}, u32[]{:S(2)}, u32[]{:S(2)}) collective-permute-start(f32[64,512]{1,0:T(8,128)S(1)} %shard_map.95.refs_0_), channel_id=1, source_target_pairs={{0,16},{8,24},{16,0},{24,8},{1,17},{9,25},{17,1},{25,9},{2,18},{10... | collective-permute-start | bytes 393224 | tf_op jit(solution)/shard_map/ppermute | solution.py:369
  54.8 6.6 %collective-permute-start.26 = (f32[64,512]{1,0:T(8,128)S(1)}, f32[64,512]{1,0:T(8,128)S(1)}, u32[]{:S(2)}, u32[]{:S(2)}) collective-permute-start(f32[64,512]{1,0:T(8,128)S(1)} %shard_map.95.refs_0_), channel_id=1, source_target_pairs={{0,8},{8,0},{16,24},{24,16},{1,9},{9,1},{17,25},{25,17},{2,10},{10... | collective-permute-start | bytes 393224 | tf_op jit(solution)/shard_map/ppermute | solution.py:369
  55.3 5.6 %collective-permute-start.21 = (f32[4,4224]{1,0:T(4,128)S(1)}, f32[4,4224]{1,0:T(4,128)S(1)}, u32[]{:S(2)}, u32[]{:S(2)}) collective-permute-start(f32[4,4224]{1,0:T(4,128)S(1)} %get-tuple-element.72), channel_id=1, source_target_pairs={{0,7},{1,6},{2,5},{3,4},{4,3},{5,2},{6,1},{7,0},{8,15},{9,14},{10,... | collective-permute-start | bytes 202760 | tf_op jit(solution)/shard_map/ppermute | solution.py:355
  55.7 6.3 %collective-permute-start.22 = (f32[64,512]{1,0:T(8,128)S(1)}, f32[64,512]{1,0:T(8,128)S(1)}, u32[]{:S(2)}, u32[]{:S(2)}) collective-permute-start(f32[64,512]{1,0:T(8,128)S(1)} %shard_map.95.refs_0_), channel_id=1, source_target_pairs={{0,1},{1,0},{2,3},{3,2},{4,5},{5,4},{6,7},{7,6},{8,9},{9,8},{10,11... | collective-permute-start | bytes 393224 | tf_op jit(solution)/shard_map/ppermute | solution.py:366
  60.9 1.3 %collective-permute-start.23 = (f32[64,512]{1,0:T(8,128)S(1)}, f32[64,512]{1,0:T(8,128)S(1)}, u32[]{:S(2)}, u32[]{:S(2)}) collective-permute-start(f32[64,512]{1,0:T(8,128)S(1)} %collective-permute-done.20.refs_1_), channel_id=1, source_target_pairs={{0,1},{1,0},{2,3},{3,2},{4,5},{5,4},{6,7},{7,6},{8,9},{9,8},{10,11... | collective-permute-start | bytes 393224 | tf_op jit(solution)/shard_map/ppermute | solution.py:366
  60.9 1.5 %collective-permute-start.25 = (f32[64,512]{1,0:T(8,128)S(1)}, f32[64,512]{1,0:T(8,128)S(1)}, u32[]{:S(2)}, u32[]{:S(2)}) collective-permute-start(f32[64,512]{1,0:T(8,128)S(1)} %collective-permute-done.24.refs_2_), channel_id=1, source_target_pairs={{0,1},{1,0},{2,3},{3,2},{4,5},{5,4},{6,7},{7,6},{8,9},{9,8},{10,11... | collective-permute-start | bytes 393224 | tf_op jit(solution)/shard_map/ppermute | solution.py:366
  61.4 1.3 %collective-permute-start.27 = (f32[64,512]{1,0:T(8,128)S(1)}, f32[64,512]{1,0:T(8,128)S(1)}, u32[]{:S(2)}, u32[]{:S(2)}) collective-permute-start(f32[64,512]{1,0:T(8,128)S(1)} %collective-permute-done.26.refs_3_), channel_id=1, source_target_pairs={{0,1},{1,0},{2,3},{3,2},{4,5},{5,4},{6,7},{7,6},{8,9},{9,8},{10,11... | collective-permute-start | bytes 393224 | tf_op jit(solution)/shard_map/ppermute | solution.py:366
  63.3 4.9 %collective-permute-start.28 = (f32[16,128]{1,0:T(8,128)S(1)}, f32[16,128]{1,0:T(8,128)S(1)}, u32[]{:S(2)}, u32[]{:S(2)}) collective-permute-start(f32[16,128]{1,0:T(8,128)S(1)} %get-tuple-element.76.refs_4_), channel_id=1, source_target_pairs={{0,7},{1,6},{2,5},{3,4},{4,3},{5,2},{6,1},{7,0},{8,15},{9,14},{10,... | collective-permute-start | bytes 24584 | tf_op jit(solution)/shard_map/ppermute | solution.py:355
  64.8 4.5 %collective-permute-start.29 = (f32[16,128]{1,0:T(8,128)S(1)}, f32[16,128]{1,0:T(8,128)S(1)}, u32[]{:S(2)}, u32[]{:S(2)}) collective-permute-start(f32[16,128]{1,0:T(8,128)S(1)} %get-tuple-element.76.refs_4_), channel_id=1, source_target_pairs={{0,4},{1,5},{2,6},{3,7},{4,0},{5,1},{6,2},{7,3},{8,12},{9,13},{10,... | collective-permute-start | bytes 24584 | tf_op jit(solution)/shard_map/ppermute | solution.py:355
  65.6 3.8 %collective-permute-start.30 = (f32[16,128]{1,0:T(8,128)S(1)}, f32[16,128]{1,0:T(8,128)S(1)}, u32[]{:S(2)}, u32[]{:S(2)}) collective-permute-start(f32[16,128]{1,0:T(8,128)S(1)} %get-tuple-element.76.refs_4_), channel_id=1, source_target_pairs={{0,3},{1,2},{2,1},{3,0},{4,7},{5,6},{6,5},{7,4},{8,11},{9,10},{10,... | collective-permute-start | bytes 24584 | tf_op jit(solution)/shard_map/ppermute | solution.py:355
  70.0 4.8 %collective-permute-start.31 = (f32[4,128]{1,0:T(4,128)S(1)}, f32[4,128]{1,0:T(4,128)S(1)}, u32[]{:S(2)}, u32[]{:S(2)}) collective-permute-start(f32[4,128]{1,0:T(4,128)S(1)} %get-tuple-element.83), channel_id=1, source_target_pairs={{0,7},{1,6},{2,5},{3,4},{4,3},{5,2},{6,1},{7,0},{8,15},{9,14},{10,... | collective-permute-start | bytes 6152 | tf_op jit(solution)/shard_map/ppermute | solution.py:355
  71.0 4.5 %collective-permute-start.32 = (f32[4,128]{1,0:T(4,128)S(1)}, f32[4,128]{1,0:T(4,128)S(1)}, u32[]{:S(2)}, u32[]{:S(2)}) collective-permute-start(f32[4,128]{1,0:T(4,128)S(1)} %get-tuple-element.84), channel_id=1, source_target_pairs={{0,4},{1,5},{2,6},{3,7},{4,0},{5,1},{6,2},{7,3},{8,12},{9,13},{10,... | collective-permute-start | bytes 6152 | tf_op jit(solution)/shard_map/ppermute | solution.py:355
  72.4 3.1 %collective-permute-start.33 = (f32[4,128]{1,0:T(4,128)S(1)}, f32[4,128]{1,0:T(4,128)S(1)}, u32[]{:S(2)}, u32[]{:S(2)}) collective-permute-start(f32[4,128]{1,0:T(4,128)S(1)} %get-tuple-element.85), channel_id=1, source_target_pairs={{0,3},{1,2},{2,1},{3,0},{4,7},{5,6},{6,5},{7,4},{8,11},{9,10},{10,... | collective-permute-start | bytes 6152 | tf_op jit(solution)/shard_map/ppermute | solution.py:355

commit v4 on v3

--- a/solution.py
+++ b/solution.py
@@ -410,7 +410,7 @@
     )
 
     update_flops = 2 * 2 * 4 * rows * topic_count * span
-    count_order = [chips // 2] + [s for s in range(1, chips) if s != chips // 2] + [0]
+    count_order = [chips - 1] + list(range(1, chips - 1)) + [0]
     topics, part, *weighted = call(
         functools.partial(first_kernel, chips, cores, count_order),
         [shape(rows, 2 * topic_count), shape(rows // 2 + 8, 2 * topic_count)]
@@ -431,7 +431,7 @@
         topics, *outs = call(
             functools.partial(update_kernel, chips),
             [shape(rows, 2 * topic_count)]
-            + [shape(rows // 2 + 8 * (step - 1), 2 * topic_count) for step in range(1, chips)]
+            + [shape(rows // 2 + (0 if totals else step - 1), 2 * topic_count) for step in range(1, chips)]
             + ([] if totals else [shape(8, 2 * topic_count)]),
             wide,
             tall,

time: 76.3 us -> 76.2 us (level)
  waiting for transfers between devices: 29 us -> 28.1 us
    ppermute x21, waiting for transfers between devices: 27.4 us -> 26.6 us  [over_chips(): lax.ppermute(array, 'doc', [(c * cores + k, (c ^ step) * cores + (k + ste...]
    ppermute x21, starting transfers between devices: 26.9 us -> 27.7 us  [over_chips(): lax.ppermute(array, 'doc', [(c * cores + k, (c ^ step) * cores + (k + ste...]
  transfers between devices with their start and end apart: 34 -> 34, of which waited for: 17 -> 18; matrix products, arithmetic and copies ran while one was open for 1% -> 1% of each run, Pallas kernels for 7% -> 7%
where the time goes in v4:
time: 76.2 us; the launch traced here: 76 us
  starting transfers between devices  37.4 us (49%)
  waiting for transfers between devices  28.1 us (37%)
  Pallas kernels  8.04 us (11%)
  local copies, waits for them, and re-layouts  1.67 us (2%)
  between operations  0.77 us (1%)
    ppermute x21, starting transfers between devices, over_chips(): lax.ppermute(array, 'doc', [(c * cores + k, (c ^ step) * cores + (k + ste...  27.7 us
    ppermute x21, waiting for transfers between devices, over_chips(): lax.ppermute(array, 'doc', [(c * cores + k, (c ^ step) * cores + (k + ste...  26.6 us
    ppermute x6, starting transfers between devices, over_pert(): return lax.ppermute(array, 'pert', [(m, m ^ step) for m in range(members)])  7.11 us
    pallas_call x13, Pallas kernels, call(): pl.pallas_call(kernel, out_shape=outs, in_specs=[pl.BlockSpec(memory_spac...  6.09 us
    ppermute x7, starting transfers between devices, over_cores(): return lax.ppermute(array, 'doc', [(d, d ^ 1) for d in range(doc_size)])  2.6 us
    pallas_call x1, Pallas kernels, per_device(): pl.pallas_call(functools.partial(spread_kernel, chips, cores, owned), out...  1.95 us
    unnamed x9, local copies, waits for them, and re-layouts  1.62 us
  transfers between devices with their start and end apart: 34, of which 18 were waited for; matrix products, arithmetic and copies ran while one was open for 1% of the time, Pallas kernels for 7%

profile of v4, /device:TPU:0, one launch (start us, length us, event | category | flops | bytes accessed | tf_op | source)
XLA Modules:
  0.0 76.0 jit_solution(16026483776468868357)
XLA Ops:
  0.6 0.5 collective-permute-start
  1.2 2.0 %shard_map.87 = (f32[8,4224]{1,0:T(8,128)S(1)}, f32[8,4224]{1,0:T(8,128)S(1)}, f32[8,4224]{1,0:T(8,128)S(1)}, f32[8,4224]{1,0:T(8,128)S(1)}) custom-call(s32[8,128]{1,0:T(8,128)} %bitcast.13, f32[8,64]{1,0:T(8,128)} %bitcast.14, s32[1,64]{1,0:T(1,128)} %perm_hbm.1, s32[8,16384]{1,0:T(8,128)} %bitcast.12), custom_call_target="tpu_custom_call" | custom-call | bytes 1572864 | tf_op jit(solution)/shard_map/pallas_call | solution.py:371
  3.1 4.8 %collective-permute-start.1 = (f32[8,4224]{1,0:T(8,128)S(1)}, f32[8,4224]{1,0:T(8,128)S(1)}, u32[]{:S(2)}, u32[]{:S(2)}) collective-permute-start(f32[8,4224]{1,0:T(8,128)S(1)} %get-tuple-element.47), channel_id=1, source_target_pairs={{0,7},{1,6},{2,5},{3,4},{4,3},{5,2},{6,1},{7,0},{8,15},{9,14},{10,... | collective-permute-start | bytes 405512 | tf_op jit(solution)/shard_map/ppermute | solution.py:355
  7.9 0.6 collective-permute-start.3
  8.6 0.9 %copy-done.1 = s32[4,16384]{1,0:T(4,128)S(1)} copy-done((s32[4,16384]{1,0:T(4,128)S(1)}, s32[4,16384]{1,0:T(4,128)}, u32[]{:S(2)}) %copy-start.1) | copy-done | bytes 262168
  9.5 0.1 shard_map.88
  9.6 1.1 %collective-permute-start.4 = (f32[4,4224]{1,0:T(4,128)S(1)}, f32[4,4224]{1,0:T(4,128)S(1)}, u32[]{:S(2)}, u32[]{:S(2)}) collective-permute-start(f32[4,4224]{1,0:T(4,128)S(1)} %get-tuple-element.51), channel_id=1, source_target_pairs={{0,3},{1,2},{2,1},{3,0},{4,7},{5,6},{6,5},{7,4},{8,11},{9,10},{10,... | collective-permute-start | bytes 202760 | tf_op jit(solution)/shard_map/ppermute | solution.py:355
  10.7 1.1 %shard_map.86 = (bf16[128,4096]{1,0:T(8,128)(2,1)S(1)}, bf16[4096,128]{1,0:T(8,128)(2,1)S(1)}, f32[8,128]{1,0:T(8,128)S(1)}, f32[64,2048]{1,0:T(8,128)S(1)}) custom-call(s32[1,64]{1,0:T(1,128)S(1)} %copy-done.3, f32[64,2048]{1,0:T(8,128)S(1)} %bitcast.11, f32[64,2048]{1,0:T(8,128)S(1)} %collective-permute-done.refs_1_), custom_call_target="tpu_custom_call" | custom-call | bytes 4194304 | tf_op jit(solution)/shard_map/pallas_call | solution.py:37
  11.8 6.8 %collective-permute-done.4.refs_4_.refs_5_.refs_1_ = f32[4,4224]{1,0:T(4,128)S(1)} collective-permute-done((f32[4,4224]{1,0:T(4,128)S(1)}, f32[4,4224]{1,0:T(4,128)S(1)}, u32[]{:S(2)}, u32[]{:S(2)}) %collective-permute-start.4) | collective-permute-done | bytes 67616 | tf_op jit(solution)/shard_map/ppermute | solution.py:355
  18.6 1.2 %collective-permute-done.3.refs_2_.refs_1_ = f32[8,4224]{1,0:T(8,128)S(1)} collective-permute-done((f32[8,4224]{1,0:T(8,128)S(1)}, f32[8,4224]{1,0:T(8,128)S(1)}, u32[]{:S(2)}, u32[]{:S(2)}) %collective-permute-start.3) | collective-permute-done | bytes 135200 | tf_op jit(solution)/shard_map/ppermute | solution.py:355
  19.8 0.5 shard_map.89
  20.4 2.6 %collective-permute-start.5 = (f32[24,128]{1,0:T(8,128)S(1)}, f32[24,128]{1,0:T(8,128)S(1)}, u32[]{:S(2)}, u32[]{:S(2)}) collective-permute-start(f32[24,128]{1,0:T(8,128)S(1)} %get-tuple-element.53.refs_4_), channel_id=1, source_target_pairs={{0,7},{1,6},{2,5},{3,4},{4,3},{5,2},{6,1},{7,0},{8,15},{9,14},{10,... | collective-permute-start | bytes 36872 | tf_op jit(solution)/shard_map/ppermute | solution.py:355
  23.0 1.3 %collective-permute-start.7 = (f32[24,128]{1,0:T(8,128)S(1)}, f32[24,128]{1,0:T(8,128)S(1)}, u32[]{:S(2)}, u32[]{:S(2)}) collective-permute-start(f32[24,128]{1,0:T(8,128)S(1)} %get-tuple-element.53.refs_4_), channel_id=1, source_target_pairs={{0,3},{1,2},{2,1},{3,0},{4,7},{5,6},{6,5},{7,4},{8,11},{9,10},{10,... | collective-permute-start | bytes 36872 | tf_op jit(solution)/shard_map/ppermute | solution.py:355
  24.3 1.1 %collective-permute-done.5.refs_5_ = f32[24,128]{1,0:T(8,128)S(1)} collective-permute-done((f32[24,128]{1,0:T(8,128)S(1)}, f32[24,128]{1,0:T(8,128)S(1)}, u32[]{:S(2)}, u32[]{:S(2)}) %collective-permute-start.5) | collective-permute-done | bytes 12320 | tf_op jit(solution)/shard_map/ppermute | solution.py:355
  25.4 2.2 %collective-permute-done.6.refs_6_ = f32[24,128]{1,0:T(8,128)S(1)} collective-permute-done((f32[24,128]{1,0:T(8,128)S(1)}, f32[24,128]{1,0:T(8,128)S(1)}, u32[]{:S(2)}, u32[]{:S(2)}) %collective-permute-start.6) | collective-permute-done | bytes 12320 | tf_op jit(solution)/shard_map/ppermute | solution.py:355
  27.6 0.6 shard_map.90
  28.2 1.1 %collective-permute-start.8 = (f32[18,128]{1,0:T(8,128)S(1)}, f32[18,128]{1,0:T(8,128)S(1)}, u32[]{:S(2)}, u32[]{:S(2)}) collective-permute-start(f32[18,128]{1,0:T(8,128)S(1)} %get-tuple-element.57), channel_id=1, source_target_pairs={{0,7},{1,6},{2,5},{3,4},{4,3},{5,2},{6,1},{7,0},{8,15},{9,14},{10,... | collective-permute-start | bytes 27656 | tf_op jit(solution)/shard_map/ppermute | solution.py:355
  29.2 0.6 collective-permute-start.9
  29.8 2.1 %collective-permute-start.10 = (f32[16,128]{1,0:T(8,128)S(1)}, f32[16,128]{1,0:T(8,128)S(1)}, u32[]{:S(2)}, u32[]{:S(2)}) collective-permute-start(f32[16,128]{1,0:T(8,128)S(1)} %get-tuple-element.56.refs_5_), channel_id=1, source_target_pairs={{0,3},{1,2},{2,1},{3,0},{4,7},{5,6},{6,5},{7,4},{8,11},{9,10},{10,... | collective-permute-start | bytes 24584 | tf_op jit(solution)/shard_map/ppermute | solution.py:355
  32.0 1.5 %collective-permute-done.10.refs_8_ = f32[16,128]{1,0:T(8,128)S(1)} collective-permute-done((f32[16,128]{1,0:T(8,128)S(1)}, f32[16,128]{1,0:T(8,128)S(1)}, u32[]{:S(2)}, u32[]{:S(2)}) %collective-permute-start.10) | collective-permute-done | bytes 8224 | tf_op jit(solution)/shard_map/ppermute | solution.py:355
  33.5 0.4 collective-permute-done.9.refs_7_
  33.8 0.6 shard_map.91
  34.4 1.4 %collective-permute-start.11 = (f32[16,128]{1,0:T(8,128)S(1)}, f32[16,128]{1,0:T(8,128)S(1)}, u32[]{:S(2)}, u32[]{:S(2)}) collective-permute-start(f32[16,128]{1,0:T(8,128)S(1)} %get-tuple-element.61), channel_id=1, source_target_pairs={{0,7},{1,6},{2,5},{3,4},{4,3},{5,2},{6,1},{7,0},{8,15},{9,14},{10,... | collective-permute-start | bytes 24584 | tf_op jit(solution)/shard_map/ppermute | solution.py:355
  35.8 1.3 %collective-permute-start.12 = (f32[16,128]{1,0:T(8,128)S(1)}, f32[16,128]{1,0:T(8,128)S(1)}, u32[]{:S(2)}, u32[]{:S(2)}) collective-permute-start(f32[16,128]{1,0:T(8,128)S(1)} %get-tuple-element.62), channel_id=1, source_target_pairs={{0,4},{1,5},{2,6},{3,7},{4,0},{5,1},{6,2},{7,3},{8,12},{9,13},{10,... | collective-permute-start | bytes 24584 | tf_op jit(solution)/shard_map/ppermute | solution.py:355
  37.1 1.1 %collective-permute-start.13 = (f32[16,128]{1,0:T(8,128)S(1)}, f32[16,128]{1,0:T(8,128)S(1)}, u32[]{:S(2)}, u32[]{:S(2)}) collective-permute-start(f32[16,128]{1,0:T(8,128)S(1)} %get-tuple-element.60.refs_0_), channel_id=1, source_target_pairs={{0,3},{1,2},{2,1},{3,0},{4,7},{5,6},{6,5},{7,4},{8,11},{9,10},{10,... | collective-permute-start | bytes 24584 | tf_op jit(solution)/shard_map/ppermute | solution.py:355
  38.2 1.1 %collective-permute-done.11.refs_1_ = f32[16,128]{1,0:T(8,128)S(1)} collective-permute-done((f32[16,128]{1,0:T(8,128)S(1)}, f32[16,128]{1,0:T(8,128)S(1)}, u32[]{:S(2)}, u32[]{:S(2)}) %collective-permute-start.11) | collective-permute-done | bytes 8224 | tf_op jit(solution)/shard_map/ppermute | solution.py:355
  39.3 1.1 %collective-permute-done.12.refs_2_ = f32[16,128]{1,0:T(8,128)S(1)} collective-permute-done((f32[16,128]{1,0:T(8,128)S(1)}, f32[16,128]{1,0:T(8,128)S(1)}, u32[]{:S(2)}, u32[]{:S(2)}) %collective-permute-start.12) | collective-permute-done | bytes 8224 | tf_op jit(solution)/shard_map/ppermute | solution.py:355
  40.4 0.1 shard_map.92.topics_ref
  40.5 0.0 collective-permute-start.15
  40.5 0.4 shard_map.93.refs_1_
  40.9 0.8 collective-permute-done.15.topics_ref
  41.7 0.4 shard_map.94
  42.1 2.5 %collective-permute-start.16 = (f32[64,512]{1,0:T(8,128)S(1)}, f32[64,512]{1,0:T(8,128)S(1)}, u32[]{:S(2)}, u32[]{:S(2)}) collective-permute-start(f32[64,512]{1,0:T(8,128)S(1)} %get-tuple-element.88), channel_id=1, source_target_pairs={{0,24},{8,16},{16,8},{24,0},{1,25},{9,17},{17,9},{25,1},{2,26},{10... | collective-permute-start | bytes 393224 | tf_op jit(solution)/shard_map/ppermute | solution.py:369
  44.7 0.5 collective-permute-start.17
  45.1 0.5 collective-permute-start.18
  45.7 1.4 %collective-permute-start.19 = (f32[4,4224]{1,0:T(4,128)S(1)}, f32[4,4224]{1,0:T(4,128)S(1)}, u32[]{:S(2)}, u32[]{:S(2)}) collective-permute-start(f32[4,4224]{1,0:T(4,128)S(1)} %get-tuple-element.70), channel_id=1, source_target_pairs={{0,4},{1,5},{2,6},{3,7},{4,0},{5,1},{6,2},{7,3},{8,12},{9,13},{10,... | collective-permute-start | bytes 202760 | tf_op jit(solution)/shard_map/ppermute | solution.py:355
  47.1 4.5 %collective-permute-done.19.refs_4_.refs_6_.refs_2_ = f32[4,4224]{1,0:T(4,128)S(1)} collective-permute-done((f32[4,4224]{1,0:T(4,128)S(1)}, f32[4,4224]{1,0:T(4,128)S(1)}, u32[]{:S(2)}, u32[]{:S(2)}) %collective-permute-start.19) | collective-permute-done | bytes 67616 | tf_op jit(solution)/shard_map/ppermute | solution.py:355
  51.6 0.1 shard_map.95.refs_0_
  51.7 2.5 %collective-permute-start.20 = (f32[64,512]{1,0:T(8,128)S(1)}, f32[64,512]{1,0:T(8,128)S(1)}, u32[]{:S(2)}, u32[]{:S(2)}) collective-permute-start(f32[64,512]{1,0:T(8,128)S(1)} %shard_map.95.refs_0_), channel_id=1, source_target_pairs={{0,24},{8,16},{16,8},{24,0},{1,25},{9,17},{17,9},{25,1},{2,26},{10... | collective-permute-start | bytes 393224 | tf_op jit(solution)/shard_map/ppermute | solution.py:369
  54.2 0.5 collective-permute-start.24
  54.7 0.5 collective-permute-start.26
  55.2 0.4 collective-permute-start.21
  55.6 1.5 %collective-permute-start.22 = (f32[64,512]{1,0:T(8,128)S(1)}, f32[64,512]{1,0:T(8,128)S(1)}, u32[]{:S(2)}, u32[]{:S(2)}) collective-permute-start(f32[64,512]{1,0:T(8,128)S(1)} %shard_map.95.refs_0_), channel_id=1, source_target_pairs={{0,1},{1,0},{2,3},{3,2},{4,5},{5,4},{6,7},{7,6},{8,9},{9,8},{10,11... | collective-permute-start | bytes 393224 | tf_op jit(solution)/shard_map/ppermute | solution.py:366
  57.1 3.7 %collective-permute-done.21.refs_7_.refs_3_ = f32[4,4224]{1,0:T(4,128)S(1)} collective-permute-done((f32[4,4224]{1,0:T(4,128)S(1)}, f32[4,4224]{1,0:T(4,128)S(1)}, u32[]{:S(2)}, u32[]{:S(2)}) %collective-permute-start.21) | collective-permute-done | bytes 67616 | tf_op jit(solution)/shard_map/ppermute | solution.py:355
  60.8 0.5 collective-permute-start.25
  61.3 0.1 collective-permute-start.27
  61.4 0.5 shard_map.96
  61.9 0.2 collective-permute-done.23.refs_1_
  62.1 0.2 collective-permute-done.25.refs_2_
  62.3 0.3 collective-permute-done.27.refs_3_
  62.7 0.5 shard_map.97
  63.2 1.6 %collective-permute-start.28 = (f32[16,128]{1,0:T(8,128)S(1)}, f32[16,128]{1,0:T(8,128)S(1)}, u32[]{:S(2)}, u32[]{:S(2)}) collective-permute-start(f32[16,128]{1,0:T(8,128)S(1)} %get-tuple-element.76.refs_4_), channel_id=1, source_target_pairs={{0,7},{1,6},{2,5},{3,4},{4,3},{5,2},{6,1},{7,0},{8,15},{9,14},{10,... | collective-permute-start | bytes 24584 | tf_op jit(solution)/shard_map/ppermute | solution.py:355
  64.7 0.6 collective-permute-start.29
  65.4 1.7 %collective-permute-start.30 = (f32[16,128]{1,0:T(8,128)S(1)}, f32[16,128]{1,0:T(8,128)S(1)}, u32[]{:S(2)}, u32[]{:S(2)}) collective-permute-start(f32[16,128]{1,0:T(8,128)S(1)} %get-tuple-element.76.refs_4_), channel_id=1, source_target_pairs={{0,3},{1,2},{2,1},{3,0},{4,7},{5,6},{6,5},{7,4},{8,11},{9,10},{10,... | collective-permute-start | bytes 24584 | tf_op jit(solution)/shard_map/ppermute | solution.py:355
  67.0 1.0 %collective-permute-done.28.refs_5_ = f32[16,128]{1,0:T(8,128)S(1)} collective-permute-done((f32[16,128]{1,0:T(8,128)S(1)}, f32[16,128]{1,0:T(8,128)S(1)}, u32[]{:S(2)}, u32[]{:S(2)}) %collective-permute-start.28) | collective-permute-done | bytes 8224 | tf_op jit(solution)/shard_map/ppermute | solution.py:355
  68.1 1.2 %collective-permute-done.29.refs_6_ = f32[16,128]{1,0:T(8,128)S(1)} collective-permute-done((f32[16,128]{1,0:T(8,128)S(1)}, f32[16,128]{1,0:T(8,128)S(1)}, u32[]{:S(2)}, u32[]{:S(2)}) %collective-permute-start.29) | collective-permute-done | bytes 8224 | tf_op jit(solution)/shard_map/ppermute | solution.py:355
  69.3 0.7 shard_map.98
  70.0 0.9 %collective-permute-start.31 = (f32[4,128]{1,0:T(4,128)S(1)}, f32[4,128]{1,0:T(4,128)S(1)}, u32[]{:S(2)}, u32[]{:S(2)}) collective-permute-start(f32[4,128]{1,0:T(4,128)S(1)} %get-tuple-element.83), channel_id=1, source_target_pairs={{0,7},{1,6},{2,5},{3,4},{4,3},{5,2},{6,1},{7,0},{8,15},{9,14},{10,... | collective-permute-start | bytes 6152 | tf_op jit(solution)/shard_map/ppermute | solution.py:355
  70.9 1.4 %collective-permute-start.32 = (f32[4,128]{1,0:T(4,128)S(1)}, f32[4,128]{1,0:T(4,128)S(1)}, u32[]{:S(2)}, u32[]{:S(2)}) collective-permute-start(f32[4,128]{1,0:T(4,128)S(1)} %get-tuple-element.84), channel_id=1, source_target_pairs={{0,4},{1,5},{2,6},{3,7},{4,0},{5,1},{6,2},{7,3},{8,12},{9,13},{10,... | collective-permute-start | bytes 6152 | tf_op jit(solution)/shard_map/ppermute | solution.py:355
  72.4 1.5 %collective-permute-start.33 = (f32[4,128]{1,0:T(4,128)S(1)}, f32[4,128]{1,0:T(4,128)S(1)}, u32[]{:S(2)}, u32[]{:S(2)}) collective-permute-start(f32[4,128]{1,0:T(4,128)S(1)} %get-tuple-element.85), channel_id=1, source_target_pairs={{0,3},{1,2},{2,1},{3,0},{4,7},{5,6},{6,5},{7,4},{8,11},{9,10},{10,... | collective-permute-start | bytes 6152 | tf_op jit(solution)/shard_map/ppermute | solution.py:355
  73.8 0.7 copy.9
  74.5 0.3 collective-permute-done.31.refs_1_
  74.8 0.6 collective-permute-done.32.refs_2_
  75.4 0.6 shard_map.99
  (28 shorter events, 0.1 us)
Async XLA Ops:
  0.6 10.1 %copy-start = (f32[1,2048,64]{1,2,0:T(8,128)S(1)}, f32[1,2048,64]{1,2,0:T(8,128)}, u32[]{:S(2)}) copy-start(f32[1,2048,64]{1,2,0:T(8,128)} %param.10) | copy-start | bytes 1572868
  0.6 10.1 %collective-permute-start = (f32[64,2048]{1,0:T(8,128)}, f32[64,2048]{1,0:T(8,128)S(1)}, u32[]{:S(2)}, u32[]{:S(2)}) collective-permute-start(f32[64,2048]{1,0:T(8,128)} %bitcast.10), channel_id=1, source_target_pairs={{0,1},{1,0},{2,3},{3,2},{4,5},{5,4},{6,7},{7,6},{8,9},{9,8},{10,11... | collective-permute-start | bytes 1572872 | tf_op jit(solution)/shard_map/ppermute | solution.py:366
  3.1 5.4 %copy-start.2 = (f32[4,64]{1,0:T(4,128)S(1)}, f32[4,64]{1,0:T(4,128)}, u32[]{:S(2)}) copy-start(f32[4,64]{1,0:T(4,128)} %topics_ref.1) | copy-start | bytes 3076
  3.1 15.5 %collective-permute-start.1 = (f32[8,4224]{1,0:T(8,128)S(1)}, f32[8,4224]{1,0:T(8,128)S(1)}, u32[]{:S(2)}, u32[]{:S(2)}) collective-permute-start(f32[8,4224]{1,0:T(8,128)S(1)} %get-tuple-element.47), channel_id=1, source_target_pairs={{0,7},{1,6},{2,5},{3,4},{4,3},{5,2},{6,1},{7,0},{8,15},{9,14},{10,... | collective-permute-start | bytes 405512 | tf_op jit(solution)/shard_map/ppermute | solution.py:355
  7.9 10.7 %collective-permute-start.2 = (f32[8,4224]{1,0:T(8,128)S(1)}, f32[8,4224]{1,0:T(8,128)S(1)}, u32[]{:S(2)}, u32[]{:S(2)}) collective-permute-start(f32[8,4224]{1,0:T(8,128)S(1)} %get-tuple-element.48), channel_id=1, source_target_pairs={{0,3},{1,2},{2,1},{3,0},{4,7},{5,6},{6,5},{7,4},{8,11},{9,10},{10,... | collective-permute-start | bytes 405512 | tf_op jit(solution)/shard_map/ppermute | solution.py:355
  7.9 11.9 %collective-permute-start.3 = (f32[8,4224]{1,0:T(8,128)S(1)}, f32[8,4224]{1,0:T(8,128)S(1)}, u32[]{:S(2)}, u32[]{:S(2)}) collective-permute-start(f32[8,4224]{1,0:T(8,128)S(1)} %get-tuple-element.49), channel_id=1, source_target_pairs={{0,4},{1,5},{2,6},{3,7},{4,0},{5,1},{6,2},{7,3},{8,12},{9,13},{10,... | collective-permute-start | bytes 405512 | tf_op jit(solution)/shard_map/ppermute | solution.py:355
  8.6 1.0 %copy-start.1 = (s32[4,16384]{1,0:T(4,128)S(1)}, s32[4,16384]{1,0:T(4,128)}, u32[]{:S(2)}) copy-start(s32[4,16384]{1,0:T(4,128)} %counts_ref.1) | copy-start | bytes 786436
  9.6 1.2 %copy-start.3 = (s32[1,64]{1,0:T(1,128)S(1)}, s32[1,64]{1,0:T(1,128)}, u32[]{:S(2)}) copy-start(s32[1,64]{1,0:T(1,128)} %perm_hbm.1) | copy-start | bytes 772
  9.6 9.0 %collective-permute-start.4 = (f32[4,4224]{1,0:T(4,128)S(1)}, f32[4,4224]{1,0:T(4,128)S(1)}, u32[]{:S(2)}, u32[]{:S(2)}) collective-permute-start(f32[4,4224]{1,0:T(4,128)S(1)} %get-tuple-element.51), channel_id=1, source_target_pairs={{0,3},{1,2},{2,1},{3,0},{4,7},{5,6},{6,5},{7,4},{8,11},{9,10},{10,... | collective-permute-start | bytes 202760 | tf_op jit(solution)/shard_map/ppermute | solution.py:355
  20.4 20.0 %collective-permute-start.14 = (f32[32,2048]{1,0:T(8,128)S(1)}, f32[32,2048]{1,0:T(8,128)S(1)}, u32[]{:S(2)}, u32[]{:S(2)}) collective-permute-start(f32[32,2048]{1,0:T(8,128)S(1)} %get-tuple-element.63), channel_id=1, source_target_pairs={{0,1},{1,0},{2,3},{3,2},{4,5},{5,4},{6,7},{7,6},{8,9},{9,8},{10,11... | collective-permute-start | bytes 786440 | tf_op jit(solution)/shard_map/ppermute | solution.py:366
  20.4 5.0 %collective-permute-start.5 = (f32[24,128]{1,0:T(8,128)S(1)}, f32[24,128]{1,0:T(8,128)S(1)}, u32[]{:S(2)}, u32[]{:S(2)}) collective-permute-start(f32[24,128]{1,0:T(8,128)S(1)} %get-tuple-element.53.refs_4_), channel_id=1, source_target_pairs={{0,7},{1,6},{2,5},{3,4},{4,3},{5,2},{6,1},{7,0},{8,15},{9,14},{10,... | collective-permute-start | bytes 36872 | tf_op jit(solution)/shard_map/ppermute | solution.py:355
  23.0 4.6 %collective-permute-start.6 = (f32[24,128]{1,0:T(8,128)S(1)}, f32[24,128]{1,0:T(8,128)S(1)}, u32[]{:S(2)}, u32[]{:S(2)}) collective-permute-start(f32[24,128]{1,0:T(8,128)S(1)} %get-tuple-element.53.refs_4_), channel_id=1, source_target_pairs={{0,4},{1,5},{2,6},{3,7},{4,0},{5,1},{6,2},{7,3},{8,12},{9,13},{10,... | collective-permute-start | bytes 36872 | tf_op jit(solution)/shard_map/ppermute | solution.py:355
  23.0 4.6 %collective-permute-start.7 = (f32[24,128]{1,0:T(8,128)S(1)}, f32[24,128]{1,0:T(8,128)S(1)}, u32[]{:S(2)}, u32[]{:S(2)}) collective-permute-start(f32[24,128]{1,0:T(8,128)S(1)} %get-tuple-element.53.refs_4_), channel_id=1, source_target_pairs={{0,3},{1,2},{2,1},{3,0},{4,7},{5,6},{6,5},{7,4},{8,11},{9,10},{10,... | collective-permute-start | bytes 36872 | tf_op jit(solution)/shard_map/ppermute | solution.py:355
  28.2 5.7 %collective-permute-start.8 = (f32[18,128]{1,0:T(8,128)S(1)}, f32[18,128]{1,0:T(8,128)S(1)}, u32[]{:S(2)}, u32[]{:S(2)}) collective-permute-start(f32[18,128]{1,0:T(8,128)S(1)} %get-tuple-element.57), channel_id=1, source_target_pairs={{0,7},{1,6},{2,5},{3,4},{4,3},{5,2},{6,1},{7,0},{8,15},{9,14},{10,... | collective-permute-start | bytes 27656 | tf_op jit(solution)/shard_map/ppermute | solution.py:355
  29.2 4.6 %collective-permute-start.9 = (f32[17,128]{1,0:T(8,128)S(1)}, f32[17,128]{1,0:T(8,128)S(1)}, u32[]{:S(2)}, u32[]{:S(2)}) collective-permute-start(f32[17,128]{1,0:T(8,128)S(1)} %get-tuple-element.58), channel_id=1, source_target_pairs={{0,4},{1,5},{2,6},{3,7},{4,0},{5,1},{6,2},{7,3},{8,12},{9,13},{10,... | collective-permute-start | bytes 26120 | tf_op jit(solution)/shard_map/ppermute | solution.py:355
  29.8 3.6 %collective-permute-start.10 = (f32[16,128]{1,0:T(8,128)S(1)}, f32[16,128]{1,0:T(8,128)S(1)}, u32[]{:S(2)}, u32[]{:S(2)}) collective-permute-start(f32[16,128]{1,0:T(8,128)S(1)} %get-tuple-element.56.refs_5_), channel_id=1, source_target_pairs={{0,3},{1,2},{2,1},{3,0},{4,7},{5,6},{6,5},{7,4},{8,11},{9,10},{10,... | collective-permute-start | bytes 24584 | tf_op jit(solution)/shard_map/ppermute | solution.py:355
  34.4 4.9 %collective-permute-start.11 = (f32[16,128]{1,0:T(8,128)S(1)}, f32[16,128]{1,0:T(8,128)S(1)}, u32[]{:S(2)}, u32[]{:S(2)}) collective-permute-start(f32[16,128]{1,0:T(8,128)S(1)} %get-tuple-element.61), channel_id=1, source_target_pairs={{0,7},{1,6},{2,5},{3,4},{4,3},{5,2},{6,1},{7,0},{8,15},{9,14},{10,... | collective-permute-start | bytes 24584 | tf_op jit(solution)/shard_map/ppermute | solution.py:355
  35.8 4.5 %collective-permute-start.12 = (f32[16,128]{1,0:T(8,128)S(1)}, f32[16,128]{1,0:T(8,128)S(1)}, u32[]{:S(2)}, u32[]{:S(2)}) collective-permute-start(f32[16,128]{1,0:T(8,128)S(1)} %get-tuple-element.62), channel_id=1, source_target_pairs={{0,4},{1,5},{2,6},{3,7},{4,0},{5,1},{6,2},{7,3},{8,12},{9,13},{10,... | collective-permute-start | bytes 24584 | tf_op jit(solution)/shard_map/ppermute | solution.py:355
  37.1 3.3 %collective-permute-start.13 = (f32[16,128]{1,0:T(8,128)S(1)}, f32[16,128]{1,0:T(8,128)S(1)}, u32[]{:S(2)}, u32[]{:S(2)}) collective-permute-start(f32[16,128]{1,0:T(8,128)S(1)} %get-tuple-element.60.refs_0_), channel_id=1, source_target_pairs={{0,3},{1,2},{2,1},{3,0},{4,7},{5,6},{6,5},{7,4},{8,11},{9,10},{10,... | collective-permute-start | bytes 24584 | tf_op jit(solution)/shard_map/ppermute | solution.py:355
  40.5 1.2 %collective-permute-start.15 = (f32[32,128]{1,0:T(8,128)S(1)}, f32[32,128]{1,0:T(8,128)S(1)}, u32[]{:S(2)}, u32[]{:S(2)}) collective-permute-start(f32[32,128]{1,0:T(8,128)S(1)} %shard_map.92.topics_ref), channel_id=1, source_target_pairs={{0,1},{1,0},{2,3},{3,2},{4,5},{5,4},{6,7},{7,6},{8,9},{9,8},{10,11... | collective-permute-start | bytes 49160 | tf_op jit(solution)/shard_map/ppermute | solution.py:366
  42.1 9.5 %collective-permute-start.16 = (f32[64,512]{1,0:T(8,128)S(1)}, f32[64,512]{1,0:T(8,128)S(1)}, u32[]{:S(2)}, u32[]{:S(2)}) collective-permute-start(f32[64,512]{1,0:T(8,128)S(1)} %get-tuple-element.88), channel_id=1, source_target_pairs={{0,24},{8,16},{16,8},{24,0},{1,25},{9,17},{17,9},{25,1},{2,26},{10... | collective-permute-start | bytes 393224 | tf_op jit(solution)/shard_map/ppermute | solution.py:369
  44.7 6.9 %collective-permute-start.17 = (f32[64,512]{1,0:T(8,128)S(1)}, f32[64,512]{1,0:T(8,128)S(1)}, u32[]{:S(2)}, u32[]{:S(2)}) collective-permute-start(f32[64,512]{1,0:T(8,128)S(1)} %get-tuple-element.87), channel_id=1, source_target_pairs={{0,16},{8,24},{16,0},{24,8},{1,17},{9,25},{17,1},{25,9},{2,18},{10... | collective-permute-start | bytes 393224 | tf_op jit(solution)/shard_map/ppermute | solution.py:369
  45.1 6.5 %collective-permute-start.18 = (f32[64,512]{1,0:T(8,128)S(1)}, f32[64,512]{1,0:T(8,128)S(1)}, u32[]{:S(2)}, u32[]{:S(2)}) collective-permute-start(f32[64,512]{1,0:T(8,128)S(1)} %get-tuple-element.86), channel_id=1, source_target_pairs={{0,8},{8,0},{16,24},{24,16},{1,9},{9,1},{17,25},{25,17},{2,10},{10... | collective-permute-start | bytes 393224 | tf_op jit(solution)/shard_map/ppermute | solution.py:369
  45.7 5.9 %collective-permute-start.19 = (f32[4,4224]{1,0:T(4,128)S(1)}, f32[4,4224]{1,0:T(4,128)S(1)}, u32[]{:S(2)}, u32[]{:S(2)}) collective-permute-start(f32[4,4224]{1,0:T(4,128)S(1)} %get-tuple-element.70), channel_id=1, source_target_pairs={{0,4},{1,5},{2,6},{3,7},{4,0},{5,1},{6,2},{7,3},{8,12},{9,13},{10,... | collective-permute-start | bytes 202760 | tf_op jit(solution)/shard_map/ppermute | solution.py:355
  51.7 9.1 %collective-permute-start.20 = (f32[64,512]{1,0:T(8,128)S(1)}, f32[64,512]{1,0:T(8,128)S(1)}, u32[]{:S(2)}, u32[]{:S(2)}) collective-permute-start(f32[64,512]{1,0:T(8,128)S(1)} %shard_map.95.refs_0_), channel_id=1, source_target_pairs={{0,24},{8,16},{16,8},{24,0},{1,25},{9,17},{17,9},{25,1},{2,26},{10... | collective-permute-start | bytes 393224 | tf_op jit(solution)/shard_map/ppermute | solution.py:369
  54.2 6.6 %collective-permute-start.24 = (f32[64,512]{1,0:T(8,128)S(1)}, f32[64,512]{1,0:T(8,128)S(1)}, u32[]{:S(2)}, u32[]{:S(2)}) collective-permute-start(f32[64,512]{1,0:T(8,128)S(1)} %shard_map.95.refs_0_), channel_id=1, source_target_pairs={{0,16},{8,24},{16,0},{24,8},{1,17},{9,25},{17,1},{25,9},{2,18},{10... | collective-permute-start | bytes 393224 | tf_op jit(solution)/shard_map/ppermute | solution.py:369
  54.7 6.6 %collective-permute-start.26 = (f32[64,512]{1,0:T(8,128)S(1)}, f32[64,512]{1,0:T(8,128)S(1)}, u32[]{:S(2)}, u32[]{:S(2)}) collective-permute-start(f32[64,512]{1,0:T(8,128)S(1)} %shard_map.95.refs_0_), channel_id=1, source_target_pairs={{0,8},{8,0},{16,24},{24,16},{1,9},{9,1},{17,25},{25,17},{2,10},{10... | collective-permute-start | bytes 393224 | tf_op jit(solution)/shard_map/ppermute | solution.py:369
  55.2 5.6 %collective-permute-start.21 = (f32[4,4224]{1,0:T(4,128)S(1)}, f32[4,4224]{1,0:T(4,128)S(1)}, u32[]{:S(2)}, u32[]{:S(2)}) collective-permute-start(f32[4,4224]{1,0:T(4,128)S(1)} %get-tuple-element.72), channel_id=1, source_target_pairs={{0,7},{1,6},{2,5},{3,4},{4,3},{5,2},{6,1},{7,0},{8,15},{9,14},{10,... | collective-permute-start | bytes 202760 | tf_op jit(solution)/shard_map/ppermute | solution.py:355
  55.6 6.3 %collective-permute-start.22 = (f32[64,512]{1,0:T(8,128)S(1)}, f32[64,512]{1,0:T(8,128)S(1)}, u32[]{:S(2)}, u32[]{:S(2)}) collective-permute-start(f32[64,512]{1,0:T(8,128)S(1)} %shard_map.95.refs_0_), channel_id=1, source_target_pairs={{0,1},{1,0},{2,3},{3,2},{4,5},{5,4},{6,7},{7,6},{8,9},{9,8},{10,11... | collective-permute-start | bytes 393224 | tf_op jit(solution)/shard_map/ppermute | solution.py:366
  60.8 1.3 %collective-permute-start.23 = (f32[64,512]{1,0:T(8,128)S(1)}, f32[64,512]{1,0:T(8,128)S(1)}, u32[]{:S(2)}, u32[]{:S(2)}) collective-permute-start(f32[64,512]{1,0:T(8,128)S(1)} %collective-permute-done.20.refs_1_), channel_id=1, source_target_pairs={{0,1},{1,0},{2,3},{3,2},{4,5},{5,4},{6,7},{7,6},{8,9},{9,8},{10,11... | collective-permute-start | bytes 393224 | tf_op jit(solution)/shard_map/ppermute | solution.py:366
  60.8 1.5 %collective-permute-start.25 = (f32[64,512]{1,0:T(8,128)S(1)}, f32[64,512]{1,0:T(8,128)S(1)}, u32[]{:S(2)}, u32[]{:S(2)}) collective-permute-start(f32[64,512]{1,0:T(8,128)S(1)} %collective-permute-done.24.refs_2_), channel_id=1, source_target_pairs={{0,1},{1,0},{2,3},{3,2},{4,5},{5,4},{6,7},{7,6},{8,9},{9,8},{10,11... | collective-permute-start | bytes 393224 | tf_op jit(solution)/shard_map/ppermute | solution.py:366
  61.3 1.3 %collective-permute-start.27 = (f32[64,512]{1,0:T(8,128)S(1)}, f32[64,512]{1,0:T(8,128)S(1)}, u32[]{:S(2)}, u32[]{:S(2)}) collective-permute-start(f32[64,512]{1,0:T(8,128)S(1)} %collective-permute-done.26.refs_3_), channel_id=1, source_target_pairs={{0,1},{1,0},{2,3},{3,2},{4,5},{5,4},{6,7},{7,6},{8,9},{9,8},{10,11... | collective-permute-start | bytes 393224 | tf_op jit(solution)/shard_map/ppermute | solution.py:366
  63.2 4.9 %collective-permute-start.28 = (f32[16,128]{1,0:T(8,128)S(1)}, f32[16,128]{1,0:T(8,128)S(1)}, u32[]{:S(2)}, u32[]{:S(2)}) collective-permute-start(f32[16,128]{1,0:T(8,128)S(1)} %get-tuple-element.76.refs_4_), channel_id=1, source_target_pairs={{0,7},{1,6},{2,5},{3,4},{4,3},{5,2},{6,1},{7,0},{8,15},{9,14},{10,... | collective-permute-start | bytes 24584 | tf_op jit(solution)/shard_map/ppermute | solution.py:355
  64.7 4.5 %collective-permute-start.29 = (f32[16,128]{1,0:T(8,128)S(1)}, f32[16,128]{1,0:T(8,128)S(1)}, u32[]{:S(2)}, u32[]{:S(2)}) collective-permute-start(f32[16,128]{1,0:T(8,128)S(1)} %get-tuple-element.76.refs_4_), channel_id=1, source_target_pairs={{0,4},{1,5},{2,6},{3,7},{4,0},{5,1},{6,2},{7,3},{8,12},{9,13},{10,... | collective-permute-start | bytes 24584 | tf_op jit(solution)/shard_map/ppermute | solution.py:355
  65.4 3.9 %collective-permute-start.30 = (f32[16,128]{1,0:T(8,128)S(1)}, f32[16,128]{1,0:T(8,128)S(1)}, u32[]{:S(2)}, u32[]{:S(2)}) collective-permute-start(f32[16,128]{1,0:T(8,128)S(1)} %get-tuple-element.76.refs_4_), channel_id=1, source_target_pairs={{0,3},{1,2},{2,1},{3,0},{4,7},{5,6},{6,5},{7,4},{8,11},{9,10},{10,... | collective-permute-start | bytes 24584 | tf_op jit(solution)/shard_map/ppermute | solution.py:355
  70.0 4.8 %collective-permute-start.31 = (f32[4,128]{1,0:T(4,128)S(1)}, f32[4,128]{1,0:T(4,128)S(1)}, u32[]{:S(2)}, u32[]{:S(2)}) collective-permute-start(f32[4,128]{1,0:T(4,128)S(1)} %get-tuple-element.83), channel_id=1, source_target_pairs={{0,7},{1,6},{2,5},{3,4},{4,3},{5,2},{6,1},{7,0},{8,15},{9,14},{10,... | collective-permute-start | bytes 6152 | tf_op jit(solution)/shard_map/ppermute | solution.py:355
  70.9 4.5 %collective-permute-start.32 = (f32[4,128]{1,0:T(4,128)S(1)}, f32[4,128]{1,0:T(4,128)S(1)}, u32[]{:S(2)}, u32[]{:S(2)}) collective-permute-start(f32[4,128]{1,0:T(4,128)S(1)} %get-tuple-element.84), channel_id=1, source_target_pairs={{0,4},{1,5},{2,6},{3,7},{4,0},{5,1},{6,2},{7,3},{8,12},{9,13},{10,... | collective-permute-start | bytes 6152 | tf_op jit(solution)/shard_map/ppermute | solution.py:355
  72.4 3.1 %collective-permute-start.33 = (f32[4,128]{1,0:T(4,128)S(1)}, f32[4,128]{1,0:T(4,128)S(1)}, u32[]{:S(2)}, u32[]{:S(2)}) collective-permute-start(f32[4,128]{1,0:T(4,128)S(1)} %get-tuple-element.85), channel_id=1, source_target_pairs={{0,3},{1,2},{2,1},{3,0},{4,7},{5,6},{6,5},{7,4},{8,11},{9,10},{10,... | collective-permute-start | bytes 6152 | tf_op jit(solution)/shard_map/ppermute | solution.py:355

commit v5 on v4

--- a/solution.py
+++ b/solution.py
@@ -79,16 +79,16 @@
     for copy in small:
         copy.start()
     steps = list(range(chips - 1, -1, -1))
+    at_chip = lax.axis_index("doc") // cores
     arriving = {}
     for step in steps:
-        for half, block in enumerate(blocks_of(chips, cores, step)):
-            at = slice(half * own_words, (half + 1) * own_words)
-            arriving[step, half] = pltpu.make_async_copy(
-                counts_hbm.at[:, pl.ds(pl.multiple_of(block * own_words, 128), own_words)],
-                counts_ref.at[step, :, at],
-                in_sems.at[step, half],
-            )
-            arriving[step, half].start()
+        first = (at_chip ^ step) * cores * own_words
+        arriving[step] = pltpu.make_async_copy(
+            counts_hbm.at[:, pl.ds(pl.multiple_of(first, 128), cores * own_words)],
+            counts_ref.at[step],
+            in_sems.at[step],
+        )
+        arriving[step].start()
     docs, tiles = mask_ref.shape
     width = chips * cores * own_words // tiles
     own_tiles = own_words // width
@@ -106,10 +106,13 @@
     for step in steps:
         for half, block in enumerate(blocks_of(chips, cores, step)):
             near = pltpu.roll(occupied, lax.rem(tiles - block * own_tiles, tiles), 1)
-            arriving[step, half].wait()
+            if half == 0:
+                arriving[step].wait()
+            first = lax.rem(block, cores) * own_words
             for tile in range(own_tiles):
                 at = slice(half * own_words + tile * width, half * own_words + (tile + 1) * width)
-                picked = counts_ref[step, :, at].astype(jnp.float32)
+                picked = counts_ref[step, :, pl.ds(pl.multiple_of(first + tile * width, 128), width)]
+                picked = picked.astype(jnp.float32)
                 out_refs[step][:, at] = picked * near[:, tile : tile + 1]
         out_refs[step][:, cores * own_words :] = topics
 
@@ -379,7 +382,7 @@
             pltpu.VMEM(align_perm.shape, jnp.int32),
             pltpu.VMEM((chips, docs, span), jnp.int32),
             pltpu.SemaphoreType.DMA((3,)),
-            pltpu.SemaphoreType.DMA((chips, cores)),
+            pltpu.SemaphoreType.DMA((chips,)),
         ],
         compiler_params=pltpu.CompilerParams(vmem_limit_bytes=VMEM_BYTES),
         cost_estimate=pl.CostEstimate(flops=0, bytes_accessed=12 * counts.size, transcendentals=0),

time: 76.2 us -> 75.9 us (level)
  transfers between devices with their start and end apart: 34 -> 34, of which waited for: 18 -> 18; matrix products, arithmetic and copies ran while one was open for 1% -> 1% of each run, Pallas kernels for 7% -> 6%
where the time goes in v5:
time: 75.9 us; the launch traced here: 75.7 us
  starting transfers between devices  37.4 us (49%)
  waiting for transfers between devices  28.2 us (37%)
  Pallas kernels  7.75 us (10%)
  local copies, waits for them, and re-layouts  1.67 us (2%)
  between operations  0.77 us (1%)
    ppermute x21, starting transfers between devices, over_chips(): lax.ppermute(array, 'doc', [(c * cores + k, (c ^ step) * cores + (k + ste...  27.7 us
    ppermute x21, waiting for transfers between devices, over_chips(): lax.ppermute(array, 'doc', [(c * cores + k, (c ^ step) * cores + (k + ste...  26.6 us
    ppermute x6, starting transfers between devices, over_pert(): return lax.ppermute(array, 'pert', [(m, m ^ step) for m in range(members)])  7.11 us
    pallas_call x13, Pallas kernels, call(): pl.pallas_call(kernel, out_shape=outs, in_specs=[pl.BlockSpec(memory_spac...  6.08 us
    ppermute x7, starting transfers between devices, over_cores(): return lax.ppermute(array, 'doc', [(d, d ^ 1) for d in range(doc_size)])  2.6 us
    pallas_call x1, Pallas kernels, per_device(): pl.pallas_call(functools.partial(spread_kernel, chips, cores, owned), out...  1.67 us
    unnamed x9, local copies, waits for them, and re-layouts  1.62 us
    ppermute x7, waiting for transfers between devices, over_cores(): return lax.ppermute(array, 'doc', [(d, d ^ 1) for d in range(doc_size)])  1.52 us
  transfers between devices with their start and end apart: 34, of which 18 were waited for; matrix products, arithmetic and copies ran while one was open for 1% of the time, Pallas kernels for 6%

profile of v5, /device:TPU:0, one launch (start us, length us, event | category | flops | bytes accessed | tf_op | source)
XLA Modules:
  0.0 75.7 jit_solution(15147552850709540468)
XLA Ops:
  0.6 0.5 collective-permute-start
  1.2 1.7 %shard_map.87 = (f32[8,4224]{1,0:T(8,128)S(1)}, f32[8,4224]{1,0:T(8,128)S(1)}, f32[8,4224]{1,0:T(8,128)S(1)}, f32[8,4224]{1,0:T(8,128)S(1)}) custom-call(s32[8,128]{1,0:T(8,128)} %bitcast.13, f32[8,64]{1,0:T(8,128)} %bitcast.14, s32[1,64]{1,0:T(1,128)} %perm_hbm.1, s32[8,16384]{1,0:T(8,128)} %bitcast.12), custom_call_target="tpu_custom_call" | custom-call | bytes 1572864 | tf_op jit(solution)/shard_map/pallas_call | solution.py:374
  2.9 4.8 %collective-permute-start.1 = (f32[8,4224]{1,0:T(8,128)S(1)}, f32[8,4224]{1,0:T(8,128)S(1)}, u32[]{:S(2)}, u32[]{:S(2)}) collective-permute-start(f32[8,4224]{1,0:T(8,128)S(1)} %get-tuple-element.47), channel_id=1, source_target_pairs={{0,7},{1,6},{2,5},{3,4},{4,3},{5,2},{6,1},{7,0},{8,15},{9,14},{10,... | collective-permute-start | bytes 405512 | tf_op jit(solution)/shard_map/ppermute | solution.py:358
  7.6 0.6 collective-permute-start.3
  8.3 0.9 %copy-done.1 = s32[4,16384]{1,0:T(4,128)S(1)} copy-done((s32[4,16384]{1,0:T(4,128)S(1)}, s32[4,16384]{1,0:T(4,128)}, u32[]{:S(2)}) %copy-start.1) | copy-done | bytes 262168
  9.2 0.1 shard_map.88
  9.3 1.1 %collective-permute-start.4 = (f32[4,4224]{1,0:T(4,128)S(1)}, f32[4,4224]{1,0:T(4,128)S(1)}, u32[]{:S(2)}, u32[]{:S(2)}) collective-permute-start(f32[4,4224]{1,0:T(4,128)S(1)} %get-tuple-element.51), channel_id=1, source_target_pairs={{0,3},{1,2},{2,1},{3,0},{4,7},{5,6},{6,5},{7,4},{8,11},{9,10},{10,... | collective-permute-start | bytes 202760 | tf_op jit(solution)/shard_map/ppermute | solution.py:358
  10.4 1.1 %shard_map.86 = (bf16[128,4096]{1,0:T(8,128)(2,1)S(1)}, bf16[4096,128]{1,0:T(8,128)(2,1)S(1)}, f32[8,128]{1,0:T(8,128)S(1)}, f32[64,2048]{1,0:T(8,128)S(1)}) custom-call(s32[1,64]{1,0:T(1,128)S(1)} %copy-done.3, f32[64,2048]{1,0:T(8,128)S(1)} %bitcast.11, f32[64,2048]{1,0:T(8,128)S(1)} %collective-permute-done.refs_1_), custom_call_target="tpu_custom_call" | custom-call | bytes 4194304 | tf_op jit(solution)/shard_map/pallas_call | solution.py:37
  11.6 6.8 %collective-permute-done.4.refs_4_.refs_5_.refs_1_ = f32[4,4224]{1,0:T(4,128)S(1)} collective-permute-done((f32[4,4224]{1,0:T(4,128)S(1)}, f32[4,4224]{1,0:T(4,128)S(1)}, u32[]{:S(2)}, u32[]{:S(2)}) %collective-permute-start.4) | collective-permute-done | bytes 67616 | tf_op jit(solution)/shard_map/ppermute | solution.py:358
  18.3 1.2 %collective-permute-done.3.refs_2_.refs_1_ = f32[8,4224]{1,0:T(8,128)S(1)} collective-permute-done((f32[8,4224]{1,0:T(8,128)S(1)}, f32[8,4224]{1,0:T(8,128)S(1)}, u32[]{:S(2)}, u32[]{:S(2)}) %collective-permute-start.3) | collective-permute-done | bytes 135200 | tf_op jit(solution)/shard_map/ppermute | solution.py:358
  19.6 0.5 shard_map.89
  20.1 2.6 %collective-permute-start.5 = (f32[24,128]{1,0:T(8,128)S(1)}, f32[24,128]{1,0:T(8,128)S(1)}, u32[]{:S(2)}, u32[]{:S(2)}) collective-permute-start(f32[24,128]{1,0:T(8,128)S(1)} %get-tuple-element.53.refs_4_), channel_id=1, source_target_pairs={{0,7},{1,6},{2,5},{3,4},{4,3},{5,2},{6,1},{7,0},{8,15},{9,14},{10,... | collective-permute-start | bytes 36872 | tf_op jit(solution)/shard_map/ppermute | solution.py:358
  22.7 1.3 %collective-permute-start.7 = (f32[24,128]{1,0:T(8,128)S(1)}, f32[24,128]{1,0:T(8,128)S(1)}, u32[]{:S(2)}, u32[]{:S(2)}) collective-permute-start(f32[24,128]{1,0:T(8,128)S(1)} %get-tuple-element.53.refs_4_), channel_id=1, source_target_pairs={{0,3},{1,2},{2,1},{3,0},{4,7},{5,6},{6,5},{7,4},{8,11},{9,10},{10,... | collective-permute-start | bytes 36872 | tf_op jit(solution)/shard_map/ppermute | solution.py:358
  24.0 1.1 %collective-permute-done.5.refs_5_ = f32[24,128]{1,0:T(8,128)S(1)} collective-permute-done((f32[24,128]{1,0:T(8,128)S(1)}, f32[24,128]{1,0:T(8,128)S(1)}, u32[]{:S(2)}, u32[]{:S(2)}) %collective-permute-start.5) | collective-permute-done | bytes 12320 | tf_op jit(solution)/shard_map/ppermute | solution.py:358
  25.1 2.2 %collective-permute-done.6.refs_6_ = f32[24,128]{1,0:T(8,128)S(1)} collective-permute-done((f32[24,128]{1,0:T(8,128)S(1)}, f32[24,128]{1,0:T(8,128)S(1)}, u32[]{:S(2)}, u32[]{:S(2)}) %collective-permute-start.6) | collective-permute-done | bytes 12320 | tf_op jit(solution)/shard_map/ppermute | solution.py:358
  27.3 0.6 shard_map.90
  27.9 1.1 %collective-permute-start.8 = (f32[18,128]{1,0:T(8,128)S(1)}, f32[18,128]{1,0:T(8,128)S(1)}, u32[]{:S(2)}, u32[]{:S(2)}) collective-permute-start(f32[18,128]{1,0:T(8,128)S(1)} %get-tuple-element.57), channel_id=1, source_target_pairs={{0,7},{1,6},{2,5},{3,4},{4,3},{5,2},{6,1},{7,0},{8,15},{9,14},{10,... | collective-permute-start | bytes 27656 | tf_op jit(solution)/shard_map/ppermute | solution.py:358
  28.9 0.6 collective-permute-start.9
  29.6 2.2 %collective-permute-start.10 = (f32[16,128]{1,0:T(8,128)S(1)}, f32[16,128]{1,0:T(8,128)S(1)}, u32[]{:S(2)}, u32[]{:S(2)}) collective-permute-start(f32[16,128]{1,0:T(8,128)S(1)} %get-tuple-element.56.refs_5_), channel_id=1, source_target_pairs={{0,3},{1,2},{2,1},{3,0},{4,7},{5,6},{6,5},{7,4},{8,11},{9,10},{10,... | collective-permute-start | bytes 24584 | tf_op jit(solution)/shard_map/ppermute | solution.py:358
  31.7 1.5 %collective-permute-done.10.refs_8_ = f32[16,128]{1,0:T(8,128)S(1)} collective-permute-done((f32[16,128]{1,0:T(8,128)S(1)}, f32[16,128]{1,0:T(8,128)S(1)}, u32[]{:S(2)}, u32[]{:S(2)}) %collective-permute-start.10) | collective-permute-done | bytes 8224 | tf_op jit(solution)/shard_map/ppermute | solution.py:358
  33.2 0.4 collective-permute-done.9.refs_7_
  33.5 0.6 shard_map.91
  34.1 1.4 %collective-permute-start.11 = (f32[16,128]{1,0:T(8,128)S(1)}, f32[16,128]{1,0:T(8,128)S(1)}, u32[]{:S(2)}, u32[]{:S(2)}) collective-permute-start(f32[16,128]{1,0:T(8,128)S(1)} %get-tuple-element.61), channel_id=1, source_target_pairs={{0,7},{1,6},{2,5},{3,4},{4,3},{5,2},{6,1},{7,0},{8,15},{9,14},{10,... | collective-permute-start | bytes 24584 | tf_op jit(solution)/shard_map/ppermute | solution.py:358
  35.6 1.3 %collective-permute-start.12 = (f32[16,128]{1,0:T(8,128)S(1)}, f32[16,128]{1,0:T(8,128)S(1)}, u32[]{:S(2)}, u32[]{:S(2)}) collective-permute-start(f32[16,128]{1,0:T(8,128)S(1)} %get-tuple-element.62), channel_id=1, source_target_pairs={{0,4},{1,5},{2,6},{3,7},{4,0},{5,1},{6,2},{7,3},{8,12},{9,13},{10,... | collective-permute-start | bytes 24584 | tf_op jit(solution)/shard_map/ppermute | solution.py:358
  36.8 1.1 %collective-permute-start.13 = (f32[16,128]{1,0:T(8,128)S(1)}, f32[16,128]{1,0:T(8,128)S(1)}, u32[]{:S(2)}, u32[]{:S(2)}) collective-permute-start(f32[16,128]{1,0:T(8,128)S(1)} %get-tuple-element.60.refs_0_), channel_id=1, source_target_pairs={{0,3},{1,2},{2,1},{3,0},{4,7},{5,6},{6,5},{7,4},{8,11},{9,10},{10,... | collective-permute-start | bytes 24584 | tf_op jit(solution)/shard_map/ppermute | solution.py:358
  38.0 1.1 %collective-permute-done.11.refs_1_ = f32[16,128]{1,0:T(8,128)S(1)} collective-permute-done((f32[16,128]{1,0:T(8,128)S(1)}, f32[16,128]{1,0:T(8,128)S(1)}, u32[]{:S(2)}, u32[]{:S(2)}) %collective-permute-start.11) | collective-permute-done | bytes 8224 | tf_op jit(solution)/shard_map/ppermute | solution.py:358
  39.0 1.1 %collective-permute-done.12.refs_2_ = f32[16,128]{1,0:T(8,128)S(1)} collective-permute-done((f32[16,128]{1,0:T(8,128)S(1)}, f32[16,128]{1,0:T(8,128)S(1)}, u32[]{:S(2)}, u32[]{:S(2)}) %collective-permute-start.12) | collective-permute-done | bytes 8224 | tf_op jit(solution)/shard_map/ppermute | solution.py:358
  40.1 0.1 shard_map.92.topics_ref
  40.2 0.0 collective-permute-start.15
  40.2 0.4 shard_map.93.refs_1_
  40.6 0.8 collective-permute-done.15.topics_ref
  41.4 0.4 shard_map.94
  41.8 2.5 %collective-permute-start.16 = (f32[64,512]{1,0:T(8,128)S(1)}, f32[64,512]{1,0:T(8,128)S(1)}, u32[]{:S(2)}, u32[]{:S(2)}) collective-permute-start(f32[64,512]{1,0:T(8,128)S(1)} %get-tuple-element.88), channel_id=1, source_target_pairs={{0,24},{8,16},{16,8},{24,0},{1,25},{9,17},{17,9},{25,1},{2,26},{10... | collective-permute-start | bytes 393224 | tf_op jit(solution)/shard_map/ppermute | solution.py:372
  44.4 0.5 collective-permute-start.17
  44.9 0.5 collective-permute-start.18
  45.4 1.4 %collective-permute-start.19 = (f32[4,4224]{1,0:T(4,128)S(1)}, f32[4,4224]{1,0:T(4,128)S(1)}, u32[]{:S(2)}, u32[]{:S(2)}) collective-permute-start(f32[4,4224]{1,0:T(4,128)S(1)} %get-tuple-element.70), channel_id=1, source_target_pairs={{0,4},{1,5},{2,6},{3,7},{4,0},{5,1},{6,2},{7,3},{8,12},{9,13},{10,... | collective-permute-start | bytes 202760 | tf_op jit(solution)/shard_map/ppermute | solution.py:358
  46.8 4.5 %collective-permute-done.19.refs_4_.refs_6_.refs_2_ = f32[4,4224]{1,0:T(4,128)S(1)} collective-permute-done((f32[4,4224]{1,0:T(4,128)S(1)}, f32[4,4224]{1,0:T(4,128)S(1)}, u32[]{:S(2)}, u32[]{:S(2)}) %collective-permute-start.19) | collective-permute-done | bytes 67616 | tf_op jit(solution)/shard_map/ppermute | solution.py:358
  51.3 0.1 shard_map.95.refs_0_
  51.4 2.5 %collective-permute-start.20 = (f32[64,512]{1,0:T(8,128)S(1)}, f32[64,512]{1,0:T(8,128)S(1)}, u32[]{:S(2)}, u32[]{:S(2)}) collective-permute-start(f32[64,512]{1,0:T(8,128)S(1)} %shard_map.95.refs_0_), channel_id=1, source_target_pairs={{0,24},{8,16},{16,8},{24,0},{1,25},{9,17},{17,9},{25,1},{2,26},{10... | collective-permute-start | bytes 393224 | tf_op jit(solution)/shard_map/ppermute | solution.py:372
  53.9 0.5 collective-permute-start.24
  54.4 0.5 collective-permute-start.26
  54.9 0.4 collective-permute-start.21
  55.3 1.5 %collective-permute-start.22 = (f32[64,512]{1,0:T(8,128)S(1)}, f32[64,512]{1,0:T(8,128)S(1)}, u32[]{:S(2)}, u32[]{:S(2)}) collective-permute-start(f32[64,512]{1,0:T(8,128)S(1)} %shard_map.95.refs_0_), channel_id=1, source_target_pairs={{0,1},{1,0},{2,3},{3,2},{4,5},{5,4},{6,7},{7,6},{8,9},{9,8},{10,11... | collective-permute-start | bytes 393224 | tf_op jit(solution)/shard_map/ppermute | solution.py:369
  56.8 3.7 %collective-permute-done.21.refs_7_.refs_3_ = f32[4,4224]{1,0:T(4,128)S(1)} collective-permute-done((f32[4,4224]{1,0:T(4,128)S(1)}, f32[4,4224]{1,0:T(4,128)S(1)}, u32[]{:S(2)}, u32[]{:S(2)}) %collective-permute-start.21) | collective-permute-done | bytes 67616 | tf_op jit(solution)/shard_map/ppermute | solution.py:358
  60.5 0.5 collective-permute-start.25
  61.0 0.1 collective-permute-start.27
  61.1 0.5 shard_map.96
  61.6 0.2 collective-permute-done.23.refs_1_
  61.9 0.2 collective-permute-done.25.refs_2_
  62.1 0.3 collective-permute-done.27.refs_3_
  62.4 0.5 shard_map.97
  62.9 1.5 %collective-permute-start.28 = (f32[16,128]{1,0:T(8,128)S(1)}, f32[16,128]{1,0:T(8,128)S(1)}, u32[]{:S(2)}, u32[]{:S(2)}) collective-permute-start(f32[16,128]{1,0:T(8,128)S(1)} %get-tuple-element.76.refs_4_), channel_id=1, source_target_pairs={{0,7},{1,6},{2,5},{3,4},{4,3},{5,2},{6,1},{7,0},{8,15},{9,14},{10,... | collective-permute-start | bytes 24584 | tf_op jit(solution)/shard_map/ppermute | solution.py:358
  64.5 0.6 collective-permute-start.29
  65.1 1.7 %collective-permute-start.30 = (f32[16,128]{1,0:T(8,128)S(1)}, f32[16,128]{1,0:T(8,128)S(1)}, u32[]{:S(2)}, u32[]{:S(2)}) collective-permute-start(f32[16,128]{1,0:T(8,128)S(1)} %get-tuple-element.76.refs_4_), channel_id=1, source_target_pairs={{0,3},{1,2},{2,1},{3,0},{4,7},{5,6},{6,5},{7,4},{8,11},{9,10},{10,... | collective-permute-start | bytes 24584 | tf_op jit(solution)/shard_map/ppermute | solution.py:358
  66.7 1.0 %collective-permute-done.28.refs_5_ = f32[16,128]{1,0:T(8,128)S(1)} collective-permute-done((f32[16,128]{1,0:T(8,128)S(1)}, f32[16,128]{1,0:T(8,128)S(1)}, u32[]{:S(2)}, u32[]{:S(2)}) %collective-permute-start.28) | collective-permute-done | bytes 8224 | tf_op jit(solution)/shard_map/ppermute | solution.py:358
  67.8 1.2 %collective-permute-done.29.refs_6_ = f32[16,128]{1,0:T(8,128)S(1)} collective-permute-done((f32[16,128]{1,0:T(8,128)S(1)}, f32[16,128]{1,0:T(8,128)S(1)}, u32[]{:S(2)}, u32[]{:S(2)}) %collective-permute-start.29) | collective-permute-done | bytes 8224 | tf_op jit(solution)/shard_map/ppermute | solution.py:358
  69.0 0.7 shard_map.98
  69.7 0.9 %collective-permute-start.31 = (f32[4,128]{1,0:T(4,128)S(1)}, f32[4,128]{1,0:T(4,128)S(1)}, u32[]{:S(2)}, u32[]{:S(2)}) collective-permute-start(f32[4,128]{1,0:T(4,128)S(1)} %get-tuple-element.83), channel_id=1, source_target_pairs={{0,7},{1,6},{2,5},{3,4},{4,3},{5,2},{6,1},{7,0},{8,15},{9,14},{10,... | collective-permute-start | bytes 6152 | tf_op jit(solution)/shard_map/ppermute | solution.py:358
  70.6 1.4 %collective-permute-start.32 = (f32[4,128]{1,0:T(4,128)S(1)}, f32[4,128]{1,0:T(4,128)S(1)}, u32[]{:S(2)}, u32[]{:S(2)}) collective-permute-start(f32[4,128]{1,0:T(4,128)S(1)} %get-tuple-element.84), channel_id=1, source_target_pairs={{0,4},{1,5},{2,6},{3,7},{4,0},{5,1},{6,2},{7,3},{8,12},{9,13},{10,... | collective-permute-start | bytes 6152 | tf_op jit(solution)/shard_map/ppermute | solution.py:358
  72.0 1.5 %collective-permute-start.33 = (f32[4,128]{1,0:T(4,128)S(1)}, f32[4,128]{1,0:T(4,128)S(1)}, u32[]{:S(2)}, u32[]{:S(2)}) collective-permute-start(f32[4,128]{1,0:T(4,128)S(1)} %get-tuple-element.85), channel_id=1, source_target_pairs={{0,3},{1,2},{2,1},{3,0},{4,7},{5,6},{6,5},{7,4},{8,11},{9,10},{10,... | collective-permute-start | bytes 6152 | tf_op jit(solution)/shard_map/ppermute | solution.py:358
  73.6 0.7 copy.9
  74.2 0.3 collective-permute-done.31.refs_1_
  74.5 0.6 collective-permute-done.32.refs_2_
  75.1 0.6 shard_map.99
  (28 shorter events, 0.1 us)
Async XLA Ops:
  0.6 9.8 %copy-start = (f32[1,2048,64]{1,2,0:T(8,128)S(1)}, f32[1,2048,64]{1,2,0:T(8,128)}, u32[]{:S(2)}) copy-start(f32[1,2048,64]{1,2,0:T(8,128)} %param.10) | copy-start | bytes 1572868
  0.6 9.8 %collective-permute-start = (f32[64,2048]{1,0:T(8,128)}, f32[64,2048]{1,0:T(8,128)S(1)}, u32[]{:S(2)}, u32[]{:S(2)}) collective-permute-start(f32[64,2048]{1,0:T(8,128)} %bitcast.10), channel_id=1, source_target_pairs={{0,1},{1,0},{2,3},{3,2},{4,5},{5,4},{6,7},{7,6},{8,9},{9,8},{10,11... | collective-permute-start | bytes 1572872 | tf_op jit(solution)/shard_map/ppermute | solution.py:369
  2.8 5.4 %copy-start.2 = (f32[4,64]{1,0:T(4,128)S(1)}, f32[4,64]{1,0:T(4,128)}, u32[]{:S(2)}) copy-start(f32[4,64]{1,0:T(4,128)} %topics_ref.1) | copy-start | bytes 3076
  2.9 15.5 %collective-permute-start.1 = (f32[8,4224]{1,0:T(8,128)S(1)}, f32[8,4224]{1,0:T(8,128)S(1)}, u32[]{:S(2)}, u32[]{:S(2)}) collective-permute-start(f32[8,4224]{1,0:T(8,128)S(1)} %get-tuple-element.47), channel_id=1, source_target_pairs={{0,7},{1,6},{2,5},{3,4},{4,3},{5,2},{6,1},{7,0},{8,15},{9,14},{10,... | collective-permute-start | bytes 405512 | tf_op jit(solution)/shard_map/ppermute | solution.py:358
  7.6 10.7 %collective-permute-start.2 = (f32[8,4224]{1,0:T(8,128)S(1)}, f32[8,4224]{1,0:T(8,128)S(1)}, u32[]{:S(2)}, u32[]{:S(2)}) collective-permute-start(f32[8,4224]{1,0:T(8,128)S(1)} %get-tuple-element.48), channel_id=1, source_target_pairs={{0,3},{1,2},{2,1},{3,0},{4,7},{5,6},{6,5},{7,4},{8,11},{9,10},{10,... | collective-permute-start | bytes 405512 | tf_op jit(solution)/shard_map/ppermute | solution.py:358
  7.6 11.9 %collective-permute-start.3 = (f32[8,4224]{1,0:T(8,128)S(1)}, f32[8,4224]{1,0:T(8,128)S(1)}, u32[]{:S(2)}, u32[]{:S(2)}) collective-permute-start(f32[8,4224]{1,0:T(8,128)S(1)} %get-tuple-element.49), channel_id=1, source_target_pairs={{0,4},{1,5},{2,6},{3,7},{4,0},{5,1},{6,2},{7,3},{8,12},{9,13},{10,... | collective-permute-start | bytes 405512 | tf_op jit(solution)/shard_map/ppermute | solution.py:358
  8.3 1.0 %copy-start.1 = (s32[4,16384]{1,0:T(4,128)S(1)}, s32[4,16384]{1,0:T(4,128)}, u32[]{:S(2)}) copy-start(s32[4,16384]{1,0:T(4,128)} %counts_ref.1) | copy-start | bytes 786436
  9.3 1.2 %copy-start.3 = (s32[1,64]{1,0:T(1,128)S(1)}, s32[1,64]{1,0:T(1,128)}, u32[]{:S(2)}) copy-start(s32[1,64]{1,0:T(1,128)} %perm_hbm.1) | copy-start | bytes 772
  9.3 9.0 %collective-permute-start.4 = (f32[4,4224]{1,0:T(4,128)S(1)}, f32[4,4224]{1,0:T(4,128)S(1)}, u32[]{:S(2)}, u32[]{:S(2)}) collective-permute-start(f32[4,4224]{1,0:T(4,128)S(1)} %get-tuple-element.51), channel_id=1, source_target_pairs={{0,3},{1,2},{2,1},{3,0},{4,7},{5,6},{6,5},{7,4},{8,11},{9,10},{10,... | collective-permute-start | bytes 202760 | tf_op jit(solution)/shard_map/ppermute | solution.py:358
  20.1 20.0 %collective-permute-start.14 = (f32[32,2048]{1,0:T(8,128)S(1)}, f32[32,2048]{1,0:T(8,128)S(1)}, u32[]{:S(2)}, u32[]{:S(2)}) collective-permute-start(f32[32,2048]{1,0:T(8,128)S(1)} %get-tuple-element.63), channel_id=1, source_target_pairs={{0,1},{1,0},{2,3},{3,2},{4,5},{5,4},{6,7},{7,6},{8,9},{9,8},{10,11... | collective-permute-start | bytes 786440 | tf_op jit(solution)/shard_map/ppermute | solution.py:369
  20.1 5.0 %collective-permute-start.5 = (f32[24,128]{1,0:T(8,128)S(1)}, f32[24,128]{1,0:T(8,128)S(1)}, u32[]{:S(2)}, u32[]{:S(2)}) collective-permute-start(f32[24,128]{1,0:T(8,128)S(1)} %get-tuple-element.53.refs_4_), channel_id=1, source_target_pairs={{0,7},{1,6},{2,5},{3,4},{4,3},{5,2},{6,1},{7,0},{8,15},{9,14},{10,... | collective-permute-start | bytes 36872 | tf_op jit(solution)/shard_map/ppermute | solution.py:358
  22.7 4.6 %collective-permute-start.6 = (f32[24,128]{1,0:T(8,128)S(1)}, f32[24,128]{1,0:T(8,128)S(1)}, u32[]{:S(2)}, u32[]{:S(2)}) collective-permute-start(f32[24,128]{1,0:T(8,128)S(1)} %get-tuple-element.53.refs_4_), channel_id=1, source_target_pairs={{0,4},{1,5},{2,6},{3,7},{4,0},{5,1},{6,2},{7,3},{8,12},{9,13},{10,... | collective-permute-start | bytes 36872 | tf_op jit(solution)/shard_map/ppermute | solution.py:358
  22.7 4.6 %collective-permute-start.7 = (f32[24,128]{1,0:T(8,128)S(1)}, f32[24,128]{1,0:T(8,128)S(1)}, u32[]{:S(2)}, u32[]{:S(2)}) collective-permute-start(f32[24,128]{1,0:T(8,128)S(1)} %get-tuple-element.53.refs_4_), channel_id=1, source_target_pairs={{0,3},{1,2},{2,1},{3,0},{4,7},{5,6},{6,5},{7,4},{8,11},{9,10},{10,... | collective-permute-start | bytes 36872 | tf_op jit(solution)/shard_map/ppermute | solution.py:358
  27.9 5.7 %collective-permute-start.8 = (f32[18,128]{1,0:T(8,128)S(1)}, f32[18,128]{1,0:T(8,128)S(1)}, u32[]{:S(2)}, u32[]{:S(2)}) collective-permute-start(f32[18,128]{1,0:T(8,128)S(1)} %get-tuple-element.57), channel_id=1, source_target_pairs={{0,7},{1,6},{2,5},{3,4},{4,3},{5,2},{6,1},{7,0},{8,15},{9,14},{10,... | collective-permute-start | bytes 27656 | tf_op jit(solution)/shard_map/ppermute | solution.py:358
  28.9 4.6 %collective-permute-start.9 = (f32[17,128]{1,0:T(8,128)S(1)}, f32[17,128]{1,0:T(8,128)S(1)}, u32[]{:S(2)}, u32[]{:S(2)}) collective-permute-start(f32[17,128]{1,0:T(8,128)S(1)} %get-tuple-element.58), channel_id=1, source_target_pairs={{0,4},{1,5},{2,6},{3,7},{4,0},{5,1},{6,2},{7,3},{8,12},{9,13},{10,... | collective-permute-start | bytes 26120 | tf_op jit(solution)/shard_map/ppermute | solution.py:358
  29.6 3.6 %collective-permute-start.10 = (f32[16,128]{1,0:T(8,128)S(1)}, f32[16,128]{1,0:T(8,128)S(1)}, u32[]{:S(2)}, u32[]{:S(2)}) collective-permute-start(f32[16,128]{1,0:T(8,128)S(1)} %get-tuple-element.56.refs_5_), channel_id=1, source_target_pairs={{0,3},{1,2},{2,1},{3,0},{4,7},{5,6},{6,5},{7,4},{8,11},{9,10},{10,... | collective-permute-start | bytes 24584 | tf_op jit(solution)/shard_map/ppermute | solution.py:358
  34.1 4.9 %collective-permute-start.11 = (f32[16,128]{1,0:T(8,128)S(1)}, f32[16,128]{1,0:T(8,128)S(1)}, u32[]{:S(2)}, u32[]{:S(2)}) collective-permute-start(f32[16,128]{1,0:T(8,128)S(1)} %get-tuple-element.61), channel_id=1, source_target_pairs={{0,7},{1,6},{2,5},{3,4},{4,3},{5,2},{6,1},{7,0},{8,15},{9,14},{10,... | collective-permute-start | bytes 24584 | tf_op jit(solution)/shard_map/ppermute | solution.py:358
  35.6 4.5 %collective-permute-start.12 = (f32[16,128]{1,0:T(8,128)S(1)}, f32[16,128]{1,0:T(8,128)S(1)}, u32[]{:S(2)}, u32[]{:S(2)}) collective-permute-start(f32[16,128]{1,0:T(8,128)S(1)} %get-tuple-element.62), channel_id=1, source_target_pairs={{0,4},{1,5},{2,6},{3,7},{4,0},{5,1},{6,2},{7,3},{8,12},{9,13},{10,... | collective-permute-start | bytes 24584 | tf_op jit(solution)/shard_map/ppermute | solution.py:358
  36.8 3.3 %collective-permute-start.13 = (f32[16,128]{1,0:T(8,128)S(1)}, f32[16,128]{1,0:T(8,128)S(1)}, u32[]{:S(2)}, u32[]{:S(2)}) collective-permute-start(f32[16,128]{1,0:T(8,128)S(1)} %get-tuple-element.60.refs_0_), channel_id=1, source_target_pairs={{0,3},{1,2},{2,1},{3,0},{4,7},{5,6},{6,5},{7,4},{8,11},{9,10},{10,... | collective-permute-start | bytes 24584 | tf_op jit(solution)/shard_map/ppermute | solution.py:358
  40.2 1.2 %collective-permute-start.15 = (f32[32,128]{1,0:T(8,128)S(1)}, f32[32,128]{1,0:T(8,128)S(1)}, u32[]{:S(2)}, u32[]{:S(2)}) collective-permute-start(f32[32,128]{1,0:T(8,128)S(1)} %shard_map.92.topics_ref), channel_id=1, source_target_pairs={{0,1},{1,0},{2,3},{3,2},{4,5},{5,4},{6,7},{7,6},{8,9},{9,8},{10,11... | collective-permute-start | bytes 49160 | tf_op jit(solution)/shard_map/ppermute | solution.py:369
  41.8 9.5 %collective-permute-start.16 = (f32[64,512]{1,0:T(8,128)S(1)}, f32[64,512]{1,0:T(8,128)S(1)}, u32[]{:S(2)}, u32[]{:S(2)}) collective-permute-start(f32[64,512]{1,0:T(8,128)S(1)} %get-tuple-element.88), channel_id=1, source_target_pairs={{0,24},{8,16},{16,8},{24,0},{1,25},{9,17},{17,9},{25,1},{2,26},{10... | collective-permute-start | bytes 393224 | tf_op jit(solution)/shard_map/ppermute | solution.py:372
  44.4 7.0 %collective-permute-start.17 = (f32[64,512]{1,0:T(8,128)S(1)}, f32[64,512]{1,0:T(8,128)S(1)}, u32[]{:S(2)}, u32[]{:S(2)}) collective-permute-start(f32[64,512]{1,0:T(8,128)S(1)} %get-tuple-element.87), channel_id=1, source_target_pairs={{0,16},{8,24},{16,0},{24,8},{1,17},{9,25},{17,1},{25,9},{2,18},{10... | collective-permute-start | bytes 393224 | tf_op jit(solution)/shard_map/ppermute | solution.py:372
  44.9 6.5 %collective-permute-start.18 = (f32[64,512]{1,0:T(8,128)S(1)}, f32[64,512]{1,0:T(8,128)S(1)}, u32[]{:S(2)}, u32[]{:S(2)}) collective-permute-start(f32[64,512]{1,0:T(8,128)S(1)} %get-tuple-element.86), channel_id=1, source_target_pairs={{0,8},{8,0},{16,24},{24,16},{1,9},{9,1},{17,25},{25,17},{2,10},{10... | collective-permute-start | bytes 393224 | tf_op jit(solution)/shard_map/ppermute | solution.py:372
  45.4 5.9 %collective-permute-start.19 = (f32[4,4224]{1,0:T(4,128)S(1)}, f32[4,4224]{1,0:T(4,128)S(1)}, u32[]{:S(2)}, u32[]{:S(2)}) collective-permute-start(f32[4,4224]{1,0:T(4,128)S(1)} %get-tuple-element.70), channel_id=1, source_target_pairs={{0,4},{1,5},{2,6},{3,7},{4,0},{5,1},{6,2},{7,3},{8,12},{9,13},{10,... | collective-permute-start | bytes 202760 | tf_op jit(solution)/shard_map/ppermute | solution.py:358
  51.4 9.1 %collective-permute-start.20 = (f32[64,512]{1,0:T(8,128)S(1)}, f32[64,512]{1,0:T(8,128)S(1)}, u32[]{:S(2)}, u32[]{:S(2)}) collective-permute-start(f32[64,512]{1,0:T(8,128)S(1)} %shard_map.95.refs_0_), channel_id=1, source_target_pairs={{0,24},{8,16},{16,8},{24,0},{1,25},{9,17},{17,9},{25,1},{2,26},{10... | collective-permute-start | bytes 393224 | tf_op jit(solution)/shard_map/ppermute | solution.py:372
  53.9 6.6 %collective-permute-start.24 = (f32[64,512]{1,0:T(8,128)S(1)}, f32[64,512]{1,0:T(8,128)S(1)}, u32[]{:S(2)}, u32[]{:S(2)}) collective-permute-start(f32[64,512]{1,0:T(8,128)S(1)} %shard_map.95.refs_0_), channel_id=1, source_target_pairs={{0,16},{8,24},{16,0},{24,8},{1,17},{9,25},{17,1},{25,9},{2,18},{10... | collective-permute-start | bytes 393224 | tf_op jit(solution)/shard_map/ppermute | solution.py:372
  54.4 6.6 %collective-permute-start.26 = (f32[64,512]{1,0:T(8,128)S(1)}, f32[64,512]{1,0:T(8,128)S(1)}, u32[]{:S(2)}, u32[]{:S(2)}) collective-permute-start(f32[64,512]{1,0:T(8,128)S(1)} %shard_map.95.refs_0_), channel_id=1, source_target_pairs={{0,8},{8,0},{16,24},{24,16},{1,9},{9,1},{17,25},{25,17},{2,10},{10... | collective-permute-start | bytes 393224 | tf_op jit(solution)/shard_map/ppermute | solution.py:372
  54.9 5.6 %collective-permute-start.21 = (f32[4,4224]{1,0:T(4,128)S(1)}, f32[4,4224]{1,0:T(4,128)S(1)}, u32[]{:S(2)}, u32[]{:S(2)}) collective-permute-start(f32[4,4224]{1,0:T(4,128)S(1)} %get-tuple-element.72), channel_id=1, source_target_pairs={{0,7},{1,6},{2,5},{3,4},{4,3},{5,2},{6,1},{7,0},{8,15},{9,14},{10,... | collective-permute-start | bytes 202760 | tf_op jit(solution)/shard_map/ppermute | solution.py:358
  55.3 6.3 %collective-permute-start.22 = (f32[64,512]{1,0:T(8,128)S(1)}, f32[64,512]{1,0:T(8,128)S(1)}, u32[]{:S(2)}, u32[]{:S(2)}) collective-permute-start(f32[64,512]{1,0:T(8,128)S(1)} %shard_map.95.refs_0_), channel_id=1, source_target_pairs={{0,1},{1,0},{2,3},{3,2},{4,5},{5,4},{6,7},{7,6},{8,9},{9,8},{10,11... | collective-permute-start | bytes 393224 | tf_op jit(solution)/shard_map/ppermute | solution.py:369
  60.5 1.3 %collective-permute-start.23 = (f32[64,512]{1,0:T(8,128)S(1)}, f32[64,512]{1,0:T(8,128)S(1)}, u32[]{:S(2)}, u32[]{:S(2)}) collective-permute-start(f32[64,512]{1,0:T(8,128)S(1)} %collective-permute-done.20.refs_1_), channel_id=1, source_target_pairs={{0,1},{1,0},{2,3},{3,2},{4,5},{5,4},{6,7},{7,6},{8,9},{9,8},{10,11... | collective-permute-start | bytes 393224 | tf_op jit(solution)/shard_map/ppermute | solution.py:369
  60.5 1.5 %collective-permute-start.25 = (f32[64,512]{1,0:T(8,128)S(1)}, f32[64,512]{1,0:T(8,128)S(1)}, u32[]{:S(2)}, u32[]{:S(2)}) collective-permute-start(f32[64,512]{1,0:T(8,128)S(1)} %collective-permute-done.24.refs_2_), channel_id=1, source_target_pairs={{0,1},{1,0},{2,3},{3,2},{4,5},{5,4},{6,7},{7,6},{8,9},{9,8},{10,11... | collective-permute-start | bytes 393224 | tf_op jit(solution)/shard_map/ppermute | solution.py:369
  61.0 1.3 %collective-permute-start.27 = (f32[64,512]{1,0:T(8,128)S(1)}, f32[64,512]{1,0:T(8,128)S(1)}, u32[]{:S(2)}, u32[]{:S(2)}) collective-permute-start(f32[64,512]{1,0:T(8,128)S(1)} %collective-permute-done.26.refs_3_), channel_id=1, source_target_pairs={{0,1},{1,0},{2,3},{3,2},{4,5},{5,4},{6,7},{7,6},{8,9},{9,8},{10,11... | collective-permute-start | bytes 393224 | tf_op jit(solution)/shard_map/ppermute | solution.py:369
  62.9 4.9 %collective-permute-start.28 = (f32[16,128]{1,0:T(8,128)S(1)}, f32[16,128]{1,0:T(8,128)S(1)}, u32[]{:S(2)}, u32[]{:S(2)}) collective-permute-start(f32[16,128]{1,0:T(8,128)S(1)} %get-tuple-element.76.refs_4_), channel_id=1, source_target_pairs={{0,7},{1,6},{2,5},{3,4},{4,3},{5,2},{6,1},{7,0},{8,15},{9,14},{10,... | collective-permute-start | bytes 24584 | tf_op jit(solution)/shard_map/ppermute | solution.py:358
  64.5 4.5 %collective-permute-start.29 = (f32[16,128]{1,0:T(8,128)S(1)}, f32[16,128]{1,0:T(8,128)S(1)}, u32[]{:S(2)}, u32[]{:S(2)}) collective-permute-start(f32[16,128]{1,0:T(8,128)S(1)} %get-tuple-element.76.refs_4_), channel_id=1, source_target_pairs={{0,4},{1,5},{2,6},{3,7},{4,0},{5,1},{6,2},{7,3},{8,12},{9,13},{10,... | collective-permute-start | bytes 24584 | tf_op jit(solution)/shard_map/ppermute | solution.py:358
  65.1 3.9 %collective-permute-start.30 = (f32[16,128]{1,0:T(8,128)S(1)}, f32[16,128]{1,0:T(8,128)S(1)}, u32[]{:S(2)}, u32[]{:S(2)}) collective-permute-start(f32[16,128]{1,0:T(8,128)S(1)} %get-tuple-element.76.refs_4_), channel_id=1, source_target_pairs={{0,3},{1,2},{2,1},{3,0},{4,7},{5,6},{6,5},{7,4},{8,11},{9,10},{10,... | collective-permute-start | bytes 24584 | tf_op jit(solution)/shard_map/ppermute | solution.py:358
  69.7 4.8 %collective-permute-start.31 = (f32[4,128]{1,0:T(4,128)S(1)}, f32[4,128]{1,0:T(4,128)S(1)}, u32[]{:S(2)}, u32[]{:S(2)}) collective-permute-start(f32[4,128]{1,0:T(4,128)S(1)} %get-tuple-element.83), channel_id=1, source_target_pairs={{0,7},{1,6},{2,5},{3,4},{4,3},{5,2},{6,1},{7,0},{8,15},{9,14},{10,... | collective-permute-start | bytes 6152 | tf_op jit(solution)/shard_map/ppermute | solution.py:358
  70.6 4.5 %collective-permute-start.32 = (f32[4,128]{1,0:T(4,128)S(1)}, f32[4,128]{1,0:T(4,128)S(1)}, u32[]{:S(2)}, u32[]{:S(2)}) collective-permute-start(f32[4,128]{1,0:T(4,128)S(1)} %get-tuple-element.84), channel_id=1, source_target_pairs={{0,4},{1,5},{2,6},{3,7},{4,0},{5,1},{6,2},{7,3},{8,12},{9,13},{10,... | collective-permute-start | bytes 6152 | tf_op jit(solution)/shard_map/ppermute | solution.py:358
  72.0 3.1 %collective-permute-start.33 = (f32[4,128]{1,0:T(4,128)S(1)}, f32[4,128]{1,0:T(4,128)S(1)}, u32[]{:S(2)}, u32[]{:S(2)}) collective-permute-start(f32[4,128]{1,0:T(4,128)S(1)} %get-tuple-element.85), channel_id=1, source_target_pairs={{0,3},{1,2},{2,1},{3,0},{4,7},{5,6},{6,5},{7,4},{8,11},{9,10},{10,... | collective-permute-start | bytes 6152 | tf_op jit(solution)/shard_map/ppermute | solution.py:358

commit v6 on v5

--- a/solution.py
+++ b/solution.py
@@ -106,15 +106,16 @@
     for step in steps:
         for half, block in enumerate(blocks_of(chips, cores, step)):
             near = pltpu.roll(occupied, lax.rem(tiles - block * own_tiles, tiles), 1)
-            if half == 0:
-                arriving[step].wait()
-            first = lax.rem(block, cores) * own_words
             for tile in range(own_tiles):
                 at = slice(half * own_words + tile * width, half * own_words + (tile + 1) * width)
-                picked = counts_ref[step, :, pl.ds(pl.multiple_of(first + tile * width, 128), width)]
-                picked = picked.astype(jnp.float32)
-                out_refs[step][:, at] = picked * near[:, tile : tile + 1]
+                out_refs[step][:, at] = jnp.broadcast_to(near[:, tile : tile + 1], (docs, width))
         out_refs[step][:, cores * own_words :] = topics
+    for step in steps:
+        arriving[step].wait()
+        for half, block in enumerate(blocks_of(chips, cores, step)):
+            at = slice(half * own_words, (half + 1) * own_words)
+            first = pl.multiple_of(lax.rem(block, cores) * own_words, 128)
+            out_refs[step][:, at] *= counts_ref[step, :, pl.ds(first, own_words)].astype(jnp.float32)
 
 
 def base_kernel(chips, cores, counts_ref, topics_ref, *out_refs):

time: 75.9 us -> 75.5 us (level)
  no operation moved by 1% of the time
where the time goes in v6:
time: 75.5 us; the launch traced here: 75.3 us
  starting transfers between devices  37.4 us (50%)
  waiting for transfers between devices  28.1 us (37%)
  Pallas kernels  7.4 us (10%)
  local copies, waits for them, and re-layouts  1.67 us (2%)
  between operations  0.77 us (1%)
    ppermute x21, starting transfers between devices, over_chips(): lax.ppermute(array, 'doc', [(c * cores + k, (c ^ step) * cores + (k + ste...  27.7 us
    ppermute x21, waiting for transfers between devices, over_chips(): lax.ppermute(array, 'doc', [(c * cores + k, (c ^ step) * cores + (k + ste...  26.6 us
    ppermute x6, starting transfers between devices, over_pert(): return lax.ppermute(array, 'pert', [(m, m ^ step) for m in range(members)])  7.11 us
    pallas_call x13, Pallas kernels, call(): pl.pallas_call(kernel, out_shape=outs, in_specs=[pl.BlockSpec(memory_spac...  6.09 us
    ppermute x7, starting transfers between devices, over_cores(): return lax.ppermute(array, 'doc', [(d, d ^ 1) for d in range(doc_size)])  2.6 us
    unnamed x9, local copies, waits for them, and re-layouts  1.62 us
    ppermute x7, waiting for transfers between devices, over_cores(): return lax.ppermute(array, 'doc', [(d, d ^ 1) for d in range(doc_size)])  1.52 us
  transfers between devices with their start and end apart: 34, of which 18 were waited for; matrix products, arithmetic and copies ran while one was open for 1% of the time, Pallas kernels for 6%

profile of v6, /device:TPU:0, one launch (start us, length us, event | category | flops | bytes accessed | tf_op | source)
XLA Modules:
  0.0 75.3 jit_solution(3502886039410250892)
XLA Ops:
  0.6 0.5 collective-permute-start
  1.2 1.3 %shard_map.87 = (f32[8,4224]{1,0:T(8,128)S(1)}, f32[8,4224]{1,0:T(8,128)S(1)}, f32[8,4224]{1,0:T(8,128)S(1)}, f32[8,4224]{1,0:T(8,128)S(1)}) custom-call(s32[8,128]{1,0:T(8,128)} %bitcast.13, f32[8,64]{1,0:T(8,128)} %bitcast.14, s32[1,64]{1,0:T(1,128)} %perm_hbm.1, s32[8,16384]{1,0:T(8,128)} %bitcast.12), custom_call_target="tpu_custom_call" | custom-call | bytes 1572864 | tf_op jit(solution)/shard_map/pallas_call | solution.py:375
  2.5 4.8 %collective-permute-start.1 = (f32[8,4224]{1,0:T(8,128)S(1)}, f32[8,4224]{1,0:T(8,128)S(1)}, u32[]{:S(2)}, u32[]{:S(2)}) collective-permute-start(f32[8,4224]{1,0:T(8,128)S(1)} %get-tuple-element.47), channel_id=1, source_target_pairs={{0,7},{1,6},{2,5},{3,4},{4,3},{5,2},{6,1},{7,0},{8,15},{9,14},{10,... | collective-permute-start | bytes 405512 | tf_op jit(solution)/shard_map/ppermute | solution.py:359
  7.3 0.6 collective-permute-start.3
  7.9 0.9 %copy-done.1 = s32[4,16384]{1,0:T(4,128)S(1)} copy-done((s32[4,16384]{1,0:T(4,128)S(1)}, s32[4,16384]{1,0:T(4,128)}, u32[]{:S(2)}) %copy-start.1) | copy-done | bytes 262168
  8.9 0.1 shard_map.88
  8.9 1.1 %collective-permute-start.4 = (f32[4,4224]{1,0:T(4,128)S(1)}, f32[4,4224]{1,0:T(4,128)S(1)}, u32[]{:S(2)}, u32[]{:S(2)}) collective-permute-start(f32[4,4224]{1,0:T(4,128)S(1)} %get-tuple-element.51), channel_id=1, source_target_pairs={{0,3},{1,2},{2,1},{3,0},{4,7},{5,6},{6,5},{7,4},{8,11},{9,10},{10,... | collective-permute-start | bytes 202760 | tf_op jit(solution)/shard_map/ppermute | solution.py:359
  10.1 1.1 %shard_map.86 = (bf16[128,4096]{1,0:T(8,128)(2,1)S(1)}, bf16[4096,128]{1,0:T(8,128)(2,1)S(1)}, f32[8,128]{1,0:T(8,128)S(1)}, f32[64,2048]{1,0:T(8,128)S(1)}) custom-call(s32[1,64]{1,0:T(1,128)S(1)} %copy-done.3, f32[64,2048]{1,0:T(8,128)S(1)} %bitcast.11, f32[64,2048]{1,0:T(8,128)S(1)} %collective-permute-done.refs_1_), custom_call_target="tpu_custom_call" | custom-call | bytes 4194304 | tf_op jit(solution)/shard_map/pallas_call | solution.py:37
  11.2 6.8 %collective-permute-done.4.refs_4_.refs_5_.refs_1_ = f32[4,4224]{1,0:T(4,128)S(1)} collective-permute-done((f32[4,4224]{1,0:T(4,128)S(1)}, f32[4,4224]{1,0:T(4,128)S(1)}, u32[]{:S(2)}, u32[]{:S(2)}) %collective-permute-start.4) | collective-permute-done | bytes 67616 | tf_op jit(solution)/shard_map/ppermute | solution.py:359
  18.0 1.2 %collective-permute-done.3.refs_2_.refs_1_ = f32[8,4224]{1,0:T(8,128)S(1)} collective-permute-done((f32[8,4224]{1,0:T(8,128)S(1)}, f32[8,4224]{1,0:T(8,128)S(1)}, u32[]{:S(2)}, u32[]{:S(2)}) %collective-permute-start.3) | collective-permute-done | bytes 135200 | tf_op jit(solution)/shard_map/ppermute | solution.py:359
  19.2 0.5 shard_map.89
  19.7 2.6 %collective-permute-start.5 = (f32[24,128]{1,0:T(8,128)S(1)}, f32[24,128]{1,0:T(8,128)S(1)}, u32[]{:S(2)}, u32[]{:S(2)}) collective-permute-start(f32[24,128]{1,0:T(8,128)S(1)} %get-tuple-element.53.refs_4_), channel_id=1, source_target_pairs={{0,7},{1,6},{2,5},{3,4},{4,3},{5,2},{6,1},{7,0},{8,15},{9,14},{10,... | collective-permute-start | bytes 36872 | tf_op jit(solution)/shard_map/ppermute | solution.py:359
  22.3 1.3 %collective-permute-start.7 = (f32[24,128]{1,0:T(8,128)S(1)}, f32[24,128]{1,0:T(8,128)S(1)}, u32[]{:S(2)}, u32[]{:S(2)}) collective-permute-start(f32[24,128]{1,0:T(8,128)S(1)} %get-tuple-element.53.refs_4_), channel_id=1, source_target_pairs={{0,3},{1,2},{2,1},{3,0},{4,7},{5,6},{6,5},{7,4},{8,11},{9,10},{10,... | collective-permute-start | bytes 36872 | tf_op jit(solution)/shard_map/ppermute | solution.py:359
  23.6 1.1 %collective-permute-done.5.refs_5_ = f32[24,128]{1,0:T(8,128)S(1)} collective-permute-done((f32[24,128]{1,0:T(8,128)S(1)}, f32[24,128]{1,0:T(8,128)S(1)}, u32[]{:S(2)}, u32[]{:S(2)}) %collective-permute-start.5) | collective-permute-done | bytes 12320 | tf_op jit(solution)/shard_map/ppermute | solution.py:359
  24.7 2.2 %collective-permute-done.6.refs_6_ = f32[24,128]{1,0:T(8,128)S(1)} collective-permute-done((f32[24,128]{1,0:T(8,128)S(1)}, f32[24,128]{1,0:T(8,128)S(1)}, u32[]{:S(2)}, u32[]{:S(2)}) %collective-permute-start.6) | collective-permute-done | bytes 12320 | tf_op jit(solution)/shard_map/ppermute | solution.py:359
  26.9 0.6 shard_map.90
  27.5 1.1 %collective-permute-start.8 = (f32[18,128]{1,0:T(8,128)S(1)}, f32[18,128]{1,0:T(8,128)S(1)}, u32[]{:S(2)}, u32[]{:S(2)}) collective-permute-start(f32[18,128]{1,0:T(8,128)S(1)} %get-tuple-element.57), channel_id=1, source_target_pairs={{0,7},{1,6},{2,5},{3,4},{4,3},{5,2},{6,1},{7,0},{8,15},{9,14},{10,... | collective-permute-start | bytes 27656 | tf_op jit(solution)/shard_map/ppermute | solution.py:359
  28.6 0.6 collective-permute-start.9
  29.2 2.2 %collective-permute-start.10 = (f32[16,128]{1,0:T(8,128)S(1)}, f32[16,128]{1,0:T(8,128)S(1)}, u32[]{:S(2)}, u32[]{:S(2)}) collective-permute-start(f32[16,128]{1,0:T(8,128)S(1)} %get-tuple-element.56.refs_5_), channel_id=1, source_target_pairs={{0,3},{1,2},{2,1},{3,0},{4,7},{5,6},{6,5},{7,4},{8,11},{9,10},{10,... | collective-permute-start | bytes 24584 | tf_op jit(solution)/shard_map/ppermute | solution.py:359
  31.4 1.5 %collective-permute-done.10.refs_8_ = f32[16,128]{1,0:T(8,128)S(1)} collective-permute-done((f32[16,128]{1,0:T(8,128)S(1)}, f32[16,128]{1,0:T(8,128)S(1)}, u32[]{:S(2)}, u32[]{:S(2)}) %collective-permute-start.10) | collective-permute-done | bytes 8224 | tf_op jit(solution)/shard_map/ppermute | solution.py:359
  32.8 0.4 collective-permute-done.9.refs_7_
  33.2 0.6 shard_map.91
  33.8 1.4 %collective-permute-start.11 = (f32[16,128]{1,0:T(8,128)S(1)}, f32[16,128]{1,0:T(8,128)S(1)}, u32[]{:S(2)}, u32[]{:S(2)}) collective-permute-start(f32[16,128]{1,0:T(8,128)S(1)} %get-tuple-element.61), channel_id=1, source_target_pairs={{0,7},{1,6},{2,5},{3,4},{4,3},{5,2},{6,1},{7,0},{8,15},{9,14},{10,... | collective-permute-start | bytes 24584 | tf_op jit(solution)/shard_map/ppermute | solution.py:359
  35.2 1.3 %collective-permute-start.12 = (f32[16,128]{1,0:T(8,128)S(1)}, f32[16,128]{1,0:T(8,128)S(1)}, u32[]{:S(2)}, u32[]{:S(2)}) collective-permute-start(f32[16,128]{1,0:T(8,128)S(1)} %get-tuple-element.62), channel_id=1, source_target_pairs={{0,4},{1,5},{2,6},{3,7},{4,0},{5,1},{6,2},{7,3},{8,12},{9,13},{10,... | collective-permute-start | bytes 24584 | tf_op jit(solution)/shard_map/ppermute | solution.py:359
  36.5 1.1 %collective-permute-start.13 = (f32[16,128]{1,0:T(8,128)S(1)}, f32[16,128]{1,0:T(8,128)S(1)}, u32[]{:S(2)}, u32[]{:S(2)}) collective-permute-start(f32[16,128]{1,0:T(8,128)S(1)} %get-tuple-element.60.refs_0_), channel_id=1, source_target_pairs={{0,3},{1,2},{2,1},{3,0},{4,7},{5,6},{6,5},{7,4},{8,11},{9,10},{10,... | collective-permute-start | bytes 24584 | tf_op jit(solution)/shard_map/ppermute | solution.py:359
  37.6 1.1 %collective-permute-done.11.refs_1_ = f32[16,128]{1,0:T(8,128)S(1)} collective-permute-done((f32[16,128]{1,0:T(8,128)S(1)}, f32[16,128]{1,0:T(8,128)S(1)}, u32[]{:S(2)}, u32[]{:S(2)}) %collective-permute-start.11) | collective-permute-done | bytes 8224 | tf_op jit(solution)/shard_map/ppermute | solution.py:359
  38.7 1.1 %collective-permute-done.12.refs_2_ = f32[16,128]{1,0:T(8,128)S(1)} collective-permute-done((f32[16,128]{1,0:T(8,128)S(1)}, f32[16,128]{1,0:T(8,128)S(1)}, u32[]{:S(2)}, u32[]{:S(2)}) %collective-permute-start.12) | collective-permute-done | bytes 8224 | tf_op jit(solution)/shard_map/ppermute | solution.py:359
  39.8 0.1 shard_map.92.topics_ref
  39.8 0.0 collective-permute-start.15
  39.9 0.4 shard_map.93.refs_1_
  40.3 0.8 %collective-permute-done.15.topics_ref = f32[32,128]{1,0:T(8,128)S(1)} collective-permute-done((f32[32,128]{1,0:T(8,128)S(1)}, f32[32,128]{1,0:T(8,128)S(1)}, u32[]{:S(2)}, u32[]{:S(2)}) %collective-permute-start.15) | collective-permute-done | bytes 16416 | tf_op jit(solution)/shard_map/ppermute | solution.py:370
  41.0 0.4 shard_map.94
  41.5 2.5 %collective-permute-start.16 = (f32[64,512]{1,0:T(8,128)S(1)}, f32[64,512]{1,0:T(8,128)S(1)}, u32[]{:S(2)}, u32[]{:S(2)}) collective-permute-start(f32[64,512]{1,0:T(8,128)S(1)} %get-tuple-element.88), channel_id=1, source_target_pairs={{0,24},{8,16},{16,8},{24,0},{1,25},{9,17},{17,9},{25,1},{2,26},{10... | collective-permute-start | bytes 393224 | tf_op jit(solution)/shard_map/ppermute | solution.py:373
  44.0 0.5 collective-permute-start.17
  44.5 0.5 collective-permute-start.18
  45.0 1.4 %collective-permute-start.19 = (f32[4,4224]{1,0:T(4,128)S(1)}, f32[4,4224]{1,0:T(4,128)S(1)}, u32[]{:S(2)}, u32[]{:S(2)}) collective-permute-start(f32[4,4224]{1,0:T(4,128)S(1)} %get-tuple-element.70), channel_id=1, source_target_pairs={{0,4},{1,5},{2,6},{3,7},{4,0},{5,1},{6,2},{7,3},{8,12},{9,13},{10,... | collective-permute-start | bytes 202760 | tf_op jit(solution)/shard_map/ppermute | solution.py:359
  46.5 4.5 %collective-permute-done.19.refs_4_.refs_6_.refs_2_ = f32[4,4224]{1,0:T(4,128)S(1)} collective-permute-done((f32[4,4224]{1,0:T(4,128)S(1)}, f32[4,4224]{1,0:T(4,128)S(1)}, u32[]{:S(2)}, u32[]{:S(2)}) %collective-permute-start.19) | collective-permute-done | bytes 67616 | tf_op jit(solution)/shard_map/ppermute | solution.py:359
  51.0 0.1 shard_map.95.refs_0_
  51.0 2.5 %collective-permute-start.20 = (f32[64,512]{1,0:T(8,128)S(1)}, f32[64,512]{1,0:T(8,128)S(1)}, u32[]{:S(2)}, u32[]{:S(2)}) collective-permute-start(f32[64,512]{1,0:T(8,128)S(1)} %shard_map.95.refs_0_), channel_id=1, source_target_pairs={{0,24},{8,16},{16,8},{24,0},{1,25},{9,17},{17,9},{25,1},{2,26},{10... | collective-permute-start | bytes 393224 | tf_op jit(solution)/shard_map/ppermute | solution.py:373
  53.5 0.5 collective-permute-start.24
  54.1 0.5 collective-permute-start.26
  54.6 0.4 collective-permute-start.21
  55.0 1.5 %collective-permute-start.22 = (f32[64,512]{1,0:T(8,128)S(1)}, f32[64,512]{1,0:T(8,128)S(1)}, u32[]{:S(2)}, u32[]{:S(2)}) collective-permute-start(f32[64,512]{1,0:T(8,128)S(1)} %shard_map.95.refs_0_), channel_id=1, source_target_pairs={{0,1},{1,0},{2,3},{3,2},{4,5},{5,4},{6,7},{7,6},{8,9},{9,8},{10,11... | collective-permute-start | bytes 393224 | tf_op jit(solution)/shard_map/ppermute | solution.py:370
  56.5 3.7 %collective-permute-done.21.refs_7_.refs_3_ = f32[4,4224]{1,0:T(4,128)S(1)} collective-permute-done((f32[4,4224]{1,0:T(4,128)S(1)}, f32[4,4224]{1,0:T(4,128)S(1)}, u32[]{:S(2)}, u32[]{:S(2)}) %collective-permute-start.21) | collective-permute-done | bytes 67616 | tf_op jit(solution)/shard_map/ppermute | solution.py:359
  60.2 0.5 collective-permute-start.25
  60.7 0.1 collective-permute-start.27
  60.7 0.5 shard_map.96
  61.3 0.2 collective-permute-done.23.refs_1_
  61.5 0.2 collective-permute-done.25.refs_2_
  61.7 0.3 collective-permute-done.27.refs_3_
  62.0 0.5 shard_map.97
  62.5 1.6 %collective-permute-start.28 = (f32[16,128]{1,0:T(8,128)S(1)}, f32[16,128]{1,0:T(8,128)S(1)}, u32[]{:S(2)}, u32[]{:S(2)}) collective-permute-start(f32[16,128]{1,0:T(8,128)S(1)} %get-tuple-element.76.refs_4_), channel_id=1, source_target_pairs={{0,7},{1,6},{2,5},{3,4},{4,3},{5,2},{6,1},{7,0},{8,15},{9,14},{10,... | collective-permute-start | bytes 24584 | tf_op jit(solution)/shard_map/ppermute | solution.py:359
  64.1 0.6 collective-permute-start.29
  64.7 1.7 %collective-permute-start.30 = (f32[16,128]{1,0:T(8,128)S(1)}, f32[16,128]{1,0:T(8,128)S(1)}, u32[]{:S(2)}, u32[]{:S(2)}) collective-permute-start(f32[16,128]{1,0:T(8,128)S(1)} %get-tuple-element.76.refs_4_), channel_id=1, source_target_pairs={{0,3},{1,2},{2,1},{3,0},{4,7},{5,6},{6,5},{7,4},{8,11},{9,10},{10,... | collective-permute-start | bytes 24584 | tf_op jit(solution)/shard_map/ppermute | solution.py:359
  66.4 1.0 %collective-permute-done.28.refs_5_ = f32[16,128]{1,0:T(8,128)S(1)} collective-permute-done((f32[16,128]{1,0:T(8,128)S(1)}, f32[16,128]{1,0:T(8,128)S(1)}, u32[]{:S(2)}, u32[]{:S(2)}) %collective-permute-start.28) | collective-permute-done | bytes 8224 | tf_op jit(solution)/shard_map/ppermute | solution.py:359
  67.4 1.2 %collective-permute-done.29.refs_6_ = f32[16,128]{1,0:T(8,128)S(1)} collective-permute-done((f32[16,128]{1,0:T(8,128)S(1)}, f32[16,128]{1,0:T(8,128)S(1)}, u32[]{:S(2)}, u32[]{:S(2)}) %collective-permute-start.29) | collective-permute-done | bytes 8224 | tf_op jit(solution)/shard_map/ppermute | solution.py:359
  68.7 0.7 shard_map.98
  69.3 0.9 %collective-permute-start.31 = (f32[4,128]{1,0:T(4,128)S(1)}, f32[4,128]{1,0:T(4,128)S(1)}, u32[]{:S(2)}, u32[]{:S(2)}) collective-permute-start(f32[4,128]{1,0:T(4,128)S(1)} %get-tuple-element.83), channel_id=1, source_target_pairs={{0,7},{1,6},{2,5},{3,4},{4,3},{5,2},{6,1},{7,0},{8,15},{9,14},{10,... | collective-permute-start | bytes 6152 | tf_op jit(solution)/shard_map/ppermute | solution.py:359
  70.3 1.4 %collective-permute-start.32 = (f32[4,128]{1,0:T(4,128)S(1)}, f32[4,128]{1,0:T(4,128)S(1)}, u32[]{:S(2)}, u32[]{:S(2)}) collective-permute-start(f32[4,128]{1,0:T(4,128)S(1)} %get-tuple-element.84), channel_id=1, source_target_pairs={{0,4},{1,5},{2,6},{3,7},{4,0},{5,1},{6,2},{7,3},{8,12},{9,13},{10,... | collective-permute-start | bytes 6152 | tf_op jit(solution)/shard_map/ppermute | solution.py:359
  71.7 1.5 %collective-permute-start.33 = (f32[4,128]{1,0:T(4,128)S(1)}, f32[4,128]{1,0:T(4,128)S(1)}, u32[]{:S(2)}, u32[]{:S(2)}) collective-permute-start(f32[4,128]{1,0:T(4,128)S(1)} %get-tuple-element.85), channel_id=1, source_target_pairs={{0,3},{1,2},{2,1},{3,0},{4,7},{5,6},{6,5},{7,4},{8,11},{9,10},{10,... | collective-permute-start | bytes 6152 | tf_op jit(solution)/shard_map/ppermute | solution.py:359
  73.2 0.7 copy.9
  73.8 0.3 collective-permute-done.31.refs_1_
  74.2 0.6 collective-permute-done.32.refs_2_
  74.8 0.6 shard_map.99
  (28 shorter events, 0.1 us)
Async XLA Ops:
  0.6 9.5 %copy-start = (f32[1,2048,64]{1,2,0:T(8,128)S(1)}, f32[1,2048,64]{1,2,0:T(8,128)}, u32[]{:S(2)}) copy-start(f32[1,2048,64]{1,2,0:T(8,128)} %param.10) | copy-start | bytes 1572868
  0.6 9.4 %collective-permute-start = (f32[64,2048]{1,0:T(8,128)}, f32[64,2048]{1,0:T(8,128)S(1)}, u32[]{:S(2)}, u32[]{:S(2)}) collective-permute-start(f32[64,2048]{1,0:T(8,128)} %bitcast.10), channel_id=1, source_target_pairs={{0,1},{1,0},{2,3},{3,2},{4,5},{5,4},{6,7},{7,6},{8,9},{9,8},{10,11... | collective-permute-start | bytes 1572872 | tf_op jit(solution)/shard_map/ppermute | solution.py:370
  2.5 5.4 %copy-start.2 = (f32[4,64]{1,0:T(4,128)S(1)}, f32[4,64]{1,0:T(4,128)}, u32[]{:S(2)}) copy-start(f32[4,64]{1,0:T(4,128)} %topics_ref.1) | copy-start | bytes 3076
  2.5 15.5 %collective-permute-start.1 = (f32[8,4224]{1,0:T(8,128)S(1)}, f32[8,4224]{1,0:T(8,128)S(1)}, u32[]{:S(2)}, u32[]{:S(2)}) collective-permute-start(f32[8,4224]{1,0:T(8,128)S(1)} %get-tuple-element.47), channel_id=1, source_target_pairs={{0,7},{1,6},{2,5},{3,4},{4,3},{5,2},{6,1},{7,0},{8,15},{9,14},{10,... | collective-permute-start | bytes 405512 | tf_op jit(solution)/shard_map/ppermute | solution.py:359
  7.3 10.7 %collective-permute-start.2 = (f32[8,4224]{1,0:T(8,128)S(1)}, f32[8,4224]{1,0:T(8,128)S(1)}, u32[]{:S(2)}, u32[]{:S(2)}) collective-permute-start(f32[8,4224]{1,0:T(8,128)S(1)} %get-tuple-element.48), channel_id=1, source_target_pairs={{0,3},{1,2},{2,1},{3,0},{4,7},{5,6},{6,5},{7,4},{8,11},{9,10},{10,... | collective-permute-start | bytes 405512 | tf_op jit(solution)/shard_map/ppermute | solution.py:359
  7.3 11.9 %collective-permute-start.3 = (f32[8,4224]{1,0:T(8,128)S(1)}, f32[8,4224]{1,0:T(8,128)S(1)}, u32[]{:S(2)}, u32[]{:S(2)}) collective-permute-start(f32[8,4224]{1,0:T(8,128)S(1)} %get-tuple-element.49), channel_id=1, source_target_pairs={{0,4},{1,5},{2,6},{3,7},{4,0},{5,1},{6,2},{7,3},{8,12},{9,13},{10,... | collective-permute-start | bytes 405512 | tf_op jit(solution)/shard_map/ppermute | solution.py:359
  7.9 1.0 %copy-start.1 = (s32[4,16384]{1,0:T(4,128)S(1)}, s32[4,16384]{1,0:T(4,128)}, u32[]{:S(2)}) copy-start(s32[4,16384]{1,0:T(4,128)} %counts_ref.1) | copy-start | bytes 786436
  8.9 1.2 %copy-start.3 = (s32[1,64]{1,0:T(1,128)S(1)}, s32[1,64]{1,0:T(1,128)}, u32[]{:S(2)}) copy-start(s32[1,64]{1,0:T(1,128)} %perm_hbm.1) | copy-start | bytes 772
  8.9 9.0 %collective-permute-start.4 = (f32[4,4224]{1,0:T(4,128)S(1)}, f32[4,4224]{1,0:T(4,128)S(1)}, u32[]{:S(2)}, u32[]{:S(2)}) collective-permute-start(f32[4,4224]{1,0:T(4,128)S(1)} %get-tuple-element.51), channel_id=1, source_target_pairs={{0,3},{1,2},{2,1},{3,0},{4,7},{5,6},{6,5},{7,4},{8,11},{9,10},{10,... | collective-permute-start | bytes 202760 | tf_op jit(solution)/shard_map/ppermute | solution.py:359
  19.7 20.0 %collective-permute-start.14 = (f32[32,2048]{1,0:T(8,128)S(1)}, f32[32,2048]{1,0:T(8,128)S(1)}, u32[]{:S(2)}, u32[]{:S(2)}) collective-permute-start(f32[32,2048]{1,0:T(8,128)S(1)} %get-tuple-element.63), channel_id=1, source_target_pairs={{0,1},{1,0},{2,3},{3,2},{4,5},{5,4},{6,7},{7,6},{8,9},{9,8},{10,11... | collective-permute-start | bytes 786440 | tf_op jit(solution)/shard_map/ppermute | solution.py:370
  19.7 5.0 %collective-permute-start.5 = (f32[24,128]{1,0:T(8,128)S(1)}, f32[24,128]{1,0:T(8,128)S(1)}, u32[]{:S(2)}, u32[]{:S(2)}) collective-permute-start(f32[24,128]{1,0:T(8,128)S(1)} %get-tuple-element.53.refs_4_), channel_id=1, source_target_pairs={{0,7},{1,6},{2,5},{3,4},{4,3},{5,2},{6,1},{7,0},{8,15},{9,14},{10,... | collective-permute-start | bytes 36872 | tf_op jit(solution)/shard_map/ppermute | solution.py:359
  22.3 4.6 %collective-permute-start.6 = (f32[24,128]{1,0:T(8,128)S(1)}, f32[24,128]{1,0:T(8,128)S(1)}, u32[]{:S(2)}, u32[]{:S(2)}) collective-permute-start(f32[24,128]{1,0:T(8,128)S(1)} %get-tuple-element.53.refs_4_), channel_id=1, source_target_pairs={{0,4},{1,5},{2,6},{3,7},{4,0},{5,1},{6,2},{7,3},{8,12},{9,13},{10,... | collective-permute-start | bytes 36872 | tf_op jit(solution)/shard_map/ppermute | solution.py:359
  22.3 4.6 %collective-permute-start.7 = (f32[24,128]{1,0:T(8,128)S(1)}, f32[24,128]{1,0:T(8,128)S(1)}, u32[]{:S(2)}, u32[]{:S(2)}) collective-permute-start(f32[24,128]{1,0:T(8,128)S(1)} %get-tuple-element.53.refs_4_), channel_id=1, source_target_pairs={{0,3},{1,2},{2,1},{3,0},{4,7},{5,6},{6,5},{7,4},{8,11},{9,10},{10,... | collective-permute-start | bytes 36872 | tf_op jit(solution)/shard_map/ppermute | solution.py:359
  27.5 5.7 %collective-permute-start.8 = (f32[18,128]{1,0:T(8,128)S(1)}, f32[18,128]{1,0:T(8,128)S(1)}, u32[]{:S(2)}, u32[]{:S(2)}) collective-permute-start(f32[18,128]{1,0:T(8,128)S(1)} %get-tuple-element.57), channel_id=1, source_target_pairs={{0,7},{1,6},{2,5},{3,4},{4,3},{5,2},{6,1},{7,0},{8,15},{9,14},{10,... | collective-permute-start | bytes 27656 | tf_op jit(solution)/shard_map/ppermute | solution.py:359
  28.6 4.6 %collective-permute-start.9 = (f32[17,128]{1,0:T(8,128)S(1)}, f32[17,128]{1,0:T(8,128)S(1)}, u32[]{:S(2)}, u32[]{:S(2)}) collective-permute-start(f32[17,128]{1,0:T(8,128)S(1)} %get-tuple-element.58), channel_id=1, source_target_pairs={{0,4},{1,5},{2,6},{3,7},{4,0},{5,1},{6,2},{7,3},{8,12},{9,13},{10,... | collective-permute-start | bytes 26120 | tf_op jit(solution)/shard_map/ppermute | solution.py:359
  29.2 3.6 %collective-permute-start.10 = (f32[16,128]{1,0:T(8,128)S(1)}, f32[16,128]{1,0:T(8,128)S(1)}, u32[]{:S(2)}, u32[]{:S(2)}) collective-permute-start(f32[16,128]{1,0:T(8,128)S(1)} %get-tuple-element.56.refs_5_), channel_id=1, source_target_pairs={{0,3},{1,2},{2,1},{3,0},{4,7},{5,6},{6,5},{7,4},{8,11},{9,10},{10,... | collective-permute-start | bytes 24584 | tf_op jit(solution)/shard_map/ppermute | solution.py:359
  33.8 4.9 %collective-permute-start.11 = (f32[16,128]{1,0:T(8,128)S(1)}, f32[16,128]{1,0:T(8,128)S(1)}, u32[]{:S(2)}, u32[]{:S(2)}) collective-permute-start(f32[16,128]{1,0:T(8,128)S(1)} %get-tuple-element.61), channel_id=1, source_target_pairs={{0,7},{1,6},{2,5},{3,4},{4,3},{5,2},{6,1},{7,0},{8,15},{9,14},{10,... | collective-permute-start | bytes 24584 | tf_op jit(solution)/shard_map/ppermute | solution.py:359
  35.2 4.5 %collective-permute-start.12 = (f32[16,128]{1,0:T(8,128)S(1)}, f32[16,128]{1,0:T(8,128)S(1)}, u32[]{:S(2)}, u32[]{:S(2)}) collective-permute-start(f32[16,128]{1,0:T(8,128)S(1)} %get-tuple-element.62), channel_id=1, source_target_pairs={{0,4},{1,5},{2,6},{3,7},{4,0},{5,1},{6,2},{7,3},{8,12},{9,13},{10,... | collective-permute-start | bytes 24584 | tf_op jit(solution)/shard_map/ppermute | solution.py:359
  36.5 3.3 %collective-permute-start.13 = (f32[16,128]{1,0:T(8,128)S(1)}, f32[16,128]{1,0:T(8,128)S(1)}, u32[]{:S(2)}, u32[]{:S(2)}) collective-permute-start(f32[16,128]{1,0:T(8,128)S(1)} %get-tuple-element.60.refs_0_), channel_id=1, source_target_pairs={{0,3},{1,2},{2,1},{3,0},{4,7},{5,6},{6,5},{7,4},{8,11},{9,10},{10,... | collective-permute-start | bytes 24584 | tf_op jit(solution)/shard_map/ppermute | solution.py:359
  39.8 1.2 %collective-permute-start.15 = (f32[32,128]{1,0:T(8,128)S(1)}, f32[32,128]{1,0:T(8,128)S(1)}, u32[]{:S(2)}, u32[]{:S(2)}) collective-permute-start(f32[32,128]{1,0:T(8,128)S(1)} %shard_map.92.topics_ref), channel_id=1, source_target_pairs={{0,1},{1,0},{2,3},{3,2},{4,5},{5,4},{6,7},{7,6},{8,9},{9,8},{10,11... | collective-permute-start | bytes 49160 | tf_op jit(solution)/shard_map/ppermute | solution.py:370
  41.5 9.5 %collective-permute-start.16 = (f32[64,512]{1,0:T(8,128)S(1)}, f32[64,512]{1,0:T(8,128)S(1)}, u32[]{:S(2)}, u32[]{:S(2)}) collective-permute-start(f32[64,512]{1,0:T(8,128)S(1)} %get-tuple-element.88), channel_id=1, source_target_pairs={{0,24},{8,16},{16,8},{24,0},{1,25},{9,17},{17,9},{25,1},{2,26},{10... | collective-permute-start | bytes 393224 | tf_op jit(solution)/shard_map/ppermute | solution.py:373
  44.0 7.0 %collective-permute-start.17 = (f32[64,512]{1,0:T(8,128)S(1)}, f32[64,512]{1,0:T(8,128)S(1)}, u32[]{:S(2)}, u32[]{:S(2)}) collective-permute-start(f32[64,512]{1,0:T(8,128)S(1)} %get-tuple-element.87), channel_id=1, source_target_pairs={{0,16},{8,24},{16,0},{24,8},{1,17},{9,25},{17,1},{25,9},{2,18},{10... | collective-permute-start | bytes 393224 | tf_op jit(solution)/shard_map/ppermute | solution.py:373
  44.5 6.4 %collective-permute-start.18 = (f32[64,512]{1,0:T(8,128)S(1)}, f32[64,512]{1,0:T(8,128)S(1)}, u32[]{:S(2)}, u32[]{:S(2)}) collective-permute-start(f32[64,512]{1,0:T(8,128)S(1)} %get-tuple-element.86), channel_id=1, source_target_pairs={{0,8},{8,0},{16,24},{24,16},{1,9},{9,1},{17,25},{25,17},{2,10},{10... | collective-permute-start | bytes 393224 | tf_op jit(solution)/shard_map/ppermute | solution.py:373
  45.0 5.9 %collective-permute-start.19 = (f32[4,4224]{1,0:T(4,128)S(1)}, f32[4,4224]{1,0:T(4,128)S(1)}, u32[]{:S(2)}, u32[]{:S(2)}) collective-permute-start(f32[4,4224]{1,0:T(4,128)S(1)} %get-tuple-element.70), channel_id=1, source_target_pairs={{0,4},{1,5},{2,6},{3,7},{4,0},{5,1},{6,2},{7,3},{8,12},{9,13},{10,... | collective-permute-start | bytes 202760 | tf_op jit(solution)/shard_map/ppermute | solution.py:359
  51.0 9.1 %collective-permute-start.20 = (f32[64,512]{1,0:T(8,128)S(1)}, f32[64,512]{1,0:T(8,128)S(1)}, u32[]{:S(2)}, u32[]{:S(2)}) collective-permute-start(f32[64,512]{1,0:T(8,128)S(1)} %shard_map.95.refs_0_), channel_id=1, source_target_pairs={{0,24},{8,16},{16,8},{24,0},{1,25},{9,17},{17,9},{25,1},{2,26},{10... | collective-permute-start | bytes 393224 | tf_op jit(solution)/shard_map/ppermute | solution.py:373
  53.5 6.6 %collective-permute-start.24 = (f32[64,512]{1,0:T(8,128)S(1)}, f32[64,512]{1,0:T(8,128)S(1)}, u32[]{:S(2)}, u32[]{:S(2)}) collective-permute-start(f32[64,512]{1,0:T(8,128)S(1)} %shard_map.95.refs_0_), channel_id=1, source_target_pairs={{0,16},{8,24},{16,0},{24,8},{1,17},{9,25},{17,1},{25,9},{2,18},{10... | collective-permute-start | bytes 393224 | tf_op jit(solution)/shard_map/ppermute | solution.py:373
  54.1 6.6 %collective-permute-start.26 = (f32[64,512]{1,0:T(8,128)S(1)}, f32[64,512]{1,0:T(8,128)S(1)}, u32[]{:S(2)}, u32[]{:S(2)}) collective-permute-start(f32[64,512]{1,0:T(8,128)S(1)} %shard_map.95.refs_0_), channel_id=1, source_target_pairs={{0,8},{8,0},{16,24},{24,16},{1,9},{9,1},{17,25},{25,17},{2,10},{10... | collective-permute-start | bytes 393224 | tf_op jit(solution)/shard_map/ppermute | solution.py:373
  54.6 5.6 %collective-permute-start.21 = (f32[4,4224]{1,0:T(4,128)S(1)}, f32[4,4224]{1,0:T(4,128)S(1)}, u32[]{:S(2)}, u32[]{:S(2)}) collective-permute-start(f32[4,4224]{1,0:T(4,128)S(1)} %get-tuple-element.72), channel_id=1, source_target_pairs={{0,7},{1,6},{2,5},{3,4},{4,3},{5,2},{6,1},{7,0},{8,15},{9,14},{10,... | collective-permute-start | bytes 202760 | tf_op jit(solution)/shard_map/ppermute | solution.py:359
  55.0 6.3 %collective-permute-start.22 = (f32[64,512]{1,0:T(8,128)S(1)}, f32[64,512]{1,0:T(8,128)S(1)}, u32[]{:S(2)}, u32[]{:S(2)}) collective-permute-start(f32[64,512]{1,0:T(8,128)S(1)} %shard_map.95.refs_0_), channel_id=1, source_target_pairs={{0,1},{1,0},{2,3},{3,2},{4,5},{5,4},{6,7},{7,6},{8,9},{9,8},{10,11... | collective-permute-start | bytes 393224 | tf_op jit(solution)/shard_map/ppermute | solution.py:370
  60.2 1.3 %collective-permute-start.23 = (f32[64,512]{1,0:T(8,128)S(1)}, f32[64,512]{1,0:T(8,128)S(1)}, u32[]{:S(2)}, u32[]{:S(2)}) collective-permute-start(f32[64,512]{1,0:T(8,128)S(1)} %collective-permute-done.20.refs_1_), channel_id=1, source_target_pairs={{0,1},{1,0},{2,3},{3,2},{4,5},{5,4},{6,7},{7,6},{8,9},{9,8},{10,11... | collective-permute-start | bytes 393224 | tf_op jit(solution)/shard_map/ppermute | solution.py:370
  60.2 1.5 %collective-permute-start.25 = (f32[64,512]{1,0:T(8,128)S(1)}, f32[64,512]{1,0:T(8,128)S(1)}, u32[]{:S(2)}, u32[]{:S(2)}) collective-permute-start(f32[64,512]{1,0:T(8,128)S(1)} %collective-permute-done.24.refs_2_), channel_id=1, source_target_pairs={{0,1},{1,0},{2,3},{3,2},{4,5},{5,4},{6,7},{7,6},{8,9},{9,8},{10,11... | collective-permute-start | bytes 393224 | tf_op jit(solution)/shard_map/ppermute | solution.py:370
  60.7 1.3 %collective-permute-start.27 = (f32[64,512]{1,0:T(8,128)S(1)}, f32[64,512]{1,0:T(8,128)S(1)}, u32[]{:S(2)}, u32[]{:S(2)}) collective-permute-start(f32[64,512]{1,0:T(8,128)S(1)} %collective-permute-done.26.refs_3_), channel_id=1, source_target_pairs={{0,1},{1,0},{2,3},{3,2},{4,5},{5,4},{6,7},{7,6},{8,9},{9,8},{10,11... | collective-permute-start | bytes 393224 | tf_op jit(solution)/shard_map/ppermute | solution.py:370
  62.5 4.9 %collective-permute-start.28 = (f32[16,128]{1,0:T(8,128)S(1)}, f32[16,128]{1,0:T(8,128)S(1)}, u32[]{:S(2)}, u32[]{:S(2)}) collective-permute-start(f32[16,128]{1,0:T(8,128)S(1)} %get-tuple-element.76.refs_4_), channel_id=1, source_target_pairs={{0,7},{1,6},{2,5},{3,4},{4,3},{5,2},{6,1},{7,0},{8,15},{9,14},{10,... | collective-permute-start | bytes 24584 | tf_op jit(solution)/shard_map/ppermute | solution.py:359
  64.1 4.5 %collective-permute-start.29 = (f32[16,128]{1,0:T(8,128)S(1)}, f32[16,128]{1,0:T(8,128)S(1)}, u32[]{:S(2)}, u32[]{:S(2)}) collective-permute-start(f32[16,128]{1,0:T(8,128)S(1)} %get-tuple-element.76.refs_4_), channel_id=1, source_target_pairs={{0,4},{1,5},{2,6},{3,7},{4,0},{5,1},{6,2},{7,3},{8,12},{9,13},{10,... | collective-permute-start | bytes 24584 | tf_op jit(solution)/shard_map/ppermute | solution.py:359
  64.7 3.9 %collective-permute-start.30 = (f32[16,128]{1,0:T(8,128)S(1)}, f32[16,128]{1,0:T(8,128)S(1)}, u32[]{:S(2)}, u32[]{:S(2)}) collective-permute-start(f32[16,128]{1,0:T(8,128)S(1)} %get-tuple-element.76.refs_4_), channel_id=1, source_target_pairs={{0,3},{1,2},{2,1},{3,0},{4,7},{5,6},{6,5},{7,4},{8,11},{9,10},{10,... | collective-permute-start | bytes 24584 | tf_op jit(solution)/shard_map/ppermute | solution.py:359
  69.3 4.8 %collective-permute-start.31 = (f32[4,128]{1,0:T(4,128)S(1)}, f32[4,128]{1,0:T(4,128)S(1)}, u32[]{:S(2)}, u32[]{:S(2)}) collective-permute-start(f32[4,128]{1,0:T(4,128)S(1)} %get-tuple-element.83), channel_id=1, source_target_pairs={{0,7},{1,6},{2,5},{3,4},{4,3},{5,2},{6,1},{7,0},{8,15},{9,14},{10,... | collective-permute-start | bytes 6152 | tf_op jit(solution)/shard_map/ppermute | solution.py:359
  70.3 4.5 %collective-permute-start.32 = (f32[4,128]{1,0:T(4,128)S(1)}, f32[4,128]{1,0:T(4,128)S(1)}, u32[]{:S(2)}, u32[]{:S(2)}) collective-permute-start(f32[4,128]{1,0:T(4,128)S(1)} %get-tuple-element.84), channel_id=1, source_target_pairs={{0,4},{1,5},{2,6},{3,7},{4,0},{5,1},{6,2},{7,3},{8,12},{9,13},{10,... | collective-permute-start | bytes 6152 | tf_op jit(solution)/shard_map/ppermute | solution.py:359
  71.7 3.1 %collective-permute-start.33 = (f32[4,128]{1,0:T(4,128)S(1)}, f32[4,128]{1,0:T(4,128)S(1)}, u32[]{:S(2)}, u32[]{:S(2)}) collective-permute-start(f32[4,128]{1,0:T(4,128)S(1)} %get-tuple-element.85), channel_id=1, source_target_pairs={{0,3},{1,2},{2,1},{3,0},{4,7},{5,6},{6,5},{7,4},{8,11},{9,10},{10,... | collective-permute-start | bytes 6152 | tf_op jit(solution)/shard_map/ppermute | solution.py:359

commit v7 on v6

--- a/solution.py
+++ b/solution.py
@@ -225,7 +225,7 @@
     weighted = jnp.concatenate([ref[:, :span] for ref in payload], axis=0)
     part = pack(product_of(weighted / recon_of(topics, wide_ref[...]), tall_ref[...]))
     part_ref[: part.shape[0]] = part
-    part_ref[part.shape[0] :] = col_part_ref[...]
+    part_ref[part.shape[0] :] = col_part_ref[:1]
     words = span // cores
     for half, ref in enumerate(half_refs):
         ref[...] = weighted[:, half * words : (half + 1) * words]
@@ -236,7 +236,8 @@
     if refs[-1].shape[0] == 8:
         payload, parts = refs[:chips][::-1], refs[chips : 2 * chips]
         topics_ref, *part_refs, total_ref = refs[2 * chips :]
-        total_ref[...] = sum(ref[packed:] for ref in parts)
+        total = sum(ref[packed : packed + 1] for ref in parts)
+        total_ref[...] = jnp.broadcast_to(total, total_ref.shape)
     else:
         total_ref, payload, parts = refs[0], refs[1 : chips + 1][::-1], refs[chips + 1 : 2 * chips + 1]
         topics_ref, *part_refs = refs[2 * chips + 1 :]
@@ -417,7 +418,7 @@
     count_order = [chips - 1] + list(range(1, chips - 1)) + [0]
     topics, part, *weighted = call(
         functools.partial(first_kernel, chips, cores, count_order),
-        [shape(rows, 2 * topic_count), shape(rows // 2 + 8, 2 * topic_count)]
+        [shape(rows, 2 * topic_count), shape(rows // 2 + 1, 2 * topic_count)]
         + [shape(rows, owned)] * cores,
         wide,
         tall,
@@ -429,7 +430,7 @@
         moved=4 * span * (rows + 2 * topic_count),
     )
     parts = [part] + [over_chips(part, step) for step in range(chips - 1, 0, -1)]
-    crossed = [over_cores(weighted[1])] if cores > 1 else []
+    crossed = []
     totals = []
     for update in range(1, UPDATES):
         topics, *outs = call(
@@ -447,6 +448,9 @@
             moved=4 * span * (rows + 2 * topic_count),
         )
         totals = totals or outs[chips - 1 :]
+        if update == 1 and cores > 1:
+            topics, weighted[1] = lax.optimization_barrier((topics, weighted[1]))
+            crossed = [over_cores(weighted[1])]
         parts = [outs[0]] + [over_chips(outs[step - 1], step) for step in range(chips - 1, 0, -1)]
     (col_total,) = totals
 

time: 75.5 us -> 75.3 us (level)
  transfers between devices with their start and end apart: 34 -> 34, of which waited for: 18 -> 18; matrix products, arithmetic and copies ran while one was open for 1% -> 1% of each run, Pallas kernels for 6% -> 5%
where the time goes in v7:
time: 75.3 us; the launch traced here: 75.2 us
  starting transfers between devices  37 us (49%)
  waiting for transfers between devices  28.4 us (38%)
  Pallas kernels  7.39 us (10%)
  local copies, waits for them, and re-layouts  1.67 us (2%)
  between operations  0.76 us (1%)
    ppermute x21, starting transfers between devices, over_chips(): lax.ppermute(array, 'doc', [(c * cores + k, (c ^ step) * cores + (k + ste...  27.2 us
    ppermute x21, waiting for transfers between devices, over_chips(): lax.ppermute(array, 'doc', [(c * cores + k, (c ^ step) * cores + (k + ste...  26.9 us
    ppermute x6, starting transfers between devices, over_pert(): return lax.ppermute(array, 'pert', [(m, m ^ step) for m in range(members)])  7.11 us
    pallas_call x13, Pallas kernels, call(): pl.pallas_call(kernel, out_shape=outs, in_specs=[pl.BlockSpec(memory_spac...  6.08 us
    ppermute x7, starting transfers between devices, over_cores(): return lax.ppermute(array, 'doc', [(d, d ^ 1) for d in range(doc_size)])  2.64 us
    unnamed x9, local copies, waits for them, and re-layouts  1.62 us
    ppermute x7, waiting for transfers between devices, over_cores(): return lax.ppermute(array, 'doc', [(d, d ^ 1) for d in range(doc_size)])  1.52 us
  transfers between devices with their start and end apart: 34, of which 18 were waited for; matrix products, arithmetic and copies ran while one was open for 1% of the time, Pallas kernels for 5%

profile of v7, /device:TPU:0, one launch (start us, length us, event | category | flops | bytes accessed | tf_op | source)
XLA Modules:
  0.0 75.2 jit_solution(11073039754055061532)
XLA Ops:
  0.6 0.5 collective-permute-start
  1.2 1.3 %shard_map.87 = (f32[8,4224]{1,0:T(8,128)S(1)}, f32[8,4224]{1,0:T(8,128)S(1)}, f32[8,4224]{1,0:T(8,128)S(1)}, f32[8,4224]{1,0:T(8,128)S(1)}) custom-call(s32[8,128]{1,0:T(8,128)} %bitcast.13, f32[8,64]{1,0:T(8,128)} %bitcast.14, s32[1,64]{1,0:T(1,128)} %perm_hbm.1, s32[8,16384]{1,0:T(8,128)} %bitcast.12), custom_call_target="tpu_custom_call" | custom-call | bytes 1572864 | tf_op jit(solution)/shard_map/pallas_call | solution.py:376
  2.5 4.8 %collective-permute-start.1 = (f32[8,4224]{1,0:T(8,128)S(1)}, f32[8,4224]{1,0:T(8,128)S(1)}, u32[]{:S(2)}, u32[]{:S(2)}) collective-permute-start(f32[8,4224]{1,0:T(8,128)S(1)} %get-tuple-element.49), channel_id=1, source_target_pairs={{0,7},{1,6},{2,5},{3,4},{4,3},{5,2},{6,1},{7,0},{8,15},{9,14},{10,... | collective-permute-start | bytes 405512 | tf_op jit(solution)/shard_map/ppermute | solution.py:360
  7.3 0.6 collective-permute-start.3
  7.9 0.9 %copy-done.1 = s32[4,16384]{1,0:T(4,128)S(1)} copy-done((s32[4,16384]{1,0:T(4,128)S(1)}, s32[4,16384]{1,0:T(4,128)}, u32[]{:S(2)}) %copy-start.1) | copy-done | bytes 262168
  8.9 0.1 shard_map.88
  8.9 1.1 %collective-permute-start.4 = (f32[4,4224]{1,0:T(4,128)S(1)}, f32[4,4224]{1,0:T(4,128)S(1)}, u32[]{:S(2)}, u32[]{:S(2)}) collective-permute-start(f32[4,4224]{1,0:T(4,128)S(1)} %get-tuple-element.53), channel_id=1, source_target_pairs={{0,3},{1,2},{2,1},{3,0},{4,7},{5,6},{6,5},{7,4},{8,11},{9,10},{10,... | collective-permute-start | bytes 202760 | tf_op jit(solution)/shard_map/ppermute | solution.py:360
  10.1 1.1 %shard_map.86 = (bf16[128,4096]{1,0:T(8,128)(2,1)S(1)}, bf16[4096,128]{1,0:T(8,128)(2,1)S(1)}, f32[8,128]{1,0:T(8,128)S(1)}, f32[64,2048]{1,0:T(8,128)S(1)}) custom-call(s32[1,64]{1,0:T(1,128)S(1)} %copy-done.3, f32[64,2048]{1,0:T(8,128)S(1)} %bitcast.11, f32[64,2048]{1,0:T(8,128)S(1)} %collective-permute-done.refs_1_), custom_call_target="tpu_custom_call" | custom-call | bytes 4194304 | tf_op jit(solution)/shard_map/pallas_call | solution.py:37
  11.2 6.8 %collective-permute-done.4.refs_4_.refs_5_.refs_1_ = f32[4,4224]{1,0:T(4,128)S(1)} collective-permute-done((f32[4,4224]{1,0:T(4,128)S(1)}, f32[4,4224]{1,0:T(4,128)S(1)}, u32[]{:S(2)}, u32[]{:S(2)}) %collective-permute-start.4) | collective-permute-done | bytes 67616 | tf_op jit(solution)/shard_map/ppermute | solution.py:360
  18.0 1.2 %collective-permute-done.3.refs_2_.refs_1_ = f32[8,4224]{1,0:T(8,128)S(1)} collective-permute-done((f32[8,4224]{1,0:T(8,128)S(1)}, f32[8,4224]{1,0:T(8,128)S(1)}, u32[]{:S(2)}, u32[]{:S(2)}) %collective-permute-start.3) | collective-permute-done | bytes 135200 | tf_op jit(solution)/shard_map/ppermute | solution.py:360
  19.2 0.5 shard_map.89
  19.7 1.4 %collective-permute-start.5 = (f32[17,128]{1,0:T(8,128)S(1)}, f32[17,128]{1,0:T(8,128)S(1)}, u32[]{:S(2)}, u32[]{:S(2)}) collective-permute-start(f32[17,128]{1,0:T(8,128)S(1)} %get-tuple-element.55.refs_4_), channel_id=1, source_target_pairs={{0,7},{1,6},{2,5},{3,4},{4,3},{5,2},{6,1},{7,0},{8,15},{9,14},{10,... | collective-permute-start | bytes 26120 | tf_op jit(solution)/shard_map/ppermute | solution.py:360
  21.1 0.7 collective-permute-start.6
  21.9 1.7 %collective-permute-start.7 = (f32[17,128]{1,0:T(8,128)S(1)}, f32[17,128]{1,0:T(8,128)S(1)}, u32[]{:S(2)}, u32[]{:S(2)}) collective-permute-start(f32[17,128]{1,0:T(8,128)S(1)} %get-tuple-element.55.refs_4_), channel_id=1, source_target_pairs={{0,3},{1,2},{2,1},{3,0},{4,7},{5,6},{6,5},{7,4},{8,11},{9,10},{10,... | collective-permute-start | bytes 26120 | tf_op jit(solution)/shard_map/ppermute | solution.py:360
  23.6 1.1 %collective-permute-done.5.refs_5_ = f32[17,128]{1,0:T(8,128)S(1)} collective-permute-done((f32[17,128]{1,0:T(8,128)S(1)}, f32[17,128]{1,0:T(8,128)S(1)}, u32[]{:S(2)}, u32[]{:S(2)}) %collective-permute-start.5) | collective-permute-done | bytes 8736 | tf_op jit(solution)/shard_map/ppermute | solution.py:360
  24.7 1.1 %collective-permute-done.6.refs_6_ = f32[17,128]{1,0:T(8,128)S(1)} collective-permute-done((f32[17,128]{1,0:T(8,128)S(1)}, f32[17,128]{1,0:T(8,128)S(1)}, u32[]{:S(2)}, u32[]{:S(2)}) %collective-permute-start.6) | collective-permute-done | bytes 8736 | tf_op jit(solution)/shard_map/ppermute | solution.py:360
  25.8 0.6 shard_map.90
  26.3 0.1 collective-permute-start.14
  26.4 2.0 %collective-permute-start.8 = (f32[18,128]{1,0:T(8,128)S(1)}, f32[18,128]{1,0:T(8,128)S(1)}, u32[]{:S(2)}, u32[]{:S(2)}) collective-permute-start(f32[18,128]{1,0:T(8,128)S(1)} %get-tuple-element.61), channel_id=1, source_target_pairs={{0,7},{1,6},{2,5},{3,4},{4,3},{5,2},{6,1},{7,0},{8,15},{9,14},{10,... | collective-permute-start | bytes 27656 | tf_op jit(solution)/shard_map/ppermute | solution.py:360
  28.4 0.4 collective-permute-start.9
  28.8 1.5 %collective-permute-start.10 = (f32[16,128]{1,0:T(8,128)S(1)}, f32[16,128]{1,0:T(8,128)S(1)}, u32[]{:S(2)}, u32[]{:S(2)}) collective-permute-start(f32[16,128]{1,0:T(8,128)S(1)} %get-tuple-element.60.refs_5_), channel_id=1, source_target_pairs={{0,3},{1,2},{2,1},{3,0},{4,7},{5,6},{6,5},{7,4},{8,11},{9,10},{10,... | collective-permute-start | bytes 24584 | tf_op jit(solution)/shard_map/ppermute | solution.py:360
  30.3 1.6 %collective-permute-done.10.refs_8_ = f32[16,128]{1,0:T(8,128)S(1)} collective-permute-done((f32[16,128]{1,0:T(8,128)S(1)}, f32[16,128]{1,0:T(8,128)S(1)}, u32[]{:S(2)}, u32[]{:S(2)}) %collective-permute-start.10) | collective-permute-done | bytes 8224 | tf_op jit(solution)/shard_map/ppermute | solution.py:360
  31.9 1.2 %collective-permute-done.9.refs_7_ = f32[17,128]{1,0:T(8,128)S(1)} collective-permute-done((f32[17,128]{1,0:T(8,128)S(1)}, f32[17,128]{1,0:T(8,128)S(1)}, u32[]{:S(2)}, u32[]{:S(2)}) %collective-permute-start.9) | collective-permute-done | bytes 8736 | tf_op jit(solution)/shard_map/ppermute | solution.py:360
  33.1 0.6 shard_map.91
  33.7 1.4 %collective-permute-start.11 = (f32[16,128]{1,0:T(8,128)S(1)}, f32[16,128]{1,0:T(8,128)S(1)}, u32[]{:S(2)}, u32[]{:S(2)}) collective-permute-start(f32[16,128]{1,0:T(8,128)S(1)} %get-tuple-element.65), channel_id=1, source_target_pairs={{0,7},{1,6},{2,5},{3,4},{4,3},{5,2},{6,1},{7,0},{8,15},{9,14},{10,... | collective-permute-start | bytes 24584 | tf_op jit(solution)/shard_map/ppermute | solution.py:360
  35.0 0.7 collective-permute-start.12
  35.8 1.8 %collective-permute-start.13 = (f32[16,128]{1,0:T(8,128)S(1)}, f32[16,128]{1,0:T(8,128)S(1)}, u32[]{:S(2)}, u32[]{:S(2)}) collective-permute-start(f32[16,128]{1,0:T(8,128)S(1)} %get-tuple-element.64.refs_0_), channel_id=1, source_target_pairs={{0,3},{1,2},{2,1},{3,0},{4,7},{5,6},{6,5},{7,4},{8,11},{9,10},{10,... | collective-permute-start | bytes 24584 | tf_op jit(solution)/shard_map/ppermute | solution.py:360
  37.5 1.0 %collective-permute-done.11.refs_1_ = f32[16,128]{1,0:T(8,128)S(1)} collective-permute-done((f32[16,128]{1,0:T(8,128)S(1)}, f32[16,128]{1,0:T(8,128)S(1)}, u32[]{:S(2)}, u32[]{:S(2)}) %collective-permute-start.11) | collective-permute-done | bytes 8224 | tf_op jit(solution)/shard_map/ppermute | solution.py:360
  38.5 1.0 %collective-permute-done.12.refs_2_ = f32[16,128]{1,0:T(8,128)S(1)} collective-permute-done((f32[16,128]{1,0:T(8,128)S(1)}, f32[16,128]{1,0:T(8,128)S(1)}, u32[]{:S(2)}, u32[]{:S(2)}) %collective-permute-start.12) | collective-permute-done | bytes 8224 | tf_op jit(solution)/shard_map/ppermute | solution.py:360
  39.6 0.1 shard_map.92.topics_ref
  39.7 0.4 shard_map.93.refs_1_
  40.1 0.8 %collective-permute-done.15.topics_ref = f32[32,128]{1,0:T(8,128)S(1)} collective-permute-done((f32[32,128]{1,0:T(8,128)S(1)}, f32[32,128]{1,0:T(8,128)S(1)}, u32[]{:S(2)}, u32[]{:S(2)}) %collective-permute-start.15) | collective-permute-done | bytes 16416 | tf_op jit(solution)/shard_map/ppermute | solution.py:371
  40.8 0.4 shard_map.94
  41.3 2.5 %collective-permute-start.16 = (f32[64,512]{1,0:T(8,128)S(1)}, f32[64,512]{1,0:T(8,128)S(1)}, u32[]{:S(2)}, u32[]{:S(2)}) collective-permute-start(f32[64,512]{1,0:T(8,128)S(1)} %get-tuple-element.92), channel_id=1, source_target_pairs={{0,24},{8,16},{16,8},{24,0},{1,25},{9,17},{17,9},{25,1},{2,26},{10... | collective-permute-start | bytes 393224 | tf_op jit(solution)/shard_map/ppermute | solution.py:374
  43.8 0.5 collective-permute-start.17
  44.3 0.5 collective-permute-start.18
  44.9 1.5 %collective-permute-start.19 = (f32[4,4224]{1,0:T(4,128)S(1)}, f32[4,4224]{1,0:T(4,128)S(1)}, u32[]{:S(2)}, u32[]{:S(2)}) collective-permute-start(f32[4,4224]{1,0:T(4,128)S(1)} %get-tuple-element.74), channel_id=1, source_target_pairs={{0,4},{1,5},{2,6},{3,7},{4,0},{5,1},{6,2},{7,3},{8,12},{9,13},{10,... | collective-permute-start | bytes 202760 | tf_op jit(solution)/shard_map/ppermute | solution.py:360
  46.3 4.5 %collective-permute-done.19.refs_4_.refs_6_.refs_2_ = f32[4,4224]{1,0:T(4,128)S(1)} collective-permute-done((f32[4,4224]{1,0:T(4,128)S(1)}, f32[4,4224]{1,0:T(4,128)S(1)}, u32[]{:S(2)}, u32[]{:S(2)}) %collective-permute-start.19) | collective-permute-done | bytes 67616 | tf_op jit(solution)/shard_map/ppermute | solution.py:360
  50.8 0.1 shard_map.95.refs_0_
  50.9 2.5 %collective-permute-start.20 = (f32[64,512]{1,0:T(8,128)S(1)}, f32[64,512]{1,0:T(8,128)S(1)}, u32[]{:S(2)}, u32[]{:S(2)}) collective-permute-start(f32[64,512]{1,0:T(8,128)S(1)} %shard_map.95.refs_0_), channel_id=1, source_target_pairs={{0,24},{8,16},{16,8},{24,0},{1,25},{9,17},{17,9},{25,1},{2,26},{10... | collective-permute-start | bytes 393224 | tf_op jit(solution)/shard_map/ppermute | solution.py:374
  53.4 0.5 collective-permute-start.24
  53.9 0.5 collective-permute-start.26
  54.4 1.4 %collective-permute-start.22 = (f32[64,512]{1,0:T(8,128)S(1)}, f32[64,512]{1,0:T(8,128)S(1)}, u32[]{:S(2)}, u32[]{:S(2)}) collective-permute-start(f32[64,512]{1,0:T(8,128)S(1)} %shard_map.95.refs_0_), channel_id=1, source_target_pairs={{0,1},{1,0},{2,3},{3,2},{4,5},{5,4},{6,7},{7,6},{8,9},{9,8},{10,11... | collective-permute-start | bytes 393224 | tf_op jit(solution)/shard_map/ppermute | solution.py:371
  55.8 4.1 %collective-permute-done.21.refs_7_.refs_3_ = f32[4,4224]{1,0:T(4,128)S(1)} collective-permute-done((f32[4,4224]{1,0:T(4,128)S(1)}, f32[4,4224]{1,0:T(4,128)S(1)}, u32[]{:S(2)}, u32[]{:S(2)}) %collective-permute-start.21) | collective-permute-done | bytes 67616 | tf_op jit(solution)/shard_map/ppermute | solution.py:360
  60.0 0.5 collective-permute-start.25
  60.5 0.1 collective-permute-start.27
  60.6 0.5 shard_map.96
  61.1 0.2 collective-permute-done.23.refs_1_
  61.3 0.2 collective-permute-done.25.refs_2_
  61.5 0.3 collective-permute-done.27.refs_3_
  61.8 0.5 shard_map.97
  62.4 1.1 %collective-permute-start.28 = (f32[16,128]{1,0:T(8,128)S(1)}, f32[16,128]{1,0:T(8,128)S(1)}, u32[]{:S(2)}, u32[]{:S(2)}) collective-permute-start(f32[16,128]{1,0:T(8,128)S(1)} %get-tuple-element.80.refs_4_), channel_id=1, source_target_pairs={{0,7},{1,6},{2,5},{3,4},{4,3},{5,2},{6,1},{7,0},{8,15},{9,14},{10,... | collective-permute-start | bytes 24584 | tf_op jit(solution)/shard_map/ppermute | solution.py:360
  63.5 1.1 %collective-permute-start.29 = (f32[16,128]{1,0:T(8,128)S(1)}, f32[16,128]{1,0:T(8,128)S(1)}, u32[]{:S(2)}, u32[]{:S(2)}) collective-permute-start(f32[16,128]{1,0:T(8,128)S(1)} %get-tuple-element.80.refs_4_), channel_id=1, source_target_pairs={{0,4},{1,5},{2,6},{3,7},{4,0},{5,1},{6,2},{7,3},{8,12},{9,13},{10,... | collective-permute-start | bytes 24584 | tf_op jit(solution)/shard_map/ppermute | solution.py:360
  64.6 1.6 %collective-permute-start.30 = (f32[16,128]{1,0:T(8,128)S(1)}, f32[16,128]{1,0:T(8,128)S(1)}, u32[]{:S(2)}, u32[]{:S(2)}) collective-permute-start(f32[16,128]{1,0:T(8,128)S(1)} %get-tuple-element.80.refs_4_), channel_id=1, source_target_pairs={{0,3},{1,2},{2,1},{3,0},{4,7},{5,6},{6,5},{7,4},{8,11},{9,10},{10,... | collective-permute-start | bytes 24584 | tf_op jit(solution)/shard_map/ppermute | solution.py:360
  66.2 1.0 %collective-permute-done.28.refs_5_ = f32[16,128]{1,0:T(8,128)S(1)} collective-permute-done((f32[16,128]{1,0:T(8,128)S(1)}, f32[16,128]{1,0:T(8,128)S(1)}, u32[]{:S(2)}, u32[]{:S(2)}) %collective-permute-start.28) | collective-permute-done | bytes 8224 | tf_op jit(solution)/shard_map/ppermute | solution.py:360
  67.3 0.8 %collective-permute-done.29.refs_6_ = f32[16,128]{1,0:T(8,128)S(1)} collective-permute-done((f32[16,128]{1,0:T(8,128)S(1)}, f32[16,128]{1,0:T(8,128)S(1)}, u32[]{:S(2)}, u32[]{:S(2)}) %collective-permute-start.29) | collective-permute-done | bytes 8224 | tf_op jit(solution)/shard_map/ppermute | solution.py:360
  68.1 0.7 shard_map.98
  68.8 1.4 %collective-permute-start.31 = (f32[4,128]{1,0:T(4,128)S(1)}, f32[4,128]{1,0:T(4,128)S(1)}, u32[]{:S(2)}, u32[]{:S(2)}) collective-permute-start(f32[4,128]{1,0:T(4,128)S(1)} %get-tuple-element.87), channel_id=1, source_target_pairs={{0,7},{1,6},{2,5},{3,4},{4,3},{5,2},{6,1},{7,0},{8,15},{9,14},{10,... | collective-permute-start | bytes 6152 | tf_op jit(solution)/shard_map/ppermute | solution.py:360
  70.1 1.4 %collective-permute-start.32 = (f32[4,128]{1,0:T(4,128)S(1)}, f32[4,128]{1,0:T(4,128)S(1)}, u32[]{:S(2)}, u32[]{:S(2)}) collective-permute-start(f32[4,128]{1,0:T(4,128)S(1)} %get-tuple-element.88), channel_id=1, source_target_pairs={{0,4},{1,5},{2,6},{3,7},{4,0},{5,1},{6,2},{7,3},{8,12},{9,13},{10,... | collective-permute-start | bytes 6152 | tf_op jit(solution)/shard_map/ppermute | solution.py:360
  71.5 1.1 %collective-permute-start.33 = (f32[4,128]{1,0:T(4,128)S(1)}, f32[4,128]{1,0:T(4,128)S(1)}, u32[]{:S(2)}, u32[]{:S(2)}) collective-permute-start(f32[4,128]{1,0:T(4,128)S(1)} %get-tuple-element.89), channel_id=1, source_target_pairs={{0,3},{1,2},{2,1},{3,0},{4,7},{5,6},{6,5},{7,4},{8,11},{9,10},{10,... | collective-permute-start | bytes 6152 | tf_op jit(solution)/shard_map/ppermute | solution.py:360
  72.6 0.7 copy.9
  73.3 0.3 collective-permute-done.31.refs_1_
  73.6 1.0 %collective-permute-done.32.refs_2_ = f32[4,128]{1,0:T(4,128)S(1)} collective-permute-done((f32[4,128]{1,0:T(4,128)S(1)}, f32[4,128]{1,0:T(4,128)S(1)}, u32[]{:S(2)}, u32[]{:S(2)}) %collective-permute-start.32) | collective-permute-done | bytes 2080 | tf_op jit(solution)/shard_map/ppermute | solution.py:360
  74.6 0.6 shard_map.99
  (28 shorter events, 0.1 us)
Async XLA Ops:
  0.6 9.5 %copy-start = (f32[1,2048,64]{1,2,0:T(8,128)S(1)}, f32[1,2048,64]{1,2,0:T(8,128)}, u32[]{:S(2)}) copy-start(f32[1,2048,64]{1,2,0:T(8,128)} %param.10) | copy-start | bytes 1572868
  0.6 9.4 %collective-permute-start = (f32[64,2048]{1,0:T(8,128)}, f32[64,2048]{1,0:T(8,128)S(1)}, u32[]{:S(2)}, u32[]{:S(2)}) collective-permute-start(f32[64,2048]{1,0:T(8,128)} %bitcast.10), channel_id=1, source_target_pairs={{0,1},{1,0},{2,3},{3,2},{4,5},{5,4},{6,7},{7,6},{8,9},{9,8},{10,11... | collective-permute-start | bytes 1572872 | tf_op jit(solution)/shard_map/ppermute | solution.py:371
  2.5 5.4 %copy-start.2 = (f32[4,64]{1,0:T(4,128)S(1)}, f32[4,64]{1,0:T(4,128)}, u32[]{:S(2)}) copy-start(f32[4,64]{1,0:T(4,128)} %topics_ref.1) | copy-start | bytes 3076
  2.5 15.5 %collective-permute-start.1 = (f32[8,4224]{1,0:T(8,128)S(1)}, f32[8,4224]{1,0:T(8,128)S(1)}, u32[]{:S(2)}, u32[]{:S(2)}) collective-permute-start(f32[8,4224]{1,0:T(8,128)S(1)} %get-tuple-element.49), channel_id=1, source_target_pairs={{0,7},{1,6},{2,5},{3,4},{4,3},{5,2},{6,1},{7,0},{8,15},{9,14},{10,... | collective-permute-start | bytes 405512 | tf_op jit(solution)/shard_map/ppermute | solution.py:360
  7.3 10.7 %collective-permute-start.2 = (f32[8,4224]{1,0:T(8,128)S(1)}, f32[8,4224]{1,0:T(8,128)S(1)}, u32[]{:S(2)}, u32[]{:S(2)}) collective-permute-start(f32[8,4224]{1,0:T(8,128)S(1)} %get-tuple-element.50), channel_id=1, source_target_pairs={{0,3},{1,2},{2,1},{3,0},{4,7},{5,6},{6,5},{7,4},{8,11},{9,10},{10,... | collective-permute-start | bytes 405512 | tf_op jit(solution)/shard_map/ppermute | solution.py:360
  7.3 11.9 %collective-permute-start.3 = (f32[8,4224]{1,0:T(8,128)S(1)}, f32[8,4224]{1,0:T(8,128)S(1)}, u32[]{:S(2)}, u32[]{:S(2)}) collective-permute-start(f32[8,4224]{1,0:T(8,128)S(1)} %get-tuple-element.51), channel_id=1, source_target_pairs={{0,4},{1,5},{2,6},{3,7},{4,0},{5,1},{6,2},{7,3},{8,12},{9,13},{10,... | collective-permute-start | bytes 405512 | tf_op jit(solution)/shard_map/ppermute | solution.py:360
  7.9 1.0 %copy-start.1 = (s32[4,16384]{1,0:T(4,128)S(1)}, s32[4,16384]{1,0:T(4,128)}, u32[]{:S(2)}) copy-start(s32[4,16384]{1,0:T(4,128)} %counts_ref.1) | copy-start | bytes 786436
  8.9 1.2 %copy-start.3 = (s32[1,64]{1,0:T(1,128)S(1)}, s32[1,64]{1,0:T(1,128)}, u32[]{:S(2)}) copy-start(s32[1,64]{1,0:T(1,128)} %perm_hbm.1) | copy-start | bytes 772
  8.9 9.0 %collective-permute-start.4 = (f32[4,4224]{1,0:T(4,128)S(1)}, f32[4,4224]{1,0:T(4,128)S(1)}, u32[]{:S(2)}, u32[]{:S(2)}) collective-permute-start(f32[4,4224]{1,0:T(4,128)S(1)} %get-tuple-element.53), channel_id=1, source_target_pairs={{0,3},{1,2},{2,1},{3,0},{4,7},{5,6},{6,5},{7,4},{8,11},{9,10},{10,... | collective-permute-start | bytes 202760 | tf_op jit(solution)/shard_map/ppermute | solution.py:360
  19.7 4.9 %collective-permute-start.5 = (f32[17,128]{1,0:T(8,128)S(1)}, f32[17,128]{1,0:T(8,128)S(1)}, u32[]{:S(2)}, u32[]{:S(2)}) collective-permute-start(f32[17,128]{1,0:T(8,128)S(1)} %get-tuple-element.55.refs_4_), channel_id=1, source_target_pairs={{0,7},{1,6},{2,5},{3,4},{4,3},{5,2},{6,1},{7,0},{8,15},{9,14},{10,... | collective-permute-start | bytes 26120 | tf_op jit(solution)/shard_map/ppermute | solution.py:360
  21.1 4.6 %collective-permute-start.6 = (f32[17,128]{1,0:T(8,128)S(1)}, f32[17,128]{1,0:T(8,128)S(1)}, u32[]{:S(2)}, u32[]{:S(2)}) collective-permute-start(f32[17,128]{1,0:T(8,128)S(1)} %get-tuple-element.55.refs_4_), channel_id=1, source_target_pairs={{0,4},{1,5},{2,6},{3,7},{4,0},{5,1},{6,2},{7,3},{8,12},{9,13},{10,... | collective-permute-start | bytes 26120 | tf_op jit(solution)/shard_map/ppermute | solution.py:360
  21.9 3.9 %collective-permute-start.7 = (f32[17,128]{1,0:T(8,128)S(1)}, f32[17,128]{1,0:T(8,128)S(1)}, u32[]{:S(2)}, u32[]{:S(2)}) collective-permute-start(f32[17,128]{1,0:T(8,128)S(1)} %get-tuple-element.55.refs_4_), channel_id=1, source_target_pairs={{0,3},{1,2},{2,1},{3,0},{4,7},{5,6},{6,5},{7,4},{8,11},{9,10},{10,... | collective-permute-start | bytes 26120 | tf_op jit(solution)/shard_map/ppermute | solution.py:360
  26.3 13.2 %collective-permute-start.14 = (f32[32,2048]{1,0:T(8,128)S(1)}, f32[32,2048]{1,0:T(8,128)S(1)}, u32[]{:S(2)}, u32[]{:S(2)}) collective-permute-start(f32[32,2048]{1,0:T(8,128)S(1)} %get-tuple-element.67), channel_id=1, source_target_pairs={{0,1},{1,0},{2,3},{3,2},{4,5},{5,4},{6,7},{7,6},{8,9},{9,8},{10,11... | collective-permute-start | bytes 786440 | tf_op jit(solution)/shard_map/ppermute | solution.py:371
  26.4 6.7 %collective-permute-start.8 = (f32[18,128]{1,0:T(8,128)S(1)}, f32[18,128]{1,0:T(8,128)S(1)}, u32[]{:S(2)}, u32[]{:S(2)}) collective-permute-start(f32[18,128]{1,0:T(8,128)S(1)} %get-tuple-element.61), channel_id=1, source_target_pairs={{0,7},{1,6},{2,5},{3,4},{4,3},{5,2},{6,1},{7,0},{8,15},{9,14},{10,... | collective-permute-start | bytes 27656 | tf_op jit(solution)/shard_map/ppermute | solution.py:360
  28.4 4.7 %collective-permute-start.9 = (f32[17,128]{1,0:T(8,128)S(1)}, f32[17,128]{1,0:T(8,128)S(1)}, u32[]{:S(2)}, u32[]{:S(2)}) collective-permute-start(f32[17,128]{1,0:T(8,128)S(1)} %get-tuple-element.62), channel_id=1, source_target_pairs={{0,4},{1,5},{2,6},{3,7},{4,0},{5,1},{6,2},{7,3},{8,12},{9,13},{10,... | collective-permute-start | bytes 26120 | tf_op jit(solution)/shard_map/ppermute | solution.py:360
  28.8 3.1 %collective-permute-start.10 = (f32[16,128]{1,0:T(8,128)S(1)}, f32[16,128]{1,0:T(8,128)S(1)}, u32[]{:S(2)}, u32[]{:S(2)}) collective-permute-start(f32[16,128]{1,0:T(8,128)S(1)} %get-tuple-element.60.refs_5_), channel_id=1, source_target_pairs={{0,3},{1,2},{2,1},{3,0},{4,7},{5,6},{6,5},{7,4},{8,11},{9,10},{10,... | collective-permute-start | bytes 24584 | tf_op jit(solution)/shard_map/ppermute | solution.py:360
  33.7 4.9 %collective-permute-start.11 = (f32[16,128]{1,0:T(8,128)S(1)}, f32[16,128]{1,0:T(8,128)S(1)}, u32[]{:S(2)}, u32[]{:S(2)}) collective-permute-start(f32[16,128]{1,0:T(8,128)S(1)} %get-tuple-element.65), channel_id=1, source_target_pairs={{0,7},{1,6},{2,5},{3,4},{4,3},{5,2},{6,1},{7,0},{8,15},{9,14},{10,... | collective-permute-start | bytes 24584 | tf_op jit(solution)/shard_map/ppermute | solution.py:360
  35.0 4.5 %collective-permute-start.12 = (f32[16,128]{1,0:T(8,128)S(1)}, f32[16,128]{1,0:T(8,128)S(1)}, u32[]{:S(2)}, u32[]{:S(2)}) collective-permute-start(f32[16,128]{1,0:T(8,128)S(1)} %get-tuple-element.66), channel_id=1, source_target_pairs={{0,4},{1,5},{2,6},{3,7},{4,0},{5,1},{6,2},{7,3},{8,12},{9,13},{10,... | collective-permute-start | bytes 24584 | tf_op jit(solution)/shard_map/ppermute | solution.py:360
  35.8 3.8 %collective-permute-start.13 = (f32[16,128]{1,0:T(8,128)S(1)}, f32[16,128]{1,0:T(8,128)S(1)}, u32[]{:S(2)}, u32[]{:S(2)}) collective-permute-start(f32[16,128]{1,0:T(8,128)S(1)} %get-tuple-element.64.refs_0_), channel_id=1, source_target_pairs={{0,3},{1,2},{2,1},{3,0},{4,7},{5,6},{6,5},{7,4},{8,11},{9,10},{10,... | collective-permute-start | bytes 24584 | tf_op jit(solution)/shard_map/ppermute | solution.py:360
  39.7 1.2 %collective-permute-start.15 = (f32[32,128]{1,0:T(8,128)S(1)}, f32[32,128]{1,0:T(8,128)S(1)}, u32[]{:S(2)}, u32[]{:S(2)}) collective-permute-start(f32[32,128]{1,0:T(8,128)S(1)} %shard_map.92.topics_ref), channel_id=1, source_target_pairs={{0,1},{1,0},{2,3},{3,2},{4,5},{5,4},{6,7},{7,6},{8,9},{9,8},{10,11... | collective-permute-start | bytes 49160 | tf_op jit(solution)/shard_map/ppermute | solution.py:371
  41.3 9.5 %collective-permute-start.16 = (f32[64,512]{1,0:T(8,128)S(1)}, f32[64,512]{1,0:T(8,128)S(1)}, u32[]{:S(2)}, u32[]{:S(2)}) collective-permute-start(f32[64,512]{1,0:T(8,128)S(1)} %get-tuple-element.92), channel_id=1, source_target_pairs={{0,24},{8,16},{16,8},{24,0},{1,25},{9,17},{17,9},{25,1},{2,26},{10... | collective-permute-start | bytes 393224 | tf_op jit(solution)/shard_map/ppermute | solution.py:374
  43.8 6.9 %collective-permute-start.17 = (f32[64,512]{1,0:T(8,128)S(1)}, f32[64,512]{1,0:T(8,128)S(1)}, u32[]{:S(2)}, u32[]{:S(2)}) collective-permute-start(f32[64,512]{1,0:T(8,128)S(1)} %get-tuple-element.91), channel_id=1, source_target_pairs={{0,16},{8,24},{16,0},{24,8},{1,17},{9,25},{17,1},{25,9},{2,18},{10... | collective-permute-start | bytes 393224 | tf_op jit(solution)/shard_map/ppermute | solution.py:374
  44.3 6.4 %collective-permute-start.18 = (f32[64,512]{1,0:T(8,128)S(1)}, f32[64,512]{1,0:T(8,128)S(1)}, u32[]{:S(2)}, u32[]{:S(2)}) collective-permute-start(f32[64,512]{1,0:T(8,128)S(1)} %get-tuple-element.90), channel_id=1, source_target_pairs={{0,8},{8,0},{16,24},{24,16},{1,9},{9,1},{17,25},{25,17},{2,10},{10... | collective-permute-start | bytes 393224 | tf_op jit(solution)/shard_map/ppermute | solution.py:374
  44.9 5.9 %collective-permute-start.19 = (f32[4,4224]{1,0:T(4,128)S(1)}, f32[4,4224]{1,0:T(4,128)S(1)}, u32[]{:S(2)}, u32[]{:S(2)}) collective-permute-start(f32[4,4224]{1,0:T(4,128)S(1)} %get-tuple-element.74), channel_id=1, source_target_pairs={{0,4},{1,5},{2,6},{3,7},{4,0},{5,1},{6,2},{7,3},{8,12},{9,13},{10,... | collective-permute-start | bytes 202760 | tf_op jit(solution)/shard_map/ppermute | solution.py:360
  50.9 9.1 %collective-permute-start.20 = (f32[64,512]{1,0:T(8,128)S(1)}, f32[64,512]{1,0:T(8,128)S(1)}, u32[]{:S(2)}, u32[]{:S(2)}) collective-permute-start(f32[64,512]{1,0:T(8,128)S(1)} %shard_map.95.refs_0_), channel_id=1, source_target_pairs={{0,24},{8,16},{16,8},{24,0},{1,25},{9,17},{17,9},{25,1},{2,26},{10... | collective-permute-start | bytes 393224 | tf_op jit(solution)/shard_map/ppermute | solution.py:374
  53.4 6.6 %collective-permute-start.24 = (f32[64,512]{1,0:T(8,128)S(1)}, f32[64,512]{1,0:T(8,128)S(1)}, u32[]{:S(2)}, u32[]{:S(2)}) collective-permute-start(f32[64,512]{1,0:T(8,128)S(1)} %shard_map.95.refs_0_), channel_id=1, source_target_pairs={{0,16},{8,24},{16,0},{24,8},{1,17},{9,25},{17,1},{25,9},{2,18},{10... | collective-permute-start | bytes 393224 | tf_op jit(solution)/shard_map/ppermute | solution.py:374
  53.9 6.6 %collective-permute-start.26 = (f32[64,512]{1,0:T(8,128)S(1)}, f32[64,512]{1,0:T(8,128)S(1)}, u32[]{:S(2)}, u32[]{:S(2)}) collective-permute-start(f32[64,512]{1,0:T(8,128)S(1)} %shard_map.95.refs_0_), channel_id=1, source_target_pairs={{0,8},{8,0},{16,24},{24,16},{1,9},{9,1},{17,25},{25,17},{2,10},{10... | collective-permute-start | bytes 393224 | tf_op jit(solution)/shard_map/ppermute | solution.py:374
  54.4 5.6 %collective-permute-start.21 = (f32[4,4224]{1,0:T(4,128)S(1)}, f32[4,4224]{1,0:T(4,128)S(1)}, u32[]{:S(2)}, u32[]{:S(2)}) collective-permute-start(f32[4,4224]{1,0:T(4,128)S(1)} %get-tuple-element.76), channel_id=1, source_target_pairs={{0,7},{1,6},{2,5},{3,4},{4,3},{5,2},{6,1},{7,0},{8,15},{9,14},{10,... | collective-permute-start | bytes 202760 | tf_op jit(solution)/shard_map/ppermute | solution.py:360
  54.4 6.7 %collective-permute-start.22 = (f32[64,512]{1,0:T(8,128)S(1)}, f32[64,512]{1,0:T(8,128)S(1)}, u32[]{:S(2)}, u32[]{:S(2)}) collective-permute-start(f32[64,512]{1,0:T(8,128)S(1)} %shard_map.95.refs_0_), channel_id=1, source_target_pairs={{0,1},{1,0},{2,3},{3,2},{4,5},{5,4},{6,7},{7,6},{8,9},{9,8},{10,11... | collective-permute-start | bytes 393224 | tf_op jit(solution)/shard_map/ppermute | solution.py:371
  60.0 1.3 %collective-permute-start.23 = (f32[64,512]{1,0:T(8,128)S(1)}, f32[64,512]{1,0:T(8,128)S(1)}, u32[]{:S(2)}, u32[]{:S(2)}) collective-permute-start(f32[64,512]{1,0:T(8,128)S(1)} %collective-permute-done.20.refs_1_), channel_id=1, source_target_pairs={{0,1},{1,0},{2,3},{3,2},{4,5},{5,4},{6,7},{7,6},{8,9},{9,8},{10,11... | collective-permute-start | bytes 393224 | tf_op jit(solution)/shard_map/ppermute | solution.py:371
  60.0 1.5 %collective-permute-start.25 = (f32[64,512]{1,0:T(8,128)S(1)}, f32[64,512]{1,0:T(8,128)S(1)}, u32[]{:S(2)}, u32[]{:S(2)}) collective-permute-start(f32[64,512]{1,0:T(8,128)S(1)} %collective-permute-done.24.refs_2_), channel_id=1, source_target_pairs={{0,1},{1,0},{2,3},{3,2},{4,5},{5,4},{6,7},{7,6},{8,9},{9,8},{10,11... | collective-permute-start | bytes 393224 | tf_op jit(solution)/shard_map/ppermute | solution.py:371
  60.5 1.3 %collective-permute-start.27 = (f32[64,512]{1,0:T(8,128)S(1)}, f32[64,512]{1,0:T(8,128)S(1)}, u32[]{:S(2)}, u32[]{:S(2)}) collective-permute-start(f32[64,512]{1,0:T(8,128)S(1)} %collective-permute-done.26.refs_3_), channel_id=1, source_target_pairs={{0,1},{1,0},{2,3},{3,2},{4,5},{5,4},{6,7},{7,6},{8,9},{9,8},{10,11... | collective-permute-start | bytes 393224 | tf_op jit(solution)/shard_map/ppermute | solution.py:371
  62.4 4.9 %collective-permute-start.28 = (f32[16,128]{1,0:T(8,128)S(1)}, f32[16,128]{1,0:T(8,128)S(1)}, u32[]{:S(2)}, u32[]{:S(2)}) collective-permute-start(f32[16,128]{1,0:T(8,128)S(1)} %get-tuple-element.80.refs_4_), channel_id=1, source_target_pairs={{0,7},{1,6},{2,5},{3,4},{4,3},{5,2},{6,1},{7,0},{8,15},{9,14},{10,... | collective-permute-start | bytes 24584 | tf_op jit(solution)/shard_map/ppermute | solution.py:360
  63.5 4.5 %collective-permute-start.29 = (f32[16,128]{1,0:T(8,128)S(1)}, f32[16,128]{1,0:T(8,128)S(1)}, u32[]{:S(2)}, u32[]{:S(2)}) collective-permute-start(f32[16,128]{1,0:T(8,128)S(1)} %get-tuple-element.80.refs_4_), channel_id=1, source_target_pairs={{0,4},{1,5},{2,6},{3,7},{4,0},{5,1},{6,2},{7,3},{8,12},{9,13},{10,... | collective-permute-start | bytes 24584 | tf_op jit(solution)/shard_map/ppermute | solution.py:360
  64.6 3.4 %collective-permute-start.30 = (f32[16,128]{1,0:T(8,128)S(1)}, f32[16,128]{1,0:T(8,128)S(1)}, u32[]{:S(2)}, u32[]{:S(2)}) collective-permute-start(f32[16,128]{1,0:T(8,128)S(1)} %get-tuple-element.80.refs_4_), channel_id=1, source_target_pairs={{0,3},{1,2},{2,1},{3,0},{4,7},{5,6},{6,5},{7,4},{8,11},{9,10},{10,... | collective-permute-start | bytes 24584 | tf_op jit(solution)/shard_map/ppermute | solution.py:360
  68.8 4.8 %collective-permute-start.31 = (f32[4,128]{1,0:T(4,128)S(1)}, f32[4,128]{1,0:T(4,128)S(1)}, u32[]{:S(2)}, u32[]{:S(2)}) collective-permute-start(f32[4,128]{1,0:T(4,128)S(1)} %get-tuple-element.87), channel_id=1, source_target_pairs={{0,7},{1,6},{2,5},{3,4},{4,3},{5,2},{6,1},{7,0},{8,15},{9,14},{10,... | collective-permute-start | bytes 6152 | tf_op jit(solution)/shard_map/ppermute | solution.py:360
  70.1 4.5 %collective-permute-start.32 = (f32[4,128]{1,0:T(4,128)S(1)}, f32[4,128]{1,0:T(4,128)S(1)}, u32[]{:S(2)}, u32[]{:S(2)}) collective-permute-start(f32[4,128]{1,0:T(4,128)S(1)} %get-tuple-element.88), channel_id=1, source_target_pairs={{0,4},{1,5},{2,6},{3,7},{4,0},{5,1},{6,2},{7,3},{8,12},{9,13},{10,... | collective-permute-start | bytes 6152 | tf_op jit(solution)/shard_map/ppermute | solution.py:360
  71.5 3.1 %collective-permute-start.33 = (f32[4,128]{1,0:T(4,128)S(1)}, f32[4,128]{1,0:T(4,128)S(1)}, u32[]{:S(2)}, u32[]{:S(2)}) collective-permute-start(f32[4,128]{1,0:T(4,128)S(1)} %get-tuple-element.89), channel_id=1, source_target_pairs={{0,3},{1,2},{2,1},{3,0},{4,7},{5,6},{6,5},{7,4},{8,11},{9,10},{10,... | collective-permute-start | bytes 6152 | tf_op jit(solution)/shard_map/ppermute | solution.py:360

commit v8 on v6

--- a/solution.py
+++ b/solution.py
@@ -320,12 +320,10 @@
     total = sum_packed(chips, [ref[:packed] for ref in parts])
     refit = base_rows_of(payload, slice(span, None)) / median_total * total
     scale_ref[...] = refit[:base_docs] / median_total
-    part = None
-    for half in range(cores):
-        weighted = base_rows_of(payload, slice(half * words, (half + 1) * words))
-        wide_ref, tall_ref = halves[2 * half], halves[2 * half + 1]
-        new = product_of(weighted / recon_of(refit, wide_ref[...]), tall_ref[...])
-        part = new if part is None else part + new
+    wide = jnp.concatenate([ref[...] for ref in halves[0::2]], axis=1)
+    tall = jnp.concatenate([ref[...] for ref in halves[1::2]], axis=0)
+    weighted = base_rows_of(payload, slice(0, cores * words))
+    part = product_of(weighted / recon_of(refit, wide), tall)
     for step in range(chips):
         part_refs[step][...] = part[step * base_docs : (step + 1) * base_docs]
 

time: 75.5 us -> 75.4 us (level)
  no operation moved by 1% of the time
where the time goes in v8:
time: 75.4 us; the launch traced here: 75.2 us
  starting transfers between devices  37.4 us (50%)
  waiting for transfers between devices  28.1 us (37%)
  Pallas kernels  7.26 us (10%)
  local copies, waits for them, and re-layouts  1.67 us (2%)
  between operations  0.77 us (1%)
    ppermute x21, starting transfers between devices, over_chips(): lax.ppermute(array, 'doc', [(c * cores + k, (c ^ step) * cores + (k + ste...  27.7 us
    ppermute x21, waiting for transfers between devices, over_chips(): lax.ppermute(array, 'doc', [(c * cores + k, (c ^ step) * cores + (k + ste...  26.6 us
    ppermute x6, starting transfers between devices, over_pert(): return lax.ppermute(array, 'pert', [(m, m ^ step) for m in range(members)])  7.11 us
    pallas_call x13, Pallas kernels, call(): pl.pallas_call(kernel, out_shape=outs, in_specs=[pl.BlockSpec(memory_spac...  5.94 us
    ppermute x7, starting transfers between devices, over_cores(): return lax.ppermute(array, 'doc', [(d, d ^ 1) for d in range(doc_size)])  2.6 us
    unnamed x9, local copies, waits for them, and re-layouts  1.62 us
    ppermute x7, waiting for transfers between devices, over_cores(): return lax.ppermute(array, 'doc', [(d, d ^ 1) for d in range(doc_size)])  1.52 us
  transfers between devices with their start and end apart: 34, of which 18 were waited for; matrix products, arithmetic and copies ran while one was open for 1% of the time, Pallas kernels for 6%

profile of v8, /device:TPU:0, one launch (start us, length us, event | category | flops | bytes accessed | tf_op | source)
XLA Modules:
  0.0 75.2 jit_solution(17623591550863642357)
XLA Ops:
  0.6 0.5 collective-permute-start
  1.2 1.3 %shard_map.87 = (f32[8,4224]{1,0:T(8,128)S(1)}, f32[8,4224]{1,0:T(8,128)S(1)}, f32[8,4224]{1,0:T(8,128)S(1)}, f32[8,4224]{1,0:T(8,128)S(1)}) custom-call(s32[8,128]{1,0:T(8,128)} %bitcast.13, f32[8,64]{1,0:T(8,128)} %bitcast.14, s32[1,64]{1,0:T(1,128)} %perm_hbm.1, s32[8,16384]{1,0:T(8,128)} %bitcast.12), custom_call_target="tpu_custom_call" | custom-call | bytes 1572864 | tf_op jit(solution)/shard_map/pallas_call | solution.py:373
  2.5 4.8 %collective-permute-start.1 = (f32[8,4224]{1,0:T(8,128)S(1)}, f32[8,4224]{1,0:T(8,128)S(1)}, u32[]{:S(2)}, u32[]{:S(2)}) collective-permute-start(f32[8,4224]{1,0:T(8,128)S(1)} %get-tuple-element.47), channel_id=1, source_target_pairs={{0,7},{1,6},{2,5},{3,4},{4,3},{5,2},{6,1},{7,0},{8,15},{9,14},{10,... | collective-permute-start | bytes 405512 | tf_op jit(solution)/shard_map/ppermute | solution.py:357
  7.3 0.6 collective-permute-start.3
  7.9 0.9 %copy-done.1 = s32[4,16384]{1,0:T(4,128)S(1)} copy-done((s32[4,16384]{1,0:T(4,128)S(1)}, s32[4,16384]{1,0:T(4,128)}, u32[]{:S(2)}) %copy-start.1) | copy-done | bytes 262168
  8.9 0.1 shard_map.88
  8.9 1.1 %collective-permute-start.4 = (f32[4,4224]{1,0:T(4,128)S(1)}, f32[4,4224]{1,0:T(4,128)S(1)}, u32[]{:S(2)}, u32[]{:S(2)}) collective-permute-start(f32[4,4224]{1,0:T(4,128)S(1)} %get-tuple-element.51), channel_id=1, source_target_pairs={{0,3},{1,2},{2,1},{3,0},{4,7},{5,6},{6,5},{7,4},{8,11},{9,10},{10,... | collective-permute-start | bytes 202760 | tf_op jit(solution)/shard_map/ppermute | solution.py:357
  10.1 1.1 %shard_map.86 = (bf16[128,4096]{1,0:T(8,128)(2,1)S(1)}, bf16[4096,128]{1,0:T(8,128)(2,1)S(1)}, f32[8,128]{1,0:T(8,128)S(1)}, f32[64,2048]{1,0:T(8,128)S(1)}) custom-call(s32[1,64]{1,0:T(1,128)S(1)} %copy-done.3, f32[64,2048]{1,0:T(8,128)S(1)} %bitcast.11, f32[64,2048]{1,0:T(8,128)S(1)} %collective-permute-done.refs_1_), custom_call_target="tpu_custom_call" | custom-call | bytes 4194304 | tf_op jit(solution)/shard_map/pallas_call | solution.py:37
  11.2 6.8 %collective-permute-done.4.refs_4_.refs_5_.refs_1_ = f32[4,4224]{1,0:T(4,128)S(1)} collective-permute-done((f32[4,4224]{1,0:T(4,128)S(1)}, f32[4,4224]{1,0:T(4,128)S(1)}, u32[]{:S(2)}, u32[]{:S(2)}) %collective-permute-start.4) | collective-permute-done | bytes 67616 | tf_op jit(solution)/shard_map/ppermute | solution.py:357
  18.0 1.2 %collective-permute-done.3.refs_2_.refs_1_ = f32[8,4224]{1,0:T(8,128)S(1)} collective-permute-done((f32[8,4224]{1,0:T(8,128)S(1)}, f32[8,4224]{1,0:T(8,128)S(1)}, u32[]{:S(2)}, u32[]{:S(2)}) %collective-permute-start.3) | collective-permute-done | bytes 135200 | tf_op jit(solution)/shard_map/ppermute | solution.py:357
  19.2 0.5 shard_map.89
  19.7 2.6 %collective-permute-start.5 = (f32[24,128]{1,0:T(8,128)S(1)}, f32[24,128]{1,0:T(8,128)S(1)}, u32[]{:S(2)}, u32[]{:S(2)}) collective-permute-start(f32[24,128]{1,0:T(8,128)S(1)} %get-tuple-element.53.refs_4_), channel_id=1, source_target_pairs={{0,7},{1,6},{2,5},{3,4},{4,3},{5,2},{6,1},{7,0},{8,15},{9,14},{10,... | collective-permute-start | bytes 36872 | tf_op jit(solution)/shard_map/ppermute | solution.py:357
  22.3 1.3 %collective-permute-start.7 = (f32[24,128]{1,0:T(8,128)S(1)}, f32[24,128]{1,0:T(8,128)S(1)}, u32[]{:S(2)}, u32[]{:S(2)}) collective-permute-start(f32[24,128]{1,0:T(8,128)S(1)} %get-tuple-element.53.refs_4_), channel_id=1, source_target_pairs={{0,3},{1,2},{2,1},{3,0},{4,7},{5,6},{6,5},{7,4},{8,11},{9,10},{10,... | collective-permute-start | bytes 36872 | tf_op jit(solution)/shard_map/ppermute | solution.py:357
  23.6 1.1 %collective-permute-done.5.refs_5_ = f32[24,128]{1,0:T(8,128)S(1)} collective-permute-done((f32[24,128]{1,0:T(8,128)S(1)}, f32[24,128]{1,0:T(8,128)S(1)}, u32[]{:S(2)}, u32[]{:S(2)}) %collective-permute-start.5) | collective-permute-done | bytes 12320 | tf_op jit(solution)/shard_map/ppermute | solution.py:357
  24.7 2.2 %collective-permute-done.6.refs_6_ = f32[24,128]{1,0:T(8,128)S(1)} collective-permute-done((f32[24,128]{1,0:T(8,128)S(1)}, f32[24,128]{1,0:T(8,128)S(1)}, u32[]{:S(2)}, u32[]{:S(2)}) %collective-permute-start.6) | collective-permute-done | bytes 12320 | tf_op jit(solution)/shard_map/ppermute | solution.py:357
  26.9 0.6 shard_map.90
  27.5 1.1 %collective-permute-start.8 = (f32[18,128]{1,0:T(8,128)S(1)}, f32[18,128]{1,0:T(8,128)S(1)}, u32[]{:S(2)}, u32[]{:S(2)}) collective-permute-start(f32[18,128]{1,0:T(8,128)S(1)} %get-tuple-element.57), channel_id=1, source_target_pairs={{0,7},{1,6},{2,5},{3,4},{4,3},{5,2},{6,1},{7,0},{8,15},{9,14},{10,... | collective-permute-start | bytes 27656 | tf_op jit(solution)/shard_map/ppermute | solution.py:357
  28.6 0.6 collective-permute-start.9
  29.2 2.2 %collective-permute-start.10 = (f32[16,128]{1,0:T(8,128)S(1)}, f32[16,128]{1,0:T(8,128)S(1)}, u32[]{:S(2)}, u32[]{:S(2)}) collective-permute-start(f32[16,128]{1,0:T(8,128)S(1)} %get-tuple-element.56.refs_5_), channel_id=1, source_target_pairs={{0,3},{1,2},{2,1},{3,0},{4,7},{5,6},{6,5},{7,4},{8,11},{9,10},{10,... | collective-permute-start | bytes 24584 | tf_op jit(solution)/shard_map/ppermute | solution.py:357
  31.4 1.5 %collective-permute-done.10.refs_8_ = f32[16,128]{1,0:T(8,128)S(1)} collective-permute-done((f32[16,128]{1,0:T(8,128)S(1)}, f32[16,128]{1,0:T(8,128)S(1)}, u32[]{:S(2)}, u32[]{:S(2)}) %collective-permute-start.10) | collective-permute-done | bytes 8224 | tf_op jit(solution)/shard_map/ppermute | solution.py:357
  32.8 0.4 collective-permute-done.9.refs_7_
  33.2 0.6 shard_map.91
  33.8 1.4 %collective-permute-start.11 = (f32[16,128]{1,0:T(8,128)S(1)}, f32[16,128]{1,0:T(8,128)S(1)}, u32[]{:S(2)}, u32[]{:S(2)}) collective-permute-start(f32[16,128]{1,0:T(8,128)S(1)} %get-tuple-element.61), channel_id=1, source_target_pairs={{0,7},{1,6},{2,5},{3,4},{4,3},{5,2},{6,1},{7,0},{8,15},{9,14},{10,... | collective-permute-start | bytes 24584 | tf_op jit(solution)/shard_map/ppermute | solution.py:357
  35.2 1.3 %collective-permute-start.12 = (f32[16,128]{1,0:T(8,128)S(1)}, f32[16,128]{1,0:T(8,128)S(1)}, u32[]{:S(2)}, u32[]{:S(2)}) collective-permute-start(f32[16,128]{1,0:T(8,128)S(1)} %get-tuple-element.62), channel_id=1, source_target_pairs={{0,4},{1,5},{2,6},{3,7},{4,0},{5,1},{6,2},{7,3},{8,12},{9,13},{10,... | collective-permute-start | bytes 24584 | tf_op jit(solution)/shard_map/ppermute | solution.py:357
  36.5 1.1 %collective-permute-start.13 = (f32[16,128]{1,0:T(8,128)S(1)}, f32[16,128]{1,0:T(8,128)S(1)}, u32[]{:S(2)}, u32[]{:S(2)}) collective-permute-start(f32[16,128]{1,0:T(8,128)S(1)} %get-tuple-element.60.refs_0_), channel_id=1, source_target_pairs={{0,3},{1,2},{2,1},{3,0},{4,7},{5,6},{6,5},{7,4},{8,11},{9,10},{10,... | collective-permute-start | bytes 24584 | tf_op jit(solution)/shard_map/ppermute | solution.py:357
  37.6 1.1 %collective-permute-done.11.refs_1_ = f32[16,128]{1,0:T(8,128)S(1)} collective-permute-done((f32[16,128]{1,0:T(8,128)S(1)}, f32[16,128]{1,0:T(8,128)S(1)}, u32[]{:S(2)}, u32[]{:S(2)}) %collective-permute-start.11) | collective-permute-done | bytes 8224 | tf_op jit(solution)/shard_map/ppermute | solution.py:357
  38.7 1.1 %collective-permute-done.12.refs_2_ = f32[16,128]{1,0:T(8,128)S(1)} collective-permute-done((f32[16,128]{1,0:T(8,128)S(1)}, f32[16,128]{1,0:T(8,128)S(1)}, u32[]{:S(2)}, u32[]{:S(2)}) %collective-permute-start.12) | collective-permute-done | bytes 8224 | tf_op jit(solution)/shard_map/ppermute | solution.py:357
  39.8 0.1 shard_map.92.topics_ref
  39.8 0.0 collective-permute-start.15
  39.9 0.4 shard_map.93.refs_1_
  40.3 0.8 %collective-permute-done.15.topics_ref = f32[32,128]{1,0:T(8,128)S(1)} collective-permute-done((f32[32,128]{1,0:T(8,128)S(1)}, f32[32,128]{1,0:T(8,128)S(1)}, u32[]{:S(2)}, u32[]{:S(2)}) %collective-permute-start.15) | collective-permute-done | bytes 16416 | tf_op jit(solution)/shard_map/ppermute | solution.py:368
  41.0 0.4 shard_map.94
  41.5 2.5 %collective-permute-start.16 = (f32[64,512]{1,0:T(8,128)S(1)}, f32[64,512]{1,0:T(8,128)S(1)}, u32[]{:S(2)}, u32[]{:S(2)}) collective-permute-start(f32[64,512]{1,0:T(8,128)S(1)} %get-tuple-element.88), channel_id=1, source_target_pairs={{0,24},{8,16},{16,8},{24,0},{1,25},{9,17},{17,9},{25,1},{2,26},{10... | collective-permute-start | bytes 393224 | tf_op jit(solution)/shard_map/ppermute | solution.py:371
  44.0 0.5 collective-permute-start.17
  44.5 0.5 collective-permute-start.18
  45.0 1.4 %collective-permute-start.19 = (f32[4,4224]{1,0:T(4,128)S(1)}, f32[4,4224]{1,0:T(4,128)S(1)}, u32[]{:S(2)}, u32[]{:S(2)}) collective-permute-start(f32[4,4224]{1,0:T(4,128)S(1)} %get-tuple-element.70), channel_id=1, source_target_pairs={{0,4},{1,5},{2,6},{3,7},{4,0},{5,1},{6,2},{7,3},{8,12},{9,13},{10,... | collective-permute-start | bytes 202760 | tf_op jit(solution)/shard_map/ppermute | solution.py:357
  46.5 4.5 %collective-permute-done.19.refs_4_.refs_6_.refs_2_ = f32[4,4224]{1,0:T(4,128)S(1)} collective-permute-done((f32[4,4224]{1,0:T(4,128)S(1)}, f32[4,4224]{1,0:T(4,128)S(1)}, u32[]{:S(2)}, u32[]{:S(2)}) %collective-permute-start.19) | collective-permute-done | bytes 67616 | tf_op jit(solution)/shard_map/ppermute | solution.py:357
  51.0 0.1 shard_map.95.refs_0_
  51.0 2.5 %collective-permute-start.20 = (f32[64,512]{1,0:T(8,128)S(1)}, f32[64,512]{1,0:T(8,128)S(1)}, u32[]{:S(2)}, u32[]{:S(2)}) collective-permute-start(f32[64,512]{1,0:T(8,128)S(1)} %shard_map.95.refs_0_), channel_id=1, source_target_pairs={{0,24},{8,16},{16,8},{24,0},{1,25},{9,17},{17,9},{25,1},{2,26},{10... | collective-permute-start | bytes 393224 | tf_op jit(solution)/shard_map/ppermute | solution.py:371
  53.5 0.5 collective-permute-start.24
  54.1 0.5 collective-permute-start.26
  54.6 0.4 collective-permute-start.21
  55.0 1.5 %collective-permute-start.22 = (f32[64,512]{1,0:T(8,128)S(1)}, f32[64,512]{1,0:T(8,128)S(1)}, u32[]{:S(2)}, u32[]{:S(2)}) collective-permute-start(f32[64,512]{1,0:T(8,128)S(1)} %shard_map.95.refs_0_), channel_id=1, source_target_pairs={{0,1},{1,0},{2,3},{3,2},{4,5},{5,4},{6,7},{7,6},{8,9},{9,8},{10,11... | collective-permute-start | bytes 393224 | tf_op jit(solution)/shard_map/ppermute | solution.py:368
  56.5 3.7 %collective-permute-done.21.refs_7_.refs_3_ = f32[4,4224]{1,0:T(4,128)S(1)} collective-permute-done((f32[4,4224]{1,0:T(4,128)S(1)}, f32[4,4224]{1,0:T(4,128)S(1)}, u32[]{:S(2)}, u32[]{:S(2)}) %collective-permute-start.21) | collective-permute-done | bytes 67616 | tf_op jit(solution)/shard_map/ppermute | solution.py:357
  60.2 0.5 collective-permute-start.25
  60.7 0.1 collective-permute-start.27
  60.7 0.5 shard_map.96
  61.3 0.2 collective-permute-done.23.refs_1_
  61.5 0.2 collective-permute-done.25.refs_2_
  61.7 0.3 collective-permute-done.27.refs_3_
  62.0 0.5 shard_map.97
  62.5 1.6 %collective-permute-start.28 = (f32[16,128]{1,0:T(8,128)S(1)}, f32[16,128]{1,0:T(8,128)S(1)}, u32[]{:S(2)}, u32[]{:S(2)}) collective-permute-start(f32[16,128]{1,0:T(8,128)S(1)} %get-tuple-element.76.refs_4_), channel_id=1, source_target_pairs={{0,7},{1,6},{2,5},{3,4},{4,3},{5,2},{6,1},{7,0},{8,15},{9,14},{10,... | collective-permute-start | bytes 24584 | tf_op jit(solution)/shard_map/ppermute | solution.py:357
  64.1 0.6 collective-permute-start.29
  64.7 1.7 %collective-permute-start.30 = (f32[16,128]{1,0:T(8,128)S(1)}, f32[16,128]{1,0:T(8,128)S(1)}, u32[]{:S(2)}, u32[]{:S(2)}) collective-permute-start(f32[16,128]{1,0:T(8,128)S(1)} %get-tuple-element.76.refs_4_), channel_id=1, source_target_pairs={{0,3},{1,2},{2,1},{3,0},{4,7},{5,6},{6,5},{7,4},{8,11},{9,10},{10,... | collective-permute-start | bytes 24584 | tf_op jit(solution)/shard_map/ppermute | solution.py:357
  66.4 1.0 %collective-permute-done.28.refs_5_ = f32[16,128]{1,0:T(8,128)S(1)} collective-permute-done((f32[16,128]{1,0:T(8,128)S(1)}, f32[16,128]{1,0:T(8,128)S(1)}, u32[]{:S(2)}, u32[]{:S(2)}) %collective-permute-start.28) | collective-permute-done | bytes 8224 | tf_op jit(solution)/shard_map/ppermute | solution.py:357
  67.4 1.2 %collective-permute-done.29.refs_6_ = f32[16,128]{1,0:T(8,128)S(1)} collective-permute-done((f32[16,128]{1,0:T(8,128)S(1)}, f32[16,128]{1,0:T(8,128)S(1)}, u32[]{:S(2)}, u32[]{:S(2)}) %collective-permute-start.29) | collective-permute-done | bytes 8224 | tf_op jit(solution)/shard_map/ppermute | solution.py:357
  68.7 0.5 shard_map.98
  69.2 0.9 %collective-permute-start.31 = (f32[4,128]{1,0:T(4,128)S(1)}, f32[4,128]{1,0:T(4,128)S(1)}, u32[]{:S(2)}, u32[]{:S(2)}) collective-permute-start(f32[4,128]{1,0:T(4,128)S(1)} %get-tuple-element.83), channel_id=1, source_target_pairs={{0,7},{1,6},{2,5},{3,4},{4,3},{5,2},{6,1},{7,0},{8,15},{9,14},{10,... | collective-permute-start | bytes 6152 | tf_op jit(solution)/shard_map/ppermute | solution.py:357
  70.1 1.4 %collective-permute-start.32 = (f32[4,128]{1,0:T(4,128)S(1)}, f32[4,128]{1,0:T(4,128)S(1)}, u32[]{:S(2)}, u32[]{:S(2)}) collective-permute-start(f32[4,128]{1,0:T(4,128)S(1)} %get-tuple-element.84), channel_id=1, source_target_pairs={{0,4},{1,5},{2,6},{3,7},{4,0},{5,1},{6,2},{7,3},{8,12},{9,13},{10,... | collective-permute-start | bytes 6152 | tf_op jit(solution)/shard_map/ppermute | solution.py:357
  71.5 1.5 %collective-permute-start.33 = (f32[4,128]{1,0:T(4,128)S(1)}, f32[4,128]{1,0:T(4,128)S(1)}, u32[]{:S(2)}, u32[]{:S(2)}) collective-permute-start(f32[4,128]{1,0:T(4,128)S(1)} %get-tuple-element.85), channel_id=1, source_target_pairs={{0,3},{1,2},{2,1},{3,0},{4,7},{5,6},{6,5},{7,4},{8,11},{9,10},{10,... | collective-permute-start | bytes 6152 | tf_op jit(solution)/shard_map/ppermute | solution.py:357
  73.1 0.7 copy.9
  73.7 0.3 collective-permute-done.31.refs_1_
  74.0 0.6 collective-permute-done.32.refs_2_
  74.6 0.6 shard_map.99
  (28 shorter events, 0.1 us)
Async XLA Ops:
  0.6 9.5 %copy-start = (f32[1,2048,64]{1,2,0:T(8,128)S(1)}, f32[1,2048,64]{1,2,0:T(8,128)}, u32[]{:S(2)}) copy-start(f32[1,2048,64]{1,2,0:T(8,128)} %param.10) | copy-start | bytes 1572868
  0.6 9.4 %collective-permute-start = (f32[64,2048]{1,0:T(8,128)}, f32[64,2048]{1,0:T(8,128)S(1)}, u32[]{:S(2)}, u32[]{:S(2)}) collective-permute-start(f32[64,2048]{1,0:T(8,128)} %bitcast.10), channel_id=1, source_target_pairs={{0,1},{1,0},{2,3},{3,2},{4,5},{5,4},{6,7},{7,6},{8,9},{9,8},{10,11... | collective-permute-start | bytes 1572872 | tf_op jit(solution)/shard_map/ppermute | solution.py:368
  2.5 5.4 %copy-start.2 = (f32[4,64]{1,0:T(4,128)S(1)}, f32[4,64]{1,0:T(4,128)}, u32[]{:S(2)}) copy-start(f32[4,64]{1,0:T(4,128)} %topics_ref.1) | copy-start | bytes 3076
  2.5 15.5 %collective-permute-start.1 = (f32[8,4224]{1,0:T(8,128)S(1)}, f32[8,4224]{1,0:T(8,128)S(1)}, u32[]{:S(2)}, u32[]{:S(2)}) collective-permute-start(f32[8,4224]{1,0:T(8,128)S(1)} %get-tuple-element.47), channel_id=1, source_target_pairs={{0,7},{1,6},{2,5},{3,4},{4,3},{5,2},{6,1},{7,0},{8,15},{9,14},{10,... | collective-permute-start | bytes 405512 | tf_op jit(solution)/shard_map/ppermute | solution.py:357
  7.3 10.7 %collective-permute-start.2 = (f32[8,4224]{1,0:T(8,128)S(1)}, f32[8,4224]{1,0:T(8,128)S(1)}, u32[]{:S(2)}, u32[]{:S(2)}) collective-permute-start(f32[8,4224]{1,0:T(8,128)S(1)} %get-tuple-element.48), channel_id=1, source_target_pairs={{0,3},{1,2},{2,1},{3,0},{4,7},{5,6},{6,5},{7,4},{8,11},{9,10},{10,... | collective-permute-start | bytes 405512 | tf_op jit(solution)/shard_map/ppermute | solution.py:357
  7.3 11.9 %collective-permute-start.3 = (f32[8,4224]{1,0:T(8,128)S(1)}, f32[8,4224]{1,0:T(8,128)S(1)}, u32[]{:S(2)}, u32[]{:S(2)}) collective-permute-start(f32[8,4224]{1,0:T(8,128)S(1)} %get-tuple-element.49), channel_id=1, source_target_pairs={{0,4},{1,5},{2,6},{3,7},{4,0},{5,1},{6,2},{7,3},{8,12},{9,13},{10,... | collective-permute-start | bytes 405512 | tf_op jit(solution)/shard_map/ppermute | solution.py:357
  7.9 1.0 %copy-start.1 = (s32[4,16384]{1,0:T(4,128)S(1)}, s32[4,16384]{1,0:T(4,128)}, u32[]{:S(2)}) copy-start(s32[4,16384]{1,0:T(4,128)} %counts_ref.1) | copy-start | bytes 786436
  8.9 1.2 %copy-start.3 = (s32[1,64]{1,0:T(1,128)S(1)}, s32[1,64]{1,0:T(1,128)}, u32[]{:S(2)}) copy-start(s32[1,64]{1,0:T(1,128)} %perm_hbm.1) | copy-start | bytes 772
  8.9 9.0 %collective-permute-start.4 = (f32[4,4224]{1,0:T(4,128)S(1)}, f32[4,4224]{1,0:T(4,128)S(1)}, u32[]{:S(2)}, u32[]{:S(2)}) collective-permute-start(f32[4,4224]{1,0:T(4,128)S(1)} %get-tuple-element.51), channel_id=1, source_target_pairs={{0,3},{1,2},{2,1},{3,0},{4,7},{5,6},{6,5},{7,4},{8,11},{9,10},{10,... | collective-permute-start | bytes 202760 | tf_op jit(solution)/shard_map/ppermute | solution.py:357
  19.7 20.0 %collective-permute-start.14 = (f32[32,2048]{1,0:T(8,128)S(1)}, f32[32,2048]{1,0:T(8,128)S(1)}, u32[]{:S(2)}, u32[]{:S(2)}) collective-permute-start(f32[32,2048]{1,0:T(8,128)S(1)} %get-tuple-element.63), channel_id=1, source_target_pairs={{0,1},{1,0},{2,3},{3,2},{4,5},{5,4},{6,7},{7,6},{8,9},{9,8},{10,11... | collective-permute-start | bytes 786440 | tf_op jit(solution)/shard_map/ppermute | solution.py:368
  19.7 5.0 %collective-permute-start.5 = (f32[24,128]{1,0:T(8,128)S(1)}, f32[24,128]{1,0:T(8,128)S(1)}, u32[]{:S(2)}, u32[]{:S(2)}) collective-permute-start(f32[24,128]{1,0:T(8,128)S(1)} %get-tuple-element.53.refs_4_), channel_id=1, source_target_pairs={{0,7},{1,6},{2,5},{3,4},{4,3},{5,2},{6,1},{7,0},{8,15},{9,14},{10,... | collective-permute-start | bytes 36872 | tf_op jit(solution)/shard_map/ppermute | solution.py:357
  22.3 4.6 %collective-permute-start.6 = (f32[24,128]{1,0:T(8,128)S(1)}, f32[24,128]{1,0:T(8,128)S(1)}, u32[]{:S(2)}, u32[]{:S(2)}) collective-permute-start(f32[24,128]{1,0:T(8,128)S(1)} %get-tuple-element.53.refs_4_), channel_id=1, source_target_pairs={{0,4},{1,5},{2,6},{3,7},{4,0},{5,1},{6,2},{7,3},{8,12},{9,13},{10,... | collective-permute-start | bytes 36872 | tf_op jit(solution)/shard_map/ppermute | solution.py:357
  22.3 4.6 %collective-permute-start.7 = (f32[24,128]{1,0:T(8,128)S(1)}, f32[24,128]{1,0:T(8,128)S(1)}, u32[]{:S(2)}, u32[]{:S(2)}) collective-permute-start(f32[24,128]{1,0:T(8,128)S(1)} %get-tuple-element.53.refs_4_), channel_id=1, source_target_pairs={{0,3},{1,2},{2,1},{3,0},{4,7},{5,6},{6,5},{7,4},{8,11},{9,10},{10,... | collective-permute-start | bytes 36872 | tf_op jit(solution)/shard_map/ppermute | solution.py:357
  27.5 5.7 %collective-permute-start.8 = (f32[18,128]{1,0:T(8,128)S(1)}, f32[18,128]{1,0:T(8,128)S(1)}, u32[]{:S(2)}, u32[]{:S(2)}) collective-permute-start(f32[18,128]{1,0:T(8,128)S(1)} %get-tuple-element.57), channel_id=1, source_target_pairs={{0,7},{1,6},{2,5},{3,4},{4,3},{5,2},{6,1},{7,0},{8,15},{9,14},{10,... | collective-permute-start | bytes 27656 | tf_op jit(solution)/shard_map/ppermute | solution.py:357
  28.6 4.6 %collective-permute-start.9 = (f32[17,128]{1,0:T(8,128)S(1)}, f32[17,128]{1,0:T(8,128)S(1)}, u32[]{:S(2)}, u32[]{:S(2)}) collective-permute-start(f32[17,128]{1,0:T(8,128)S(1)} %get-tuple-element.58), channel_id=1, source_target_pairs={{0,4},{1,5},{2,6},{3,7},{4,0},{5,1},{6,2},{7,3},{8,12},{9,13},{10,... | collective-permute-start | bytes 26120 | tf_op jit(solution)/shard_map/ppermute | solution.py:357
  29.2 3.6 %collective-permute-start.10 = (f32[16,128]{1,0:T(8,128)S(1)}, f32[16,128]{1,0:T(8,128)S(1)}, u32[]{:S(2)}, u32[]{:S(2)}) collective-permute-start(f32[16,128]{1,0:T(8,128)S(1)} %get-tuple-element.56.refs_5_), channel_id=1, source_target_pairs={{0,3},{1,2},{2,1},{3,0},{4,7},{5,6},{6,5},{7,4},{8,11},{9,10},{10,... | collective-permute-start | bytes 24584 | tf_op jit(solution)/shard_map/ppermute | solution.py:357
  33.8 4.9 %collective-permute-start.11 = (f32[16,128]{1,0:T(8,128)S(1)}, f32[16,128]{1,0:T(8,128)S(1)}, u32[]{:S(2)}, u32[]{:S(2)}) collective-permute-start(f32[16,128]{1,0:T(8,128)S(1)} %get-tuple-element.61), channel_id=1, source_target_pairs={{0,7},{1,6},{2,5},{3,4},{4,3},{5,2},{6,1},{7,0},{8,15},{9,14},{10,... | collective-permute-start | bytes 24584 | tf_op jit(solution)/shard_map/ppermute | solution.py:357
  35.2 4.5 %collective-permute-start.12 = (f32[16,128]{1,0:T(8,128)S(1)}, f32[16,128]{1,0:T(8,128)S(1)}, u32[]{:S(2)}, u32[]{:S(2)}) collective-permute-start(f32[16,128]{1,0:T(8,128)S(1)} %get-tuple-element.62), channel_id=1, source_target_pairs={{0,4},{1,5},{2,6},{3,7},{4,0},{5,1},{6,2},{7,3},{8,12},{9,13},{10,... | collective-permute-start | bytes 24584 | tf_op jit(solution)/shard_map/ppermute | solution.py:357
  36.5 3.3 %collective-permute-start.13 = (f32[16,128]{1,0:T(8,128)S(1)}, f32[16,128]{1,0:T(8,128)S(1)}, u32[]{:S(2)}, u32[]{:S(2)}) collective-permute-start(f32[16,128]{1,0:T(8,128)S(1)} %get-tuple-element.60.refs_0_), channel_id=1, source_target_pairs={{0,3},{1,2},{2,1},{3,0},{4,7},{5,6},{6,5},{7,4},{8,11},{9,10},{10,... | collective-permute-start | bytes 24584 | tf_op jit(solution)/shard_map/ppermute | solution.py:357
  39.8 1.2 %collective-permute-start.15 = (f32[32,128]{1,0:T(8,128)S(1)}, f32[32,128]{1,0:T(8,128)S(1)}, u32[]{:S(2)}, u32[]{:S(2)}) collective-permute-start(f32[32,128]{1,0:T(8,128)S(1)} %shard_map.92.topics_ref), channel_id=1, source_target_pairs={{0,1},{1,0},{2,3},{3,2},{4,5},{5,4},{6,7},{7,6},{8,9},{9,8},{10,11... | collective-permute-start | bytes 49160 | tf_op jit(solution)/shard_map/ppermute | solution.py:368
  41.5 9.5 %collective-permute-start.16 = (f32[64,512]{1,0:T(8,128)S(1)}, f32[64,512]{1,0:T(8,128)S(1)}, u32[]{:S(2)}, u32[]{:S(2)}) collective-permute-start(f32[64,512]{1,0:T(8,128)S(1)} %get-tuple-element.88), channel_id=1, source_target_pairs={{0,24},{8,16},{16,8},{24,0},{1,25},{9,17},{17,9},{25,1},{2,26},{10... | collective-permute-start | bytes 393224 | tf_op jit(solution)/shard_map/ppermute | solution.py:371
  44.0 7.0 %collective-permute-start.17 = (f32[64,512]{1,0:T(8,128)S(1)}, f32[64,512]{1,0:T(8,128)S(1)}, u32[]{:S(2)}, u32[]{:S(2)}) collective-permute-start(f32[64,512]{1,0:T(8,128)S(1)} %get-tuple-element.87), channel_id=1, source_target_pairs={{0,16},{8,24},{16,0},{24,8},{1,17},{9,25},{17,1},{25,9},{2,18},{10... | collective-permute-start | bytes 393224 | tf_op jit(solution)/shard_map/ppermute | solution.py:371
  44.5 6.4 %collective-permute-start.18 = (f32[64,512]{1,0:T(8,128)S(1)}, f32[64,512]{1,0:T(8,128)S(1)}, u32[]{:S(2)}, u32[]{:S(2)}) collective-permute-start(f32[64,512]{1,0:T(8,128)S(1)} %get-tuple-element.86), channel_id=1, source_target_pairs={{0,8},{8,0},{16,24},{24,16},{1,9},{9,1},{17,25},{25,17},{2,10},{10... | collective-permute-start | bytes 393224 | tf_op jit(solution)/shard_map/ppermute | solution.py:371
  45.0 5.9 %collective-permute-start.19 = (f32[4,4224]{1,0:T(4,128)S(1)}, f32[4,4224]{1,0:T(4,128)S(1)}, u32[]{:S(2)}, u32[]{:S(2)}) collective-permute-start(f32[4,4224]{1,0:T(4,128)S(1)} %get-tuple-element.70), channel_id=1, source_target_pairs={{0,4},{1,5},{2,6},{3,7},{4,0},{5,1},{6,2},{7,3},{8,12},{9,13},{10,... | collective-permute-start | bytes 202760 | tf_op jit(solution)/shard_map/ppermute | solution.py:357
  51.0 9.1 %collective-permute-start.20 = (f32[64,512]{1,0:T(8,128)S(1)}, f32[64,512]{1,0:T(8,128)S(1)}, u32[]{:S(2)}, u32[]{:S(2)}) collective-permute-start(f32[64,512]{1,0:T(8,128)S(1)} %shard_map.95.refs_0_), channel_id=1, source_target_pairs={{0,24},{8,16},{16,8},{24,0},{1,25},{9,17},{17,9},{25,1},{2,26},{10... | collective-permute-start | bytes 393224 | tf_op jit(solution)/shard_map/ppermute | solution.py:371
  53.5 6.6 %collective-permute-start.24 = (f32[64,512]{1,0:T(8,128)S(1)}, f32[64,512]{1,0:T(8,128)S(1)}, u32[]{:S(2)}, u32[]{:S(2)}) collective-permute-start(f32[64,512]{1,0:T(8,128)S(1)} %shard_map.95.refs_0_), channel_id=1, source_target_pairs={{0,16},{8,24},{16,0},{24,8},{1,17},{9,25},{17,1},{25,9},{2,18},{10... | collective-permute-start | bytes 393224 | tf_op jit(solution)/shard_map/ppermute | solution.py:371
  54.1 6.6 %collective-permute-start.26 = (f32[64,512]{1,0:T(8,128)S(1)}, f32[64,512]{1,0:T(8,128)S(1)}, u32[]{:S(2)}, u32[]{:S(2)}) collective-permute-start(f32[64,512]{1,0:T(8,128)S(1)} %shard_map.95.refs_0_), channel_id=1, source_target_pairs={{0,8},{8,0},{16,24},{24,16},{1,9},{9,1},{17,25},{25,17},{2,10},{10... | collective-permute-start | bytes 393224 | tf_op jit(solution)/shard_map/ppermute | solution.py:371
  54.6 5.6 %collective-permute-start.21 = (f32[4,4224]{1,0:T(4,128)S(1)}, f32[4,4224]{1,0:T(4,128)S(1)}, u32[]{:S(2)}, u32[]{:S(2)}) collective-permute-start(f32[4,4224]{1,0:T(4,128)S(1)} %get-tuple-element.72), channel_id=1, source_target_pairs={{0,7},{1,6},{2,5},{3,4},{4,3},{5,2},{6,1},{7,0},{8,15},{9,14},{10,... | collective-permute-start | bytes 202760 | tf_op jit(solution)/shard_map/ppermute | solution.py:357
  55.0 6.3 %collective-permute-start.22 = (f32[64,512]{1,0:T(8,128)S(1)}, f32[64,512]{1,0:T(8,128)S(1)}, u32[]{:S(2)}, u32[]{:S(2)}) collective-permute-start(f32[64,512]{1,0:T(8,128)S(1)} %shard_map.95.refs_0_), channel_id=1, source_target_pairs={{0,1},{1,0},{2,3},{3,2},{4,5},{5,4},{6,7},{7,6},{8,9},{9,8},{10,11... | collective-permute-start | bytes 393224 | tf_op jit(solution)/shard_map/ppermute | solution.py:368
  60.2 1.3 %collective-permute-start.23 = (f32[64,512]{1,0:T(8,128)S(1)}, f32[64,512]{1,0:T(8,128)S(1)}, u32[]{:S(2)}, u32[]{:S(2)}) collective-permute-start(f32[64,512]{1,0:T(8,128)S(1)} %collective-permute-done.20.refs_1_), channel_id=1, source_target_pairs={{0,1},{1,0},{2,3},{3,2},{4,5},{5,4},{6,7},{7,6},{8,9},{9,8},{10,11... | collective-permute-start | bytes 393224 | tf_op jit(solution)/shard_map/ppermute | solution.py:368
  60.2 1.5 %collective-permute-start.25 = (f32[64,512]{1,0:T(8,128)S(1)}, f32[64,512]{1,0:T(8,128)S(1)}, u32[]{:S(2)}, u32[]{:S(2)}) collective-permute-start(f32[64,512]{1,0:T(8,128)S(1)} %collective-permute-done.24.refs_2_), channel_id=1, source_target_pairs={{0,1},{1,0},{2,3},{3,2},{4,5},{5,4},{6,7},{7,6},{8,9},{9,8},{10,11... | collective-permute-start | bytes 393224 | tf_op jit(solution)/shard_map/ppermute | solution.py:368
  60.7 1.3 %collective-permute-start.27 = (f32[64,512]{1,0:T(8,128)S(1)}, f32[64,512]{1,0:T(8,128)S(1)}, u32[]{:S(2)}, u32[]{:S(2)}) collective-permute-start(f32[64,512]{1,0:T(8,128)S(1)} %collective-permute-done.26.refs_3_), channel_id=1, source_target_pairs={{0,1},{1,0},{2,3},{3,2},{4,5},{5,4},{6,7},{7,6},{8,9},{9,8},{10,11... | collective-permute-start | bytes 393224 | tf_op jit(solution)/shard_map/ppermute | solution.py:368
  62.5 4.9 %collective-permute-start.28 = (f32[16,128]{1,0:T(8,128)S(1)}, f32[16,128]{1,0:T(8,128)S(1)}, u32[]{:S(2)}, u32[]{:S(2)}) collective-permute-start(f32[16,128]{1,0:T(8,128)S(1)} %get-tuple-element.76.refs_4_), channel_id=1, source_target_pairs={{0,7},{1,6},{2,5},{3,4},{4,3},{5,2},{6,1},{7,0},{8,15},{9,14},{10,... | collective-permute-start | bytes 24584 | tf_op jit(solution)/shard_map/ppermute | solution.py:357
  64.1 4.5 %collective-permute-start.29 = (f32[16,128]{1,0:T(8,128)S(1)}, f32[16,128]{1,0:T(8,128)S(1)}, u32[]{:S(2)}, u32[]{:S(2)}) collective-permute-start(f32[16,128]{1,0:T(8,128)S(1)} %get-tuple-element.76.refs_4_), channel_id=1, source_target_pairs={{0,4},{1,5},{2,6},{3,7},{4,0},{5,1},{6,2},{7,3},{8,12},{9,13},{10,... | collective-permute-start | bytes 24584 | tf_op jit(solution)/shard_map/ppermute | solution.py:357
  64.7 3.9 %collective-permute-start.30 = (f32[16,128]{1,0:T(8,128)S(1)}, f32[16,128]{1,0:T(8,128)S(1)}, u32[]{:S(2)}, u32[]{:S(2)}) collective-permute-start(f32[16,128]{1,0:T(8,128)S(1)} %get-tuple-element.76.refs_4_), channel_id=1, source_target_pairs={{0,3},{1,2},{2,1},{3,0},{4,7},{5,6},{6,5},{7,4},{8,11},{9,10},{10,... | collective-permute-start | bytes 24584 | tf_op jit(solution)/shard_map/ppermute | solution.py:357
  69.2 4.8 %collective-permute-start.31 = (f32[4,128]{1,0:T(4,128)S(1)}, f32[4,128]{1,0:T(4,128)S(1)}, u32[]{:S(2)}, u32[]{:S(2)}) collective-permute-start(f32[4,128]{1,0:T(4,128)S(1)} %get-tuple-element.83), channel_id=1, source_target_pairs={{0,7},{1,6},{2,5},{3,4},{4,3},{5,2},{6,1},{7,0},{8,15},{9,14},{10,... | collective-permute-start | bytes 6152 | tf_op jit(solution)/shard_map/ppermute | solution.py:357
  70.1 4.5 %collective-permute-start.32 = (f32[4,128]{1,0:T(4,128)S(1)}, f32[4,128]{1,0:T(4,128)S(1)}, u32[]{:S(2)}, u32[]{:S(2)}) collective-permute-start(f32[4,128]{1,0:T(4,128)S(1)} %get-tuple-element.84), channel_id=1, source_target_pairs={{0,4},{1,5},{2,6},{3,7},{4,0},{5,1},{6,2},{7,3},{8,12},{9,13},{10,... | collective-permute-start | bytes 6152 | tf_op jit(solution)/shard_map/ppermute | solution.py:357
  71.5 3.1 %collective-permute-start.33 = (f32[4,128]{1,0:T(4,128)S(1)}, f32[4,128]{1,0:T(4,128)S(1)}, u32[]{:S(2)}, u32[]{:S(2)}) collective-permute-start(f32[4,128]{1,0:T(4,128)S(1)} %get-tuple-element.85), channel_id=1, source_target_pairs={{0,3},{1,2},{2,1},{3,0},{4,7},{5,6},{6,5},{7,4},{8,11},{9,10},{10,... | collective-permute-start | bytes 6152 | tf_op jit(solution)/shard_map/ppermute | solution.py:357

commit v9 on v8

--- a/solution.py
+++ b/solution.py
@@ -299,8 +299,8 @@
     words = median_ref.shape[1]
     span = payload[0].shape[1] - part_ref.shape[1]
     wide = jnp.concatenate(high_low(median_ref[...]), axis=0)
-    tall = wide.T.astype(jnp.bfloat16)
     wide = wide.astype(jnp.bfloat16)
+    tall = wide.T
     wide_ref[...] = wide
     tall_ref[...] = tall
     weighted = base_rows_of(payload, slice(half * words, (half + 1) * words))

time: 75.4 us -> 75.3 us (level)
  no operation moved by 1% of the time
where the time goes in v9:
time: 75.3 us; the launch traced here: 75.2 us
  starting transfers between devices  37.4 us (50%)
  waiting for transfers between devices  28.2 us (37%)
  Pallas kernels  7.18 us (10%)
  local copies, waits for them, and re-layouts  1.67 us (2%)
  between operations  0.77 us (1%)
    ppermute x21, starting transfers between devices, over_chips(): lax.ppermute(array, 'doc', [(c * cores + k, (c ^ step) * cores + (k + ste...  27.7 us
    ppermute x21, waiting for transfers between devices, over_chips(): lax.ppermute(array, 'doc', [(c * cores + k, (c ^ step) * cores + (k + ste...  26.6 us
    ppermute x6, starting transfers between devices, over_pert(): return lax.ppermute(array, 'pert', [(m, m ^ step) for m in range(members)])  7.11 us
    pallas_call x13, Pallas kernels, call(): pl.pallas_call(kernel, out_shape=outs, in_specs=[pl.BlockSpec(memory_spac...  5.87 us
    ppermute x7, starting transfers between devices, over_cores(): return lax.ppermute(array, 'doc', [(d, d ^ 1) for d in range(doc_size)])  2.6 us
    unnamed x9, local copies, waits for them, and re-layouts  1.62 us
    ppermute x7, waiting for transfers between devices, over_cores(): return lax.ppermute(array, 'doc', [(d, d ^ 1) for d in range(doc_size)])  1.56 us
  transfers between devices with their start and end apart: 34, of which 18 were waited for; matrix products, arithmetic and copies ran while one was open for 1% of the time, Pallas kernels for 6%

profile of v9, /device:TPU:0, one launch (start us, length us, event | category | flops | bytes accessed | tf_op | source)
XLA Modules:
  0.0 75.2 jit_solution(3246495012306386321)
XLA Ops:
  0.6 0.5 collective-permute-start
  1.2 1.3 %shard_map.87 = (f32[8,4224]{1,0:T(8,128)S(1)}, f32[8,4224]{1,0:T(8,128)S(1)}, f32[8,4224]{1,0:T(8,128)S(1)}, f32[8,4224]{1,0:T(8,128)S(1)}) custom-call(s32[8,128]{1,0:T(8,128)} %bitcast.13, f32[8,64]{1,0:T(8,128)} %bitcast.14, s32[1,64]{1,0:T(1,128)} %perm_hbm.1, s32[8,16384]{1,0:T(8,128)} %bitcast.12), custom_call_target="tpu_custom_call" | custom-call | bytes 1572864 | tf_op jit(solution)/shard_map/pallas_call | solution.py:373
  2.5 4.8 %collective-permute-start.1 = (f32[8,4224]{1,0:T(8,128)S(1)}, f32[8,4224]{1,0:T(8,128)S(1)}, u32[]{:S(2)}, u32[]{:S(2)}) collective-permute-start(f32[8,4224]{1,0:T(8,128)S(1)} %get-tuple-element.47), channel_id=1, source_target_pairs={{0,7},{1,6},{2,5},{3,4},{4,3},{5,2},{6,1},{7,0},{8,15},{9,14},{10,... | collective-permute-start | bytes 405512 | tf_op jit(solution)/shard_map/ppermute | solution.py:357
  7.3 0.6 collective-permute-start.3
  7.9 0.9 %copy-done.1 = s32[4,16384]{1,0:T(4,128)S(1)} copy-done((s32[4,16384]{1,0:T(4,128)S(1)}, s32[4,16384]{1,0:T(4,128)}, u32[]{:S(2)}) %copy-start.1) | copy-done | bytes 262168
  8.9 0.1 shard_map.88
  8.9 1.1 %collective-permute-start.4 = (f32[4,4224]{1,0:T(4,128)S(1)}, f32[4,4224]{1,0:T(4,128)S(1)}, u32[]{:S(2)}, u32[]{:S(2)}) collective-permute-start(f32[4,4224]{1,0:T(4,128)S(1)} %get-tuple-element.51), channel_id=1, source_target_pairs={{0,3},{1,2},{2,1},{3,0},{4,7},{5,6},{6,5},{7,4},{8,11},{9,10},{10,... | collective-permute-start | bytes 202760 | tf_op jit(solution)/shard_map/ppermute | solution.py:357
  10.1 1.1 %shard_map.86 = (bf16[128,4096]{1,0:T(8,128)(2,1)S(1)}, bf16[4096,128]{1,0:T(8,128)(2,1)S(1)}, f32[8,128]{1,0:T(8,128)S(1)}, f32[64,2048]{1,0:T(8,128)S(1)}) custom-call(s32[1,64]{1,0:T(1,128)S(1)} %copy-done.3, f32[64,2048]{1,0:T(8,128)S(1)} %bitcast.11, f32[64,2048]{1,0:T(8,128)S(1)} %collective-permute-done.refs_1_), custom_call_target="tpu_custom_call" | custom-call | bytes 4194304 | tf_op jit(solution)/shard_map/pallas_call | solution.py:37
  11.2 6.8 %collective-permute-done.4.refs_4_.refs_5_.refs_1_ = f32[4,4224]{1,0:T(4,128)S(1)} collective-permute-done((f32[4,4224]{1,0:T(4,128)S(1)}, f32[4,4224]{1,0:T(4,128)S(1)}, u32[]{:S(2)}, u32[]{:S(2)}) %collective-permute-start.4) | collective-permute-done | bytes 67616 | tf_op jit(solution)/shard_map/ppermute | solution.py:357
  18.0 1.2 %collective-permute-done.3.refs_2_.refs_1_ = f32[8,4224]{1,0:T(8,128)S(1)} collective-permute-done((f32[8,4224]{1,0:T(8,128)S(1)}, f32[8,4224]{1,0:T(8,128)S(1)}, u32[]{:S(2)}, u32[]{:S(2)}) %collective-permute-start.3) | collective-permute-done | bytes 135200 | tf_op jit(solution)/shard_map/ppermute | solution.py:357
  19.2 0.5 shard_map.89
  19.7 2.6 %collective-permute-start.5 = (f32[24,128]{1,0:T(8,128)S(1)}, f32[24,128]{1,0:T(8,128)S(1)}, u32[]{:S(2)}, u32[]{:S(2)}) collective-permute-start(f32[24,128]{1,0:T(8,128)S(1)} %get-tuple-element.53.refs_4_), channel_id=1, source_target_pairs={{0,7},{1,6},{2,5},{3,4},{4,3},{5,2},{6,1},{7,0},{8,15},{9,14},{10,... | collective-permute-start | bytes 36872 | tf_op jit(solution)/shard_map/ppermute | solution.py:357
  22.3 1.3 %collective-permute-start.7 = (f32[24,128]{1,0:T(8,128)S(1)}, f32[24,128]{1,0:T(8,128)S(1)}, u32[]{:S(2)}, u32[]{:S(2)}) collective-permute-start(f32[24,128]{1,0:T(8,128)S(1)} %get-tuple-element.53.refs_4_), channel_id=1, source_target_pairs={{0,3},{1,2},{2,1},{3,0},{4,7},{5,6},{6,5},{7,4},{8,11},{9,10},{10,... | collective-permute-start | bytes 36872 | tf_op jit(solution)/shard_map/ppermute | solution.py:357
  23.6 1.1 %collective-permute-done.5.refs_5_ = f32[24,128]{1,0:T(8,128)S(1)} collective-permute-done((f32[24,128]{1,0:T(8,128)S(1)}, f32[24,128]{1,0:T(8,128)S(1)}, u32[]{:S(2)}, u32[]{:S(2)}) %collective-permute-start.5) | collective-permute-done | bytes 12320 | tf_op jit(solution)/shard_map/ppermute | solution.py:357
  24.7 2.2 %collective-permute-done.6.refs_6_ = f32[24,128]{1,0:T(8,128)S(1)} collective-permute-done((f32[24,128]{1,0:T(8,128)S(1)}, f32[24,128]{1,0:T(8,128)S(1)}, u32[]{:S(2)}, u32[]{:S(2)}) %collective-permute-start.6) | collective-permute-done | bytes 12320 | tf_op jit(solution)/shard_map/ppermute | solution.py:357
  26.9 0.6 shard_map.90
  27.5 1.1 %collective-permute-start.8 = (f32[18,128]{1,0:T(8,128)S(1)}, f32[18,128]{1,0:T(8,128)S(1)}, u32[]{:S(2)}, u32[]{:S(2)}) collective-permute-start(f32[18,128]{1,0:T(8,128)S(1)} %get-tuple-element.57), channel_id=1, source_target_pairs={{0,7},{1,6},{2,5},{3,4},{4,3},{5,2},{6,1},{7,0},{8,15},{9,14},{10,... | collective-permute-start | bytes 27656 | tf_op jit(solution)/shard_map/ppermute | solution.py:357
  28.6 0.6 collective-permute-start.9
  29.2 2.2 %collective-permute-start.10 = (f32[16,128]{1,0:T(8,128)S(1)}, f32[16,128]{1,0:T(8,128)S(1)}, u32[]{:S(2)}, u32[]{:S(2)}) collective-permute-start(f32[16,128]{1,0:T(8,128)S(1)} %get-tuple-element.56.refs_5_), channel_id=1, source_target_pairs={{0,3},{1,2},{2,1},{3,0},{4,7},{5,6},{6,5},{7,4},{8,11},{9,10},{10,... | collective-permute-start | bytes 24584 | tf_op jit(solution)/shard_map/ppermute | solution.py:357
  31.4 1.5 %collective-permute-done.10.refs_8_ = f32[16,128]{1,0:T(8,128)S(1)} collective-permute-done((f32[16,128]{1,0:T(8,128)S(1)}, f32[16,128]{1,0:T(8,128)S(1)}, u32[]{:S(2)}, u32[]{:S(2)}) %collective-permute-start.10) | collective-permute-done | bytes 8224 | tf_op jit(solution)/shard_map/ppermute | solution.py:357
  32.8 0.4 collective-permute-done.9.refs_7_
  33.2 0.6 shard_map.91
  33.8 1.4 %collective-permute-start.11 = (f32[16,128]{1,0:T(8,128)S(1)}, f32[16,128]{1,0:T(8,128)S(1)}, u32[]{:S(2)}, u32[]{:S(2)}) collective-permute-start(f32[16,128]{1,0:T(8,128)S(1)} %get-tuple-element.61), channel_id=1, source_target_pairs={{0,7},{1,6},{2,5},{3,4},{4,3},{5,2},{6,1},{7,0},{8,15},{9,14},{10,... | collective-permute-start | bytes 24584 | tf_op jit(solution)/shard_map/ppermute | solution.py:357
  35.2 1.3 %collective-permute-start.12 = (f32[16,128]{1,0:T(8,128)S(1)}, f32[16,128]{1,0:T(8,128)S(1)}, u32[]{:S(2)}, u32[]{:S(2)}) collective-permute-start(f32[16,128]{1,0:T(8,128)S(1)} %get-tuple-element.62), channel_id=1, source_target_pairs={{0,4},{1,5},{2,6},{3,7},{4,0},{5,1},{6,2},{7,3},{8,12},{9,13},{10,... | collective-permute-start | bytes 24584 | tf_op jit(solution)/shard_map/ppermute | solution.py:357
  36.5 1.1 %collective-permute-start.13 = (f32[16,128]{1,0:T(8,128)S(1)}, f32[16,128]{1,0:T(8,128)S(1)}, u32[]{:S(2)}, u32[]{:S(2)}) collective-permute-start(f32[16,128]{1,0:T(8,128)S(1)} %get-tuple-element.60.refs_0_), channel_id=1, source_target_pairs={{0,3},{1,2},{2,1},{3,0},{4,7},{5,6},{6,5},{7,4},{8,11},{9,10},{10,... | collective-permute-start | bytes 24584 | tf_op jit(solution)/shard_map/ppermute | solution.py:357
  37.6 1.1 %collective-permute-done.11.refs_1_ = f32[16,128]{1,0:T(8,128)S(1)} collective-permute-done((f32[16,128]{1,0:T(8,128)S(1)}, f32[16,128]{1,0:T(8,128)S(1)}, u32[]{:S(2)}, u32[]{:S(2)}) %collective-permute-start.11) | collective-permute-done | bytes 8224 | tf_op jit(solution)/shard_map/ppermute | solution.py:357
  38.7 1.1 %collective-permute-done.12.refs_2_ = f32[16,128]{1,0:T(8,128)S(1)} collective-permute-done((f32[16,128]{1,0:T(8,128)S(1)}, f32[16,128]{1,0:T(8,128)S(1)}, u32[]{:S(2)}, u32[]{:S(2)}) %collective-permute-start.12) | collective-permute-done | bytes 8224 | tf_op jit(solution)/shard_map/ppermute | solution.py:357
  39.8 0.1 shard_map.92.topics_ref
  39.8 0.0 collective-permute-start.15
  39.9 0.4 shard_map.93.refs_1_
  40.3 0.8 %collective-permute-done.15.topics_ref = f32[32,128]{1,0:T(8,128)S(1)} collective-permute-done((f32[32,128]{1,0:T(8,128)S(1)}, f32[32,128]{1,0:T(8,128)S(1)}, u32[]{:S(2)}, u32[]{:S(2)}) %collective-permute-start.15) | collective-permute-done | bytes 16416 | tf_op jit(solution)/shard_map/ppermute | solution.py:368
  41.0 0.4 shard_map.94
  41.5 2.5 %collective-permute-start.16 = (f32[64,512]{1,0:T(8,128)S(1)}, f32[64,512]{1,0:T(8,128)S(1)}, u32[]{:S(2)}, u32[]{:S(2)}) collective-permute-start(f32[64,512]{1,0:T(8,128)S(1)} %get-tuple-element.88), channel_id=1, source_target_pairs={{0,24},{8,16},{16,8},{24,0},{1,25},{9,17},{17,9},{25,1},{2,26},{10... | collective-permute-start | bytes 393224 | tf_op jit(solution)/shard_map/ppermute | solution.py:371
  44.0 0.5 collective-permute-start.17
  44.5 0.5 collective-permute-start.18
  45.0 1.4 %collective-permute-start.19 = (f32[4,4224]{1,0:T(4,128)S(1)}, f32[4,4224]{1,0:T(4,128)S(1)}, u32[]{:S(2)}, u32[]{:S(2)}) collective-permute-start(f32[4,4224]{1,0:T(4,128)S(1)} %get-tuple-element.70), channel_id=1, source_target_pairs={{0,4},{1,5},{2,6},{3,7},{4,0},{5,1},{6,2},{7,3},{8,12},{9,13},{10,... | collective-permute-start | bytes 202760 | tf_op jit(solution)/shard_map/ppermute | solution.py:357
  46.5 4.5 %collective-permute-done.19.refs_4_.refs_6_.refs_2_ = f32[4,4224]{1,0:T(4,128)S(1)} collective-permute-done((f32[4,4224]{1,0:T(4,128)S(1)}, f32[4,4224]{1,0:T(4,128)S(1)}, u32[]{:S(2)}, u32[]{:S(2)}) %collective-permute-start.19) | collective-permute-done | bytes 67616 | tf_op jit(solution)/shard_map/ppermute | solution.py:357
  51.0 0.1 shard_map.95.refs_0_
  51.0 2.5 %collective-permute-start.20 = (f32[64,512]{1,0:T(8,128)S(1)}, f32[64,512]{1,0:T(8,128)S(1)}, u32[]{:S(2)}, u32[]{:S(2)}) collective-permute-start(f32[64,512]{1,0:T(8,128)S(1)} %shard_map.95.refs_0_), channel_id=1, source_target_pairs={{0,24},{8,16},{16,8},{24,0},{1,25},{9,17},{17,9},{25,1},{2,26},{10... | collective-permute-start | bytes 393224 | tf_op jit(solution)/shard_map/ppermute | solution.py:371
  53.5 0.5 collective-permute-start.24
  54.1 0.5 collective-permute-start.26
  54.6 0.4 collective-permute-start.21
  55.0 1.5 %collective-permute-start.22 = (f32[64,512]{1,0:T(8,128)S(1)}, f32[64,512]{1,0:T(8,128)S(1)}, u32[]{:S(2)}, u32[]{:S(2)}) collective-permute-start(f32[64,512]{1,0:T(8,128)S(1)} %shard_map.95.refs_0_), channel_id=1, source_target_pairs={{0,1},{1,0},{2,3},{3,2},{4,5},{5,4},{6,7},{7,6},{8,9},{9,8},{10,11... | collective-permute-start | bytes 393224 | tf_op jit(solution)/shard_map/ppermute | solution.py:368
  56.5 3.7 %collective-permute-done.21.refs_7_.refs_3_ = f32[4,4224]{1,0:T(4,128)S(1)} collective-permute-done((f32[4,4224]{1,0:T(4,128)S(1)}, f32[4,4224]{1,0:T(4,128)S(1)}, u32[]{:S(2)}, u32[]{:S(2)}) %collective-permute-start.21) | collective-permute-done | bytes 67616 | tf_op jit(solution)/shard_map/ppermute | solution.py:357
  60.2 0.5 collective-permute-start.25
  60.7 0.1 collective-permute-start.27
  60.7 0.5 shard_map.96
  61.2 0.3 collective-permute-done.23.refs_1_
  61.5 0.2 collective-permute-done.25.refs_2_
  61.7 0.3 collective-permute-done.27.refs_3_
  62.0 0.5 shard_map.97
  62.5 1.6 %collective-permute-start.28 = (f32[16,128]{1,0:T(8,128)S(1)}, f32[16,128]{1,0:T(8,128)S(1)}, u32[]{:S(2)}, u32[]{:S(2)}) collective-permute-start(f32[16,128]{1,0:T(8,128)S(1)} %get-tuple-element.76.refs_4_), channel_id=1, source_target_pairs={{0,7},{1,6},{2,5},{3,4},{4,3},{5,2},{6,1},{7,0},{8,15},{9,14},{10,... | collective-permute-start | bytes 24584 | tf_op jit(solution)/shard_map/ppermute | solution.py:357
  64.1 0.6 collective-permute-start.29
  64.7 1.7 %collective-permute-start.30 = (f32[16,128]{1,0:T(8,128)S(1)}, f32[16,128]{1,0:T(8,128)S(1)}, u32[]{:S(2)}, u32[]{:S(2)}) collective-permute-start(f32[16,128]{1,0:T(8,128)S(1)} %get-tuple-element.76.refs_4_), channel_id=1, source_target_pairs={{0,3},{1,2},{2,1},{3,0},{4,7},{5,6},{6,5},{7,4},{8,11},{9,10},{10,... | collective-permute-start | bytes 24584 | tf_op jit(solution)/shard_map/ppermute | solution.py:357
  66.3 1.0 %collective-permute-done.28.refs_5_ = f32[16,128]{1,0:T(8,128)S(1)} collective-permute-done((f32[16,128]{1,0:T(8,128)S(1)}, f32[16,128]{1,0:T(8,128)S(1)}, u32[]{:S(2)}, u32[]{:S(2)}) %collective-permute-start.28) | collective-permute-done | bytes 8224 | tf_op jit(solution)/shard_map/ppermute | solution.py:357
  67.4 1.2 %collective-permute-done.29.refs_6_ = f32[16,128]{1,0:T(8,128)S(1)} collective-permute-done((f32[16,128]{1,0:T(8,128)S(1)}, f32[16,128]{1,0:T(8,128)S(1)}, u32[]{:S(2)}, u32[]{:S(2)}) %collective-permute-start.29) | collective-permute-done | bytes 8224 | tf_op jit(solution)/shard_map/ppermute | solution.py:357
  68.6 0.5 shard_map.98
  69.2 0.9 %collective-permute-start.31 = (f32[4,128]{1,0:T(4,128)S(1)}, f32[4,128]{1,0:T(4,128)S(1)}, u32[]{:S(2)}, u32[]{:S(2)}) collective-permute-start(f32[4,128]{1,0:T(4,128)S(1)} %get-tuple-element.83), channel_id=1, source_target_pairs={{0,7},{1,6},{2,5},{3,4},{4,3},{5,2},{6,1},{7,0},{8,15},{9,14},{10,... | collective-permute-start | bytes 6152 | tf_op jit(solution)/shard_map/ppermute | solution.py:357
  70.1 1.4 %collective-permute-start.32 = (f32[4,128]{1,0:T(4,128)S(1)}, f32[4,128]{1,0:T(4,128)S(1)}, u32[]{:S(2)}, u32[]{:S(2)}) collective-permute-start(f32[4,128]{1,0:T(4,128)S(1)} %get-tuple-element.84), channel_id=1, source_target_pairs={{0,4},{1,5},{2,6},{3,7},{4,0},{5,1},{6,2},{7,3},{8,12},{9,13},{10,... | collective-permute-start | bytes 6152 | tf_op jit(solution)/shard_map/ppermute | solution.py:357
  71.5 1.5 %collective-permute-start.33 = (f32[4,128]{1,0:T(4,128)S(1)}, f32[4,128]{1,0:T(4,128)S(1)}, u32[]{:S(2)}, u32[]{:S(2)}) collective-permute-start(f32[4,128]{1,0:T(4,128)S(1)} %get-tuple-element.85), channel_id=1, source_target_pairs={{0,3},{1,2},{2,1},{3,0},{4,7},{5,6},{6,5},{7,4},{8,11},{9,10},{10,... | collective-permute-start | bytes 6152 | tf_op jit(solution)/shard_map/ppermute | solution.py:357
  73.0 0.7 copy.9
  73.7 0.3 collective-permute-done.31.refs_1_
  74.0 0.6 collective-permute-done.32.refs_2_
  74.6 0.6 shard_map.99
  (28 shorter events, 0.1 us)
Async XLA Ops:
  0.6 9.5 %copy-start = (f32[1,2048,64]{1,2,0:T(8,128)S(1)}, f32[1,2048,64]{1,2,0:T(8,128)}, u32[]{:S(2)}) copy-start(f32[1,2048,64]{1,2,0:T(8,128)} %param.10) | copy-start | bytes 1572868
  0.6 9.4 %collective-permute-start = (f32[64,2048]{1,0:T(8,128)}, f32[64,2048]{1,0:T(8,128)S(1)}, u32[]{:S(2)}, u32[]{:S(2)}) collective-permute-start(f32[64,2048]{1,0:T(8,128)} %bitcast.10), channel_id=1, source_target_pairs={{0,1},{1,0},{2,3},{3,2},{4,5},{5,4},{6,7},{7,6},{8,9},{9,8},{10,11... | collective-permute-start | bytes 1572872 | tf_op jit(solution)/shard_map/ppermute | solution.py:368
  2.5 5.4 %copy-start.2 = (f32[4,64]{1,0:T(4,128)S(1)}, f32[4,64]{1,0:T(4,128)}, u32[]{:S(2)}) copy-start(f32[4,64]{1,0:T(4,128)} %topics_ref.1) | copy-start | bytes 3076
  2.5 15.5 %collective-permute-start.1 = (f32[8,4224]{1,0:T(8,128)S(1)}, f32[8,4224]{1,0:T(8,128)S(1)}, u32[]{:S(2)}, u32[]{:S(2)}) collective-permute-start(f32[8,4224]{1,0:T(8,128)S(1)} %get-tuple-element.47), channel_id=1, source_target_pairs={{0,7},{1,6},{2,5},{3,4},{4,3},{5,2},{6,1},{7,0},{8,15},{9,14},{10,... | collective-permute-start | bytes 405512 | tf_op jit(solution)/shard_map/ppermute | solution.py:357
  7.3 10.7 %collective-permute-start.2 = (f32[8,4224]{1,0:T(8,128)S(1)}, f32[8,4224]{1,0:T(8,128)S(1)}, u32[]{:S(2)}, u32[]{:S(2)}) collective-permute-start(f32[8,4224]{1,0:T(8,128)S(1)} %get-tuple-element.48), channel_id=1, source_target_pairs={{0,3},{1,2},{2,1},{3,0},{4,7},{5,6},{6,5},{7,4},{8,11},{9,10},{10,... | collective-permute-start | bytes 405512 | tf_op jit(solution)/shard_map/ppermute | solution.py:357
  7.3 11.9 %collective-permute-start.3 = (f32[8,4224]{1,0:T(8,128)S(1)}, f32[8,4224]{1,0:T(8,128)S(1)}, u32[]{:S(2)}, u32[]{:S(2)}) collective-permute-start(f32[8,4224]{1,0:T(8,128)S(1)} %get-tuple-element.49), channel_id=1, source_target_pairs={{0,4},{1,5},{2,6},{3,7},{4,0},{5,1},{6,2},{7,3},{8,12},{9,13},{10,... | collective-permute-start | bytes 405512 | tf_op jit(solution)/shard_map/ppermute | solution.py:357
  7.9 1.0 %copy-start.1 = (s32[4,16384]{1,0:T(4,128)S(1)}, s32[4,16384]{1,0:T(4,128)}, u32[]{:S(2)}) copy-start(s32[4,16384]{1,0:T(4,128)} %counts_ref.1) | copy-start | bytes 786436
  8.9 1.2 %copy-start.3 = (s32[1,64]{1,0:T(1,128)S(1)}, s32[1,64]{1,0:T(1,128)}, u32[]{:S(2)}) copy-start(s32[1,64]{1,0:T(1,128)} %perm_hbm.1) | copy-start | bytes 772
  8.9 9.0 %collective-permute-start.4 = (f32[4,4224]{1,0:T(4,128)S(1)}, f32[4,4224]{1,0:T(4,128)S(1)}, u32[]{:S(2)}, u32[]{:S(2)}) collective-permute-start(f32[4,4224]{1,0:T(4,128)S(1)} %get-tuple-element.51), channel_id=1, source_target_pairs={{0,3},{1,2},{2,1},{3,0},{4,7},{5,6},{6,5},{7,4},{8,11},{9,10},{10,... | collective-permute-start | bytes 202760 | tf_op jit(solution)/shard_map/ppermute | solution.py:357
  19.7 20.0 %collective-permute-start.14 = (f32[32,2048]{1,0:T(8,128)S(1)}, f32[32,2048]{1,0:T(8,128)S(1)}, u32[]{:S(2)}, u32[]{:S(2)}) collective-permute-start(f32[32,2048]{1,0:T(8,128)S(1)} %get-tuple-element.63), channel_id=1, source_target_pairs={{0,1},{1,0},{2,3},{3,2},{4,5},{5,4},{6,7},{7,6},{8,9},{9,8},{10,11... | collective-permute-start | bytes 786440 | tf_op jit(solution)/shard_map/ppermute | solution.py:368
  19.7 5.0 %collective-permute-start.5 = (f32[24,128]{1,0:T(8,128)S(1)}, f32[24,128]{1,0:T(8,128)S(1)}, u32[]{:S(2)}, u32[]{:S(2)}) collective-permute-start(f32[24,128]{1,0:T(8,128)S(1)} %get-tuple-element.53.refs_4_), channel_id=1, source_target_pairs={{0,7},{1,6},{2,5},{3,4},{4,3},{5,2},{6,1},{7,0},{8,15},{9,14},{10,... | collective-permute-start | bytes 36872 | tf_op jit(solution)/shard_map/ppermute | solution.py:357
  22.3 4.6 %collective-permute-start.6 = (f32[24,128]{1,0:T(8,128)S(1)}, f32[24,128]{1,0:T(8,128)S(1)}, u32[]{:S(2)}, u32[]{:S(2)}) collective-permute-start(f32[24,128]{1,0:T(8,128)S(1)} %get-tuple-element.53.refs_4_), channel_id=1, source_target_pairs={{0,4},{1,5},{2,6},{3,7},{4,0},{5,1},{6,2},{7,3},{8,12},{9,13},{10,... | collective-permute-start | bytes 36872 | tf_op jit(solution)/shard_map/ppermute | solution.py:357
  22.3 4.6 %collective-permute-start.7 = (f32[24,128]{1,0:T(8,128)S(1)}, f32[24,128]{1,0:T(8,128)S(1)}, u32[]{:S(2)}, u32[]{:S(2)}) collective-permute-start(f32[24,128]{1,0:T(8,128)S(1)} %get-tuple-element.53.refs_4_), channel_id=1, source_target_pairs={{0,3},{1,2},{2,1},{3,0},{4,7},{5,6},{6,5},{7,4},{8,11},{9,10},{10,... | collective-permute-start | bytes 36872 | tf_op jit(solution)/shard_map/ppermute | solution.py:357
  27.5 5.7 %collective-permute-start.8 = (f32[18,128]{1,0:T(8,128)S(1)}, f32[18,128]{1,0:T(8,128)S(1)}, u32[]{:S(2)}, u32[]{:S(2)}) collective-permute-start(f32[18,128]{1,0:T(8,128)S(1)} %get-tuple-element.57), channel_id=1, source_target_pairs={{0,7},{1,6},{2,5},{3,4},{4,3},{5,2},{6,1},{7,0},{8,15},{9,14},{10,... | collective-permute-start | bytes 27656 | tf_op jit(solution)/shard_map/ppermute | solution.py:357
  28.6 4.6 %collective-permute-start.9 = (f32[17,128]{1,0:T(8,128)S(1)}, f32[17,128]{1,0:T(8,128)S(1)}, u32[]{:S(2)}, u32[]{:S(2)}) collective-permute-start(f32[17,128]{1,0:T(8,128)S(1)} %get-tuple-element.58), channel_id=1, source_target_pairs={{0,4},{1,5},{2,6},{3,7},{4,0},{5,1},{6,2},{7,3},{8,12},{9,13},{10,... | collective-permute-start | bytes 26120 | tf_op jit(solution)/shard_map/ppermute | solution.py:357
  29.2 3.6 %collective-permute-start.10 = (f32[16,128]{1,0:T(8,128)S(1)}, f32[16,128]{1,0:T(8,128)S(1)}, u32[]{:S(2)}, u32[]{:S(2)}) collective-permute-start(f32[16,128]{1,0:T(8,128)S(1)} %get-tuple-element.56.refs_5_), channel_id=1, source_target_pairs={{0,3},{1,2},{2,1},{3,0},{4,7},{5,6},{6,5},{7,4},{8,11},{9,10},{10,... | collective-permute-start | bytes 24584 | tf_op jit(solution)/shard_map/ppermute | solution.py:357
  33.8 4.9 %collective-permute-start.11 = (f32[16,128]{1,0:T(8,128)S(1)}, f32[16,128]{1,0:T(8,128)S(1)}, u32[]{:S(2)}, u32[]{:S(2)}) collective-permute-start(f32[16,128]{1,0:T(8,128)S(1)} %get-tuple-element.61), channel_id=1, source_target_pairs={{0,7},{1,6},{2,5},{3,4},{4,3},{5,2},{6,1},{7,0},{8,15},{9,14},{10,... | collective-permute-start | bytes 24584 | tf_op jit(solution)/shard_map/ppermute | solution.py:357
  35.2 4.5 %collective-permute-start.12 = (f32[16,128]{1,0:T(8,128)S(1)}, f32[16,128]{1,0:T(8,128)S(1)}, u32[]{:S(2)}, u32[]{:S(2)}) collective-permute-start(f32[16,128]{1,0:T(8,128)S(1)} %get-tuple-element.62), channel_id=1, source_target_pairs={{0,4},{1,5},{2,6},{3,7},{4,0},{5,1},{6,2},{7,3},{8,12},{9,13},{10,... | collective-permute-start | bytes 24584 | tf_op jit(solution)/shard_map/ppermute | solution.py:357
  36.5 3.3 %collective-permute-start.13 = (f32[16,128]{1,0:T(8,128)S(1)}, f32[16,128]{1,0:T(8,128)S(1)}, u32[]{:S(2)}, u32[]{:S(2)}) collective-permute-start(f32[16,128]{1,0:T(8,128)S(1)} %get-tuple-element.60.refs_0_), channel_id=1, source_target_pairs={{0,3},{1,2},{2,1},{3,0},{4,7},{5,6},{6,5},{7,4},{8,11},{9,10},{10,... | collective-permute-start | bytes 24584 | tf_op jit(solution)/shard_map/ppermute | solution.py:357
  39.8 1.2 %collective-permute-start.15 = (f32[32,128]{1,0:T(8,128)S(1)}, f32[32,128]{1,0:T(8,128)S(1)}, u32[]{:S(2)}, u32[]{:S(2)}) collective-permute-start(f32[32,128]{1,0:T(8,128)S(1)} %shard_map.92.topics_ref), channel_id=1, source_target_pairs={{0,1},{1,0},{2,3},{3,2},{4,5},{5,4},{6,7},{7,6},{8,9},{9,8},{10,11... | collective-permute-start | bytes 49160 | tf_op jit(solution)/shard_map/ppermute | solution.py:368
  41.5 9.5 %collective-permute-start.16 = (f32[64,512]{1,0:T(8,128)S(1)}, f32[64,512]{1,0:T(8,128)S(1)}, u32[]{:S(2)}, u32[]{:S(2)}) collective-permute-start(f32[64,512]{1,0:T(8,128)S(1)} %get-tuple-element.88), channel_id=1, source_target_pairs={{0,24},{8,16},{16,8},{24,0},{1,25},{9,17},{17,9},{25,1},{2,26},{10... | collective-permute-start | bytes 393224 | tf_op jit(solution)/shard_map/ppermute | solution.py:371
  44.0 7.0 %collective-permute-start.17 = (f32[64,512]{1,0:T(8,128)S(1)}, f32[64,512]{1,0:T(8,128)S(1)}, u32[]{:S(2)}, u32[]{:S(2)}) collective-permute-start(f32[64,512]{1,0:T(8,128)S(1)} %get-tuple-element.87), channel_id=1, source_target_pairs={{0,16},{8,24},{16,0},{24,8},{1,17},{9,25},{17,1},{25,9},{2,18},{10... | collective-permute-start | bytes 393224 | tf_op jit(solution)/shard_map/ppermute | solution.py:371
  44.5 6.4 %collective-permute-start.18 = (f32[64,512]{1,0:T(8,128)S(1)}, f32[64,512]{1,0:T(8,128)S(1)}, u32[]{:S(2)}, u32[]{:S(2)}) collective-permute-start(f32[64,512]{1,0:T(8,128)S(1)} %get-tuple-element.86), channel_id=1, source_target_pairs={{0,8},{8,0},{16,24},{24,16},{1,9},{9,1},{17,25},{25,17},{2,10},{10... | collective-permute-start | bytes 393224 | tf_op jit(solution)/shard_map/ppermute | solution.py:371
  45.0 5.9 %collective-permute-start.19 = (f32[4,4224]{1,0:T(4,128)S(1)}, f32[4,4224]{1,0:T(4,128)S(1)}, u32[]{:S(2)}, u32[]{:S(2)}) collective-permute-start(f32[4,4224]{1,0:T(4,128)S(1)} %get-tuple-element.70), channel_id=1, source_target_pairs={{0,4},{1,5},{2,6},{3,7},{4,0},{5,1},{6,2},{7,3},{8,12},{9,13},{10,... | collective-permute-start | bytes 202760 | tf_op jit(solution)/shard_map/ppermute | solution.py:357
  51.0 9.1 %collective-permute-start.20 = (f32[64,512]{1,0:T(8,128)S(1)}, f32[64,512]{1,0:T(8,128)S(1)}, u32[]{:S(2)}, u32[]{:S(2)}) collective-permute-start(f32[64,512]{1,0:T(8,128)S(1)} %shard_map.95.refs_0_), channel_id=1, source_target_pairs={{0,24},{8,16},{16,8},{24,0},{1,25},{9,17},{17,9},{25,1},{2,26},{10... | collective-permute-start | bytes 393224 | tf_op jit(solution)/shard_map/ppermute | solution.py:371
  53.5 6.6 %collective-permute-start.24 = (f32[64,512]{1,0:T(8,128)S(1)}, f32[64,512]{1,0:T(8,128)S(1)}, u32[]{:S(2)}, u32[]{:S(2)}) collective-permute-start(f32[64,512]{1,0:T(8,128)S(1)} %shard_map.95.refs_0_), channel_id=1, source_target_pairs={{0,16},{8,24},{16,0},{24,8},{1,17},{9,25},{17,1},{25,9},{2,18},{10... | collective-permute-start | bytes 393224 | tf_op jit(solution)/shard_map/ppermute | solution.py:371
  54.1 6.6 %collective-permute-start.26 = (f32[64,512]{1,0:T(8,128)S(1)}, f32[64,512]{1,0:T(8,128)S(1)}, u32[]{:S(2)}, u32[]{:S(2)}) collective-permute-start(f32[64,512]{1,0:T(8,128)S(1)} %shard_map.95.refs_0_), channel_id=1, source_target_pairs={{0,8},{8,0},{16,24},{24,16},{1,9},{9,1},{17,25},{25,17},{2,10},{10... | collective-permute-start | bytes 393224 | tf_op jit(solution)/shard_map/ppermute | solution.py:371
  54.6 5.6 %collective-permute-start.21 = (f32[4,4224]{1,0:T(4,128)S(1)}, f32[4,4224]{1,0:T(4,128)S(1)}, u32[]{:S(2)}, u32[]{:S(2)}) collective-permute-start(f32[4,4224]{1,0:T(4,128)S(1)} %get-tuple-element.72), channel_id=1, source_target_pairs={{0,7},{1,6},{2,5},{3,4},{4,3},{5,2},{6,1},{7,0},{8,15},{9,14},{10,... | collective-permute-start | bytes 202760 | tf_op jit(solution)/shard_map/ppermute | solution.py:357
  55.0 6.2 %collective-permute-start.22 = (f32[64,512]{1,0:T(8,128)S(1)}, f32[64,512]{1,0:T(8,128)S(1)}, u32[]{:S(2)}, u32[]{:S(2)}) collective-permute-start(f32[64,512]{1,0:T(8,128)S(1)} %shard_map.95.refs_0_), channel_id=1, source_target_pairs={{0,1},{1,0},{2,3},{3,2},{4,5},{5,4},{6,7},{7,6},{8,9},{9,8},{10,11... | collective-permute-start | bytes 393224 | tf_op jit(solution)/shard_map/ppermute | solution.py:368
  60.2 1.3 %collective-permute-start.23 = (f32[64,512]{1,0:T(8,128)S(1)}, f32[64,512]{1,0:T(8,128)S(1)}, u32[]{:S(2)}, u32[]{:S(2)}) collective-permute-start(f32[64,512]{1,0:T(8,128)S(1)} %collective-permute-done.20.refs_1_), channel_id=1, source_target_pairs={{0,1},{1,0},{2,3},{3,2},{4,5},{5,4},{6,7},{7,6},{8,9},{9,8},{10,11... | collective-permute-start | bytes 393224 | tf_op jit(solution)/shard_map/ppermute | solution.py:368
  60.2 1.5 %collective-permute-start.25 = (f32[64,512]{1,0:T(8,128)S(1)}, f32[64,512]{1,0:T(8,128)S(1)}, u32[]{:S(2)}, u32[]{:S(2)}) collective-permute-start(f32[64,512]{1,0:T(8,128)S(1)} %collective-permute-done.24.refs_2_), channel_id=1, source_target_pairs={{0,1},{1,0},{2,3},{3,2},{4,5},{5,4},{6,7},{7,6},{8,9},{9,8},{10,11... | collective-permute-start | bytes 393224 | tf_op jit(solution)/shard_map/ppermute | solution.py:368
  60.7 1.3 %collective-permute-start.27 = (f32[64,512]{1,0:T(8,128)S(1)}, f32[64,512]{1,0:T(8,128)S(1)}, u32[]{:S(2)}, u32[]{:S(2)}) collective-permute-start(f32[64,512]{1,0:T(8,128)S(1)} %collective-permute-done.26.refs_3_), channel_id=1, source_target_pairs={{0,1},{1,0},{2,3},{3,2},{4,5},{5,4},{6,7},{7,6},{8,9},{9,8},{10,11... | collective-permute-start | bytes 393224 | tf_op jit(solution)/shard_map/ppermute | solution.py:368
  62.5 4.9 %collective-permute-start.28 = (f32[16,128]{1,0:T(8,128)S(1)}, f32[16,128]{1,0:T(8,128)S(1)}, u32[]{:S(2)}, u32[]{:S(2)}) collective-permute-start(f32[16,128]{1,0:T(8,128)S(1)} %get-tuple-element.76.refs_4_), channel_id=1, source_target_pairs={{0,7},{1,6},{2,5},{3,4},{4,3},{5,2},{6,1},{7,0},{8,15},{9,14},{10,... | collective-permute-start | bytes 24584 | tf_op jit(solution)/shard_map/ppermute | solution.py:357
  64.1 4.5 %collective-permute-start.29 = (f32[16,128]{1,0:T(8,128)S(1)}, f32[16,128]{1,0:T(8,128)S(1)}, u32[]{:S(2)}, u32[]{:S(2)}) collective-permute-start(f32[16,128]{1,0:T(8,128)S(1)} %get-tuple-element.76.refs_4_), channel_id=1, source_target_pairs={{0,4},{1,5},{2,6},{3,7},{4,0},{5,1},{6,2},{7,3},{8,12},{9,13},{10,... | collective-permute-start | bytes 24584 | tf_op jit(solution)/shard_map/ppermute | solution.py:357
  64.7 3.9 %collective-permute-start.30 = (f32[16,128]{1,0:T(8,128)S(1)}, f32[16,128]{1,0:T(8,128)S(1)}, u32[]{:S(2)}, u32[]{:S(2)}) collective-permute-start(f32[16,128]{1,0:T(8,128)S(1)} %get-tuple-element.76.refs_4_), channel_id=1, source_target_pairs={{0,3},{1,2},{2,1},{3,0},{4,7},{5,6},{6,5},{7,4},{8,11},{9,10},{10,... | collective-permute-start | bytes 24584 | tf_op jit(solution)/shard_map/ppermute | solution.py:357
  69.2 4.8 %collective-permute-start.31 = (f32[4,128]{1,0:T(4,128)S(1)}, f32[4,128]{1,0:T(4,128)S(1)}, u32[]{:S(2)}, u32[]{:S(2)}) collective-permute-start(f32[4,128]{1,0:T(4,128)S(1)} %get-tuple-element.83), channel_id=1, source_target_pairs={{0,7},{1,6},{2,5},{3,4},{4,3},{5,2},{6,1},{7,0},{8,15},{9,14},{10,... | collective-permute-start | bytes 6152 | tf_op jit(solution)/shard_map/ppermute | solution.py:357
  70.1 4.5 %collective-permute-start.32 = (f32[4,128]{1,0:T(4,128)S(1)}, f32[4,128]{1,0:T(4,128)S(1)}, u32[]{:S(2)}, u32[]{:S(2)}) collective-permute-start(f32[4,128]{1,0:T(4,128)S(1)} %get-tuple-element.84), channel_id=1, source_target_pairs={{0,4},{1,5},{2,6},{3,7},{4,0},{5,1},{6,2},{7,3},{8,12},{9,13},{10,... | collective-permute-start | bytes 6152 | tf_op jit(solution)/shard_map/ppermute | solution.py:357
  71.5 3.1 %collective-permute-start.33 = (f32[4,128]{1,0:T(4,128)S(1)}, f32[4,128]{1,0:T(4,128)S(1)}, u32[]{:S(2)}, u32[]{:S(2)}) collective-permute-start(f32[4,128]{1,0:T(4,128)S(1)} %get-tuple-element.85), channel_id=1, source_target_pairs={{0,3},{1,2},{2,1},{3,0},{4,7},{5,6},{6,5},{7,4},{8,11},{9,10},{10,... | collective-permute-start | bytes 6152 | tf_op jit(solution)/shard_map/ppermute | solution.py:357

commit v10 on v9

--- a/solution.py
+++ b/solution.py
@@ -225,7 +225,7 @@
     weighted = jnp.concatenate([ref[:, :span] for ref in payload], axis=0)
     part = pack(product_of(weighted / recon_of(topics, wide_ref[...]), tall_ref[...]))
     part_ref[: part.shape[0]] = part
-    part_ref[part.shape[0] :] = col_part_ref[...]
+    part_ref[part.shape[0] :] = col_part_ref[:1]
     words = span // cores
     for half, ref in enumerate(half_refs):
         ref[...] = weighted[:, half * words : (half + 1) * words]
@@ -236,7 +236,8 @@
     if refs[-1].shape[0] == 8:
         payload, parts = refs[:chips][::-1], refs[chips : 2 * chips]
         topics_ref, *part_refs, total_ref = refs[2 * chips :]
-        total_ref[...] = sum(ref[packed:] for ref in parts)
+        total = sum(ref[packed : packed + 1] for ref in parts)
+        total_ref[...] = jnp.broadcast_to(total, total_ref.shape)
     else:
         total_ref, payload, parts = refs[0], refs[1 : chips + 1][::-1], refs[chips + 1 : 2 * chips + 1]
         topics_ref, *part_refs = refs[2 * chips + 1 :]
@@ -415,7 +416,7 @@
     count_order = [chips - 1] + list(range(1, chips - 1)) + [0]
     topics, part, *weighted = call(
         functools.partial(first_kernel, chips, cores, count_order),
-        [shape(rows, 2 * topic_count), shape(rows // 2 + 8, 2 * topic_count)]
+        [shape(rows, 2 * topic_count), shape(rows // 2 + 1, 2 * topic_count)]
         + [shape(rows, owned)] * cores,
         wide,
         tall,

time: 75.3 us -> 75.3 us (level)
  no operation moved by 1% of the time
where the time goes in v10:
time: 75.3 us; the launch traced here: 75.2 us
  starting transfers between devices  37.4 us (50%)
  waiting for transfers between devices  28.2 us (37%)
  Pallas kernels  7.18 us (10%)
  local copies, waits for them, and re-layouts  1.67 us (2%)
  between operations  0.77 us (1%)
    ppermute x21, starting transfers between devices, over_chips(): lax.ppermute(array, 'doc', [(c * cores + k, (c ^ step) * cores + (k + ste...  27.7 us
    ppermute x21, waiting for transfers between devices, over_chips(): lax.ppermute(array, 'doc', [(c * cores + k, (c ^ step) * cores + (k + ste...  26.6 us
    ppermute x6, starting transfers between devices, over_pert(): return lax.ppermute(array, 'pert', [(m, m ^ step) for m in range(members)])  7.11 us
    pallas_call x13, Pallas kernels, call(): pl.pallas_call(kernel, out_shape=outs, in_specs=[pl.BlockSpec(memory_spac...  5.87 us
    ppermute x7, starting transfers between devices, over_cores(): return lax.ppermute(array, 'doc', [(d, d ^ 1) for d in range(doc_size)])  2.6 us
    unnamed x9, local copies, waits for them, and re-layouts  1.62 us
    ppermute x7, waiting for transfers between devices, over_cores(): return lax.ppermute(array, 'doc', [(d, d ^ 1) for d in range(doc_size)])  1.56 us
  transfers between devices with their start and end apart: 34, of which 18 were waited for; matrix products, arithmetic and copies ran while one was open for 1% of the time, Pallas kernels for 6%

profile of v10, /device:TPU:0, one launch (start us, length us, event | category | flops | bytes accessed | tf_op | source)
XLA Modules:
  0.0 75.2 jit_solution(37787309857281679)
XLA Ops:
  0.6 0.5 collective-permute-start
  1.2 1.3 %shard_map.87 = (f32[8,4224]{1,0:T(8,128)S(1)}, f32[8,4224]{1,0:T(8,128)S(1)}, f32[8,4224]{1,0:T(8,128)S(1)}, f32[8,4224]{1,0:T(8,128)S(1)}) custom-call(s32[8,128]{1,0:T(8,128)} %bitcast.13, f32[8,64]{1,0:T(8,128)} %bitcast.14, s32[1,64]{1,0:T(1,128)} %perm_hbm.1, s32[8,16384]{1,0:T(8,128)} %bitcast.12), custom_call_target="tpu_custom_call" | custom-call | bytes 1572864 | tf_op jit(solution)/shard_map/pallas_call | solution.py:374
  2.5 4.8 %collective-permute-start.1 = (f32[8,4224]{1,0:T(8,128)S(1)}, f32[8,4224]{1,0:T(8,128)S(1)}, u32[]{:S(2)}, u32[]{:S(2)}) collective-permute-start(f32[8,4224]{1,0:T(8,128)S(1)} %get-tuple-element.47), channel_id=1, source_target_pairs={{0,7},{1,6},{2,5},{3,4},{4,3},{5,2},{6,1},{7,0},{8,15},{9,14},{10,... | collective-permute-start | bytes 405512 | tf_op jit(solution)/shard_map/ppermute | solution.py:358
  7.3 0.6 collective-permute-start.3
  7.9 0.9 %copy-done.1 = s32[4,16384]{1,0:T(4,128)S(1)} copy-done((s32[4,16384]{1,0:T(4,128)S(1)}, s32[4,16384]{1,0:T(4,128)}, u32[]{:S(2)}) %copy-start.1) | copy-done | bytes 262168
  8.9 0.1 shard_map.88
  8.9 1.1 %collective-permute-start.4 = (f32[4,4224]{1,0:T(4,128)S(1)}, f32[4,4224]{1,0:T(4,128)S(1)}, u32[]{:S(2)}, u32[]{:S(2)}) collective-permute-start(f32[4,4224]{1,0:T(4,128)S(1)} %get-tuple-element.51), channel_id=1, source_target_pairs={{0,3},{1,2},{2,1},{3,0},{4,7},{5,6},{6,5},{7,4},{8,11},{9,10},{10,... | collective-permute-start | bytes 202760 | tf_op jit(solution)/shard_map/ppermute | solution.py:358
  10.1 1.1 %shard_map.86 = (bf16[128,4096]{1,0:T(8,128)(2,1)S(1)}, bf16[4096,128]{1,0:T(8,128)(2,1)S(1)}, f32[8,128]{1,0:T(8,128)S(1)}, f32[64,2048]{1,0:T(8,128)S(1)}) custom-call(s32[1,64]{1,0:T(1,128)S(1)} %copy-done.3, f32[64,2048]{1,0:T(8,128)S(1)} %bitcast.11, f32[64,2048]{1,0:T(8,128)S(1)} %collective-permute-done.refs_1_), custom_call_target="tpu_custom_call" | custom-call | bytes 4194304 | tf_op jit(solution)/shard_map/pallas_call | solution.py:37
  11.2 6.8 %collective-permute-done.4.refs_4_.refs_5_.refs_1_ = f32[4,4224]{1,0:T(4,128)S(1)} collective-permute-done((f32[4,4224]{1,0:T(4,128)S(1)}, f32[4,4224]{1,0:T(4,128)S(1)}, u32[]{:S(2)}, u32[]{:S(2)}) %collective-permute-start.4) | collective-permute-done | bytes 67616 | tf_op jit(solution)/shard_map/ppermute | solution.py:358
  18.0 1.2 %collective-permute-done.3.refs_2_.refs_1_ = f32[8,4224]{1,0:T(8,128)S(1)} collective-permute-done((f32[8,4224]{1,0:T(8,128)S(1)}, f32[8,4224]{1,0:T(8,128)S(1)}, u32[]{:S(2)}, u32[]{:S(2)}) %collective-permute-start.3) | collective-permute-done | bytes 135200 | tf_op jit(solution)/shard_map/ppermute | solution.py:358
  19.2 0.5 shard_map.89
  19.7 2.6 %collective-permute-start.5 = (f32[17,128]{1,0:T(8,128)S(1)}, f32[17,128]{1,0:T(8,128)S(1)}, u32[]{:S(2)}, u32[]{:S(2)}) collective-permute-start(f32[17,128]{1,0:T(8,128)S(1)} %get-tuple-element.53.refs_4_), channel_id=1, source_target_pairs={{0,7},{1,6},{2,5},{3,4},{4,3},{5,2},{6,1},{7,0},{8,15},{9,14},{10,... | collective-permute-start | bytes 26120 | tf_op jit(solution)/shard_map/ppermute | solution.py:358
  22.3 1.3 %collective-permute-start.7 = (f32[17,128]{1,0:T(8,128)S(1)}, f32[17,128]{1,0:T(8,128)S(1)}, u32[]{:S(2)}, u32[]{:S(2)}) collective-permute-start(f32[17,128]{1,0:T(8,128)S(1)} %get-tuple-element.53.refs_4_), channel_id=1, source_target_pairs={{0,3},{1,2},{2,1},{3,0},{4,7},{5,6},{6,5},{7,4},{8,11},{9,10},{10,... | collective-permute-start | bytes 26120 | tf_op jit(solution)/shard_map/ppermute | solution.py:358
  23.6 1.1 %collective-permute-done.5.refs_5_ = f32[17,128]{1,0:T(8,128)S(1)} collective-permute-done((f32[17,128]{1,0:T(8,128)S(1)}, f32[17,128]{1,0:T(8,128)S(1)}, u32[]{:S(2)}, u32[]{:S(2)}) %collective-permute-start.5) | collective-permute-done | bytes 8736 | tf_op jit(solution)/shard_map/ppermute | solution.py:358
  24.7 2.2 %collective-permute-done.6.refs_6_ = f32[17,128]{1,0:T(8,128)S(1)} collective-permute-done((f32[17,128]{1,0:T(8,128)S(1)}, f32[17,128]{1,0:T(8,128)S(1)}, u32[]{:S(2)}, u32[]{:S(2)}) %collective-permute-start.6) | collective-permute-done | bytes 8736 | tf_op jit(solution)/shard_map/ppermute | solution.py:358
  26.9 0.6 shard_map.90
  27.5 1.1 %collective-permute-start.8 = (f32[18,128]{1,0:T(8,128)S(1)}, f32[18,128]{1,0:T(8,128)S(1)}, u32[]{:S(2)}, u32[]{:S(2)}) collective-permute-start(f32[18,128]{1,0:T(8,128)S(1)} %get-tuple-element.57), channel_id=1, source_target_pairs={{0,7},{1,6},{2,5},{3,4},{4,3},{5,2},{6,1},{7,0},{8,15},{9,14},{10,... | collective-permute-start | bytes 27656 | tf_op jit(solution)/shard_map/ppermute | solution.py:358
  28.6 0.6 collective-permute-start.9
  29.2 2.2 %collective-permute-start.10 = (f32[16,128]{1,0:T(8,128)S(1)}, f32[16,128]{1,0:T(8,128)S(1)}, u32[]{:S(2)}, u32[]{:S(2)}) collective-permute-start(f32[16,128]{1,0:T(8,128)S(1)} %get-tuple-element.56.refs_5_), channel_id=1, source_target_pairs={{0,3},{1,2},{2,1},{3,0},{4,7},{5,6},{6,5},{7,4},{8,11},{9,10},{10,... | collective-permute-start | bytes 24584 | tf_op jit(solution)/shard_map/ppermute | solution.py:358
  31.4 1.5 %collective-permute-done.10.refs_8_ = f32[16,128]{1,0:T(8,128)S(1)} collective-permute-done((f32[16,128]{1,0:T(8,128)S(1)}, f32[16,128]{1,0:T(8,128)S(1)}, u32[]{:S(2)}, u32[]{:S(2)}) %collective-permute-start.10) | collective-permute-done | bytes 8224 | tf_op jit(solution)/shard_map/ppermute | solution.py:358
  32.8 0.4 collective-permute-done.9.refs_7_
  33.2 0.6 shard_map.91
  33.8 1.4 %collective-permute-start.11 = (f32[16,128]{1,0:T(8,128)S(1)}, f32[16,128]{1,0:T(8,128)S(1)}, u32[]{:S(2)}, u32[]{:S(2)}) collective-permute-start(f32[16,128]{1,0:T(8,128)S(1)} %get-tuple-element.61), channel_id=1, source_target_pairs={{0,7},{1,6},{2,5},{3,4},{4,3},{5,2},{6,1},{7,0},{8,15},{9,14},{10,... | collective-permute-start | bytes 24584 | tf_op jit(solution)/shard_map/ppermute | solution.py:358
  35.2 1.3 %collective-permute-start.12 = (f32[16,128]{1,0:T(8,128)S(1)}, f32[16,128]{1,0:T(8,128)S(1)}, u32[]{:S(2)}, u32[]{:S(2)}) collective-permute-start(f32[16,128]{1,0:T(8,128)S(1)} %get-tuple-element.62), channel_id=1, source_target_pairs={{0,4},{1,5},{2,6},{3,7},{4,0},{5,1},{6,2},{7,3},{8,12},{9,13},{10,... | collective-permute-start | bytes 24584 | tf_op jit(solution)/shard_map/ppermute | solution.py:358
  36.5 1.1 %collective-permute-start.13 = (f32[16,128]{1,0:T(8,128)S(1)}, f32[16,128]{1,0:T(8,128)S(1)}, u32[]{:S(2)}, u32[]{:S(2)}) collective-permute-start(f32[16,128]{1,0:T(8,128)S(1)} %get-tuple-element.60.refs_0_), channel_id=1, source_target_pairs={{0,3},{1,2},{2,1},{3,0},{4,7},{5,6},{6,5},{7,4},{8,11},{9,10},{10,... | collective-permute-start | bytes 24584 | tf_op jit(solution)/shard_map/ppermute | solution.py:358
  37.6 1.1 %collective-permute-done.11.refs_1_ = f32[16,128]{1,0:T(8,128)S(1)} collective-permute-done((f32[16,128]{1,0:T(8,128)S(1)}, f32[16,128]{1,0:T(8,128)S(1)}, u32[]{:S(2)}, u32[]{:S(2)}) %collective-permute-start.11) | collective-permute-done | bytes 8224 | tf_op jit(solution)/shard_map/ppermute | solution.py:358
  38.7 1.1 %collective-permute-done.12.refs_2_ = f32[16,128]{1,0:T(8,128)S(1)} collective-permute-done((f32[16,128]{1,0:T(8,128)S(1)}, f32[16,128]{1,0:T(8,128)S(1)}, u32[]{:S(2)}, u32[]{:S(2)}) %collective-permute-start.12) | collective-permute-done | bytes 8224 | tf_op jit(solution)/shard_map/ppermute | solution.py:358
  39.8 0.1 shard_map.92.topics_ref
  39.8 0.0 collective-permute-start.15
  39.9 0.4 shard_map.93.refs_1_
  40.3 0.8 %collective-permute-done.15.topics_ref = f32[32,128]{1,0:T(8,128)S(1)} collective-permute-done((f32[32,128]{1,0:T(8,128)S(1)}, f32[32,128]{1,0:T(8,128)S(1)}, u32[]{:S(2)}, u32[]{:S(2)}) %collective-permute-start.15) | collective-permute-done | bytes 16416 | tf_op jit(solution)/shard_map/ppermute | solution.py:369
  41.0 0.4 shard_map.94
  41.5 2.5 %collective-permute-start.16 = (f32[64,512]{1,0:T(8,128)S(1)}, f32[64,512]{1,0:T(8,128)S(1)}, u32[]{:S(2)}, u32[]{:S(2)}) collective-permute-start(f32[64,512]{1,0:T(8,128)S(1)} %get-tuple-element.88), channel_id=1, source_target_pairs={{0,24},{8,16},{16,8},{24,0},{1,25},{9,17},{17,9},{25,1},{2,26},{10... | collective-permute-start | bytes 393224 | tf_op jit(solution)/shard_map/ppermute | solution.py:372
  44.0 0.5 collective-permute-start.17
  44.5 0.5 collective-permute-start.18
  45.0 1.4 %collective-permute-start.19 = (f32[4,4224]{1,0:T(4,128)S(1)}, f32[4,4224]{1,0:T(4,128)S(1)}, u32[]{:S(2)}, u32[]{:S(2)}) collective-permute-start(f32[4,4224]{1,0:T(4,128)S(1)} %get-tuple-element.70), channel_id=1, source_target_pairs={{0,4},{1,5},{2,6},{3,7},{4,0},{5,1},{6,2},{7,3},{8,12},{9,13},{10,... | collective-permute-start | bytes 202760 | tf_op jit(solution)/shard_map/ppermute | solution.py:358
  46.5 4.5 %collective-permute-done.19.refs_4_.refs_6_.refs_2_ = f32[4,4224]{1,0:T(4,128)S(1)} collective-permute-done((f32[4,4224]{1,0:T(4,128)S(1)}, f32[4,4224]{1,0:T(4,128)S(1)}, u32[]{:S(2)}, u32[]{:S(2)}) %collective-permute-start.19) | collective-permute-done | bytes 67616 | tf_op jit(solution)/shard_map/ppermute | solution.py:358
  51.0 0.1 shard_map.95.refs_0_
  51.0 2.5 %collective-permute-start.20 = (f32[64,512]{1,0:T(8,128)S(1)}, f32[64,512]{1,0:T(8,128)S(1)}, u32[]{:S(2)}, u32[]{:S(2)}) collective-permute-start(f32[64,512]{1,0:T(8,128)S(1)} %shard_map.95.refs_0_), channel_id=1, source_target_pairs={{0,24},{8,16},{16,8},{24,0},{1,25},{9,17},{17,9},{25,1},{2,26},{10... | collective-permute-start | bytes 393224 | tf_op jit(solution)/shard_map/ppermute | solution.py:372
  53.5 0.5 collective-permute-start.24
  54.1 0.5 collective-permute-start.26
  54.6 0.4 collective-permute-start.21
  55.0 1.5 %collective-permute-start.22 = (f32[64,512]{1,0:T(8,128)S(1)}, f32[64,512]{1,0:T(8,128)S(1)}, u32[]{:S(2)}, u32[]{:S(2)}) collective-permute-start(f32[64,512]{1,0:T(8,128)S(1)} %shard_map.95.refs_0_), channel_id=1, source_target_pairs={{0,1},{1,0},{2,3},{3,2},{4,5},{5,4},{6,7},{7,6},{8,9},{9,8},{10,11... | collective-permute-start | bytes 393224 | tf_op jit(solution)/shard_map/ppermute | solution.py:369
  56.5 3.7 %collective-permute-done.21.refs_7_.refs_3_ = f32[4,4224]{1,0:T(4,128)S(1)} collective-permute-done((f32[4,4224]{1,0:T(4,128)S(1)}, f32[4,4224]{1,0:T(4,128)S(1)}, u32[]{:S(2)}, u32[]{:S(2)}) %collective-permute-start.21) | collective-permute-done | bytes 67616 | tf_op jit(solution)/shard_map/ppermute | solution.py:358
  60.2 0.5 collective-permute-start.25
  60.7 0.1 collective-permute-start.27
  60.7 0.5 shard_map.96
  61.2 0.3 collective-permute-done.23.refs_1_
  61.5 0.2 collective-permute-done.25.refs_2_
  61.7 0.3 collective-permute-done.27.refs_3_
  62.0 0.5 shard_map.97
  62.5 1.6 %collective-permute-start.28 = (f32[16,128]{1,0:T(8,128)S(1)}, f32[16,128]{1,0:T(8,128)S(1)}, u32[]{:S(2)}, u32[]{:S(2)}) collective-permute-start(f32[16,128]{1,0:T(8,128)S(1)} %get-tuple-element.76.refs_4_), channel_id=1, source_target_pairs={{0,7},{1,6},{2,5},{3,4},{4,3},{5,2},{6,1},{7,0},{8,15},{9,14},{10,... | collective-permute-start | bytes 24584 | tf_op jit(solution)/shard_map/ppermute | solution.py:358
  64.1 0.6 collective-permute-start.29
  64.7 1.7 %collective-permute-start.30 = (f32[16,128]{1,0:T(8,128)S(1)}, f32[16,128]{1,0:T(8,128)S(1)}, u32[]{:S(2)}, u32[]{:S(2)}) collective-permute-start(f32[16,128]{1,0:T(8,128)S(1)} %get-tuple-element.76.refs_4_), channel_id=1, source_target_pairs={{0,3},{1,2},{2,1},{3,0},{4,7},{5,6},{6,5},{7,4},{8,11},{9,10},{10,... | collective-permute-start | bytes 24584 | tf_op jit(solution)/shard_map/ppermute | solution.py:358
  66.3 1.0 %collective-permute-done.28.refs_5_ = f32[16,128]{1,0:T(8,128)S(1)} collective-permute-done((f32[16,128]{1,0:T(8,128)S(1)}, f32[16,128]{1,0:T(8,128)S(1)}, u32[]{:S(2)}, u32[]{:S(2)}) %collective-permute-start.28) | collective-permute-done | bytes 8224 | tf_op jit(solution)/shard_map/ppermute | solution.py:358
  67.4 1.2 %collective-permute-done.29.refs_6_ = f32[16,128]{1,0:T(8,128)S(1)} collective-permute-done((f32[16,128]{1,0:T(8,128)S(1)}, f32[16,128]{1,0:T(8,128)S(1)}, u32[]{:S(2)}, u32[]{:S(2)}) %collective-permute-start.29) | collective-permute-done | bytes 8224 | tf_op jit(solution)/shard_map/ppermute | solution.py:358
  68.6 0.5 shard_map.98
  69.2 0.9 %collective-permute-start.31 = (f32[4,128]{1,0:T(4,128)S(1)}, f32[4,128]{1,0:T(4,128)S(1)}, u32[]{:S(2)}, u32[]{:S(2)}) collective-permute-start(f32[4,128]{1,0:T(4,128)S(1)} %get-tuple-element.83), channel_id=1, source_target_pairs={{0,7},{1,6},{2,5},{3,4},{4,3},{5,2},{6,1},{7,0},{8,15},{9,14},{10,... | collective-permute-start | bytes 6152 | tf_op jit(solution)/shard_map/ppermute | solution.py:358
  70.1 1.4 %collective-permute-start.32 = (f32[4,128]{1,0:T(4,128)S(1)}, f32[4,128]{1,0:T(4,128)S(1)}, u32[]{:S(2)}, u32[]{:S(2)}) collective-permute-start(f32[4,128]{1,0:T(4,128)S(1)} %get-tuple-element.84), channel_id=1, source_target_pairs={{0,4},{1,5},{2,6},{3,7},{4,0},{5,1},{6,2},{7,3},{8,12},{9,13},{10,... | collective-permute-start | bytes 6152 | tf_op jit(solution)/shard_map/ppermute | solution.py:358
  71.5 1.5 %collective-permute-start.33 = (f32[4,128]{1,0:T(4,128)S(1)}, f32[4,128]{1,0:T(4,128)S(1)}, u32[]{:S(2)}, u32[]{:S(2)}) collective-permute-start(f32[4,128]{1,0:T(4,128)S(1)} %get-tuple-element.85), channel_id=1, source_target_pairs={{0,3},{1,2},{2,1},{3,0},{4,7},{5,6},{6,5},{7,4},{8,11},{9,10},{10,... | collective-permute-start | bytes 6152 | tf_op jit(solution)/shard_map/ppermute | solution.py:358
  73.0 0.7 copy.9
  73.7 0.3 collective-permute-done.31.refs_1_
  74.0 0.6 collective-permute-done.32.refs_2_
  74.6 0.6 shard_map.99
  (28 shorter events, 0.1 us)
Async XLA Ops:
  0.6 9.5 %copy-start = (f32[1,2048,64]{1,2,0:T(8,128)S(1)}, f32[1,2048,64]{1,2,0:T(8,128)}, u32[]{:S(2)}) copy-start(f32[1,2048,64]{1,2,0:T(8,128)} %param.10) | copy-start | bytes 1572868
  0.6 9.4 %collective-permute-start = (f32[64,2048]{1,0:T(8,128)}, f32[64,2048]{1,0:T(8,128)S(1)}, u32[]{:S(2)}, u32[]{:S(2)}) collective-permute-start(f32[64,2048]{1,0:T(8,128)} %bitcast.10), channel_id=1, source_target_pairs={{0,1},{1,0},{2,3},{3,2},{4,5},{5,4},{6,7},{7,6},{8,9},{9,8},{10,11... | collective-permute-start | bytes 1572872 | tf_op jit(solution)/shard_map/ppermute | solution.py:369
  2.5 5.4 %copy-start.2 = (f32[4,64]{1,0:T(4,128)S(1)}, f32[4,64]{1,0:T(4,128)}, u32[]{:S(2)}) copy-start(f32[4,64]{1,0:T(4,128)} %topics_ref.1) | copy-start | bytes 3076
  2.5 15.5 %collective-permute-start.1 = (f32[8,4224]{1,0:T(8,128)S(1)}, f32[8,4224]{1,0:T(8,128)S(1)}, u32[]{:S(2)}, u32[]{:S(2)}) collective-permute-start(f32[8,4224]{1,0:T(8,128)S(1)} %get-tuple-element.47), channel_id=1, source_target_pairs={{0,7},{1,6},{2,5},{3,4},{4,3},{5,2},{6,1},{7,0},{8,15},{9,14},{10,... | collective-permute-start | bytes 405512 | tf_op jit(solution)/shard_map/ppermute | solution.py:358
  7.3 10.7 %collective-permute-start.2 = (f32[8,4224]{1,0:T(8,128)S(1)}, f32[8,4224]{1,0:T(8,128)S(1)}, u32[]{:S(2)}, u32[]{:S(2)}) collective-permute-start(f32[8,4224]{1,0:T(8,128)S(1)} %get-tuple-element.48), channel_id=1, source_target_pairs={{0,3},{1,2},{2,1},{3,0},{4,7},{5,6},{6,5},{7,4},{8,11},{9,10},{10,... | collective-permute-start | bytes 405512 | tf_op jit(solution)/shard_map/ppermute | solution.py:358
  7.3 11.9 %collective-permute-start.3 = (f32[8,4224]{1,0:T(8,128)S(1)}, f32[8,4224]{1,0:T(8,128)S(1)}, u32[]{:S(2)}, u32[]{:S(2)}) collective-permute-start(f32[8,4224]{1,0:T(8,128)S(1)} %get-tuple-element.49), channel_id=1, source_target_pairs={{0,4},{1,5},{2,6},{3,7},{4,0},{5,1},{6,2},{7,3},{8,12},{9,13},{10,... | collective-permute-start | bytes 405512 | tf_op jit(solution)/shard_map/ppermute | solution.py:358
  7.9 1.0 %copy-start.1 = (s32[4,16384]{1,0:T(4,128)S(1)}, s32[4,16384]{1,0:T(4,128)}, u32[]{:S(2)}) copy-start(s32[4,16384]{1,0:T(4,128)} %counts_ref.1) | copy-start | bytes 786436
  8.9 1.2 %copy-start.3 = (s32[1,64]{1,0:T(1,128)S(1)}, s32[1,64]{1,0:T(1,128)}, u32[]{:S(2)}) copy-start(s32[1,64]{1,0:T(1,128)} %perm_hbm.1) | copy-start | bytes 772
  8.9 9.0 %collective-permute-start.4 = (f32[4,4224]{1,0:T(4,128)S(1)}, f32[4,4224]{1,0:T(4,128)S(1)}, u32[]{:S(2)}, u32[]{:S(2)}) collective-permute-start(f32[4,4224]{1,0:T(4,128)S(1)} %get-tuple-element.51), channel_id=1, source_target_pairs={{0,3},{1,2},{2,1},{3,0},{4,7},{5,6},{6,5},{7,4},{8,11},{9,10},{10,... | collective-permute-start | bytes 202760 | tf_op jit(solution)/shard_map/ppermute | solution.py:358
  19.7 20.0 %collective-permute-start.14 = (f32[32,2048]{1,0:T(8,128)S(1)}, f32[32,2048]{1,0:T(8,128)S(1)}, u32[]{:S(2)}, u32[]{:S(2)}) collective-permute-start(f32[32,2048]{1,0:T(8,128)S(1)} %get-tuple-element.63), channel_id=1, source_target_pairs={{0,1},{1,0},{2,3},{3,2},{4,5},{5,4},{6,7},{7,6},{8,9},{9,8},{10,11... | collective-permute-start | bytes 786440 | tf_op jit(solution)/shard_map/ppermute | solution.py:369
  19.7 5.0 %collective-permute-start.5 = (f32[17,128]{1,0:T(8,128)S(1)}, f32[17,128]{1,0:T(8,128)S(1)}, u32[]{:S(2)}, u32[]{:S(2)}) collective-permute-start(f32[17,128]{1,0:T(8,128)S(1)} %get-tuple-element.53.refs_4_), channel_id=1, source_target_pairs={{0,7},{1,6},{2,5},{3,4},{4,3},{5,2},{6,1},{7,0},{8,15},{9,14},{10,... | collective-permute-start | bytes 26120 | tf_op jit(solution)/shard_map/ppermute | solution.py:358
  22.3 4.6 %collective-permute-start.6 = (f32[17,128]{1,0:T(8,128)S(1)}, f32[17,128]{1,0:T(8,128)S(1)}, u32[]{:S(2)}, u32[]{:S(2)}) collective-permute-start(f32[17,128]{1,0:T(8,128)S(1)} %get-tuple-element.53.refs_4_), channel_id=1, source_target_pairs={{0,4},{1,5},{2,6},{3,7},{4,0},{5,1},{6,2},{7,3},{8,12},{9,13},{10,... | collective-permute-start | bytes 26120 | tf_op jit(solution)/shard_map/ppermute | solution.py:358
  22.3 4.6 %collective-permute-start.7 = (f32[17,128]{1,0:T(8,128)S(1)}, f32[17,128]{1,0:T(8,128)S(1)}, u32[]{:S(2)}, u32[]{:S(2)}) collective-permute-start(f32[17,128]{1,0:T(8,128)S(1)} %get-tuple-element.53.refs_4_), channel_id=1, source_target_pairs={{0,3},{1,2},{2,1},{3,0},{4,7},{5,6},{6,5},{7,4},{8,11},{9,10},{10,... | collective-permute-start | bytes 26120 | tf_op jit(solution)/shard_map/ppermute | solution.py:358
  27.5 5.7 %collective-permute-start.8 = (f32[18,128]{1,0:T(8,128)S(1)}, f32[18,128]{1,0:T(8,128)S(1)}, u32[]{:S(2)}, u32[]{:S(2)}) collective-permute-start(f32[18,128]{1,0:T(8,128)S(1)} %get-tuple-element.57), channel_id=1, source_target_pairs={{0,7},{1,6},{2,5},{3,4},{4,3},{5,2},{6,1},{7,0},{8,15},{9,14},{10,... | collective-permute-start | bytes 27656 | tf_op jit(solution)/shard_map/ppermute | solution.py:358
  28.6 4.6 %collective-permute-start.9 = (f32[17,128]{1,0:T(8,128)S(1)}, f32[17,128]{1,0:T(8,128)S(1)}, u32[]{:S(2)}, u32[]{:S(2)}) collective-permute-start(f32[17,128]{1,0:T(8,128)S(1)} %get-tuple-element.58), channel_id=1, source_target_pairs={{0,4},{1,5},{2,6},{3,7},{4,0},{5,1},{6,2},{7,3},{8,12},{9,13},{10,... | collective-permute-start | bytes 26120 | tf_op jit(solution)/shard_map/ppermute | solution.py:358
  29.2 3.6 %collective-permute-start.10 = (f32[16,128]{1,0:T(8,128)S(1)}, f32[16,128]{1,0:T(8,128)S(1)}, u32[]{:S(2)}, u32[]{:S(2)}) collective-permute-start(f32[16,128]{1,0:T(8,128)S(1)} %get-tuple-element.56.refs_5_), channel_id=1, source_target_pairs={{0,3},{1,2},{2,1},{3,0},{4,7},{5,6},{6,5},{7,4},{8,11},{9,10},{10,... | collective-permute-start | bytes 24584 | tf_op jit(solution)/shard_map/ppermute | solution.py:358
  33.8 4.9 %collective-permute-start.11 = (f32[16,128]{1,0:T(8,128)S(1)}, f32[16,128]{1,0:T(8,128)S(1)}, u32[]{:S(2)}, u32[]{:S(2)}) collective-permute-start(f32[16,128]{1,0:T(8,128)S(1)} %get-tuple-element.61), channel_id=1, source_target_pairs={{0,7},{1,6},{2,5},{3,4},{4,3},{5,2},{6,1},{7,0},{8,15},{9,14},{10,... | collective-permute-start | bytes 24584 | tf_op jit(solution)/shard_map/ppermute | solution.py:358
  35.2 4.5 %collective-permute-start.12 = (f32[16,128]{1,0:T(8,128)S(1)}, f32[16,128]{1,0:T(8,128)S(1)}, u32[]{:S(2)}, u32[]{:S(2)}) collective-permute-start(f32[16,128]{1,0:T(8,128)S(1)} %get-tuple-element.62), channel_id=1, source_target_pairs={{0,4},{1,5},{2,6},{3,7},{4,0},{5,1},{6,2},{7,3},{8,12},{9,13},{10,... | collective-permute-start | bytes 24584 | tf_op jit(solution)/shard_map/ppermute | solution.py:358
  36.5 3.3 %collective-permute-start.13 = (f32[16,128]{1,0:T(8,128)S(1)}, f32[16,128]{1,0:T(8,128)S(1)}, u32[]{:S(2)}, u32[]{:S(2)}) collective-permute-start(f32[16,128]{1,0:T(8,128)S(1)} %get-tuple-element.60.refs_0_), channel_id=1, source_target_pairs={{0,3},{1,2},{2,1},{3,0},{4,7},{5,6},{6,5},{7,4},{8,11},{9,10},{10,... | collective-permute-start | bytes 24584 | tf_op jit(solution)/shard_map/ppermute | solution.py:358
  39.8 1.2 %collective-permute-start.15 = (f32[32,128]{1,0:T(8,128)S(1)}, f32[32,128]{1,0:T(8,128)S(1)}, u32[]{:S(2)}, u32[]{:S(2)}) collective-permute-start(f32[32,128]{1,0:T(8,128)S(1)} %shard_map.92.topics_ref), channel_id=1, source_target_pairs={{0,1},{1,0},{2,3},{3,2},{4,5},{5,4},{6,7},{7,6},{8,9},{9,8},{10,11... | collective-permute-start | bytes 49160 | tf_op jit(solution)/shard_map/ppermute | solution.py:369
  41.5 9.5 %collective-permute-start.16 = (f32[64,512]{1,0:T(8,128)S(1)}, f32[64,512]{1,0:T(8,128)S(1)}, u32[]{:S(2)}, u32[]{:S(2)}) collective-permute-start(f32[64,512]{1,0:T(8,128)S(1)} %get-tuple-element.88), channel_id=1, source_target_pairs={{0,24},{8,16},{16,8},{24,0},{1,25},{9,17},{17,9},{25,1},{2,26},{10... | collective-permute-start | bytes 393224 | tf_op jit(solution)/shard_map/ppermute | solution.py:372
  44.0 7.0 %collective-permute-start.17 = (f32[64,512]{1,0:T(8,128)S(1)}, f32[64,512]{1,0:T(8,128)S(1)}, u32[]{:S(2)}, u32[]{:S(2)}) collective-permute-start(f32[64,512]{1,0:T(8,128)S(1)} %get-tuple-element.87), channel_id=1, source_target_pairs={{0,16},{8,24},{16,0},{24,8},{1,17},{9,25},{17,1},{25,9},{2,18},{10... | collective-permute-start | bytes 393224 | tf_op jit(solution)/shard_map/ppermute | solution.py:372
  44.5 6.4 %collective-permute-start.18 = (f32[64,512]{1,0:T(8,128)S(1)}, f32[64,512]{1,0:T(8,128)S(1)}, u32[]{:S(2)}, u32[]{:S(2)}) collective-permute-start(f32[64,512]{1,0:T(8,128)S(1)} %get-tuple-element.86), channel_id=1, source_target_pairs={{0,8},{8,0},{16,24},{24,16},{1,9},{9,1},{17,25},{25,17},{2,10},{10... | collective-permute-start | bytes 393224 | tf_op jit(solution)/shard_map/ppermute | solution.py:372
  45.0 5.9 %collective-permute-start.19 = (f32[4,4224]{1,0:T(4,128)S(1)}, f32[4,4224]{1,0:T(4,128)S(1)}, u32[]{:S(2)}, u32[]{:S(2)}) collective-permute-start(f32[4,4224]{1,0:T(4,128)S(1)} %get-tuple-element.70), channel_id=1, source_target_pairs={{0,4},{1,5},{2,6},{3,7},{4,0},{5,1},{6,2},{7,3},{8,12},{9,13},{10,... | collective-permute-start | bytes 202760 | tf_op jit(solution)/shard_map/ppermute | solution.py:358
  51.0 9.1 %collective-permute-start.20 = (f32[64,512]{1,0:T(8,128)S(1)}, f32[64,512]{1,0:T(8,128)S(1)}, u32[]{:S(2)}, u32[]{:S(2)}) collective-permute-start(f32[64,512]{1,0:T(8,128)S(1)} %shard_map.95.refs_0_), channel_id=1, source_target_pairs={{0,24},{8,16},{16,8},{24,0},{1,25},{9,17},{17,9},{25,1},{2,26},{10... | collective-permute-start | bytes 393224 | tf_op jit(solution)/shard_map/ppermute | solution.py:372
  53.5 6.6 %collective-permute-start.24 = (f32[64,512]{1,0:T(8,128)S(1)}, f32[64,512]{1,0:T(8,128)S(1)}, u32[]{:S(2)}, u32[]{:S(2)}) collective-permute-start(f32[64,512]{1,0:T(8,128)S(1)} %shard_map.95.refs_0_), channel_id=1, source_target_pairs={{0,16},{8,24},{16,0},{24,8},{1,17},{9,25},{17,1},{25,9},{2,18},{10... | collective-permute-start | bytes 393224 | tf_op jit(solution)/shard_map/ppermute | solution.py:372
  54.1 6.6 %collective-permute-start.26 = (f32[64,512]{1,0:T(8,128)S(1)}, f32[64,512]{1,0:T(8,128)S(1)}, u32[]{:S(2)}, u32[]{:S(2)}) collective-permute-start(f32[64,512]{1,0:T(8,128)S(1)} %shard_map.95.refs_0_), channel_id=1, source_target_pairs={{0,8},{8,0},{16,24},{24,16},{1,9},{9,1},{17,25},{25,17},{2,10},{10... | collective-permute-start | bytes 393224 | tf_op jit(solution)/shard_map/ppermute | solution.py:372
  54.6 5.6 %collective-permute-start.21 = (f32[4,4224]{1,0:T(4,128)S(1)}, f32[4,4224]{1,0:T(4,128)S(1)}, u32[]{:S(2)}, u32[]{:S(2)}) collective-permute-start(f32[4,4224]{1,0:T(4,128)S(1)} %get-tuple-element.72), channel_id=1, source_target_pairs={{0,7},{1,6},{2,5},{3,4},{4,3},{5,2},{6,1},{7,0},{8,15},{9,14},{10,... | collective-permute-start | bytes 202760 | tf_op jit(solution)/shard_map/ppermute | solution.py:358
  55.0 6.2 %collective-permute-start.22 = (f32[64,512]{1,0:T(8,128)S(1)}, f32[64,512]{1,0:T(8,128)S(1)}, u32[]{:S(2)}, u32[]{:S(2)}) collective-permute-start(f32[64,512]{1,0:T(8,128)S(1)} %shard_map.95.refs_0_), channel_id=1, source_target_pairs={{0,1},{1,0},{2,3},{3,2},{4,5},{5,4},{6,7},{7,6},{8,9},{9,8},{10,11... | collective-permute-start | bytes 393224 | tf_op jit(solution)/shard_map/ppermute | solution.py:369
  60.2 1.3 %collective-permute-start.23 = (f32[64,512]{1,0:T(8,128)S(1)}, f32[64,512]{1,0:T(8,128)S(1)}, u32[]{:S(2)}, u32[]{:S(2)}) collective-permute-start(f32[64,512]{1,0:T(8,128)S(1)} %collective-permute-done.20.refs_1_), channel_id=1, source_target_pairs={{0,1},{1,0},{2,3},{3,2},{4,5},{5,4},{6,7},{7,6},{8,9},{9,8},{10,11... | collective-permute-start | bytes 393224 | tf_op jit(solution)/shard_map/ppermute | solution.py:369
  60.2 1.5 %collective-permute-start.25 = (f32[64,512]{1,0:T(8,128)S(1)}, f32[64,512]{1,0:T(8,128)S(1)}, u32[]{:S(2)}, u32[]{:S(2)}) collective-permute-start(f32[64,512]{1,0:T(8,128)S(1)} %collective-permute-done.24.refs_2_), channel_id=1, source_target_pairs={{0,1},{1,0},{2,3},{3,2},{4,5},{5,4},{6,7},{7,6},{8,9},{9,8},{10,11... | collective-permute-start | bytes 393224 | tf_op jit(solution)/shard_map/ppermute | solution.py:369
  60.7 1.3 %collective-permute-start.27 = (f32[64,512]{1,0:T(8,128)S(1)}, f32[64,512]{1,0:T(8,128)S(1)}, u32[]{:S(2)}, u32[]{:S(2)}) collective-permute-start(f32[64,512]{1,0:T(8,128)S(1)} %collective-permute-done.26.refs_3_), channel_id=1, source_target_pairs={{0,1},{1,0},{2,3},{3,2},{4,5},{5,4},{6,7},{7,6},{8,9},{9,8},{10,11... | collective-permute-start | bytes 393224 | tf_op jit(solution)/shard_map/ppermute | solution.py:369
  62.5 4.9 %collective-permute-start.28 = (f32[16,128]{1,0:T(8,128)S(1)}, f32[16,128]{1,0:T(8,128)S(1)}, u32[]{:S(2)}, u32[]{:S(2)}) collective-permute-start(f32[16,128]{1,0:T(8,128)S(1)} %get-tuple-element.76.refs_4_), channel_id=1, source_target_pairs={{0,7},{1,6},{2,5},{3,4},{4,3},{5,2},{6,1},{7,0},{8,15},{9,14},{10,... | collective-permute-start | bytes 24584 | tf_op jit(solution)/shard_map/ppermute | solution.py:358
  64.1 4.5 %collective-permute-start.29 = (f32[16,128]{1,0:T(8,128)S(1)}, f32[16,128]{1,0:T(8,128)S(1)}, u32[]{:S(2)}, u32[]{:S(2)}) collective-permute-start(f32[16,128]{1,0:T(8,128)S(1)} %get-tuple-element.76.refs_4_), channel_id=1, source_target_pairs={{0,4},{1,5},{2,6},{3,7},{4,0},{5,1},{6,2},{7,3},{8,12},{9,13},{10,... | collective-permute-start | bytes 24584 | tf_op jit(solution)/shard_map/ppermute | solution.py:358
  64.7 3.9 %collective-permute-start.30 = (f32[16,128]{1,0:T(8,128)S(1)}, f32[16,128]{1,0:T(8,128)S(1)}, u32[]{:S(2)}, u32[]{:S(2)}) collective-permute-start(f32[16,128]{1,0:T(8,128)S(1)} %get-tuple-element.76.refs_4_), channel_id=1, source_target_pairs={{0,3},{1,2},{2,1},{3,0},{4,7},{5,6},{6,5},{7,4},{8,11},{9,10},{10,... | collective-permute-start | bytes 24584 | tf_op jit(solution)/shard_map/ppermute | solution.py:358
  69.2 4.8 %collective-permute-start.31 = (f32[4,128]{1,0:T(4,128)S(1)}, f32[4,128]{1,0:T(4,128)S(1)}, u32[]{:S(2)}, u32[]{:S(2)}) collective-permute-start(f32[4,128]{1,0:T(4,128)S(1)} %get-tuple-element.83), channel_id=1, source_target_pairs={{0,7},{1,6},{2,5},{3,4},{4,3},{5,2},{6,1},{7,0},{8,15},{9,14},{10,... | collective-permute-start | bytes 6152 | tf_op jit(solution)/shard_map/ppermute | solution.py:358
  70.1 4.5 %collective-permute-start.32 = (f32[4,128]{1,0:T(4,128)S(1)}, f32[4,128]{1,0:T(4,128)S(1)}, u32[]{:S(2)}, u32[]{:S(2)}) collective-permute-start(f32[4,128]{1,0:T(4,128)S(1)} %get-tuple-element.84), channel_id=1, source_target_pairs={{0,4},{1,5},{2,6},{3,7},{4,0},{5,1},{6,2},{7,3},{8,12},{9,13},{10,... | collective-permute-start | bytes 6152 | tf_op jit(solution)/shard_map/ppermute | solution.py:358
  71.5 3.1 %collective-permute-start.33 = (f32[4,128]{1,0:T(4,128)S(1)}, f32[4,128]{1,0:T(4,128)S(1)}, u32[]{:S(2)}, u32[]{:S(2)}) collective-permute-start(f32[4,128]{1,0:T(4,128)S(1)} %get-tuple-element.85), channel_id=1, source_target_pairs={{0,3},{1,2},{2,1},{3,0},{4,7},{5,6},{6,5},{7,4},{8,11},{9,10},{10,... | collective-permute-start | bytes 6152 | tf_op jit(solution)/shard_map/ppermute | solution.py:358
